TPU v7x, 32 devices: a whole 2x2x4 slice. The times are simulated.
32 devices in a mesh: seq: 4 (over x, core), fsdp: 8 (over z, y).
Axes of the slice: x: 2, y: 2, z: 4, core: 2. Of those that a mesh axis runs over, the one named last changes fastest.
Arguments:
- tokens: bfloat16 [8, 1024, 1536], P('fsdp', 'seq'), may hold values from -6 to 6
- positions: int32 [8, 1024], P('fsdp'), may hold values from 0 to 1021, as said below
- w_query: bfloat16 [1536, 1536], P('fsdp'), may hold values from -0.15625 to 0.15625
- w_key: bfloat16 [1536, 256], P('fsdp'), may hold values from -0.15625 to 0.15625
- w_value: bfloat16 [1536, 256], P('fsdp'), may hold values from -0.15625 to 0.15625
- w_output: bfloat16 [1536, 1536], P('fsdp'), may hold values from -0.625 to 0.625
- gate_up: bfloat16 [1536, 2, 8960], P('fsdp'), may hold values from -0.15625 to 0.15625
- w_down: bfloat16 [1536, 8960], P('fsdp'), may hold values from -0.0625 to 0.0625
- bias_query: bfloat16 [1536], P('fsdp'), may hold values from -3 to 3
- bias_key: bfloat16 [256], P('fsdp'), may hold values from -3 to 3
- bias_value: bfloat16 [256], P('fsdp'), may hold values from -1.1953125 to 1.1953125
- gain_attn: bfloat16 [1536], P('fsdp'), may hold values from 0.5 to 1.5
- gain_mlp: bfloat16 [1536], P('fsdp'), may hold values from 0.5 to 1.5
- cotangent: bfloat16 [8, 1024, 1536], P('fsdp', 'seq'), may hold values from -6 to 6
Outputs:
- mixed: bfloat16 [8, 1024, 1536], P('fsdp', 'seq')
- d_tokens: float32 [8, 1024, 1536], P('fsdp', 'seq')
- d_w_query: float32 [1536, 1536], P(('seq', 'fsdp'))
- d_w_key: float32 [1536, 256], P(('seq', 'fsdp'))
- d_w_value: float32 [1536, 256], P(('seq', 'fsdp'))
- d_w_output: float32 [1536, 1536], P(('seq', 'fsdp'))
- d_gate_up: float32 [1536, 2, 8960], P(('seq', 'fsdp'))
- d_w_down: float32 [1536, 8960], P(('seq', 'fsdp'))
- d_bias_query: float32 [1536], P(('seq', 'fsdp'))
- d_bias_key: float32 [256], P(('seq', 'fsdp'))
- d_bias_value: float32 [256], P(('seq', 'fsdp'))
- d_gain_attn: float32 [1536], P(('seq', 'fsdp'))
- d_gain_mlp: float32 [1536], P(('seq', 'fsdp'))
Inputs may be any that keep to these rules, and one draw needn't show every extreme that they name: `positions`: each row counts up by one from 0 within each document of its sequence, and a 0 starts a new document. Every row starts with 0, and holds one document that begins at an index from 1 to 128 and whose successor begins at an index from 896 to 1023. In some row that document begins at index 1 and its successor at index 1023.
All inputs are finite; a program needn't handle non-finite values.
Results may differ from a plain program's by a relative error of at most 0.025.
Values may be sent and summed in bfloat16 or wider, within the bound.
No kernel may reach another device: no remote copies, remote signals or barrier semaphores. Data moves between devices by JAX's collectives and lax.ppermute only.
A program may use at most 640 MiB of HBM per device.

v0:
```python
import jax
import jax.numpy as jnp
from jax import lax
from jax.sharding import PartitionSpec as P

D = 1536
HEADS = 12
KV = 2
HD = 128
FF = 8960


epsilon = 1e-06
rope_base = 1000000.0
masked_value = -1e30


def rope_tables(positions):
    ladder = jnp.arange(HD // 2, dtype=jnp.float32)
    inverse = rope_base ** (-2.0 * ladder / HD)
    angles = positions.astype(jnp.float32)[:, None] * inverse[None, :]
    angles = jnp.concatenate([angles, angles], axis=-1)
    return (jnp.cos(angles), jnp.sin(angles))


def rotate(value, cosine, sine):
    halfway = HD // 2
    turned = jnp.concatenate([-value[..., halfway:], value[..., :halfway]], axis=-1)
    return value * cosine[:, None, :] + turned * sine[:, None, :]


def unrotate(grad, cosine, sine):
    halfway = HD // 2
    scaled = grad * sine[:, None, :]
    turned = jnp.concatenate([scaled[..., halfway:], -scaled[..., :halfway]], axis=-1)
    return grad * cosine[:, None, :] + turned


def rms_forward(value, gain):
    factor = lax.rsqrt(jnp.mean(value * value, axis=-1, keepdims=True) + epsilon)
    return (value * factor * gain, factor)


def rms_backward(value, factor, gain, grad):
    unit = value * factor
    weighted = grad * gain
    grad_gain = jnp.sum(grad * unit, axis=0)
    inner = jnp.mean(weighted * unit, axis=-1, keepdims=True)
    return (factor * (weighted - unit * inner), grad_gain)


def masked_scores(query_block, keys, documents, first_row):
    block_rows = query_block.shape[0]
    query_place = first_row + jnp.arange(block_rows, dtype=jnp.int32)
    key_place = jnp.arange(keys.shape[0], dtype=jnp.int32)
    query_docs = lax.dynamic_slice_in_dim(documents, first_row, block_rows)
    allowed = (key_place[None, :] <= query_place[:, None]) & (
        documents[None, :] == query_docs[:, None]
    )
    raw = jnp.einsum("qhd,kd->hqk", query_block, keys, preferred_element_type=jnp.float32) * HD ** (
        -0.5
    )
    return jnp.where(allowed[None], raw, masked_value)


def attention_forward(queries, keys, values, documents):
    length = queries.shape[0]
    block_rows = min(512, length)

    def one_block(block_index):
        first_row = block_index * block_rows
        query_block = lax.dynamic_slice_in_dim(queries, first_row, block_rows, 0)
        scores = masked_scores(query_block, keys, documents, first_row)
        row_top = jnp.max(scores, axis=-1, keepdims=True)
        shifted = jnp.exp(scores - row_top)
        row_total = jnp.sum(shifted, axis=-1, keepdims=True)
        probability = (shifted / row_total).astype(jnp.bfloat16)
        outcome = jnp.einsum("hqk,kd->qhd", probability, values, preferred_element_type=jnp.float32)
        return (outcome.astype(jnp.bfloat16), row_top, row_total)

    outcome, tops, totals = lax.map(one_block, jnp.arange(length // block_rows, dtype=jnp.int32))
    return (outcome.reshape(queries.shape), tops, totals)


def attention_backward(queries, keys, values, documents, tops, totals, grad_attended):
    length = queries.shape[0]
    block_rows = min(512, length)
    scaling = HD ** (-0.5)

    def one_block(running, inputs_block):
        block_index, row_top, row_total = inputs_block
        first_row = block_index * block_rows
        query_block = lax.dynamic_slice_in_dim(queries, first_row, block_rows, 0)
        grad_block = lax.dynamic_slice_in_dim(grad_attended, first_row, block_rows, 0)
        scores = masked_scores(query_block, keys, documents, first_row)
        probability = jnp.exp(scores - row_top) / row_total
        prob_low = probability.astype(jnp.bfloat16)
        grad_prob = jnp.einsum(
            "qhd,kd->hqk", grad_block, values, preferred_element_type=jnp.float32
        )
        grad_scores = probability * (
            grad_prob - jnp.sum(probability * grad_prob, axis=-1, keepdims=True)
        )
        grad_low = grad_scores.astype(jnp.bfloat16)
        grad_query = (
            jnp.einsum("hqk,kd->qhd", grad_low, keys, preferred_element_type=jnp.float32) * scaling
        )
        grad_keys = (
            running[0]
            + jnp.einsum("hqk,qhd->kd", grad_low, query_block, preferred_element_type=jnp.float32)
            * scaling
        )
        grad_values = running[1] + jnp.einsum(
            "hqk,qhd->kd", prob_low, grad_block, preferred_element_type=jnp.float32
        )
        return ((grad_keys, grad_values), grad_query.astype(jnp.bfloat16))

    empty = jnp.zeros(keys.shape, jnp.float32)
    steps_in = (jnp.arange(length // block_rows, dtype=jnp.int32), tops, totals)
    (grad_keys, grad_values), grad_queries = lax.scan(one_block, (empty, empty), steps_in)
    return (
        grad_queries.reshape(queries.shape),
        grad_keys.astype(jnp.bfloat16),
        grad_values.astype(jnp.bfloat16),
    )


def weight_term(left_side, right_side):
    return lax.dot_general(
        left_side, right_side, (((0,), (0,)), ((), ())), preferred_element_type=jnp.float32
    )


def local(
    tokens,
    positions,
    w_query,
    w_key,
    w_value,
    w_output,
    gate_up,
    w_down,
    bias_query,
    bias_key,
    bias_value,
    gain_attn,
    gain_mlp,
    cotangent,
):
    groups = lax.axis_size("seq")
    fsdp_count = lax.axis_size("fsdp")
    per_group = HEADS // groups
    repeats = groups // KV
    tok_rows = tokens.shape[1]
    length = tok_rows * groups
    inputs = tokens[0].astype(jnp.float32)
    seq_positions = positions[0]
    own_positions = lax.dynamic_slice_in_dim(
        seq_positions, lax.axis_index("seq") * tok_rows, tok_rows
    )
    cosine, sine = rope_tables(own_positions)
    documents = jnp.cumsum((seq_positions == 0).astype(jnp.int32))
    gathered = (
        lax.all_gather(w_query, "fsdp", axis=0, tiled=True),
        lax.all_gather(w_key, "fsdp", axis=0, tiled=True),
        lax.all_gather(w_value, "fsdp", axis=0, tiled=True),
        lax.all_gather(w_output, "fsdp", axis=0, tiled=True),
        lax.all_gather(bias_query, "fsdp", axis=0, tiled=True),
        lax.all_gather(bias_key, "fsdp", axis=0, tiled=True),
        lax.all_gather(bias_value, "fsdp", axis=0, tiled=True),
        lax.all_gather(gain_attn, "fsdp", axis=0, tiled=True),
        lax.all_gather(gain_mlp, "fsdp", axis=0, tiled=True),
    )
    (
        query_all,
        key_all,
        value_all,
        output_all,
        bias_q_all,
        bias_k_all,
        bias_v_all,
        gain_a_all,
        gain_m_all,
    ) = gathered
    gain_a_f32 = gain_a_all.astype(jnp.float32)
    gain_m_f32 = gain_m_all.astype(jnp.float32)
    normed_attn, factor_attn = rms_forward(inputs, gain_a_f32)
    normed_low = normed_attn.astype(jnp.bfloat16)
    queries_pre = (
        jnp.dot(normed_low, query_all, preferred_element_type=jnp.float32)
        + bias_q_all.astype(jnp.float32)
    ).reshape(tok_rows, HEADS, HD)
    keys_pre = (
        jnp.dot(normed_low, key_all, preferred_element_type=jnp.float32)
        + bias_k_all.astype(jnp.float32)
    ).reshape(tok_rows, KV, HD)
    values_pre = (
        jnp.dot(normed_low, value_all, preferred_element_type=jnp.float32)
        + bias_v_all.astype(jnp.float32)
    ).reshape(tok_rows, KV, HD)
    queries_low = rotate(queries_pre, cosine, sine).astype(jnp.bfloat16)
    keys_low = rotate(keys_pre, cosine, sine).astype(jnp.bfloat16)
    values_low = values_pre.astype(jnp.bfloat16)
    keys_dup = jnp.repeat(keys_low, repeats, axis=1)
    values_dup = jnp.repeat(values_low, repeats, axis=1)
    packed = jnp.concatenate(
        [
            queries_low.reshape(tok_rows, groups, per_group, HD),
            keys_dup[:, :, None, :],
            values_dup[:, :, None, :],
        ],
        axis=2,
    )
    arrived = lax.all_to_all(packed, "seq", split_axis=1, concat_axis=0, tiled=True).reshape(
        length, per_group + 2, HD
    )
    head_queries = arrived[:, :per_group]
    head_keys = arrived[:, per_group]
    head_values = arrived[:, per_group + 1]
    attended, tops, totals = attention_forward(head_queries, head_keys, head_values, documents)
    returned = lax.all_to_all(attended[:, None], "seq", split_axis=0, concat_axis=1, tiled=True)
    mixed_heads = returned.reshape(tok_rows, HEADS * HD)
    branch_attn = lax.dot_general(
        mixed_heads, output_all, (((1,), (1,)), ((), ())), preferred_element_type=jnp.float32
    )
    hidden_attn = inputs + branch_attn
    normed_mlp, factor_mlp = rms_forward(hidden_attn, gain_m_f32)
    normed_mlp_low = normed_mlp.astype(jnp.bfloat16)
    columns = normed_mlp_low
    gate_up_acts = jnp.einsum(
        "td,dgf->tgf",
        columns,
        lax.all_gather(gate_up, "fsdp", axis=0, tiled=True),
        preferred_element_type=jnp.float32,
    )
    gate_acts = gate_up_acts[:, 0]
    up_acts = gate_up_acts[:, 1]
    sigma = jax.nn.sigmoid(gate_acts)
    silu_gate = gate_acts * sigma
    activated = (silu_gate * up_acts).astype(jnp.bfloat16)
    branch_mlp = lax.dot_general(
        activated,
        lax.all_gather(w_down, "fsdp", axis=0, tiled=True),
        (((1,), (1,)), ((), ())),
        preferred_element_type=jnp.float32,
    )
    result = (hidden_attn + branch_mlp).astype(jnp.bfloat16)
    grad_out = cotangent[0]
    columns = grad_out
    grad_act = jnp.dot(
        columns,
        lax.all_gather(w_down, "fsdp", axis=0, tiled=True),
        preferred_element_type=jnp.float32,
    )
    grad_gate = grad_act * up_acts * sigma * (1.0 + gate_acts * (1.0 - sigma))
    grad_up = grad_act * silu_gate
    gate_up_grads = jnp.stack([grad_gate, grad_up], axis=1).astype(jnp.bfloat16)
    grad_normed_mlp = jnp.einsum(
        "tgf,dgf->td",
        gate_up_grads,
        lax.all_gather(gate_up, "fsdp", axis=0, tiled=True),
        preferred_element_type=jnp.float32,
    )
    grad_hidden_norm, grad_gain_mlp = rms_backward(
        hidden_attn, factor_mlp, gain_m_f32, grad_normed_mlp
    )
    grad_hidden = grad_out.astype(jnp.float32) + grad_hidden_norm
    grad_hidden_low = grad_hidden.astype(jnp.bfloat16)
    grad_heads = jnp.dot(grad_hidden_low, output_all, preferred_element_type=jnp.float32).astype(
        jnp.bfloat16
    )
    grad_arrived = lax.all_to_all(
        grad_heads.reshape(tok_rows, groups, per_group, HD),
        "seq",
        split_axis=1,
        concat_axis=0,
        tiled=True,
    )
    grad_attended = grad_arrived.reshape(length, per_group, HD)
    grad_q_heads, grad_k_head, grad_v_head = attention_backward(
        head_queries, head_keys, head_values, documents, tops, totals, grad_attended
    )
    packed_back = jnp.concatenate(
        [grad_q_heads, grad_k_head[:, None, :], grad_v_head[:, None, :]], axis=1
    )
    back = lax.all_to_all(packed_back[:, None], "seq", split_axis=0, concat_axis=1, tiled=True)
    grad_q_rot = back[:, :, :per_group].reshape(tok_rows, HEADS, HD).astype(jnp.float32)
    grad_k_rot = jnp.sum(
        back[:, :, per_group].astype(jnp.float32).reshape(tok_rows, KV, repeats, HD), axis=2
    )
    grad_v_sum = jnp.sum(
        back[:, :, per_group + 1].astype(jnp.float32).reshape(tok_rows, KV, repeats, HD), axis=2
    )
    grad_q_low = (
        unrotate(grad_q_rot, cosine, sine).reshape(tok_rows, HEADS * HD).astype(jnp.bfloat16)
    )
    grad_k_low = unrotate(grad_k_rot, cosine, sine).reshape(tok_rows, KV * HD).astype(jnp.bfloat16)
    grad_v_low = grad_v_sum.reshape(tok_rows, KV * HD).astype(jnp.bfloat16)
    transposed = (((1,), (1,)), ((), ()))
    grad_normed_attn = lax.dot_general(
        grad_q_low, query_all, transposed, preferred_element_type=jnp.float32
    )
    grad_normed_attn = grad_normed_attn + lax.dot_general(
        grad_k_low, key_all, transposed, preferred_element_type=jnp.float32
    )
    grad_normed_attn = grad_normed_attn + lax.dot_general(
        grad_v_low, value_all, transposed, preferred_element_type=jnp.float32
    )
    grad_input_norm, grad_gain_attn = rms_backward(
        inputs, factor_attn, gain_a_f32, grad_normed_attn
    )
    grad_input = grad_hidden + grad_input_norm
    grad_bias_query = jnp.sum(grad_q_low.astype(jnp.float32), axis=0)
    grad_bias_key = jnp.sum(grad_k_low.astype(jnp.float32), axis=0)
    grad_bias_value = jnp.sum(grad_v_low.astype(jnp.float32), axis=0)
    small = (
        lax.psum_scatter(grad_gain_attn, ("seq", "fsdp"), scatter_dimension=0, tiled=True),
        lax.psum_scatter(grad_gain_mlp, ("seq", "fsdp"), scatter_dimension=0, tiled=True),
        lax.psum_scatter(grad_bias_query, ("seq", "fsdp"), scatter_dimension=0, tiled=True),
        lax.psum_scatter(grad_bias_key, ("seq", "fsdp"), scatter_dimension=0, tiled=True),
        lax.psum_scatter(grad_bias_value, ("seq", "fsdp"), scatter_dimension=0, tiled=True),
    )
    qkv_grads = jnp.concatenate([grad_q_low, grad_k_low, grad_v_low], axis=1)
    left_sides = (normed_low, grad_hidden_low, normed_mlp_low, grad_out)
    right_sides = (qkv_grads, mixed_heads, gate_up_grads.reshape(tok_rows, 2 * FF), activated)
    owned = D // (groups * fsdp_count)
    pieces = [
        lax.psum_scatter(
            weight_term(left_side, right_side), ("seq", "fsdp"), scatter_dimension=0, tiled=True
        )
        for left_side, right_side in zip(left_sides, right_sides)
    ]
    owner_sums = jnp.concatenate(pieces, axis=1)
    query_cols = HEADS * HD
    kv_cols = KV * HD
    edge_value = query_cols + kv_cols
    edge_output = edge_value + kv_cols
    edge_gate = edge_output + query_cols
    edge_down = edge_gate + 2 * FF
    d_w_query = owner_sums[:, :query_cols]
    d_w_key = owner_sums[:, query_cols:edge_value]
    d_w_value = owner_sums[:, edge_value:edge_output]
    d_w_output = owner_sums[:, edge_output:edge_gate]
    d_gate_up = owner_sums[:, edge_gate:edge_down].reshape(owned, 2, FF)
    d_w_down = owner_sums[:, edge_down:]
    return (
        result[None],
        grad_input[None],
        d_w_query,
        d_w_key,
        d_w_value,
        d_w_output,
        d_gate_up,
        d_w_down,
        small[2],
        small[3],
        small[4],
        small[0],
        small[1],
    )


def solution(mesh):
    placed = (
        P("fsdp", "seq", None),
        P("fsdp", None),
        P("fsdp", None),
        P("fsdp", None),
        P("fsdp", None),
        P("fsdp", None),
        P("fsdp", None, None),
        P("fsdp", None),
        P("fsdp"),
        P("fsdp"),
        P("fsdp"),
        P("fsdp"),
        P("fsdp"),
        P("fsdp", "seq", None),
    )
    return jax.shard_map(
        local,
        mesh=mesh,
        in_specs=placed,
        out_specs=(
            P("fsdp", "seq", None),
            P("fsdp", "seq", None),
            P(("seq", "fsdp"), None),
            P(("seq", "fsdp"), None),
            P(("seq", "fsdp"), None),
            P(("seq", "fsdp"), None),
            P(("seq", "fsdp"), None, None),
            P(("seq", "fsdp"), None),
            P(("seq", "fsdp")),
            P(("seq", "fsdp")),
            P(("seq", "fsdp")),
            P(("seq", "fsdp")),
            P(("seq", "fsdp")),
        ),
        check_vma=False,
    )
```

profile of v0, /device:TPU:0, one launch (start us, length us, event | category | flops | bytes accessed | tf_op | source)
XLA Modules:
  0.0 3592.5 jit_solution(15781944580271303272)
XLA Ops:
  8.7 6.4 copy.125
  19.0 39.7 %all-reduce.11 = (bf16[256]{0:T(256)(128)(2,1)S(1)}, bf16[1536]{0:T(1024)(128)(2,1)S(1)}, bf16[256]{0:T(256)(128)(2,1)S(1)}, bf16[1536]{0:T(1024)(128)(2,1)S(1)}, bf16[1536]{0:T(1024)(128)(2,1)}) all-reduce(bf16[256]{0:T(256)(128)(2,1)S(1)} %dynamic-update-slice.3, ...), channel_id=1, replica_groups=mesh['seq'=4,'fsdp'=8] {'fsdp'}, use_global_device_ids=true, to_apply=%add.3 | all-reduce | flops 5120 | bytes 20480
  59.7 34.2 all_gather.38
  95.6 33.5 all_gather.40
  130.7 4.9 convolution_add_fusion.3
  140.0 4.0 all-to-all-start
  144.6 16.6 all-to-all-done
  165.8 20.1 while.29
  167.7 2.4 bitcast_reduce_fusion.3
  172.0 3.3 fusion.159
  177.7 2.5 bitcast_reduce_fusion.3
  182.0 3.3 fusion.159
  187.5 3.7 all-to-all-start.1
  191.2 14.4 all-to-all-done.1
  206.9 4.7 multiply_reduce_fusion.2
  211.6 1024.4 %all-gather.9.cloned.1.call-done = bf16[1536,2,8960]{2,0,1:T(8,128)(2,1)} async-done(((bf16[192,2,8960]{2,0,1:T(8,128)(2,1)}), bf16[1536,2,8960]{2,0,1:T(8,128)(2,1)}) %all-gather.9.cloned.1.call-update) | async-done | bytes 55050256 | tf_op jit(solution)/shard_map/all_gather | solution.py:233
  1236.0 29.2 fusion.91
  1265.2 496.9 %all-gather.11.cloned.1.call-done = bf16[1536,8960]{1,0:T(8,128)(2,1)} async-done(((bf16[192,8960]{1,0:T(8,128)(2,1)}), bf16[1536,8960]{1,0:T(8,128)(2,1)}) %all-gather.11.cloned.1.call-update) | async-done | bytes 27525136 | tf_op jit(solution)/shard_map/all_gather | solution.py:243
  1762.1 24.0 fusion.48
  1786.1 26.2 multiply_reduce_fusion
  1815.3 3.7 convolution_convert_fusion
  1820.2 3.7 all-to-all-start.2
  1823.9 11.6 all-to-all-done.2
  1837.4 32.5 while.30
  1842.5 4.2 fusion.170
  1850.5 2.3 fusion.174
  1858.8 4.2 fusion.170
  1866.7 2.3 fusion.174
  1873.6 3.7 all-to-all-start.3
  1878.6 24.5 all-to-all-done.3
  1904.3 2.9 copy.131
  1920.9 6.6 fusion.82
  1927.5 8.1 maximum_convert_fusion
  1935.7 12.9 copy.137
  1948.5 44.7 %fusion.104 = f32[1536,17920]{1,0:T(8,128)} fusion(bf16[256,17920]{0,1:T(8,128)(2,1)} %bitcast.294, f32[256,1536]{1,0:T(8,128)S(1)} %copy-done.5, f32[1536]{0:T(1024)S(1)} %convert_element_type.198, f32[256]{0:T(256)S(1)} %copy-done.38), kind=kOutput, calls=%fused_computation.170 | convolution fusion | flops 14094041088 | bytes 120855552 | tf_op jit(solution)/shard_map/dot_general | solution.py:129
  1994.6 6.2 fusion.93
  2001.0 25.8 convolution_bitcast_fusion.1
  2026.8 54.8 %copy.145 = f32[1536,8960]{1,0:T(8,128)} copy(f32[1536,8960]{0,1:T(8,128)} %convolution_bitcast_fusion.1) | data formatting | bytes 110100480
  2081.7 19.3 fusion.62
  2100.9 3.3 copy.138
  2105.5 2.5 convert_reduce_fusion
  2108.1 4.8 fusion.116
  2116.5 40.0 %all-reduce.10 = (f32[1536]{0:T(1024)S(1)}, f32[256]{0:T(256)S(1)}, f32[256]{0:T(256)S(1)}, f32[1536]{0:T(1024)S(1)}, f32[1536]{0:T(1024)S(1)}) all-reduce(f32[1536]{0:T(1024)S(1)} %reduce_sum.130, f32[256]{0:T(256)S(1)} %bitcast.328, f32[256]{0:T(256)S(1)} %bitcast.329, ...), channel_id=6, replica_groups=mesh['seq'=4,'fsdp'=8] {'seq','fsdp'}, use_global_device_ids=true, to_apply=%region_20.21.clone | all-reduce | flops 5120 | bytes 40960
  2159.4 3.2 fusion.74
  2165.9 808.8 %reduce-scatter.11.cloned.1.call-done = f32[48,17920]{1,0:T(8,128)} async-done(((f32[1536,17920]{1,0:T(8,128)}), f32[48,17920]{1,0:T(8,128)}) %reduce-scatter.11.cloned.1.call-update) | async-done | bytes 3440656 | tf_op jit(solution)/shard_map/reduce_scatter | solution.py:328
  2974.7 5.5 reshape.332
  2980.2 135.5 %reduce-scatter.9.cloned.1.call-done = f32[48,1536]{1,0:T(8,128)} async-done(((f32[1536,1536]{1,0:T(8,128)}), f32[48,1536]{1,0:T(8,128)}) %reduce-scatter.9.cloned.1.call-update) | async-done | bytes 294928 | tf_op jit(solution)/shard_map/reduce_scatter | solution.py:328
  3115.7 469.7 %reduce-scatter.13.cloned.1.call-done = f32[48,8960]{1,0:T(8,128)} async-done(((f32[1536,8960]{1,0:T(8,128)}), f32[48,8960]{1,0:T(8,128)}) %reduce-scatter.13.cloned.1.call-update) | async-done | bytes 1720336
  (270 shorter events, 84.2 us)
Async XLA Ops:
  7.2 123.6 %all-gather.5.cloned.1.call-start = ((), (), s32[]{:S(2)}) async-start(), calls=%async_computation.8 | async-start | bytes 5308416 | tf_op jit(solution)/shard_map/all_gather | solution.py:164
  7.9 199.0 %all-gather.7.cloned.1.call-start = ((), (), s32[]{:S(2)}) async-start(), calls=%async_computation.9 | async-start | bytes 5308416 | tf_op jit(solution)/shard_map/all_gather | solution.py:167
  8.7 1227.4 %all-gather.9.cloned.1.call-start = ((), (), s32[]{:S(2)}) async-start(), calls=%async_computation.10 | async-start | bytes 61931520 | tf_op jit(solution)/shard_map/all_gather | solution.py:233
  15.2 2.6 copy-start.54
  15.2 2.8 copy-start.55
  15.2 3.1 copy-start.56
  15.2 3.3 copy-start.57
  15.2 3.6 copy-start.58
  15.2 43.6 %copy-start.51 = (s32[1,1024]{1,0:T(1,128)S(1)}, s32[1,1024]{1,0:T(1,128)}, u32[]{:S(2)}) copy-start(s32[1,1024]{1,0:T(1,128)} %param.19) | copy-start | bytes 12292
  15.2 44.1 %copy-start.9 = (bf16[1,256,1536]{2,1,0:T(8,128)(2,1)S(1)}, bf16[1,256,1536]{2,1,0:T(8,128)(2,1)}, u32[]{:S(2)}) copy-start(bf16[1,256,1536]{2,1,0:T(8,128)(2,1)} %param.18) | copy-start | bytes 2359300
  15.2 44.4 %copy-start.45 = (bf16[192,256]{1,0:T(8,128)(2,1)S(1)}, bf16[192,256]{1,0:T(8,128)(2,1)}, u32[]{:S(2)}) copy-start(bf16[192,256]{1,0:T(8,128)(2,1)} %param.21) | copy-start | bytes 294916
  15.3 1746.8 %all-gather.11.cloned.1.call-start = ((), (), s32[]{:S(2)}) async-start(), calls=%async_computation.11 | async-start | bytes 30965760 | tf_op jit(solution)/shard_map/all_gather | solution.py:243
  58.8 72.0 %copy-start.42 = (f32[1536]{0:T(1024)}, f32[1536]{0:T(1024)S(1)}, u32[]{:S(2)}) copy-start(f32[1536]{0:T(1024)S(1)} %convert_element_type.187) | copy-start | bytes 18436
  59.4 78.3 %copy-start.14 = (f32[256,128]{0,1:T(8,128)}, f32[256,128]{0,1:T(8,128)S(1)}, u32[]{:S(2)}) copy-start(f32[256,128]{0,1:T(8,128)S(1)} %get-tuple-element.318) | copy-start | bytes 393220
  59.4 78.3 %copy-start.17 = (f32[256,128]{0,1:T(8,128)}, f32[256,128]{0,1:T(8,128)S(1)}, u32[]{:S(2)}) copy-start(f32[256,128]{0,1:T(8,128)S(1)} %get-tuple-element.319) | copy-start | bytes 393220
  59.7 71.1 %copy-start.47 = (f32[256]{0:T(256)}, f32[256]{0:T(256)S(1)}, u32[]{:S(2)}) copy-start(f32[256]{0:T(256)S(1)} %add_rsqrt_fusion.1) | copy-start | bytes 3076
  129.1 6.5 copy-start.27
  140.0 21.2 all-to-all-start
  185.9 5.3 copy-start.53
  187.5 18.1 all-to-all-start.1
  211.6 1600.7 %copy-start.4 = (f32[256,1536]{1,0:T(8,128)}, f32[256,1536]{1,0:T(8,128)S(1)}, u32[]{:S(2)}) copy-start(f32[256,1536]{1,0:T(8,128)S(1)} %get-tuple-element.321) | copy-start | bytes 4718596
  211.6 1600.7 %copy-start.37 = (f32[256]{0:T(256)}, f32[256]{0:T(256)S(1)}, u32[]{:S(2)}) copy-start(f32[256]{0:T(256)S(1)} %add_rsqrt_fusion) | copy-start | bytes 3076
  1236.0 526.1 %copy-start.19 = (bf16[1,256,1536]{2,1,0:T(8,128)(2,1)S(1)}, bf16[1,256,1536]{2,1,0:T(8,128)(2,1)}, u32[]{:S(2)}) copy-start(bf16[1,256,1536]{2,1,0:T(8,128)(2,1)} %param.31) | copy-start | bytes 2359300
  1820.2 15.3 all-to-all-start.2
  1850.5 2.3 copy-start.1
  1866.7 2.3 copy-start.1
  1873.6 4.2 copy-start.18
  1873.6 29.4 all-to-all-start.3
  1877.4 285.3 %reduce-scatter.7.cloned.1.call-start = ((), (), s32[]{:S(2)}) async-start(), calls=%async_computation.12 | async-start | bytes 12976128 | tf_op jit(solution)/shard_map/reduce_scatter | solution.py:328
  1907.2 2.3 copy-start.12
  1916.6 1.9 copy-start.15
  1918.5 2.3 copy-start.10
  1918.6 2.3 copy-start.29
  1918.6 2.3 copy-start.43
  1918.6 2.3 copy-start.48
  1927.5 1047.2 %reduce-scatter.11.cloned.1.call-start = ((), (), s32[]{:S(2)}) async-start(), calls=%async_computation.14 | async-start | bytes 113541120 | tf_op jit(solution)/shard_map/reduce_scatter | solution.py:328
  1935.6 12.9 copy-start.5
  1935.7 12.9 copy-start.38
  1993.2 1122.5 %reduce-scatter.9.cloned.1.call-start = ((), (), s32[]{:S(2)}) async-start(), calls=%async_computation.13 | async-start | bytes 9732096 | tf_op jit(solution)/shard_map/reduce_scatter | solution.py:328
  2000.8 1584.6 %reduce-scatter.13.cloned.1.call-start = ((), (), s32[]{:S(2)}) async-start(), calls=%async_computation.15 | async-start | bytes 56770560
  2100.9 3.3 copy-start.7
  2100.9 4.6 copy-start.16
  2104.2 3.8 copy-start.34
  2105.5 2.6 copy-start.21
  2108.1 4.9 copy-start.26
  2108.1 4.9 copy-start.32
  2114.6 1.9 copy-start.50
  2114.6 1.9 copy-start.52
  (28 other events, 34.5 us)
Sparse Core Ops, SparseCore 0:
  10.2 104.3 all-gather.4
  116.8 78.6 all-gather.6
  197.0 1038.9 all-gather.8
  1237.4 524.6 all-gather.10
  1927.6 154.3 reduce-scatter.6
  2089.4 885.2 reduce-scatter.10
  2981.2 134.5 reduce-scatter.8
  3123.9 461.5 reduce-scatter.12
where the time goes:
time: 3600 us; the launch traced here: 3590 us
  waiting for transfers between devices  3000 us (83%)
  matrix products  236 us (7%)
  blocking collectives  147 us (4%)
  local copies, waits for them, and re-layouts  135 us (4%)
    all_gather x1, waiting for transfers between devices, local(): lax.all_gather(gate_up, 'fsdp', axis=0, tiled=True)  1020 us
    reduce_scatter x3, waiting for transfers between devices, local(): lax.psum_scatter(weight_term(left_side, right_side), ('seq', 'fsdp'), sca...  944 us
    all_gather x1, waiting for transfers between devices, local(): lax.all_gather(w_down, 'fsdp', axis=0, tiled=True)  497 us
    unnamed x9, waiting for transfers between devices  472 us
    dot_general x4, matrix products, weight_term(): lax.dot_general(left_side, right_side, (((0,), (0,)), ((), ())), preferre...  83.2 us
    unnamed x2, blocking collectives  79.7 us
    unnamed x130, local copies, waits for them, and re-layouts  74.9 us
  transfers between devices with their start and end apart: 12, of which 9 were waited for; matrix products, arithmetic and copies ran while one was open for 8% of the time, Pallas kernels for 0%

commit v1 on v0

v1 whole, which is shorter than its diff:
```python
import jax
import jax.numpy as jnp
from jax import lax
from jax.sharding import PartitionSpec as P

D = 1536
HEADS = 12
KV = 2
HD = 128
FF = 8960
LANE = 128

epsilon = 1e-06
rope_base = 1000000.0
masked_value = -1e30
BF = jnp.bfloat16
F32 = jnp.float32

FF_BLOCKS = FF // LANE
CHIP_BLOCKS = -(-FF_BLOCKS // 4)
CORE_BLOCKS = CHIP_BLOCKS // 2
CORE_COLS = CORE_BLOCKS * LANE
CHIP_STARTS = (0, 18, 36, 52)
CHIP_VALID = ((0, 18), (0, 18), (0, 17), (1, 18))
CHUNKS = ((0, 768), (768, 1152))


def rope_tables(positions):
    ladder = jnp.arange(HD // 2, dtype=F32)
    inverse = rope_base ** (-2.0 * ladder / HD)
    angles = positions.astype(F32)[:, None] * inverse[None, :]
    angles = jnp.concatenate([angles, angles], axis=-1)
    return (jnp.cos(angles), jnp.sin(angles))


def rotate(value, cosine, sine):
    halfway = HD // 2
    turned = jnp.concatenate([-value[..., halfway:], value[..., :halfway]], axis=-1)
    return value * cosine[:, None, :] + turned * sine[:, None, :]


def unrotate(grad, cosine, sine):
    halfway = HD // 2
    scaled = grad * sine[:, None, :]
    turned = jnp.concatenate([scaled[..., halfway:], -scaled[..., :halfway]], axis=-1)
    return grad * cosine[:, None, :] + turned


def rms_factor(value):
    return lax.rsqrt(jnp.mean(value * value, axis=-1, keepdims=True) + epsilon)


def rms_backward(value, factor, gain, grad):
    unit = value * factor
    weighted = grad * gain
    grad_gain = jnp.sum(grad * unit, axis=0)
    inner = jnp.mean(weighted * unit, axis=-1, keepdims=True)
    return (factor * (weighted - unit * inner), grad_gain)


def masked_scores(query_block, keys, documents, first_row):
    block_rows = query_block.shape[0]
    query_place = first_row + jnp.arange(block_rows, dtype=jnp.int32)
    key_place = jnp.arange(keys.shape[0], dtype=jnp.int32)
    query_docs = lax.dynamic_slice_in_dim(documents, first_row, block_rows)
    allowed = (key_place[None, :] <= query_place[:, None]) & (
        documents[None, :] == query_docs[:, None]
    )
    raw = jnp.einsum("qhd,kd->hqk", query_block, keys, preferred_element_type=F32) * HD ** (-0.5)
    return jnp.where(allowed[None], raw, masked_value)


def attention_forward(queries, keys, values, documents):
    length = queries.shape[0]
    block_rows = min(512, length)

    def one_block(block_index):
        first_row = block_index * block_rows
        query_block = lax.dynamic_slice_in_dim(queries, first_row, block_rows, 0)
        scores = masked_scores(query_block, keys, documents, first_row)
        row_top = jnp.max(scores, axis=-1, keepdims=True)
        shifted = jnp.exp(scores - row_top)
        row_total = jnp.sum(shifted, axis=-1, keepdims=True)
        probability = (shifted / row_total).astype(BF)
        outcome = jnp.einsum("hqk,kd->qhd", probability, values, preferred_element_type=F32)
        return (outcome.astype(BF), row_top, row_total)

    outcome, tops, totals = lax.map(one_block, jnp.arange(length // block_rows, dtype=jnp.int32))
    return (outcome.reshape(queries.shape), tops, totals)


def attention_backward(queries, keys, values, documents, tops, totals, grad_attended):
    length = queries.shape[0]
    block_rows = min(512, length)
    scaling = HD ** (-0.5)

    def one_block(running, inputs_block):
        block_index, row_top, row_total = inputs_block
        first_row = block_index * block_rows
        query_block = lax.dynamic_slice_in_dim(queries, first_row, block_rows, 0)
        grad_block = lax.dynamic_slice_in_dim(grad_attended, first_row, block_rows, 0)
        scores = masked_scores(query_block, keys, documents, first_row)
        probability = jnp.exp(scores - row_top) / row_total
        prob_low = probability.astype(BF)
        grad_prob = jnp.einsum("qhd,kd->hqk", grad_block, values, preferred_element_type=F32)
        grad_scores = probability * (
            grad_prob - jnp.sum(probability * grad_prob, axis=-1, keepdims=True)
        )
        grad_low = grad_scores.astype(BF)
        grad_query = jnp.einsum("hqk,kd->qhd", grad_low, keys, preferred_element_type=F32) * scaling
        grad_keys = (
            running[0]
            + jnp.einsum("hqk,qhd->kd", grad_low, query_block, preferred_element_type=F32)
            * scaling
        )
        grad_values = running[1] + jnp.einsum(
            "hqk,qhd->kd", prob_low, grad_block, preferred_element_type=F32
        )
        return ((grad_keys, grad_values), grad_query.astype(BF))

    empty = jnp.zeros(keys.shape, F32)
    steps_in = (jnp.arange(length // block_rows, dtype=jnp.int32), tops, totals)
    (grad_keys, grad_values), grad_queries = lax.scan(one_block, (empty, empty), steps_in)
    return (grad_queries.reshape(queries.shape), grad_keys.astype(BF), grad_values.astype(BF))


def dot(left, right):
    return jnp.dot(left, right, preferred_element_type=F32)


def dot_t(left, right):
    return lax.dot_general(left, right, (((1,), (1,)), ((), ())), preferred_element_type=F32)


def t_dot(left, right):
    return lax.dot_general(left, right, (((0,), (0,)), ((), ())), preferred_element_type=F32)


def pick(array, index, axis=0):
    return lax.dynamic_index_in_dim(array, index, axis, keepdims=False)


def build(seq_count, fsdp_count):
    planes = fsdp_count // 2
    order = list(range(0, 1)) + list(range(1, planes, 2)) + list(range(2, planes, 2))[::-1]
    place = [order.index(plane) for plane in range(planes)]
    after = {order[i]: order[(i + 1) % planes] for i in range(planes)}
    ring_perm = [(2 * z + y, 2 * after[z] + y) for z in range(planes) for y in range(2)]
    y_perm = [(i, i ^ 1) for i in range(fsdp_count)]
    x_perm = [(i, i ^ 2) for i in range(seq_count)]
    c_perm = [(i, i ^ 1) for i in range(seq_count)]

    def swap_x(value):
        return lax.ppermute(value, "seq", x_perm)

    def swap_c(value):
        return lax.ppermute(value, "seq", c_perm)

    def swap_y(value):
        return lax.ppermute(value, "fsdp", y_perm)

    def ring(value):
        return lax.ppermute(value, "fsdp", ring_perm)

    def ordered(flag, first, second, axis):
        return jnp.where(
            flag == 0, jnp.stack([first, second], axis), jnp.stack([second, first], axis)
        )

    def local(
        tokens,
        positions,
        w_query,
        w_key,
        w_value,
        w_output,
        gate_up,
        w_down,
        bias_query,
        bias_key,
        bias_value,
        gain_attn,
        gain_mlp,
        cotangent,
    ):
        s = lax.axis_index("seq")
        f = lax.axis_index("fsdp")
        x, c = s // 2, s % 2
        z, y = f // 2, f % 2
        ring_order = jnp.array(order, jnp.int32)
        ring_place = jnp.array(place, jnp.int32)

        def plane_at(back):
            return ring_order[(ring_place[z] - back) % planes]

        tok_rows = tokens.shape[1]
        length = tok_rows * seq_count
        per_group = HEADS // seq_count
        group_cols = per_group * HD
        w_rows = w_query.shape[0]
        own_rows = D // (seq_count * fsdp_count)

        def ring_gather(payload):
            pieces = [payload]
            for _ in range(planes - 1):
                pieces.append(ring(pieces[-1]))
            return pieces

        def by_plane(pieces, axis):
            shape = list(pieces[0].shape)
            shape.insert(axis, planes)
            whole = jnp.zeros(shape, pieces[0].dtype)
            for back, piece in enumerate(pieces):
                whole = lax.dynamic_update_index_in_dim(whole, piece, plane_at(back), axis)
            return whole

        def gather_sequence(own):
            over_x = ordered(x, own, swap_x(own), 0)
            return ordered(c, over_x, swap_c(over_x), 1).reshape((length,) + own.shape[1:])

        def scatter_sequence(partial):
            parts = partial.reshape(2, 2, tok_rows, D)
            away = swap_c(pick(parts, 1 - c, 1).astype(BF))
            halves = pick(parts, c, 1) + away.astype(F32)
            back = swap_x(pick(halves, 1 - x).astype(BF))
            return pick(halves, x) + back.astype(F32)

        half = D // 2

        def gather_plane(own):
            first, second = own[:, :half], own[:, half:]
            a1 = swap_x(first)
            b1 = swap_y(second)
            a2 = swap_y(jnp.stack([first, a1]))
            b2 = swap_x(jnp.stack([second, b1]))
            left = jnp.concatenate([first, a2[0], a1, a2[1]], axis=0)
            right = jnp.concatenate([second, b1, b2[0], b2[1]], axis=0)
            return jnp.concatenate([left, right], axis=1)

        def scatter_plane(partial):
            parts = partial.reshape(2, 2, tok_rows, D)
            first, second = parts[..., :half], parts[..., half:]
            a1 = first[:, 0] + swap_y(first[:, 1].astype(BF)).astype(F32)
            b1 = second[0] + swap_x(second[1].astype(BF)).astype(F32)
            a2 = a1[0] + swap_x(a1[1].astype(BF)).astype(F32)
            b2 = b1[0] + swap_y(b1[1].astype(BF)).astype(F32)
            return jnp.concatenate([a2, b2], axis=1)

        kv = x
        small_row = jnp.concatenate(
            [gain_attn, gain_mlp, bias_query, bias_key, bias_value, jnp.zeros((640 - 3 * w_rows - 2 * (256 // fsdp_count),), BF)]
        )
        qkv_own = jnp.concatenate(
            [
                lax.dynamic_slice_in_dim(w_query, s * group_cols, group_cols, 1),
                lax.dynamic_slice_in_dim(w_key, kv * HD, HD, 1),
                lax.dynamic_slice_in_dim(w_value, kv * HD, HD, 1),
            ],
            axis=1,
        )
        pad_rows = jnp.zeros((15, 640), BF)
        qkv_payload = jnp.concatenate([qkv_own, small_row[None], pad_rows], axis=0)
        tokens_all = gather_sequence(tokens[0])

        def gather_attn(payload):
            mine = by_plane(ring_gather(payload), 0)
            both = ordered(y, mine, swap_y(mine), 1)
            return both.reshape((fsdp_count,) + payload.shape)

        qkv_blocks = gather_attn(qkv_payload)
        qkv_all = qkv_blocks[:, :w_rows].reshape(D, 640)
        smalls = qkv_blocks[:, w_rows]
        gain_a = smalls[:, :w_rows].reshape(D).astype(F32)
        gain_m = smalls[:, w_rows : 2 * w_rows].reshape(D).astype(F32)
        bias_q = smalls[:, 2 * w_rows : 3 * w_rows].reshape(D).astype(F32)
        kv_own = 256 // fsdp_count
        edge = 3 * w_rows
        bias_k = smalls[:, edge : edge + kv_own].reshape(KV * HD).astype(F32)
        bias_v = smalls[:, edge + kv_own : edge + 2 * kv_own].reshape(KV * HD).astype(F32)
        output_own = lax.dynamic_slice_in_dim(w_output, s * group_cols, group_cols, 1)
        output_all = gather_attn(output_own).reshape(D, group_cols)

        starts = jnp.array(CHIP_STARTS, jnp.int32)
        valid_low = jnp.array([v[0] for v in CHIP_VALID], jnp.int32)
        valid_high = jnp.array([v[1] for v in CHIP_VALID], jnp.int32)

        def columns_for(chip):
            first = (starts[chip] + c * CORE_BLOCKS) * LANE
            block = c * CORE_BLOCKS + jnp.arange(CORE_COLS, dtype=jnp.int32) // LANE
            valid = (block >= valid_low[chip]) & (block < valid_high[chip])
            both = lax.dynamic_slice_in_dim(gate_up, first, CORE_COLS, 2)
            down = lax.dynamic_slice_in_dim(w_down, first, CORE_COLS, 1)
            kinds = jnp.stack([both[:, 0], both[:, 1], down])
            return jnp.where(valid[None, None], kinds, jnp.zeros((), BF))

        chip = 2 * x + y
        kept = columns_for(chip)
        came = swap_y(columns_for(2 * x + (1 - y)))
        plane_rows = ordered(y, kept, came, 1).reshape(3, 2 * w_rows, CORE_COLS)

        mlp_weights = []
        for low, high in CHUNKS:
            mine = by_plane(ring_gather(plane_rows[:, :, low:high]), 1).reshape(3, D, high - low)
            mlp_weights.append(jnp.concatenate([mine, swap_c(mine)], axis=2))

        cot_all = gather_plane(cotangent[0])

        inputs_all = tokens_all.astype(F32)
        normed_attn = (inputs_all * rms_factor(inputs_all) * gain_a).astype(BF)
        bias_all = jnp.concatenate(
            [
                lax.dynamic_slice_in_dim(bias_q, s * group_cols, group_cols),
                lax.dynamic_slice_in_dim(bias_k, kv * HD, HD),
                lax.dynamic_slice_in_dim(bias_v, kv * HD, HD),
            ]
        )
        qkv = dot(normed_attn, qkv_all) + bias_all
        seq_positions = positions[0]
        cosine, sine = rope_tables(seq_positions)
        documents = jnp.cumsum((seq_positions == 0).astype(jnp.int32))
        turned = rotate(qkv[:, : group_cols + HD].reshape(length, per_group + 1, HD), cosine, sine)
        turned = turned.astype(BF)
        queries = turned[:, :per_group]
        keys = turned[:, per_group]
        values = qkv[:, group_cols + HD :].astype(BF)
        attended, tops, totals = attention_forward(queries, keys, values, documents)
        attended = attended.reshape(length, group_cols)
        branch_attn = scatter_sequence(dot_t(attended, output_all))

        inputs = tokens[0].astype(F32)
        hidden = inputs + branch_attn
        factor_mlp = rms_factor(hidden)
        normed_own = (hidden * factor_mlp * gain_m).astype(BF)
        normed = gather_plane(normed_own)

        grad_normed = 0.0
        branch = 0.0
        pieces = []
        for weights in mlp_weights:
            gate = dot(normed, weights[0])
            up = dot(normed, weights[1])
            grad_act = dot(cot_all, weights[2])
            sigma = jax.nn.sigmoid(gate)
            silu = gate * sigma
            activated = (silu * up).astype(BF)
            grad_gate = (grad_act * up * sigma * (1.0 + gate * (1.0 - sigma))).astype(BF)
            grad_up = (grad_act * silu).astype(BF)
            grad_normed = grad_normed + dot_t(grad_gate, weights[0]) + dot_t(grad_up, weights[1])
            branch = branch + dot_t(activated, weights[2])
            pieces.append(
                jnp.stack(
                    [
                        t_dot(normed, grad_gate).astype(BF),
                        t_dot(normed, grad_up).astype(BF),
                        t_dot(cot_all, activated).astype(BF),
                    ]
                )
            )

        def ring_scatter(block):
            running = block(plane_at(1))
            for step in range(2, planes + 1):
                running = block(plane_at(step)) + ring(running.astype(BF)).astype(F32)
            return running

        def owner_blocks(partial, cols):
            return partial.reshape(-1, 2, 2, planes, 2, own_rows, cols)

        gathered = []
        for number, (piece, (low, high)) in enumerate(zip(pieces, CHUNKS)):
            cols = 2 * (high - low)
            rows = owner_blocks(piece, cols)
            away = swap_c(pick(rows, 1 - c, 2))
            rest = pick(rows, c, 2)

            def block(plane):
                ours = pick(rest, plane, 2).astype(F32)
                theirs = pick(away, plane, 2).astype(F32)
                theirs = jnp.concatenate(
                    [theirs[..., cols // 2 :], theirs[..., : cols // 2]], axis=-1
                )
                return ours + theirs

            total = ring_scatter(block).astype(BF)
            if number % 2 == 0:
                over_x = jnp.stack([pick(total, x, 1), swap_x(pick(total, 1 - x, 1))], 1)
                both = jnp.stack([pick(over_x, y, 2), swap_y(pick(over_x, 1 - y, 2))], 2)
            else:
                over_y = jnp.stack([pick(total, y, 2), swap_y(pick(total, 1 - y, 2))], 2)
                both = jnp.stack([pick(over_y, x, 1), swap_x(pick(over_y, 1 - x, 1))], 1)
            both = jnp.where(x == 0, both, both[:, ::-1])
            both = jnp.where(y == 0, both, both[:, :, ::-1])
            halves = both.reshape(3, 4, own_rows, 2, cols // 2)
            halves = jnp.where(c == 0, halves, halves[:, :, :, ::-1])
            gathered.append(halves)
        strips = []
        for chip_index, (low, high) in enumerate(CHIP_VALID):
            whole = jnp.concatenate(
                [part[:, chip_index, :, core] for core in range(2) for part in gathered], axis=-1
            )
            strips.append(whole[..., low * LANE : high * LANE])
        d_mlp = jnp.concatenate(strips, axis=-1).astype(F32)
        d_gate_up = jnp.stack([d_mlp[0], d_mlp[1]], axis=1)
        d_w_down = d_mlp[2]

        grad_out = cotangent[0].astype(F32)
        grad_hidden_norm, grad_gain_mlp = rms_backward(
            hidden, factor_mlp, gain_m, scatter_plane(grad_normed)
        )
        result = (hidden + scatter_plane(branch)).astype(BF)
        grad_hidden = grad_out + grad_hidden_norm
        grad_hidden_low = gather_sequence(grad_hidden.astype(BF))
        grad_attended = dot(grad_hidden_low, output_all).astype(BF)
        grad_q, grad_k, grad_v = attention_backward(
            queries,
            keys,
            values,
            documents,
            tops,
            totals,
            grad_attended.reshape(length, per_group, HD),
        )
        grad_kv = jnp.stack([grad_k, grad_v])
        grad_kv = grad_kv.astype(F32) + swap_c(grad_kv).astype(F32)
        grad_k_low = unrotate(grad_kv[0][:, None], cosine, sine)[:, 0]
        grad_one = jnp.where(c == 0, grad_k_low, grad_kv[1]).astype(BF)
        grad_q_low = unrotate(grad_q.astype(F32), cosine, sine).astype(BF)
        grad_qkv = jnp.concatenate([grad_q_low.reshape(length, group_cols), grad_one], axis=1)
        one_cols = jnp.where(
            c == 0, qkv_all[:, group_cols : group_cols + HD], qkv_all[:, group_cols + HD :]
        )
        qk_all = jnp.concatenate([qkv_all[:, :group_cols], one_cols], axis=1)
        grad_normed_attn = scatter_sequence(dot_t(grad_qkv, qk_all))
        grad_input_norm, grad_gain_attn = rms_backward(
            inputs, rms_factor(inputs), gain_a, grad_normed_attn
        )
        grad_input = grad_hidden + grad_input_norm

        d_output = t_dot(grad_hidden_low, attended)
        d_qkv = t_dot(normed_attn, grad_qkv)
        bias_sums = jnp.sum(grad_qkv.astype(F32), axis=0)
        spread = jnp.zeros((2, 2, fsdp_count, own_rows), F32)
        spread_q = lax.dynamic_update_slice(
            spread, bias_sums[:group_cols].reshape(1, 1, fsdp_count, own_rows), (x, c, 0, 0)
        )
        kv_rows = KV * HD // (seq_count * fsdp_count)
        spread_kv = lax.dynamic_update_slice(
            spread, bias_sums[group_cols:].reshape(1, 2, fsdp_count, kv_rows), (x, 0, 0, 0)
        )
        smalls_out = jnp.stack(
            [grad_gain_attn, grad_gain_mlp, spread_q.reshape(D), spread_kv.reshape(D)], axis=1
        )
        smalls_out = jnp.pad(smalls_out, ((0, 0), (0, LANE - 4)))

        def to_owners(partial):
            cols = partial.shape[1]
            rows = owner_blocks(partial, cols)[0]
            away = swap_y(pick(rows, 1 - y, 3).astype(BF))
            rest = pick(rows, y, 3)

            def block(plane):
                return pick(rest, plane, 2) + pick(away, plane, 2).astype(F32)

            total = ring_scatter(block).astype(BF)
            over_x = jnp.stack([pick(total, x), swap_x(pick(total, 1 - x))], 0)
            both = jnp.stack([pick(over_x, c, 1), swap_c(pick(over_x, 1 - c, 1))], 1)
            both = jnp.where(x == 0, both, both[::-1])
            both = jnp.where(c == 0, both, both[:, ::-1])
            return both.astype(F32)

        out_blocks = to_owners(d_output)
        d_w_output = jnp.concatenate([out_blocks[i // 2, i % 2] for i in range(4)], axis=1)
        qkv_blocks_out = to_owners(jnp.concatenate([d_qkv, smalls_out], axis=1))
        d_w_query = jnp.concatenate(
            [qkv_blocks_out[i // 2, i % 2, :, :group_cols] for i in range(4)], axis=1
        )
        last = qkv_blocks_out[:, :, :, group_cols : group_cols + HD]
        d_w_key = jnp.concatenate([last[0, 0], last[1, 0]], axis=1)
        d_w_value = jnp.concatenate([last[0, 1], last[1, 1]], axis=1)
        sums = qkv_blocks_out[:, :, :, group_cols + HD :]
        d_gain_attn = jnp.sum(sums[..., 0], axis=(0, 1))
        d_gain_mlp = jnp.sum(sums[..., 1], axis=(0, 1))
        d_bias_query = jnp.sum(sums[..., 2], axis=(0, 1))
        d_bias_key = jnp.sum(sums[:, 0, :kv_rows, 3], axis=0)
        d_bias_value = jnp.sum(sums[:, 1, :kv_rows, 3], axis=0)
        return (
            result[None],
            grad_input[None],
            d_w_query,
            d_w_key,
            d_w_value,
            d_w_output,
            d_gate_up,
            d_w_down,
            d_bias_query,
            d_bias_key,
            d_bias_value,
            d_gain_attn,
            d_gain_mlp,
        )

    return local


def solution(mesh):
    rows = P("fsdp", None)
    owners = P(("seq", "fsdp"))
    return jax.shard_map(
        build(mesh.shape["seq"], mesh.shape["fsdp"]),
        mesh=mesh,
        in_specs=(
            P("fsdp", "seq", None),
            rows,
            rows,
            rows,
            rows,
            rows,
            P("fsdp", None, None),
            rows,
            P("fsdp"),
            P("fsdp"),
            P("fsdp"),
            P("fsdp"),
            P("fsdp"),
            P("fsdp", "seq", None),
        ),
        out_specs=(
            P("fsdp", "seq", None),
            P("fsdp", "seq", None),
            P(("seq", "fsdp"), None),
            P(("seq", "fsdp"), None),
            P(("seq", "fsdp"), None),
            P(("seq", "fsdp"), None),
            P(("seq", "fsdp"), None, None),
            P(("seq", "fsdp"), None),
            owners,
            owners,
            owners,
            owners,
            owners,
        ),
        check_vma=False,
    )
```

time: 3600 us -> 956 us (0.27)
  waiting for transfers between devices: 3000 us -> 365 us
  blocking collectives: 147 us -> 0 us
  other arithmetic: 33.7 us -> 153 us
  matrix products: 236 us -> 179 us
  starting transfers between devices: 16 us -> 61.9 us
    all_gather x4 -> x0, waiting for transfers between devices: 1520 us -> none  [the longest x1 1020 us: local(): lax.all_gather(gate_up, 'fsdp', axis=0, tiled=True)]
    reduce_scatter x3 -> x0, waiting for transfers between devices: 944 us -> none  [local(): lax.psum_scatter(weight_term(left_side, right_side), ('seq', 'fsdp'), sca...]
    unnamed x9 -> x0, waiting for transfers between devices: 472 us -> none
    ppermute x0 -> x66, waiting for transfers between devices: none -> 365 us  [the longest x24 211 us: ring(): return lax.ppermute(value, 'fsdp', ring_perm)]
    unnamed x2 -> x0, blocking collectives: 79.7 us -> none
    all_gather x2 -> x0, blocking collectives: 67.7 us -> none  [the longest x1 34.2 us: local(): lax.all_gather(w_key, 'fsdp', axis=0, tiled=True)]
    all_to_all x4 -> x0, waiting for transfers between devices: 67 us -> none  [the longest x1 24.5 us: local(): lax.all_to_all(packed_back[:, None], 'seq', split_axis=0, concat_axis=1,...]
    ppermute x0 -> x66, starting transfers between devices: none -> 61.9 us  [the longest x24 22.8 us: ring(): return lax.ppermute(value, 'fsdp', ring_perm)]
  transfers between devices with their start and end apart: 12 -> 66, of which waited for: 9 -> 36; matrix products, arithmetic and copies ran while one was open for 8% -> 47% of each run, Pallas kernels for 0% -> 0%
where the time goes in v1:
time: 956 us; the launch traced here: 947 us
  waiting for transfers between devices  365 us (38%)
  matrix products  179 us (19%)
  local copies, waits for them, and re-layouts  166 us (17%)
  other arithmetic  153 us (16%)
  starting transfers between devices  61.9 us (6%)
  between operations  19.3 us (2%)
    ppermute x24, waiting for transfers between devices, ring(): return lax.ppermute(value, 'fsdp', ring_perm)  211 us
    ppermute x15, waiting for transfers between devices, swap_y(): return lax.ppermute(value, 'fsdp', y_perm)  105 us
    dot_general x8, matrix products, dot_t(): lax.dot_general(left, right, (((1,), (1,)), ((), ())), preferred_element_...  56 us
    dot_general x8, matrix products, dot(): return jnp.dot(left, right, preferred_element_type=F32)  50.5 us
    ppermute x16, waiting for transfers between devices, swap_x(): return lax.ppermute(value, 'seq', x_perm)  48 us
    dot_general x8, matrix products, t_dot(): lax.dot_general(left, right, (((0,), (0,)), ((), ())), preferred_element_...  38.9 us
    ppermute x24, starting transfers between devices, ring(): return lax.ppermute(value, 'fsdp', ring_perm)  22.8 us
    concatenate x2, other arithmetic, gather_plane(): return jnp.concatenate([left, right], axis=1)  22.7 us
  transfers between devices with their start and end apart: 66, of which 36 were waited for; matrix products, arithmetic and copies ran while one was open for 47% of the time, Pallas kernels for 0%

profile of v1, /device:TPU:0, one launch (start us, length us, event | category | flops | bytes accessed | tf_op | source)
XLA Modules:
  0.0 946.8 jit_solution(14293552021207350275)
XLA Ops:
  27.8 5.7 constant_dynamic-slice_fusion.6
  63.1 5.2 collective-permute-done.3
  82.3 7.9 collective-permute-done.9
  96.2 15.0 %collective-permute-done.5 = bf16[4,208,640]{2,1,0:T(8,128)(2,1)S(1)} collective-permute-done((bf16[4,208,640]{2,1,0:T(8,128)(2,1)}, bf16[4,208,640]{2,1,0:T(8,128)(2,1)S(1)}, u32[]{:S(2)}, u32[]{:S(2)}) %collective-permute-start.5) | collective-permute-done | bytes 1064992 | tf_op jit(solution)/shard_map/ppermute | solution.py:160
  132.0 16.2 %while.29 = (s32[]{:T(128)}, bf16[2,512,3,128]{3,1,2,0:T(8,128)(2,1)}, f32[2,3,512,1]{2,1,3,0:T(4,128)S(1)}, f32[2,3,512,1]{2,1,3,0:T(4,128)S(1)}, s32[2]{0:T(12...) while((s32[]{:T(128)}, ...), condition=%wide.region_6.7_spmd, body=%wide.region_3.6_spmd.sunk | while | flops 825947648 | bytes 22360276 | solution.py:88
  168.0 14.0 %collective-permute-done.32 = bf16[2,256,768]{2,1,0:T(8,128)(2,1)} collective-permute-done((bf16[2,256,768]{2,1,0:T(8,128)(2,1)}, bf16[2,256,768]{2,1,0:T(8,128)(2,1)}, u32[]{:S(2)}, u32[]{:S(2)}) %collective-permute-start.32) | collective-permute-done | bytes 786464 | tf_op jit(solution)/shard_map/ppermute | solution.py:154
  196.7 30.9 %collective-permute-done.17 = bf16[3,384,768]{2,1,0:T(8,128)(2,1)} collective-permute-done((bf16[3,384,768]{2,1,0:T(8,128)(2,1)}, bf16[3,384,768]{2,1,0:T(8,128)(2,1)}, u32[]{:S(2)}, u32[]{:S(2)}) %collective-permute-start.17) | collective-permute-done | bytes 1769504 | tf_op jit(solution)/shard_map/ppermute | solution.py:163
  229.7 16.7 %collective-permute-done.23 = bf16[3,384,384]{2,1,0:T(8,128)(2,1)S(1)} collective-permute-done((bf16[3,384,384]{2,1,0:T(8,128)(2,1)}, bf16[3,384,384]{2,1,0:T(8,128)(2,1)S(1)}, u32[]{:S(2)}, u32[]{:S(2)}) %collective-permute-start.23) | collective-permute-done | bytes 884768 | tf_op jit(solution)/shard_map/ppermute | solution.py:163
  250.0 10.4 %maximum_maximum_fusion.1 = bf16[1024,1536]{1,0:T(8,128)(2,1)S(1)} fusion(bf16[256,768]{1,0:T(8,128)(2,1)S(1)} %copy-done.68, bf16[256,768]{1,0:T(8,128)(2,1)S(1)} %copy-done.67, bf16[256,768]{1,0:T(8,128)(2,1)} %collective-permute-done.31, bf16[256,768]{1,0:T(8,128)(2,1)} %get-tuple-element.586, bf16[256,768]{1,0:T(8,128)(2,1)S(1)} %copy-done.70, ...), kind=kLoop, calls=%fused_computation.111 | loop fusion | flops 25165824 | bytes 6291456 | tf_op jit(solution)/shard_map/concatenate | solution.py:238
  267.6 15.3 %collective-permute-done.18 = bf16[3,384,768]{2,1,0:T(8,128)(2,1)S(1)} collective-permute-done((bf16[3,384,768]{2,1,0:T(8,128)(2,1)}, bf16[3,384,768]{2,1,0:T(8,128)(2,1)S(1)}, u32[]{:S(2)}, u32[]{:S(2)}) %collective-permute-start.18) | collective-permute-done | bytes 1769504 | tf_op jit(solution)/shard_map/ppermute | solution.py:163
  288.9 12.2 %collective-permute-done.13 = bf16[2,256,768]{2,1,0:T(8,128)(2,1)S(1)} collective-permute-done((bf16[2,256,768]{2,1,0:T(8,128)(2,1)S(1)}, bf16[2,256,768]{2,1,0:T(8,128)(2,1)S(1)}, u32[]{:S(2)}, u32[]{:S(2)}) %collective-permute-start.13) | collective-permute-done | bytes 786464 | tf_op jit(solution)/shard_map/ppermute | solution.py:160
  301.1 12.2 %maximum_maximum_fusion = bf16[1024,1536]{1,0:T(8,128)(2,1)S(1)} fusion(bf16[256,768]{1,0:T(8,128)(2,1)S(1)} %get-tuple-element.596, bf16[256,768]{1,0:T(8,128)(2,1)S(1)} %get-tuple-element.595, bf16[256,768]{1,0:T(8,128)(2,1)S(1)} %collective-permute-done.14, bf16[256,768]{1,0:T(8,128)(2,1)S(1)} %get-tuple-element.593, ...), kind=kLoop, calls=%fused_computation.110 | loop fusion | flops 25165824 | bytes 6291456 | tf_op jit(solution)/shard_map/concatenate | solution.py:238
  313.4 9.5 %collective-permute-done.19 = bf16[3,384,768]{2,1,0:T(8,128)(2,1)S(1)} collective-permute-done((bf16[3,384,768]{2,1,0:T(8,128)(2,1)S(1)}, bf16[3,384,768]{2,1,0:T(8,128)(2,1)S(1)}, u32[]{:S(2)}, u32[]{:S(2)}) %collective-permute-start.19) | collective-permute-done | bytes 1769504 | tf_op jit(solution)/shard_map/ppermute | solution.py:163
  332.9 4.8 multiply_convert_fusion.4
  368.0 5.1 fusion.46
  378.6 6.6 fusion.166
  385.4 13.9 %collective-permute-done.61 = bf16[3,2,2,48,768]{4,3,2,1,0:T(8,128)(2,1)S(1)} collective-permute-done((bf16[3,2,2,48,768]{4,3,2,1,0:T(8,128)(2,1)S(1)}, bf16[3,2,2,48,768]{4,3,2,1,0:T(8,128)(2,1)S(1)}, u32[]{:S(2)}, u32[]{:S(2)}) %collective-permute-start.61) | collective-permute-done | bytes 884768 | tf_op jit(solution)/shard_map/ppermute | solution.py:163
  399.7 6.2 fusion.164
  406.3 15.2 %collective-permute-done.62 = bf16[3,2,2,48,768]{4,3,2,1,0:T(8,128)(2,1)S(1)} collective-permute-done((bf16[3,2,2,48,768]{4,3,2,1,0:T(8,128)(2,1)S(1)}, bf16[3,2,2,48,768]{4,3,2,1,0:T(8,128)(2,1)S(1)}, u32[]{:S(2)}, u32[]{:S(2)}) %collective-permute-start.62) | collective-permute-done | bytes 884768 | tf_op jit(solution)/shard_map/ppermute | solution.py:163
  422.8 10.0 %fusion.178 = f32[1024,1536]{1,0:T(8,128)} fusion(bf16[1024,1536]{1,0:T(8,128)(2,1)S(1)} %copy-done.44, bf16[3,1536,768]{2,1,0:T(8,128)(2,1)} %bitcast.78, bf16[3,1536,768]{2,1,0:T(8,128)(2,1)} %collective-permute-done.20), kind=kOutput, calls=%fused_computation.477 | convolution fusion | flops 4841275392 | bytes 23592960 | tf_op jit(solution)/shard_map/dot_general | solution.py:128
  432.8 10.0 %fusion.182 = f32[1024,1536]{1,0:T(8,128)} fusion(bf16[1024,1536]{1,0:T(8,128)(2,1)S(1)} %copy-done.44, bf16[3,1536,768]{2,1,0:T(8,128)(2,1)} %bitcast.78, bf16[3,1536,768]{2,1,0:T(8,128)(2,1)} %collective-permute-done.20), kind=kOutput, calls=%fused_computation.479 | convolution fusion | flops 4841275392 | bytes 23592960 | tf_op jit(solution)/shard_map/dot_general | solution.py:128
  442.8 13.3 %multiply_convert_fusion = (bf16[1024,1536]{1,0:T(8,128)(2,1)S(1)}, bf16[1024,1536]{1,0:T(8,128)(2,1)S(1)}, bf16[1024,1536]{1,0:T(8,128)(2,1)}) fusion(f32[1024,1536]{1,0:T(8,128)} %fusion.178, f32[1024,1536]{1,0:T(8,128)} %fusion.182, bf16[1024,1536]{1,0:T(8,128)(2,1)} %copy-done.47, bf16[3,1536,768]{2,1,0:T(8,128)(2,1)} %collective-permute-done.20, ...), kind=kOutput, calls=%fused_computation.76 | convolution fusion | flops 4864868352 | bytes 39321600 | tf_op jit(solution)/shard_map/dot_general | solution.py:128
  456.1 10.4 %fusion.176 = f32[1024,1536]{1,0:T(8,128)} fusion(bf16[1024,1536]{1,0:T(8,128)(2,1)S(1)} %get-tuple-element.509, bf16[3,1536,768]{2,1,0:T(8,128)(2,1)} %bitcast.78, bf16[3,1536,768]{2,1,0:T(8,128)(2,1)} %collective-permute-done.20), kind=kOutput, calls=%fused_computation.476 | convolution fusion | flops 4841275392 | bytes 23592960 | tf_op jit(solution)/shard_map/dot_general | solution.py:132
  466.5 8.9 fusion.180
  475.4 9.9 %add_add_fusion = f32[1024,1536]{1,0:T(8,128)S(1)} fusion(f32[1024,1536]{1,0:T(8,128)} %fusion.166, f32[1024,1536]{1,0:T(8,128)} %fusion.176, f32[1024,1536]{1,0:T(8,128)} %fusion.180, bf16[1024,768]{1,0:T(8,128)(2,1)} %copy-done.64, bf16[3,1536,384]{2,1,0:T(8,128)(2,1)} %bitcast.90, bf16[3,1536,384]{2,1,0:T(8,128)(2,1)S(1)} %copy-done.41), kind=kOutput, calls=%fused_computation.75 | convolution fusion | flops 2425356288 | bytes 33816576 | tf_op jit(solution)/shard_map/dot_general | solution.py:132
  485.9 9.1 convolution_add_fusion
  495.5 8.1 convolution_convert_fusion
  507.8 8.6 convolution_convert_fusion.1
  516.4 7.8 collective-permute-done.33
  528.7 12.4 %collective-permute-done.25 = bf16[2,256,768]{2,1,0:T(8,128)(2,1)S(1)} collective-permute-done((bf16[2,256,768]{2,1,0:T(8,128)(2,1)S(1)}, bf16[2,256,768]{2,1,0:T(8,128)(2,1)S(1)}, u32[]{:S(2)}, u32[]{:S(2)}) %collective-permute-start.25) | collective-permute-done | bytes 786464 | tf_op jit(solution)/shard_map/ppermute | solution.py:160
  559.6 5.5 convolution_convert_fusion.2
  565.1 9.5 %collective-permute-done.37 = bf16[256,1536]{1,0:T(8,128)(2,1)S(1)} collective-permute-done((bf16[256,1536]{1,0:T(8,128)(2,1)S(1)}, bf16[256,1536]{1,0:T(8,128)(2,1)S(1)}, u32[]{:S(2)}, u32[]{:S(2)}) %collective-permute-start.37) | collective-permute-done | bytes 786464 | tf_op jit(solution)/shard_map/ppermute | solution.py:154
  575.0 6.2 pad_maximum_fusion
  584.3 6.7 copy_bitcast_fusion
  602.0 38.1 %while.30 = (s32[]{:T(128)}, f32[1024,128]{1,0:T(8,128)S(1)}, f32[1024,128]{1,0:T(8,128)S(1)}, bf16[2,512,3,128]{3,1,0,2:T(8,128)(2,1)}, s32[2]{0:T(128)S(1)}, /...) while((s32[]{:T(128)}, f32[1024,128]{1,0:T(8,128)S(1)}, ...), condition=%wide.region_12.13_spmd.clone, body=%wide.region_10.12_spmd.clone.sunk | while | flops 2031614976 | bytes 97192304 | solution.py:123
  651.4 4.9 copy.496
  674.5 5.8 rev.39
  680.4 6.1 collective-permute-done.48
  687.9 5.7 fusion.132
  700.3 8.0 bitcast_convert_fusion.1
  718.1 36.5 %collective-permute-done.51 = bf16[2,2,48,384]{3,2,1,0:T(8,128)(2,1)S(1)} collective-permute-done((bf16[2,2,48,384]{3,2,1,0:T(8,128)(2,1)S(1)}, bf16[2,2,48,384]{3,2,1,0:T(8,128)(2,1)S(1)}, u32[]{:S(2)}, u32[]{:S(2)}) %collective-permute-start.51) | collective-permute-done | bytes 147488 | tf_op jit(solution)/shard_map/ppermute | solution.py:163
  761.9 5.5 copy.492
  779.3 15.6 %collective-permute-done.42 = bf16[2,2,4,48,640]{4,3,2,1,0:T(8,128)(2,1)S(1)} collective-permute-done((bf16[2,2,4,48,640]{4,3,2,1,0:T(8,128)(2,1)S(1)}, bf16[2,2,4,48,640]{4,3,2,1,0:T(8,128)(2,1)S(1)}, u32[]{:S(2)}, u32[]{:S(2)}) %collective-permute-start.42) | collective-permute-done | bytes 983072 | tf_op jit(solution)/shard_map/ppermute | solution.py:160
  797.6 18.9 %collective-permute-done.43 = bf16[2,2,48,640]{3,2,1,0:T(8,128)(2,1)S(1)} collective-permute-done((bf16[2,2,48,640]{3,2,1,0:T(8,128)(2,1)S(1)}, bf16[2,2,48,640]{3,2,1,0:T(8,128)(2,1)S(1)}, u32[]{:S(2)}, u32[]{:S(2)}) %collective-permute-start.43) | collective-permute-done | bytes 245792 | tf_op jit(solution)/shard_map/ppermute | solution.py:163
  828.7 35.9 %collective-permute-done.45 = bf16[2,2,48,640]{3,2,1,0:T(8,128)(2,1)S(1)} collective-permute-done((bf16[2,2,48,640]{3,2,1,0:T(8,128)(2,1)S(1)}, bf16[2,2,48,640]{3,2,1,0:T(8,128)(2,1)S(1)}, u32[]{:S(2)}, u32[]{:S(2)}) %collective-permute-start.45) | collective-permute-done | bytes 245792 | tf_op jit(solution)/shard_map/ppermute | solution.py:163
  877.0 17.4 %collective-permute-done.58 = bf16[3,2,48,1536]{3,2,1,0:T(8,128)(2,1)S(1)} collective-permute-done((bf16[3,2,48,1536]{3,2,1,0:T(8,128)(2,1)S(1)}, bf16[3,2,48,1536]{3,2,1,0:T(8,128)(2,1)S(1)}, u32[]{:S(2)}, u32[]{:S(2)}) %collective-permute-start.58) | collective-permute-done | bytes 884768 | tf_op jit(solution)/shard_map/ppermute | solution.py:154
  899.4 16.4 %collective-permute-done.59 = bf16[3,2,48,1536]{3,2,1,0:T(8,128)(2,1)S(1)} collective-permute-done((bf16[3,2,48,1536]{3,2,1,0:T(8,128)(2,1)S(1)}, bf16[3,2,48,1536]{3,2,1,0:T(8,128)(2,1)S(1)}, u32[]{:S(2)}, u32[]{:S(2)}) %collective-permute-start.59) | collective-permute-done | bytes 884768 | tf_op jit(solution)/shard_map/ppermute | solution.py:160
  922.1 13.9 %rev.36 = bf16[3,4,48,2,768]{4,3,2,1,0:T(2,128)(2,1)} reverse(bf16[3,4,48,2,768]{4,3,2,1,0:T(2,128)(2,1)S(1)} %reshape.821), dimensions={3} | reverse | bytes 3538944 | tf_op jit(solution)/shard_map/rev | solution.py:394
  (650 shorter events, 390.7 us)
Async XLA Ops:
  5.9 50.6 %collective-permute-start.2 = (bf16[208,640]{1,0:T(8,128)(2,1)}, bf16[208,640]{1,0:T(8,128)(2,1)}, u32[]{:S(2)}, u32[]{:S(2)}) collective-permute-start(bf16[208,640]{1,0:T(8,128)(2,1)} %maximum_maximum_fusion.2), channel_id=1, source_target_pairs={{0,2},{1,3},{2,6},{3,7},{4,0},{5,1},{6,4},{7,5},{8,10},{9,11},{10,... | collective-permute-start | bytes 798728 | tf_op jit(solution)/shard_map/ppermute | solution.py:163
  9.0 68.9 %collective-permute-start = (bf16[256,1536]{1,0:T(8,128)(2,1)}, bf16[256,1536]{1,0:T(8,128)(2,1)}, u32[]{:S(2)}, u32[]{:S(2)}) collective-permute-start(bf16[256,1536]{1,0:T(8,128)(2,1)} %bitcast.737), channel_id=1, source_target_pairs={{0,16},{8,24},{16,0},{24,8},{1,17},{9,25},{17,1},{25,9},{2,18},{10... | collective-permute-start | bytes 2359304 | tf_op jit(solution)/shard_map/ppermute | solution.py:154
  21.4 33.7 %collective-permute-start.6 = (bf16[192,384]{1,0:T(8,128)(2,1)}, bf16[192,384]{1,0:T(8,128)(2,1)}, u32[]{:S(2)}, u32[]{:S(2)}) collective-permute-start(bf16[192,384]{1,0:T(8,128)(2,1)} %get-tuple-element.499), channel_id=1, source_target_pairs={{0,2},{1,3},{2,6},{3,7},{4,0},{5,1},{6,4},{7,5},{8,10},{9,11},{10,... | collective-permute-start | bytes 442376 | tf_op jit(solution)/shard_map/ppermute | solution.py:163
  36.9 55.3 %collective-permute-start.16 = (bf16[3,192,1152]{2,1,0:T(8,128)(2,1)}, bf16[3,192,1152]{2,1,0:T(8,128)(2,1)}, u32[]{:S(2)}, u32[]{:S(2)}) collective-permute-start(bf16[3,192,1152]{2,1,0:T(8,128)(2,1)} %maximum_select_fusion.8), channel_id=1, source_target_pairs={{0,1},{1,0},{2,3},{3,2},{4,5},{5,4},{6,7},{7,6},{8,9},{9,8},{10,11... | collective-permute-start | bytes 3981320 | tf_op jit(solution)/shard_map/ppermute | solution.py:160
  39.6 119.9 %collective-permute-start.31 = (bf16[256,768]{1,0:T(8,128)(2,1)}, bf16[256,768]{1,0:T(8,128)(2,1)}, u32[]{:S(2)}, u32[]{:S(2)}) collective-permute-start(bf16[256,768]{1,0:T(8,128)(2,1)} %get-tuple-element.586), channel_id=1, source_target_pairs={{0,1},{1,0},{2,3},{3,2},{4,5},{5,4},{6,7},{7,6},{8,9},{9,8},{10,11... | collective-permute-start | bytes 1179656 | tf_op jit(solution)/shard_map/ppermute | solution.py:160
  76.3 34.9 %collective-permute-start.5 = (bf16[4,208,640]{2,1,0:T(8,128)(2,1)}, bf16[4,208,640]{2,1,0:T(8,128)(2,1)S(1)}, u32[]{:S(2)}, u32[]{:S(2)}) collective-permute-start(bf16[4,208,640]{2,1,0:T(8,128)(2,1)} %bitcast_dynamic-update-slice_fusion.10), channel_id=1, source_target_pairs={{0,1},{1,0},{2,3},{3,2},{4,5},{5,4},{6,7},{7,6},{8,9},{9,8},{10,11... | collective-permute-start | bytes 3194888 | tf_op jit(solution)/shard_map/ppermute | solution.py:160
  80.6 34.7 %collective-permute-start.1 = (bf16[2,256,1536]{2,1,0:T(8,128)(2,1)}, bf16[2,256,1536]{2,1,0:T(8,128)(2,1)}, u32[]{:S(2)}, u32[]{:S(2)}) collective-permute-start(bf16[2,256,1536]{2,1,0:T(8,128)(2,1)} %maximum_select_fusion.5), channel_id=1, source_target_pairs={{0,8},{8,0},{16,24},{24,16},{1,9},{9,1},{17,25},{25,17},{2,10},{10... | collective-permute-start | bytes 4718600 | tf_op jit(solution)/shard_map/ppermute | solution.py:157
  90.2 72.1 %collective-permute-start.29 = (bf16[256,768]{1,0:T(8,128)(2,1)}, bf16[256,768]{1,0:T(8,128)(2,1)}, u32[]{:S(2)}, u32[]{:S(2)}) collective-permute-start(bf16[256,768]{1,0:T(8,128)(2,1)} %get-tuple-element.585), channel_id=1, source_target_pairs={{0,16},{8,24},{16,0},{24,8},{1,17},{9,25},{17,1},{25,9},{2,18},{10... | collective-permute-start | bytes 1179656 | tf_op jit(solution)/shard_map/ppermute | solution.py:154
  95.5 70.3 %collective-permute-start.21 = (bf16[3,384,384]{2,1,0:T(8,128)(2,1)}, bf16[3,384,384]{2,1,0:T(8,128)(2,1)}, u32[]{:S(2)}, u32[]{:S(2)}) collective-permute-start(bf16[3,384,384]{2,1,0:T(8,128)(2,1)} %slice.552), channel_id=1, source_target_pairs={{0,2},{1,3},{2,6},{3,7},{4,0},{5,1},{6,4},{7,5},{8,10},{9,11},{10,... | collective-permute-start | bytes 2654216 | tf_op jit(solution)/shard_map/ppermute | solution.py:163
  159.5 30.3 %collective-permute-start.10 = (bf16[2,256,1536]{2,1,0:T(8,128)(2,1)}, bf16[2,256,1536]{2,1,0:T(8,128)(2,1)}, u32[]{:S(2)}, u32[]{:S(2)}) collective-permute-start(bf16[2,256,1536]{2,1,0:T(8,128)(2,1)} %fusion.86), channel_id=1, source_target_pairs={{0,8},{8,0},{16,24},{24,16},{1,9},{9,1},{17,25},{25,17},{2,10},{10... | collective-permute-start | bytes 4718600 | tf_op jit(solution)/shard_map/ppermute | solution.py:157
  161.9 20.0 %collective-permute-start.32 = (bf16[2,256,768]{2,1,0:T(8,128)(2,1)}, bf16[2,256,768]{2,1,0:T(8,128)(2,1)}, u32[]{:S(2)}, u32[]{:S(2)}) collective-permute-start(bf16[2,256,768]{2,1,0:T(8,128)(2,1)} %pad_maximum_fusion.15), channel_id=1, source_target_pairs={{0,16},{8,24},{16,0},{24,8},{1,17},{9,25},{17,1},{25,9},{2,18},{10... | collective-permute-start | bytes 2359304 | tf_op jit(solution)/shard_map/ppermute | solution.py:154
  164.3 19.7 %collective-permute-start.30 = (bf16[2,256,768]{2,1,0:T(8,128)(2,1)}, bf16[2,256,768]{2,1,0:T(8,128)(2,1)}, u32[]{:S(2)}, u32[]{:S(2)}) collective-permute-start(bf16[2,256,768]{2,1,0:T(8,128)(2,1)} %pad_maximum_fusion.14), channel_id=1, source_target_pairs={{0,1},{1,0},{2,3},{3,2},{4,5},{5,4},{6,7},{7,6},{8,9},{9,8},{10,11... | collective-permute-start | bytes 2359304 | tf_op jit(solution)/shard_map/ppermute | solution.py:160
  165.9 23.8 %collective-permute-start.22 = (bf16[3,384,384]{2,1,0:T(8,128)(2,1)}, bf16[3,384,384]{2,1,0:T(8,128)(2,1)}, u32[]{:S(2)}, u32[]{:S(2)}) collective-permute-start(bf16[3,384,384]{2,1,0:T(8,128)(2,1)} %collective-permute-done.21), channel_id=1, source_target_pairs={{0,2},{1,3},{2,6},{3,7},{4,0},{5,1},{6,4},{7,5},{8,10},{9,11},{10,... | collective-permute-start | bytes 2654216 | tf_op jit(solution)/shard_map/ppermute | solution.py:163
  167.6 59.9 %collective-permute-start.17 = (bf16[3,384,768]{2,1,0:T(8,128)(2,1)}, bf16[3,384,768]{2,1,0:T(8,128)(2,1)}, u32[]{:S(2)}, u32[]{:S(2)}) collective-permute-start(bf16[3,384,768]{2,1,0:T(8,128)(2,1)} %slice.547), channel_id=1, source_target_pairs={{0,2},{1,3},{2,6},{3,7},{4,0},{5,1},{6,4},{7,5},{8,10},{9,11},{10,... | collective-permute-start | bytes 5308424 | tf_op jit(solution)/shard_map/ppermute | solution.py:163
  189.7 56.8 %collective-permute-start.23 = (bf16[3,384,384]{2,1,0:T(8,128)(2,1)}, bf16[3,384,384]{2,1,0:T(8,128)(2,1)S(1)}, u32[]{:S(2)}, u32[]{:S(2)}) collective-permute-start(bf16[3,384,384]{2,1,0:T(8,128)(2,1)} %collective-permute-done.22), channel_id=1, source_target_pairs={{0,2},{1,3},{2,6},{3,7},{4,0},{5,1},{6,4},{7,5},{8,10},{9,11},{10,... | collective-permute-start | bytes 2654216 | tf_op jit(solution)/shard_map/ppermute | solution.py:163
  192.8 54.7 %collective-permute-start.11 = (bf16[256,1536]{1,0:T(8,128)(2,1)S(1)}, bf16[256,1536]{1,0:T(8,128)(2,1)S(1)}, u32[]{:S(2)}, u32[]{:S(2)}) collective-permute-start(bf16[256,1536]{1,0:T(8,128)(2,1)S(1)} %fusion.103), channel_id=1, source_target_pairs={{0,16},{8,24},{16,0},{24,8},{1,17},{9,25},{17,1},{25,9},{2,18},{10... | collective-permute-start | bytes 2359304 | tf_op jit(solution)/shard_map/ppermute | solution.py:154
  227.6 55.3 %collective-permute-start.18 = (bf16[3,384,768]{2,1,0:T(8,128)(2,1)}, bf16[3,384,768]{2,1,0:T(8,128)(2,1)S(1)}, u32[]{:S(2)}, u32[]{:S(2)}) collective-permute-start(bf16[3,384,768]{2,1,0:T(8,128)(2,1)} %collective-permute-done.17), channel_id=1, source_target_pairs={{0,2},{1,3},{2,6},{3,7},{4,0},{5,1},{6,4},{7,5},{8,10},{9,11},{10,... | collective-permute-start | bytes 5308424 | tf_op jit(solution)/shard_map/ppermute | solution.py:163
  247.5 76.8 %collective-permute-start.24 = (bf16[3,1536,384]{2,1,0:T(8,128)(2,1)}, bf16[3,1536,384]{2,1,0:T(8,128)(2,1)S(1)}, u32[]{:S(2)}, u32[]{:S(2)}) collective-permute-start(bf16[3,1536,384]{2,1,0:T(8,128)(2,1)} %bitcast.90), channel_id=1, source_target_pairs={{0,8},{8,0},{16,24},{24,16},{1,9},{9,1},{17,25},{25,17},{2,10},{10... | collective-permute-start | bytes 10616840 | tf_op jit(solution)/shard_map/ppermute | solution.py:157
  260.5 22.4 %collective-permute-start.12 = (bf16[256,768]{1,0:T(8,128)(2,1)S(1)}, bf16[256,768]{1,0:T(8,128)(2,1)S(1)}, u32[]{:S(2)}, u32[]{:S(2)}) collective-permute-start(bf16[256,768]{1,0:T(8,128)(2,1)S(1)} %get-tuple-element.594), channel_id=1, source_target_pairs={{0,16},{8,24},{16,0},{24,8},{1,17},{9,25},{17,1},{25,9},{2,18},{10... | collective-permute-start | bytes 1179656 | tf_op jit(solution)/shard_map/ppermute | solution.py:154
  262.2 26.6 %collective-permute-start.15 = (bf16[2,256,768]{2,1,0:T(8,128)(2,1)S(1)}, bf16[2,256,768]{2,1,0:T(8,128)(2,1)S(1)}, u32[]{:S(2)}, u32[]{:S(2)}) collective-permute-start(bf16[2,256,768]{2,1,0:T(8,128)(2,1)S(1)} %pad_maximum_fusion.13), channel_id=1, source_target_pairs={{0,16},{8,24},{16,0},{24,8},{1,17},{9,25},{17,1},{25,9},{2,18},{10... | collective-permute-start | bytes 2359304 | tf_op jit(solution)/shard_map/ppermute | solution.py:154
  282.9 40.0 %collective-permute-start.19 = (bf16[3,384,768]{2,1,0:T(8,128)(2,1)S(1)}, bf16[3,384,768]{2,1,0:T(8,128)(2,1)S(1)}, u32[]{:S(2)}, u32[]{:S(2)}) collective-permute-start(bf16[3,384,768]{2,1,0:T(8,128)(2,1)S(1)} %collective-permute-done.18), channel_id=1, source_target_pairs={{0,2},{1,3},{2,6},{3,7},{4,0},{5,1},{6,4},{7,5},{8,10},{9,11},{10,... | collective-permute-start | bytes 5308424 | tf_op jit(solution)/shard_map/ppermute | solution.py:163
  324.2 98.5 %collective-permute-start.20 = (bf16[3,1536,768]{2,1,0:T(8,128)(2,1)}, bf16[3,1536,768]{2,1,0:T(8,128)(2,1)}, u32[]{:S(2)}, u32[]{:S(2)}) collective-permute-start(bf16[3,1536,768]{2,1,0:T(8,128)(2,1)} %bitcast.78), channel_id=1, source_target_pairs={{0,8},{8,0},{16,24},{24,16},{1,9},{9,1},{17,25},{25,17},{2,10},{10... | collective-permute-start | bytes 21233672 | tf_op jit(solution)/shard_map/ppermute | solution.py:157
  351.6 21.4 %collective-permute-start.60 = (bf16[3,2,4,2,48,768]{5,4,3,1,0,2:T(8,128)(2,1)}, bf16[3,2,4,2,48,768]{5,4,3,1,0,2:T(8,128)(2,1)}, u32[]{:S(2)}, u32[]{:S(2)}) collective-permute-start(bf16[3,2,4,2,48,768]{5,4,3,1,0,2:T(8,128)(2,1)} %copy_bitcast_fusion.1), channel_id=1, source_target_pairs={{0,8},{8,0},{16,24},{24,16},{1,9},{9,1},{17,25},{25,17},{2,10},{10... | collective-permute-start | bytes 10616840 | tf_op jit(solution)/shard_map/ppermute | solution.py:157
  376.6 22.6 %collective-permute-start.61 = (bf16[3,2,2,48,768]{4,3,2,1,0:T(8,128)(2,1)S(1)}, bf16[3,2,2,48,768]{4,3,2,1,0:T(8,128)(2,1)S(1)}, u32[]{:S(2)}, u32[]{:S(2)}) collective-permute-start(bf16[3,2,2,48,768]{4,3,2,1,0:T(8,128)(2,1)S(1)} %fusion.78), channel_id=1, source_target_pairs={{0,2},{1,3},{2,6},{3,7},{4,0},{5,1},{6,4},{7,5},{8,10},{9,11},{10,... | collective-permute-start | bytes 2654216 | tf_op jit(solution)/shard_map/ppermute | solution.py:163
  399.7 21.8 %collective-permute-start.62 = (bf16[3,2,2,48,768]{4,3,2,1,0:T(8,128)(2,1)S(1)}, bf16[3,2,2,48,768]{4,3,2,1,0:T(8,128)(2,1)S(1)}, u32[]{:S(2)}, u32[]{:S(2)}) collective-permute-start(bf16[3,2,2,48,768]{4,3,2,1,0:T(8,128)(2,1)S(1)} %fusion.77), channel_id=1, source_target_pairs={{0,2},{1,3},{2,6},{3,7},{4,0},{5,1},{6,4},{7,5},{8,10},{9,11},{10,... | collective-permute-start | bytes 2654216 | tf_op jit(solution)/shard_map/ppermute | solution.py:163
  422.8 158.4 %collective-permute-start.63 = (bf16[3,2,2,48,768]{4,3,2,1,0:T(8,128)(2,1)}, bf16[3,2,2,48,768]{4,3,2,1,0:T(8,128)(2,1)}, u32[]{:S(2)}, u32[]{:S(2)}) collective-permute-start(bf16[3,2,2,48,768]{4,3,2,1,0:T(8,128)(2,1)} %fusion.75), channel_id=1, source_target_pairs={{0,2},{1,3},{2,6},{3,7},{4,0},{5,1},{6,4},{7,5},{8,10},{9,11},{10,... | collective-permute-start | bytes 2654216 | tf_op jit(solution)/shard_map/ppermute | solution.py:163
  503.6 20.5 %collective-permute-start.33 = (bf16[2,256,768]{2,1,0:T(8,128)(2,1)S(1)}, bf16[2,256,768]{2,1,0:T(8,128)(2,1)S(1)}, u32[]{:S(2)}, u32[]{:S(2)}) collective-permute-start(bf16[2,256,768]{2,1,0:T(8,128)(2,1)S(1)} %slice_bitcast_fusion.10), channel_id=1, source_target_pairs={{0,1},{1,0},{2,3},{3,2},{4,5},{5,4},{6,7},{7,6},{8,9},{9,8},{10,11... | collective-permute-start | bytes 2359304 | tf_op jit(solution)/shard_map/ppermute | solution.py:160
  504.2 20.5 %collective-permute-start.35 = (bf16[2,256,768]{2,1,0:T(8,128)(2,1)S(1)}, bf16[2,256,768]{2,1,0:T(8,128)(2,1)S(1)}, u32[]{:S(2)}, u32[]{:S(2)}) collective-permute-start(bf16[2,256,768]{2,1,0:T(8,128)(2,1)S(1)} %slice_bitcast_fusion.8), channel_id=1, source_target_pairs={{0,16},{8,24},{16,0},{24,8},{1,17},{9,25},{17,1},{25,9},{2,18},{10... | collective-permute-start | bytes 2359304 | tf_op jit(solution)/shard_map/ppermute | solution.py:154
  506.2 34.9 %collective-permute-start.25 = (bf16[2,256,768]{2,1,0:T(8,128)(2,1)S(1)}, bf16[2,256,768]{2,1,0:T(8,128)(2,1)S(1)}, u32[]{:S(2)}, u32[]{:S(2)}) collective-permute-start(bf16[2,256,768]{2,1,0:T(8,128)(2,1)S(1)} %slice_bitcast_fusion.14), channel_id=1, source_target_pairs={{0,1},{1,0},{2,3},{3,2},{4,5},{5,4},{6,7},{7,6},{8,9},{9,8},{10,11... | collective-permute-start | bytes 2359304 | tf_op jit(solution)/shard_map/ppermute | solution.py:160
  507.6 34.0 %collective-permute-start.27 = (bf16[2,256,768]{2,1,0:T(8,128)(2,1)S(1)}, bf16[2,256,768]{2,1,0:T(8,128)(2,1)S(1)}, u32[]{:S(2)}, u32[]{:S(2)}) collective-permute-start(bf16[2,256,768]{2,1,0:T(8,128)(2,1)S(1)} %slice_bitcast_fusion.12), channel_id=1, source_target_pairs={{0,16},{8,24},{16,0},{24,8},{1,17},{9,25},{17,1},{25,9},{2,18},{10... | collective-permute-start | bytes 2359304 | tf_op jit(solution)/shard_map/ppermute | solution.py:154
  525.1 24.3 %collective-permute-start.36 = (bf16[256,768]{1,0:T(8,128)(2,1)S(1)}, bf16[256,768]{1,0:T(8,128)(2,1)S(1)}, u32[]{:S(2)}, u32[]{:S(2)}) collective-permute-start(bf16[256,768]{1,0:T(8,128)(2,1)S(1)} %fusion.131), channel_id=1, source_target_pairs={{0,1},{1,0},{2,3},{3,2},{4,5},{5,4},{6,7},{7,6},{8,9},{9,8},{10,11... | collective-permute-start | bytes 1179656 | tf_op jit(solution)/shard_map/ppermute | solution.py:160
  526.7 23.3 %collective-permute-start.34 = (bf16[256,768]{1,0:T(8,128)(2,1)S(1)}, bf16[256,768]{1,0:T(8,128)(2,1)S(1)}, u32[]{:S(2)}, u32[]{:S(2)}) collective-permute-start(bf16[256,768]{1,0:T(8,128)(2,1)S(1)} %fusion.130), channel_id=1, source_target_pairs={{0,16},{8,24},{16,0},{24,8},{1,17},{9,25},{17,1},{25,9},{2,18},{10... | collective-permute-start | bytes 1179656 | tf_op jit(solution)/shard_map/ppermute | solution.py:154
  574.9 23.4 %collective-permute-start.38 = (bf16[2,256,1536]{2,1,0:T(8,128)(2,1)S(1)}, bf16[2,256,1536]{2,1,0:T(8,128)(2,1)S(1)}, u32[]{:S(2)}, u32[]{:S(2)}) collective-permute-start(bf16[2,256,1536]{2,1,0:T(8,128)(2,1)S(1)} %maximum_select_fusion.6), channel_id=1, source_target_pairs={{0,8},{8,0},{16,24},{24,16},{1,9},{9,1},{17,25},{25,17},{2,10},{10... | collective-permute-start | bytes 4718600 | tf_op jit(solution)/shard_map/ppermute | solution.py:157
  591.0 109.3 %collective-permute-start.54 = (bf16[3,2,4,2,48,1536]{5,4,3,1,0,2:T(8,128)(2,1)}, bf16[3,2,4,2,48,1536]{5,4,3,1,0,2:T(8,128)(2,1)}, u32[]{:S(2)}, u32[]{:S(2)}) collective-permute-start(bf16[3,2,4,2,48,1536]{5,4,3,1,0,2:T(8,128)(2,1)} %copy_bitcast_fusion), channel_id=1, source_target_pairs={{0,8},{8,0},{16,24},{24,16},{1,9},{9,1},{17,25},{25,17},{2,10},{10... | collective-permute-start | bytes 21233672 | tf_op jit(solution)/shard_map/ppermute | solution.py:157
  596.4 76.5 %collective-permute-start.65 = (bf16[3,2,48,768]{3,2,1,0:T(8,128)(2,1)}, bf16[3,2,48,768]{3,2,1,0:T(8,128)(2,1)}, u32[]{:S(2)}, u32[]{:S(2)}) collective-permute-start(bf16[3,2,48,768]{3,2,1,0:T(8,128)(2,1)} %get-tuple-element.577), channel_id=1, source_target_pairs={{0,16},{8,24},{16,0},{24,8},{1,17},{9,25},{17,1},{25,9},{2,18},{10... | collective-permute-start | bytes 1327112 | tf_op jit(solution)/shard_map/ppermute | solution.py:154
  669.5 25.7 %collective-permute-start.40 = (bf16[2,256,1536]{2,1,0:T(8,128)(2,1)}, bf16[2,256,1536]{2,1,0:T(8,128)(2,1)}, u32[]{:S(2)}, u32[]{:S(2)}) collective-permute-start(bf16[2,256,1536]{2,1,0:T(8,128)(2,1)} %fusion.87), channel_id=1, source_target_pairs={{0,8},{8,0},{16,24},{24,16},{1,9},{9,1},{17,25},{25,17},{2,10},{10... | collective-permute-start | bytes 4718600 | tf_op jit(solution)/shard_map/ppermute | solution.py:157
  694.8 20.4 %collective-permute-start.50 = (bf16[2,2,48,384]{3,2,1,0:T(8,128)(2,1)S(1)}, bf16[2,2,48,384]{3,2,1,0:T(8,128)(2,1)S(1)}, u32[]{:S(2)}, u32[]{:S(2)}) collective-permute-start(bf16[2,2,48,384]{3,2,1,0:T(8,128)(2,1)S(1)} %fusion.135), channel_id=1, source_target_pairs={{0,2},{1,3},{2,6},{3,7},{4,0},{5,1},{6,4},{7,5},{8,10},{9,11},{10,... | collective-permute-start | bytes 442376 | tf_op jit(solution)/shard_map/ppermute | solution.py:163
  699.8 57.6 %collective-permute-start.41 = (bf16[256,1536]{1,0:T(8,128)(2,1)}, bf16[256,1536]{1,0:T(8,128)(2,1)}, u32[]{:S(2)}, u32[]{:S(2)}) collective-permute-start(bf16[256,1536]{1,0:T(8,128)(2,1)} %fusion.104), channel_id=1, source_target_pairs={{0,16},{8,24},{16,0},{24,8},{1,17},{9,25},{17,1},{25,9},{2,18},{10... | collective-permute-start | bytes 2359304 | tf_op jit(solution)/shard_map/ppermute | solution.py:154
  712.0 57.8 %collective-permute-start.55 = (bf16[3,2,2,48,1536]{4,3,2,1,0:T(8,128)(2,1)}, bf16[3,2,2,48,1536]{4,3,2,1,0:T(8,128)(2,1)}, u32[]{:S(2)}, u32[]{:S(2)}) collective-permute-start(bf16[3,2,2,48,1536]{4,3,2,1,0:T(8,128)(2,1)} %fusion.59), channel_id=1, source_target_pairs={{0,2},{1,3},{2,6},{3,7},{4,0},{5,1},{6,4},{7,5},{8,10},{9,11},{10,... | collective-permute-start | bytes 5308424 | tf_op jit(solution)/shard_map/ppermute | solution.py:163
  716.2 38.4 %collective-permute-start.51 = (bf16[2,2,48,384]{3,2,1,0:T(8,128)(2,1)S(1)}, bf16[2,2,48,384]{3,2,1,0:T(8,128)(2,1)S(1)}, u32[]{:S(2)}, u32[]{:S(2)}) collective-permute-start(bf16[2,2,48,384]{3,2,1,0:T(8,128)(2,1)S(1)} %fusion.137), channel_id=1, source_target_pairs={{0,2},{1,3},{2,6},{3,7},{4,0},{5,1},{6,4},{7,5},{8,10},{9,11},{10,... | collective-permute-start | bytes 442376 | tf_op jit(solution)/shard_map/ppermute | solution.py:163
  755.7 20.8 %collective-permute-start.52 = (bf16[2,48,384]{2,1,0:T(8,128)(2,1)S(1)}, bf16[2,48,384]{2,1,0:T(8,128)(2,1)S(1)}, u32[]{:S(2)}, u32[]{:S(2)}) collective-permute-start(bf16[2,48,384]{2,1,0:T(8,128)(2,1)S(1)} %get-tuple-element.619), channel_id=1, source_target_pairs={{0,16},{8,24},{16,0},{24,8},{1,17},{9,25},{17,1},{25,9},{2,18},{10... | collective-permute-start | bytes 221192 | tf_op jit(solution)/shard_map/ppermute | solution.py:154
  772.6 46.2 %collective-permute-start.56 = (bf16[3,2,2,48,1536]{4,3,2,1,0:T(8,128)(2,1)S(1)}, bf16[3,2,2,48,1536]{4,3,2,1,0:T(8,128)(2,1)S(1)}, u32[]{:S(2)}, u32[]{:S(2)}) collective-permute-start(bf16[3,2,2,48,1536]{4,3,2,1,0:T(8,128)(2,1)S(1)} %fusion.58), channel_id=1, source_target_pairs={{0,2},{1,3},{2,6},{3,7},{4,0},{5,1},{6,4},{7,5},{8,10},{9,11},{10,... | collective-permute-start | bytes 5308424 | tf_op jit(solution)/shard_map/ppermute | solution.py:163
  774.9 20.0 %collective-permute-start.42 = (bf16[2,2,4,48,640]{4,3,2,1,0:T(8,128)(2,1)S(1)}, bf16[2,2,4,48,640]{4,3,2,1,0:T(8,128)(2,1)S(1)}, u32[]{:S(2)}, u32[]{:S(2)}) collective-permute-start(bf16[2,2,4,48,640]{4,3,2,1,0:T(8,128)(2,1)S(1)} %fusion.99), channel_id=1, source_target_pairs={{0,1},{1,0},{2,3},{3,2},{4,5},{5,4},{6,7},{7,6},{8,9},{9,8},{10,11... | collective-permute-start | bytes 2949128 | tf_op jit(solution)/shard_map/ppermute | solution.py:160
  795.0 21.6 %collective-permute-start.43 = (bf16[2,2,48,640]{3,2,1,0:T(8,128)(2,1)S(1)}, bf16[2,2,48,640]{3,2,1,0:T(8,128)(2,1)S(1)}, u32[]{:S(2)}, u32[]{:S(2)}) collective-permute-start(bf16[2,2,48,640]{3,2,1,0:T(8,128)(2,1)S(1)} %fusion.118), channel_id=1, source_target_pairs={{0,2},{1,3},{2,6},{3,7},{4,0},{5,1},{6,4},{7,5},{8,10},{9,11},{10,... | collective-permute-start | bytes 737288 | tf_op jit(solution)/shard_map/ppermute | solution.py:163
  821.0 48.8 %collective-permute-start.57 = (bf16[3,2,2,48,1536]{4,3,2,1,0:T(8,128)(2,1)S(1)}, bf16[3,2,2,48,1536]{4,3,2,1,0:T(8,128)(2,1)S(1)}, u32[]{:S(2)}, u32[]{:S(2)}) collective-permute-start(bf16[3,2,2,48,1536]{4,3,2,1,0:T(8,128)(2,1)S(1)} %fusion.56), channel_id=1, source_target_pairs={{0,2},{1,3},{2,6},{3,7},{4,0},{5,1},{6,4},{7,5},{8,10},{9,11},{10,... | collective-permute-start | bytes 5308424 | tf_op jit(solution)/shard_map/ppermute | solution.py:163
  826.6 38.0 %collective-permute-start.45 = (bf16[2,2,48,640]{3,2,1,0:T(8,128)(2,1)S(1)}, bf16[2,2,48,640]{3,2,1,0:T(8,128)(2,1)S(1)}, u32[]{:S(2)}, u32[]{:S(2)}) collective-permute-start(bf16[2,2,48,640]{3,2,1,0:T(8,128)(2,1)S(1)} %fusion.122), channel_id=1, source_target_pairs={{0,2},{1,3},{2,6},{3,7},{4,0},{5,1},{6,4},{7,5},{8,10},{9,11},{10,... | collective-permute-start | bytes 737288 | tf_op jit(solution)/shard_map/ppermute | solution.py:163
  872.2 22.1 %collective-permute-start.58 = (bf16[3,2,48,1536]{3,2,1,0:T(8,128)(2,1)S(1)}, bf16[3,2,48,1536]{3,2,1,0:T(8,128)(2,1)S(1)}, u32[]{:S(2)}, u32[]{:S(2)}) collective-permute-start(bf16[3,2,48,1536]{3,2,1,0:T(8,128)(2,1)S(1)} %get-tuple-element.563), channel_id=1, source_target_pairs={{0,16},{8,24},{16,0},{24,8},{1,17},{9,25},{17,1},{25,9},{2,18},{10... | collective-permute-start | bytes 2654216 | tf_op jit(solution)/shard_map/ppermute | solution.py:154
  894.5 21.3 %collective-permute-start.59 = (bf16[3,2,48,1536]{3,2,1,0:T(8,128)(2,1)S(1)}, bf16[3,2,48,1536]{3,2,1,0:T(8,128)(2,1)S(1)}, u32[]{:S(2)}, u32[]{:S(2)}) collective-permute-start(bf16[3,2,48,1536]{3,2,1,0:T(8,128)(2,1)S(1)} %get-tuple-element.562), channel_id=1, source_target_pairs={{0,1},{1,0},{2,3},{3,2},{4,5},{5,4},{6,7},{7,6},{8,9},{9,8},{10,11... | collective-permute-start | bytes 2654216 | tf_op jit(solution)/shard_map/ppermute | solution.py:160
  (131 other events, 1406.9 us)

commit v2 on v1

v2 whole, which is shorter than its diff:
```python
import functools

import jax
import jax.numpy as jnp
from jax import lax
from jax.experimental import pallas as pl
from jax.experimental.pallas import tpu as pltpu
from jax.sharding import PartitionSpec as P

D = 1536
HEADS = 12
KV = 2
HD = 128
FF = 8960
LANE = 128

epsilon = 1e-06
rope_base = 1000000.0
masked_value = -1e30
BF = jnp.bfloat16
F32 = jnp.float32
VMEM_BYTES = 60 * 1024 * 1024

CHIP_STARTS = (0, 18, 36, 52)
CHIP_VALID = ((0, 18), (0, 18), (0, 17), (1, 18))
TILE = 256
CHUNKS = ((0, 1536), (1536, 2304))
QUERY_ROWS = 256

anywhere = pl.BlockSpec(memory_space=pl.ANY)
in_vmem = pl.BlockSpec(memory_space=pltpu.VMEM)
in_smem = pl.BlockSpec(memory_space=pltpu.SMEM)


def rope_tables(positions):
    ladder = jnp.arange(HD // 2, dtype=F32)
    inverse = rope_base ** (-2.0 * ladder / HD)
    angles = positions.astype(F32)[:, None] * inverse[None, :]
    cosine, sine = jnp.cos(angles), jnp.sin(angles)
    return (
        jnp.concatenate([cosine, cosine], axis=-1),
        jnp.concatenate([-sine, sine], axis=-1),
    )


def rms_factor(value):
    return lax.rsqrt(jnp.mean(value * value, axis=-1, keepdims=True) + epsilon)


def rms_backward(value, factor, gain, grad):
    unit = value * factor
    weighted = grad * gain
    grad_gain = jnp.sum(grad * unit, axis=0)
    inner = jnp.mean(weighted * unit, axis=-1, keepdims=True)
    return (factor * (weighted - unit * inner), grad_gain)


def dot(left, right):
    return jnp.dot(left, right, preferred_element_type=F32)


def dot_t(left, right):
    return lax.dot_general(left, right, (((1,), (1,)), ((), ())), preferred_element_type=F32)


def t_dot(left, right):
    return lax.dot_general(left, right, (((0,), (0,)), ((), ())), preferred_element_type=F32)


def pick(array, index, axis=0):
    return lax.dynamic_index_in_dim(array, index, axis, keepdims=False)


def tie(value, *others):
    return lax.optimization_barrier((value, *others))[0]


def kernel_params():
    return pltpu.CompilerParams(vmem_limit_bytes=VMEM_BYTES)


KERNEL_COST = pl.CostEstimate(flops=1_000_000, bytes_accessed=1_000_000, transcendentals=0)


def cut_body(place, gate_up, down, target, pairs, sems):
    cols = pl.ds(pl.multiple_of(place[0], LANE), target.shape[2])
    copies = [
        pltpu.make_async_copy(gate_up.at[:, :, cols], pairs, sems.at[0]),
        pltpu.make_async_copy(down.at[:, cols], target.at[2], sems.at[1]),
    ]
    for copy in copies:
        copy.start()
    copies[0].wait()
    target[0] = pairs[:, 0, :]
    target[1] = pairs[:, 1, :]
    copies[1].wait()
    empty = jnp.zeros((3, target.shape[1], LANE), BF)

    @pl.when(place[1] == 1)
    def _():
        target[:, :, 0:LANE] = empty

    @pl.when(place[1] == 2)
    def _():
        target[:, :, target.shape[2] - LANE :] = empty


def cut_columns(place, gate_up, down, cols):
    rows = down.shape[0]
    return pl.pallas_call(
        cut_body,
        out_shape=jax.ShapeDtypeStruct((3, rows, cols), BF),
        in_specs=[in_smem, anywhere, anywhere],
        out_specs=in_vmem,
        scratch_shapes=[pltpu.VMEM((rows, 2, cols), BF), pltpu.SemaphoreType.DMA((2,))],
        compiler_params=kernel_params(),
        cost_estimate=KERNEL_COST,
        name="cut_columns",
    )(place, gate_up, down)


def sequence_copies(s, sources, target, sems):
    near, far, other = sources
    rows = near.shape[0]
    x, c = s // 2, lax.rem(s, 2)
    copies = []
    for i, (source, owner) in enumerate(
        (
            (near, 2 * x + c),
            (far, 2 * (1 - x) + c),
            (other.at[0], 2 * x + 1 - c),
            (other.at[1], 2 * (1 - x) + 1 - c),
        )
    ):
        place = pl.multiple_of(owner * rows, LANE)
        copies.append(pltpu.make_async_copy(source, target.at[pl.ds(place, rows)], sems.at[i]))
    return copies


def attention_in_body(planes, rows, *refs):
    places, own = refs[0], refs[1]
    mine = refs[2 : 2 + planes]
    theirs = refs[2 + planes : 2 + 2 * planes]
    sources = refs[2 + 2 * planes : 5 + 2 * planes]
    cosine, sine, starts = refs[5 + 2 * planes : 8 + 2 * planes]
    (
        normed_t,
        queries,
        keys,
        values,
        attended,
        keep,
        send,
        weights,
        gains,
        tokens,
        small,
        sems,
        token_sems,
    ) = refs[8 + 2 * planes :]
    length = tokens.shape[0]
    group_cols = queries.shape[1]
    blocks = 2 * planes
    s, y = own[0], own[1]
    c = lax.rem(s, 2)
    copies = sequence_copies(s, sources, tokens, token_sems)
    for k in range(planes):
        for side, source in enumerate((mine[k], theirs[k])):
            block = places[k] * 2 + (y if side == 0 else 1 - y)
            first = pl.multiple_of(block * rows, 16)
            copies.append(
                pltpu.make_async_copy(
                    source.at[pl.ds(0, rows)], weights.at[pl.ds(first, rows)], sems.at[0, 2 * k + side]
                )
            )
            copies.append(
                pltpu.make_async_copy(
                    source.at[pl.ds(rows, 16)],
                    small.at[pl.ds(pl.multiple_of(block * 16, 16), 16)],
                    sems.at[1, 2 * k + side],
                )
            )
    for copy in copies:
        copy.start()
    for copy in copies:
        copy.wait()
    kv_own = KV * HD // blocks
    vectors = []
    for row, width in enumerate((rows, rows, rows, kv_own, kv_own)):
        vectors.append(
            jnp.concatenate(
                [small[pl.ds(16 * b + row, 1), 0:width].astype(F32) for b in range(blocks)], axis=1
            )
        )
    gains[0:1, :] = vectors[0]
    gains[1:2, :] = vectors[1]
    gains[2:3, :] = vectors[2]
    gains[3:4, 0 : KV * HD] = vectors[3]
    gains[4:5, 0 : KV * HD] = vectors[4]
    gain = gains[0:1, :]
    kv = s // 2
    bias = jnp.concatenate(
        [
            gains[2:3, pl.ds(pl.multiple_of(s * group_cols, LANE), group_cols)],
            gains[3:4, pl.ds(pl.multiple_of(kv * HD, LANE), HD)],
            gains[4:5, pl.ds(pl.multiple_of(kv * HD, LANE), HD)],
        ],
        axis=1,
    )
    wide = group_cols + 2 * HD
    heads = group_cols // HD
    for first in range(0, length, QUERY_ROWS):
        r = pl.ds(first, QUERY_ROWS)
        value = tokens[r, :].astype(F32)
        low = (value * rms_factor(value) * gain).astype(BF)
        normed_t[:, r] = low.T
        qkv = dot(low, weights[:, 0:wide]) + bias
        cos_rows, sin_rows = cosine[r, :], sine[r, :]
        for head in range(heads + 1):
            one = qkv[:, head * HD : (head + 1) * HD]
            turned = (one * cos_rows + pltpu.roll(one, HD // 2, 1) * sin_rows).astype(BF)
            if head < heads:
                queries[r, head * HD : (head + 1) * HD] = turned
            else:
                keys[r, :] = turned
        values[r, :] = qkv[:, group_cols + HD :].astype(BF)
    scaling = HD ** (-0.5)
    for first in range(0, length, QUERY_ROWS):
        r = pl.ds(first, QUERY_ROWS)
        reach = first + QUERY_ROWS
        query_place = first + lax.broadcasted_iota(jnp.int32, (QUERY_ROWS, reach), 0)
        key_place = lax.broadcasted_iota(jnp.int32, (QUERY_ROWS, reach), 1)
        allowed = (key_place <= query_place) & (key_place >= starts[r, :])
        for head in range(heads):
            cols = slice(head * HD, (head + 1) * HD)
            scores = dot_t(queries[r, cols], keys[0:reach, :]) * scaling
            scores = jnp.where(allowed, scores, masked_value)
            shifted = jnp.exp(scores - jnp.max(scores, axis=-1, keepdims=True))
            total = jnp.sum(shifted, axis=-1, keepdims=True)
            outcome = dot(shifted.astype(BF), values[0:reach, :])
            attended[r, cols] = (outcome / total).astype(BF)
        term = dot_t(attended[r, :], weights[:, wide:]).astype(BF)
        at = first // QUERY_ROWS

        @pl.when(c == at % 2)
        def _():
            keep[at // 2] = term

        @pl.when(c != at % 2)
        def _():
            send[at // 2] = term


def attention_in(places, own, mine, theirs, tokens, cosine, sine, starts, group_cols):
    planes = len(mine)
    rows = mine[0].shape[0] - 16
    length = cosine.shape[0]
    shapes = [
        jax.ShapeDtypeStruct((D, length), BF),
        jax.ShapeDtypeStruct((length, group_cols), BF),
        jax.ShapeDtypeStruct((length, HD), BF),
        jax.ShapeDtypeStruct((length, HD), BF),
        jax.ShapeDtypeStruct((length, group_cols), BF),
        jax.ShapeDtypeStruct((2, QUERY_ROWS, D), BF),
        jax.ShapeDtypeStruct((2, QUERY_ROWS, D), BF),
        jax.ShapeDtypeStruct((D, mine[0].shape[1]), BF),
        jax.ShapeDtypeStruct((8, D), F32),
        jax.ShapeDtypeStruct((length, D), BF),
    ]
    return pl.pallas_call(
        functools.partial(attention_in_body, planes, rows),
        out_shape=shapes,
        in_specs=[in_smem, in_smem] + [anywhere] * (2 * planes + 3) + [in_vmem] * 3,
        out_specs=[in_vmem] * len(shapes),
        scratch_shapes=[
            pltpu.VMEM((2 * planes * 16, mine[0].shape[1]), BF),
            pltpu.SemaphoreType.DMA((2, 2 * planes)),
            pltpu.SemaphoreType.DMA((4,)),
        ],
        compiler_params=kernel_params(),
        cost_estimate=KERNEL_COST,
        name="attention_in",
    )(places, own, *mine, *theirs, *tokens, cosine, sine, starts)


def attention_out_body(
    own,
    near,
    far,
    other,
    weights,
    queries,
    keys,
    values,
    cosine,
    sine,
    starts,
    grad_q,
    grad_kv,
    grad,
    grad_k,
    grad_v,
    sems,
):
    copies = sequence_copies(own[0], (near, far, other), grad, sems)
    for copy in copies:
        copy.start()
    for copy in copies:
        copy.wait()
    length = grad.shape[0]
    group_cols = queries.shape[1]
    heads = group_cols // HD
    scaling = HD ** (-0.5)
    output = weights[:, group_cols + 2 * HD :]
    grad_k[...] = jnp.zeros_like(grad_k)
    grad_v[...] = jnp.zeros_like(grad_v)
    for first in range(0, length, QUERY_ROWS):
        r = pl.ds(first, QUERY_ROWS)
        reach = first + QUERY_ROWS
        grad_heads = dot(grad[r, :], output).astype(BF)
        query_place = first + lax.broadcasted_iota(jnp.int32, (QUERY_ROWS, reach), 0)
        key_place = lax.broadcasted_iota(jnp.int32, (QUERY_ROWS, reach), 1)
        allowed = (key_place <= query_place) & (key_place >= starts[r, :])
        cos_rows, sin_rows = cosine[r, :], sine[r, :]
        for head in range(heads):
            cols = slice(head * HD, (head + 1) * HD)
            one_query = queries[r, cols]
            one_grad = grad_heads[:, cols]
            scores = dot_t(one_query, keys[0:reach, :]) * scaling
            scores = jnp.where(allowed, scores, masked_value)
            shifted = jnp.exp(scores - jnp.max(scores, axis=-1, keepdims=True))
            probability = shifted * (1.0 / jnp.sum(shifted, axis=-1, keepdims=True))
            grad_prob = dot_t(one_grad, values[0:reach, :])
            weighted = probability * grad_prob
            inner = jnp.sum(weighted, axis=-1, keepdims=True)
            grad_low = (weighted - probability * inner).astype(BF)
            turned = (dot(grad_low, keys[0:reach, :]) * scaling).astype(BF).astype(F32)
            grad_q[r, cols] = (
                turned * cos_rows - pltpu.roll(turned, HD // 2, 1) * sin_rows
            ).astype(BF)
            grad_k[0:reach, :] += t_dot(grad_low, one_query)
            grad_v[0:reach, :] += t_dot(probability.astype(BF), one_grad)
    grad_kv[0] = (grad_k[...] * scaling).astype(BF)
    grad_kv[1] = grad_v[...].astype(BF)


def attention_out(own, grad, weights, queries, keys, values, cosine, sine, starts):
    length, group_cols = queries.shape
    return pl.pallas_call(
        attention_out_body,
        out_shape=[
            jax.ShapeDtypeStruct((length, group_cols), BF),
            jax.ShapeDtypeStruct((2, length, HD), BF),
            jax.ShapeDtypeStruct((length, D), BF),
        ],
        in_specs=[in_smem] + [anywhere] * 3 + [in_vmem] * 7,
        out_specs=[in_vmem] * 3,
        scratch_shapes=[pltpu.VMEM((length, HD), F32)] * 2 + [pltpu.SemaphoreType.DMA((4,))],
        compiler_params=kernel_params(),
        cost_estimate=KERNEL_COST,
        name="attention_out",
    )(own, *grad, weights, queries, keys, values, cosine, sine, starts)


def projection_out_body(
    own_rows,
    kv_rows,
    own,
    grad_q,
    ours,
    theirs,
    weights,
    normed_t,
    cosine,
    sine,
    tokens,
    gain_mlp,
    d_qkv,
    keep,
    send,
    joined,
    sums,
):
    length, group_cols = grad_q.shape
    wide = group_cols + HD
    s = own[0]
    x, c = s // 2, lax.rem(s, 2)
    key_grad = ours[0].astype(F32) + theirs[0].astype(F32)
    key_grad = key_grad * cosine[...] - pltpu.roll(key_grad, HD // 2, 1) * sine[...]
    value_grad = ours[1].astype(F32) + theirs[1].astype(F32)
    joined[:, 0:group_cols] = grad_q[...]
    joined[:, group_cols:] = jnp.where(c == 0, key_grad, value_grad).astype(BF)
    one = jnp.where(
        c == 0,
        weights[:, group_cols : group_cols + HD],
        weights[:, group_cols + HD : group_cols + 2 * HD],
    )
    sums[...] = jnp.zeros_like(sums)
    gain_sum = jnp.zeros((1, D), F32)
    for first in range(0, length, QUERY_ROWS):
        r = pl.ds(first, QUERY_ROWS)
        term = dot_t(joined[r, 0:group_cols], weights[:, 0:group_cols]) + dot_t(
            joined[r, group_cols:], one
        )
        value = tokens[r, :].astype(F32)
        gain_sum += jnp.sum(term * (value * rms_factor(value)), axis=0, keepdims=True)
        low = term.astype(BF)
        at = first // QUERY_ROWS

        @pl.when(c == at % 2)
        def _():
            keep[at // 2] = low

        @pl.when(c != at % 2)
        def _():
            send[at // 2] = low

    bias = jnp.sum(joined[...].astype(F32), axis=0, keepdims=True)
    lane = lax.broadcasted_iota(jnp.int32, (HD, D // 2), 1)
    feature = lax.broadcasted_iota(jnp.int32, (HD, D // 2), 0)
    core, inner = lax.div(lane, D // 4), lax.rem(lane, D // 4)
    owner, row = lax.div(inner, own_rows), lax.rem(inner, own_rows)
    spot = core * (HD // 2) + owner * kv_rows + row
    chosen = jnp.where((spot == feature) & (row < kv_rows), 1.0, 0.0).astype(BF)
    spread = dot(bias[:, group_cols:].astype(BF), chosen)
    sums[0:1, :] = gain_sum
    sums[1:2, :] = gain_mlp[...]
    sums[2:3, pl.ds(pl.multiple_of(s * group_cols, LANE), group_cols)] = bias[:, 0:group_cols]
    sums[3:4, pl.ds(pl.multiple_of(x * (D // 2), LANE), D // 2)] = spread
    d_qkv[:, 0:wide] = dot(normed_t[...], joined[...]).astype(BF)
    d_qkv[:, wide:] = sums[...].T.astype(BF)


def projection_out(
    own_rows, kv_rows, own, grad_q, ours, theirs, weights, normed_t, cosine, sine, tokens, gain_mlp
):
    length, group_cols = grad_q.shape
    wide = group_cols + HD
    return pl.pallas_call(
        functools.partial(projection_out_body, own_rows, kv_rows),
        out_shape=[
            jax.ShapeDtypeStruct((D, wide + LANE), BF),
            jax.ShapeDtypeStruct((2, QUERY_ROWS, D), BF),
            jax.ShapeDtypeStruct((2, QUERY_ROWS, D), BF),
        ],
        in_specs=[in_smem] + [in_vmem] * 9,
        out_specs=[in_vmem] * 3,
        scratch_shapes=[pltpu.VMEM((length, wide), BF), pltpu.VMEM((LANE, D), F32)],
        compiler_params=kernel_params(),
        cost_estimate=KERNEL_COST,
        name="projection_out",
    )(own, grad_q, ours, theirs, weights, normed_t, cosine, sine, tokens, gain_mlp)


def plane_copies(sources, target, sems, first):
    copies = []
    rows = QUERY_ROWS
    for source, at, place, cols in sources:
        ref = source if at is None else source.at[at]
        copies.append(
            pltpu.make_async_copy(
                ref, target.at[pl.ds(place * rows, rows), cols], sems.at[first + len(copies)]
            )
        )
    return copies


def feed_forward_body(planes, rows, first, last, *refs):
    places, own = refs[0], refs[1]
    mine = refs[2 : 2 + planes]
    theirs = refs[2 + planes : 2 + 2 * planes]
    rest = list(refs[2 + 2 * planes :])
    n1, n2, na1, nb1, na2, nb2, c_own, c_x, c_y = [rest.pop(0) for _ in range(9)]
    turned_in = [] if first else [rest.pop(0) for _ in range(2)]
    totals_in = [] if first else [rest.pop(0) for _ in range(2)]
    keep, send = [rest.pop(0) for _ in range(2)]
    turned_out = [rest.pop(0) for _ in range(2)] if first else []
    totals_out = [rest.pop(0) for _ in range(8 if last else 2)]
    weights, grad_gate, grad_up, activated, grad_total, branch_total = [
        rest.pop(0) for _ in range(6)
    ]
    normed, cotangent, normed_t, cotangent_t, weight_sems, sems = [rest.pop(0) for _ in range(6)]
    low = rest
    step, steps = pl.program_id(0), pl.num_programs(0)
    tokens = normed.shape[0]
    half = D // 2
    left, right, both = pl.ds(0, half), pl.ds(half, half), pl.ds(0, D)
    c = own[0]
    normed_loads = plane_copies(
        (
            (n1, None, 0, left),
            (na2, 0, 1, left),
            (na1, None, 2, left),
            (na2, 1, 3, left),
            (n2, None, 0, right),
            (nb1, None, 1, right),
            (nb2, 0, 2, right),
            (nb2, 1, 3, right),
        ),
        normed,
        sems,
        8,
    )
    cot_loads = plane_copies(
        (
            (c_own, None, 0, both),
            (c_y, 0, 1, both),
            (c_x, None, 2, both),
            (c_y, 1, 3, both),
        ),
        cotangent,
        sems,
        16,
    )
    turned_loads = [
        pltpu.make_async_copy(source, target, sems.at[20 + i])
        for i, (source, target) in enumerate(zip(turned_in, (normed_t, cotangent_t)))
    ]
    turned_ends = [
        pltpu.make_async_copy(source, target, sems.at[20 + i])
        for i, (source, target) in enumerate(zip((normed_t, cotangent_t), turned_out))
    ]
    fills = [
        pltpu.make_async_copy(source, target, sems.at[i])
        for i, (source, target) in enumerate(zip(totals_in, (grad_total, branch_total)))
    ]
    if last:
        ends = []
        for i, source in enumerate(low):
            keep_a, send_a, keep_b, send_b = totals_out[4 * i : 4 * i + 4]
            for target, place, cols in (
                (keep_a.at[0], 0, left),
                (keep_a.at[1], 2, left),
                (send_a.at[0], 1, left),
                (send_a.at[1], 3, left),
                (keep_b.at[0], 0, right),
                (keep_b.at[1], 1, right),
                (send_b.at[0], 2, right),
                (send_b.at[1], 3, right),
            ):
                ends.append(
                    pltpu.make_async_copy(
                        source.at[pl.ds(place * QUERY_ROWS, QUERY_ROWS), cols],
                        target,
                        sems.at[len(ends)],
                    )
                )
    else:
        ends = [
            pltpu.make_async_copy(source, target, sems.at[i])
            for i, (source, target) in enumerate(zip((grad_total, branch_total), totals_out))
        ]

    def weight_copies(at, slot):
        cols = pl.ds(pl.multiple_of(at * TILE, TILE), TILE)
        copies = []
        for k in range(planes):
            base = places[k] * (2 * rows)
            for side, source in enumerate((mine[k], theirs[k])):
                start = base + (c if side == 0 else 1 - c) * rows
                copies.append(
                    pltpu.make_async_copy(
                        source.at[:, :, cols],
                        weights.at[slot, :, pl.ds(pl.multiple_of(start, 16), rows), :],
                        weight_sems.at[slot, 2 * k + side],
                    )
                )
        return copies

    slot = lax.rem(step, 2)

    @pl.when(step == 0)
    def _():
        for load in normed_loads:
            load.start()
        for copy in weight_copies(0, 0):
            copy.start()
        for load in cot_loads + turned_loads + fills:
            load.start()

    @pl.when(step + 1 < steps)
    def _():
        for copy in weight_copies(step + 1, 1 - slot):
            copy.start()

    if first:

        @pl.when(step == 0)
        def _():
            grad_total[...] = jnp.zeros_like(grad_total)
            branch_total[...] = jnp.zeros_like(branch_total)

    @pl.when(step == 0)
    def _():
        for load in normed_loads:
            load.wait()

    for copy in weight_copies(step, slot):
        copy.wait()

    @pl.when(step == 0)
    def _():
        for load in cot_loads:
            load.wait()

    block = min(256, tokens)
    for start in range(0, tokens, block):
        r = pl.ds(start, block)
        some = normed[r, :]
        gate = dot(some, weights[slot, 0])
        up = dot(some, weights[slot, 1])
        grad_act = dot(cotangent[r, :], weights[slot, 2])
        sigma = jax.nn.sigmoid(gate)
        silu = gate * sigma
        activated[r, :] = (silu * up).astype(BF)
        grad_gate[r, :] = (grad_act * up * (sigma + silu * (1.0 - sigma))).astype(BF)
        grad_up[r, :] = (grad_act * silu).astype(BF)

    @pl.when(step == 0)
    def _():
        for fill in fills:
            fill.wait()

    for start in range(0, tokens, block):
        r = pl.ds(start, block)
        grad_total[r, :] += dot_t(grad_gate[r, :], weights[slot, 0]) + dot_t(
            grad_up[r, :], weights[slot, 1]
        )
        branch_total[r, :] += dot_t(activated[r, :], weights[slot, 2])

    @pl.when(step == steps - 1)
    def _():
        if last:
            low[0][...] = grad_total[...].astype(BF)
            low[1][...] = branch_total[...].astype(BF)
        for end in ends:
            end.start()

    if first:

        @pl.when(step == 0)
        def _():
            for source, target in ((normed, normed_t), (cotangent, cotangent_t)):
                for start in range(0, D, TILE):
                    cols = pl.ds(start, TILE)
                    target[cols, :] = source[:, cols].T
            for end in turned_ends:
                end.start()

    else:

        @pl.when(step == 0)
        def _():
            for load in turned_loads:
                load.wait()

    owner_rows = D // 4
    for part in range(2):
        for target, core in ((send, 1 - c), (keep, c)):
            r = pl.ds(pl.multiple_of((2 * part + core) * owner_rows, LANE), owner_rows)
            target[0, part] = dot(normed_t[r, :], grad_gate[...]).astype(BF)
            target[1, part] = dot(normed_t[r, :], grad_up[...]).astype(BF)
            target[2, part] = dot(cotangent_t[r, :], activated[...]).astype(BF)

    @pl.when(step == steps - 1)
    def _():
        for end in ends + turned_ends:
            end.wait()


def feed_forward(places, own, mine, theirs, normed, cotangent, turned, totals, last):
    planes = len(mine)
    rows, cols = mine[0].shape[1:]
    tokens = 4 * QUERY_ROWS
    first = totals is None
    totals = () if first else totals
    owner_rows = D // 4
    piece = jax.ShapeDtypeStruct((3, 2, owner_rows, cols), BF)
    piece_spec = pl.BlockSpec((3, 2, owner_rows, TILE), lambda i, *_: (0, 0, 0, i))
    shapes = [piece, piece]
    if first:
        shapes += [jax.ShapeDtypeStruct((D, tokens), BF)] * 2
    if last:
        shapes += [jax.ShapeDtypeStruct((2, QUERY_ROWS, D // 2), BF)] * 8
    else:
        shapes += [jax.ShapeDtypeStruct((tokens, D), F32)] * 2
    scratch = [pltpu.VMEM((2, 3, D, TILE), BF)]
    scratch += [pltpu.VMEM((tokens, TILE), BF)] * 3
    scratch += [pltpu.VMEM((tokens, D), F32)] * 2
    scratch += [pltpu.VMEM((tokens, D), BF)] * 2
    scratch += [pltpu.VMEM((D, tokens), BF)] * 2
    scratch += [pltpu.SemaphoreType.DMA((2, 2 * planes)), pltpu.SemaphoreType.DMA((22,))]
    if last:
        scratch += [pltpu.VMEM((tokens, D), BF)] * 2
    inputs = [*mine, *theirs, *normed, *cotangent, *turned, *totals]
    return pl.pallas_call(
        functools.partial(feed_forward_body, planes, rows, first, last),
        grid=(cols // TILE,),
        out_shape=shapes,
        in_specs=[in_smem, in_smem] + [anywhere] * len(inputs),
        out_specs=[piece_spec, piece_spec] + [anywhere] * (len(shapes) - 2),
        scratch_shapes=scratch,
        compiler_params=kernel_params(),
        cost_estimate=KERNEL_COST,
        name="feed_forward",
    )(places, own, *inputs)


def build(seq_count, fsdp_count):
    planes = fsdp_count // 2
    order = list(range(0, 1)) + list(range(1, planes, 2)) + list(range(2, planes, 2))[::-1]
    place = [order.index(plane) for plane in range(planes)]
    after = {order[i]: order[(i + 1) % planes] for i in range(planes)}
    ring_perm = [(2 * z + y, 2 * after[z] + y) for z in range(planes) for y in range(2)]
    y_perm = [(i, i ^ 1) for i in range(fsdp_count)]
    x_perm = [(i, i ^ 2) for i in range(seq_count)]
    c_perm = [(i, i ^ 1) for i in range(seq_count)]
    rows_perm = [
        (i * fsdp_count + j, i * fsdp_count + (j ^ 1))
        for i in range(seq_count)
        for j in range(fsdp_count)
        if i % 2 == j % 2
    ]

    def swap_x(value):
        return lax.ppermute(value, "seq", x_perm)

    def swap_c(value):
        return lax.ppermute(value, "seq", c_perm)

    def swap_y(value):
        return lax.ppermute(value, "fsdp", y_perm)

    def send_rows(value):
        return lax.ppermute(value, ("seq", "fsdp"), rows_perm)

    def ring(value):
        return lax.ppermute(value, "fsdp", ring_perm)

    def ring_back(value):
        return lax.ppermute(value, "fsdp", [(j, i) for i, j in ring_perm])

    along = (planes - 1) // 2
    against = planes - 1 - along
    steps_behind = list(range(along + 1)) + [-i for i in range(1, against + 1)]

    def local(
        tokens,
        positions,
        w_query,
        w_key,
        w_value,
        w_output,
        gate_up,
        w_down,
        bias_query,
        bias_key,
        bias_value,
        gain_attn,
        gain_mlp,
        cotangent,
    ):
        s = lax.axis_index("seq")
        f = lax.axis_index("fsdp")
        x, c = s // 2, s % 2
        z, y = f // 2, f % 2
        ring_order = jnp.array(order, jnp.int32)
        ring_place = jnp.array(place, jnp.int32)
        behind = ring_order[(ring_place[z] - jnp.array(steps_behind)) % planes].astype(jnp.int32)

        def ring_gather(piece):
            ahead, back = [piece], [piece]
            for _ in range(along):
                ahead.append(ring(ahead[-1]))
            for _ in range(against):
                back.append(ring_back(back[-1]))
            return ahead + back[1:]
        core = jnp.stack([c]).astype(jnp.int32)
        own_place = jnp.stack([s, y]).astype(jnp.int32)

        tok_rows = tokens.shape[1]
        length = tok_rows * seq_count
        per_group = HEADS // seq_count
        group_cols = per_group * HD
        w_rows = w_query.shape[0]
        own_rows = D // (seq_count * fsdp_count)
        half = D // 2

        def gather_sequence(own, then=()):
            far = swap_x(own)
            return [own, far, swap_c(tie(jnp.stack([own, far]), *then))]

        def scatter_sequence(keep, send, then=()):
            halves = keep.astype(F32) + swap_c(send).astype(F32)
            back = swap_x(tie(pick(halves, 1 - x).astype(BF), *then))
            return pick(halves, x) + back.astype(F32)

        def gather_plane(own, then=()):
            first, second = own[:, :half], own[:, half:]
            a1 = swap_x(first)
            b1 = swap_y(second)
            a2 = swap_y(tie(jnp.stack([first, a1]), *then))
            b2 = swap_x(tie(jnp.stack([second, b1]), *then))
            return [first, second, a1, b1, a2, b2]

        def scatter_plane(keep_a, send_a, keep_b, send_b, then=()):
            a1 = keep_a.astype(F32) + swap_y(send_a).astype(F32)
            b1 = keep_b.astype(F32) + swap_x(send_b).astype(F32)
            a1, b1 = tie((a1, b1), *then)
            a2 = a1[0] + swap_x(a1[1].astype(BF)).astype(F32)
            b2 = b1[0] + swap_y(b1[1].astype(BF)).astype(F32)
            return jnp.concatenate([a2, b2], axis=1)

        wide = group_cols + 2 * HD
        small_rows = jnp.stack(
            [
                jnp.pad(vector, (0, wide + group_cols - vector.shape[0]))
                for vector in (gain_attn, gain_mlp, bias_query, bias_key, bias_value)
            ]
        )
        small_rows = jnp.pad(small_rows, ((0, 11), (0, 0)))
        attn_own = jnp.concatenate(
            [
                lax.dynamic_slice_in_dim(w_query, s * group_cols, group_cols, 1),
                lax.dynamic_slice_in_dim(w_key, x * HD, HD, 1),
                lax.dynamic_slice_in_dim(w_value, x * HD, HD, 1),
                lax.dynamic_slice_in_dim(w_output, s * group_cols, group_cols, 1),
            ],
            axis=1,
        )
        attn_payload = jnp.concatenate([attn_own, small_rows], axis=0)
        chunk_places = []
        for low, high in CHUNKS:
            table = []
            for start, (first, end) in zip(CHIP_STARTS, CHIP_VALID):
                edge = 1 if low == 0 and first > 0 else 0
                edge = 2 if high > end * LANE else edge
                table.append((start * LANE + low, edge))
            table = jnp.array(table, jnp.int32)
            chunk_places.append((table[2 * x + y], table[2 * x + 1 - y]))

        def cut(chunk, whose, then):
            low, high = CHUNKS[chunk]
            return cut_columns(tie(chunk_places[chunk][whose], then), gate_up, w_down, high - low)

        sent = cut(0, 1, ())
        attn_payload = tie(attn_payload, sent)
        attn_pieces = ring_gather(attn_payload)
        attn_theirs = [swap_y(piece) for piece in attn_pieces]
        token_pieces = gather_sequence(tokens[0])

        came, kept = send_rows(sent), cut(0, 0, attn_payload)
        kept, came = tie((kept, came), attn_pieces[1:], attn_theirs[0])
        payloads = [jnp.where(c == y, kept, came)]
        for chunk in range(1, len(CHUNKS)):
            sent = cut(chunk, 1, payloads[-1])
            kept, came = cut(chunk, 0, sent), send_rows(sent)
            payloads.append(jnp.where(c == y, kept, came))
        chunk_pieces = [ring_gather(payload) for payload in payloads]
        chunk_theirs = []
        for pieces in chunk_pieces:
            theirs = []
            for piece in pieces:
                theirs.append(swap_c(tie(piece, theirs[-1:])))
            chunk_theirs.append(theirs)

        cot_own = tie(cotangent[0], token_pieces[1])
        cot_far = swap_x(cot_own)
        cot_pair = tie(jnp.stack([cot_own, cot_far]), payloads[-1])
        cot_pieces = [cotangent[0], cot_far, swap_y(cot_pair)]

        seq_positions = positions[0]
        cosine, sine = rope_tables(seq_positions)
        first_keys = (jnp.arange(length, dtype=jnp.int32) - seq_positions)[:, None]
        (
            normed_attn_t,
            queries,
            keys,
            values,
            attended,
            out_keep,
            out_send,
            attn_weights,
            gains,
            tokens_all,
        ) = attention_in(
            behind,
            own_place,
            attn_pieces,
            attn_theirs,
            tie(token_pieces, sent, cot_far),
            cosine,
            sine,
            first_keys,
            group_cols,
        )
        inputs = tokens[0].astype(F32)
        out_keep, out_send, queries, keys, values, attended, gains = tie(
            (out_keep, out_send, queries, keys, values, attended, gains),
            chunk_pieces[0][along + 1],
        )
        gain_a, gain_m = gains[0], gains[1]
        hidden = inputs + scatter_sequence(out_keep, out_send)
        factor_mlp = rms_factor(hidden)
        normed_own = (hidden * factor_mlp * gain_m).astype(BF)
        normed = gather_plane(normed_own)

        def plane_ahead(steps):
            return ring_order[(ring_place[z] + steps) % planes]

        class RingScatter:
            def __init__(self, block):
                self.first, self.second, self.arrived, self.last = [], [], [], []
                self.own = block(z)
                for steps, sign, move in ((along, 1, ring), (against, -1, ring_back)):
                    if steps:
                        running = block(plane_ahead(sign * steps)).astype(BF)
                        self.first.append(running)
                        for left in range(steps - 1, 0, -1):
                            came = move(running)
                            self.arrived.append(came)
                            running = block(plane_ahead(sign * left)) + came.astype(F32)
                            running = running.astype(BF)
                            self.second.append(running)
                        came = move(running)
                        self.arrived.append(came)
                        self.last.append(came)

            def total(self, then=()):
                total = self.own
                for came in tie(self.last, then):
                    total = total + came.astype(F32)
                return total.astype(BF)

        def exchange(total, at, swap, axis):
            return jnp.stack([pick(total, at, axis), swap(pick(total, 1 - at, axis))], axis)

        def chunk_scatter(keep, send):
            away = swap_c(send)
            cols = keep.shape[-1]
            keep = keep.reshape(3, 2, planes, 2 * own_rows, cols)
            away = away.reshape(3, 2, planes, 2 * own_rows, cols)

            def block(plane):
                return pick(keep, plane, 2).astype(F32) + pick(away, plane, 2).astype(F32)

            return RingScatter(block)

        before = [(), None]
        beside = [chunk_pieces[1][1 : along + 2], None]
        turned, totals = (), None
        scatters = []
        for chunk in range(len(CHUNKS)):
            keep, send, *results = feed_forward(
                behind,
                core,
                chunk_pieces[chunk],
                chunk_theirs[chunk],
                tie(normed, before[chunk]),
                cot_pieces,
                turned,
                totals,
                chunk == len(CHUNKS) - 1,
            )
            keep, send, results = tie((keep, send, results), beside[chunk])
            if chunk == 0:
                turned, results = results[:2], results[2:]
            totals = results
            scatters.append(chunk_scatter(keep, send))
            before[1] = scatters[0].first
            beside[1] = scatters[0].arrived[along]
        grad_out = cotangent[0].astype(F32)
        grad_hidden_norm, grad_gain_mlp = rms_backward(
            hidden, factor_mlp, gain_m, scatter_plane(*totals[:4], scatters[0].second)
        )
        grad_hidden = grad_out + grad_hidden_norm
        grad_pieces = gather_sequence(
            grad_hidden.astype(BF), (scatters[1].first, scatters[0].arrived[0])
        )
        result = (hidden + scatter_plane(*tie(totals[4:], grad_pieces[1]))).astype(BF)
        grad_q, grad_kv, grad_hidden_low = attention_out(
            own_place,
            grad_pieces,
            attn_weights,
            queries,
            keys,
            values,
            cosine,
            sine,
            first_keys,
        )
        grad_q, grad_kv, grad_hidden_low = tie(
            (grad_q, grad_kv, grad_hidden_low), scatters[0].arrived[-1]
        )
        kv_rows = KV * HD // (seq_count * fsdp_count)
        d_qkv, in_keep, in_send = projection_out(
            own_rows,
            kv_rows,
            own_place,
            grad_q,
            grad_kv,
            swap_c(grad_kv),
            attn_weights,
            normed_attn_t,
            cosine,
            sine,
            tokens_all,
            grad_gain_mlp[None],
        )
        d_qkv, in_keep, in_send = tie((d_qkv, in_keep, in_send), scatters[1].arrived[along])
        in_halves = in_keep.astype(F32) + swap_c(in_send).astype(F32)
        in_leaves = tie(pick(in_halves, 1 - x).astype(BF), scatters[1].second)
        in_back = swap_x(in_leaves)
        grad_input_norm, _ = rms_backward(
            inputs,
            rms_factor(inputs),
            gain_a,
            pick(in_halves, x) + in_back.astype(F32),
        )
        grad_input = grad_hidden + grad_input_norm

        gathered = []
        for scatter, then in zip(scatters, (grad_kv, in_leaves)):
            total = scatter.total(then).reshape(3, 2, 2, own_rows, -1)
            if not gathered:
                both = exchange(tie(exchange(total, x, swap_x, 1), in_leaves), y, swap_y, 2)
            else:
                both = exchange(exchange(total, y, swap_y, 2), x, swap_x, 1)
            both = jnp.where(x == 0, both, both[:, ::-1])
            both = jnp.where(y == 0, both, both[:, :, ::-1])
            gathered.append(both)
        strips = []
        for chip_index, (low, high) in enumerate(CHIP_VALID):
            whole = jnp.concatenate(
                [part[:, chip_index // 2, chip_index % 2] for part in gathered], axis=-1
            )
            strips.append(whole[..., low * LANE : high * LANE])
        d_mlp = jnp.concatenate(strips, axis=-1).astype(F32)
        d_gate_up = jnp.stack([d_mlp[0], d_mlp[1]], axis=1)
        d_w_down = d_mlp[2]

        d_output = t_dot(grad_hidden_low, attended).astype(BF)

        def to_owners(partial, middle=(), last=()):
            cols = partial.shape[1]
            rows = partial.reshape(2, 2, planes, 2, own_rows, cols)
            away = tie(swap_y(pick(rows, 1 - y, 3)), middle)
            rest = pick(rows, y, 3)

            def block(plane):
                return pick(rest, plane, 2).astype(F32) + pick(away, plane, 2).astype(F32)

            total = tie(RingScatter(block).total(), last)
            both = exchange(exchange(total, x, swap_x, 0), c, swap_c, 1)
            both = jnp.where(x == 0, both, both[::-1])
            both = jnp.where(c == 0, both, both[:, ::-1])
            return both.astype(F32)

        out_blocks = to_owners(d_output)
        d_w_output = jnp.concatenate([out_blocks[i // 2, i % 2] for i in range(4)], axis=1)
        qkv_out = to_owners(d_qkv, in_leaves, in_back)
        d_w_query = jnp.concatenate(
            [qkv_out[i // 2, i % 2, :, :group_cols] for i in range(4)], axis=1
        )
        last = qkv_out[:, :, :, group_cols : group_cols + HD]
        d_w_key = jnp.concatenate([last[0, 0], last[1, 0]], axis=1)
        d_w_value = jnp.concatenate([last[0, 1], last[1, 1]], axis=1)
        sums = qkv_out[:, :, :, group_cols + HD :]
        d_gain_attn = jnp.sum(sums[..., 0], axis=(0, 1))
        d_gain_mlp = jnp.sum(sums[..., 1], axis=(0, 1))
        d_bias_query = jnp.sum(sums[..., 2], axis=(0, 1))
        d_bias_key = jnp.sum(sums[:, 0, :kv_rows, 3], axis=0)
        d_bias_value = jnp.sum(sums[:, 1, :kv_rows, 3], axis=0)
        return (
            result[None],
            grad_input[None],
            d_w_query,
            d_w_key,
            d_w_value,
            d_w_output,
            d_gate_up,
            d_w_down,
            d_bias_query,
            d_bias_key,
            d_bias_value,
            d_gain_attn,
            d_gain_mlp,
        )

    return local


def solution(mesh):
    rows = P("fsdp", None)
    owners = P(("seq", "fsdp"))
    return jax.shard_map(
        build(mesh.shape["seq"], mesh.shape["fsdp"]),
        mesh=mesh,
        in_specs=(
            P("fsdp", "seq", None),
            rows,
            rows,
            rows,
            rows,
            rows,
            P("fsdp", None, None),
            rows,
            P("fsdp"),
            P("fsdp"),
            P("fsdp"),
            P("fsdp"),
            P("fsdp"),
            P("fsdp", "seq", None),
        ),
        out_specs=(
            P("fsdp", "seq", None),
            P("fsdp", "seq", None),
            P(("seq", "fsdp"), None),
            P(("seq", "fsdp"), None),
            P(("seq", "fsdp"), None),
            P(("seq", "fsdp"), None),
            P(("seq", "fsdp"), None, None),
            P(("seq", "fsdp"), None),
            owners,
            owners,
            owners,
            owners,
            owners,
        ),
        check_vma=False,
    )
```

time: 956 us -> 629 us (0.66)
  matrix products: 179 us -> 3.94 us
  Pallas kernels: 0 us -> 161 us
  local copies, waits for them, and re-layouts: 166 us -> 24.6 us
  waiting for transfers between devices: 365 us -> 259 us
  other arithmetic: 153 us -> 58.6 us
  starting transfers between devices: 61.9 us -> 102 us
    ppermute x24 -> x7, waiting for transfers between devices: 211 us -> 42.8 us  [ring(): return lax.ppermute(value, 'fsdp', ring_perm)]
    pallas_call x0 -> x9, Pallas kernels: none -> 161 us  [the longest x2 90.2 us: feed_forward(): pl.pallas_call(functools.partial(feed_forward_body, planes, rows, first,...]
    dot_general x30 -> x0, matrix products: 140 us -> none  [the longest x8 56 us: dot_t(): lax.dot_general(left, right, (((1,), (1,)), ((), ())), preferred_element_...]
    ppermute x0 -> x16, waiting for transfers between devices: none -> 56.9 us  [the longest x14 56.9 us: ring_back(): return lax.ppermute(value, 'fsdp', [(j, i) for i, j in ring_perm])]
    ppermute x0 -> x16, starting transfers between devices: none -> 49.7 us  [the longest x14 28.6 us: ring_back(): return lax.ppermute(value, 'fsdp', [(j, i) for i, j in ring_perm])]
    dot_general x8 -> x1, matrix products: 38.9 us -> 3.94 us  [t_dot(): lax.dot_general(left, right, (((0,), (0,)), ((), ())), preferred_element_...]
    ppermute x15, waiting for transfers between devices: 105 us -> 71.6 us  [swap_y(): return lax.ppermute(value, 'fsdp', y_perm)]
    ppermute x16 -> x15, waiting for transfers between devices: 48 us -> 77.6 us  [swap_x(): return lax.ppermute(value, 'seq', x_perm)]
  transfers between devices with their start and end apart: 66 -> 70, of which waited for: 36 -> 32; matrix products, arithmetic and copies ran while one was open for 47% -> 12% of each run, Pallas kernels for 0% -> 25%
where the time goes in v2:
time: 629 us; the launch traced here: 619 us
  waiting for transfers between devices  259 us (41%)
  Pallas kernels  161 us (26%)
  starting transfers between devices  102 us (16%)
  other arithmetic  58.6 us (9%)
  local copies, waits for them, and re-layouts  24.6 us (4%)
  between operations  10.1 us (2%)
    pallas_call x2, Pallas kernels, feed_forward(): pl.pallas_call(functools.partial(feed_forward_body, planes, rows, first,...  90.2 us
    ppermute x15, waiting for transfers between devices, swap_x(): return lax.ppermute(value, 'seq', x_perm)  77.6 us
    ppermute x15, waiting for transfers between devices, swap_y(): return lax.ppermute(value, 'fsdp', y_perm)  71.6 us
    ppermute x14, waiting for transfers between devices, ring_back(): return lax.ppermute(value, 'fsdp', [(j, i) for i, j in ring_perm])  56.9 us
    ppermute x7, waiting for transfers between devices, ring(): return lax.ppermute(value, 'fsdp', ring_perm)  42.8 us
    ppermute x14, starting transfers between devices, ring_back(): return lax.ppermute(value, 'fsdp', [(j, i) for i, j in ring_perm])  28.6 us
    ppermute x15, starting transfers between devices, swap_y(): return lax.ppermute(value, 'fsdp', y_perm)  27.9 us
    ppermute x2, starting transfers between devices, send_rows(): return lax.ppermute(value, ('seq', 'fsdp'), rows_perm)  21 us
  transfers between devices with their start and end apart: 70, of which 32 were waited for; matrix products, arithmetic and copies ran while one was open for 12% of the time, Pallas kernels for 25%

profile of v2, /device:TPU:0, one launch (start us, length us, event | category | flops | bytes accessed | tf_op | source)
XLA Modules:
  0.0 619.5 jit_solution(5666841938117610181)
XLA Ops:
  2.1 5.9 cut_columns.4
  7.9 6.1 collective-permute-start.9
  16.8 2.6 collective-permute-start.1
  19.5 12.0 %collective-permute-done.1.refs_4_ = bf16[208,1024]{1,0:T(8,128)(2,1)} collective-permute-done((bf16[208,1024]{1,0:T(8,128)(2,1)S(1)}, bf16[208,1024]{1,0:T(8,128)(2,1)}, u32[]{:S(2)}, u32[]{:S(2)}) %collective-permute-start.1) | collective-permute-done | bytes 426016 | tf_op jit(solution)/shard_map/ppermute | solution.py:741
  31.5 3.7 collective-permute-start.2
  35.2 5.7 cut_columns.5
  44.9 3.4 collective-permute-start.11
  50.0 4.0 collective-permute-start.4
  56.0 8.9 %collective-permute-done.4.refs_7_ = bf16[208,1024]{1,0:T(8,128)(2,1)S(1)} collective-permute-done((bf16[208,1024]{1,0:T(8,128)(2,1)}, bf16[208,1024]{1,0:T(8,128)(2,1)S(1)}, u32[]{:S(2)}, u32[]{:S(2)}) %collective-permute-start.4) | collective-permute-done | bytes 426016 | tf_op jit(solution)/shard_map/ppermute | solution.py:732
  73.1 4.2 cut_columns.6
  77.4 3.5 collective-permute-done.6.refs_9_
  80.8 20.6 %attention_in.1 = (bf16[1536,1024]{1,0:T(8,128)(2,1)}, bf16[1024,384]{1,0:T(8,128)(2,1)}, bf16[1024,128]{1,0:T(8,128)(2,1)}, bf16[1024,128]{1,0:T(8,128)(2,1)}, ...) custom-call(s32[4]{0:T(128)} %gather_fusion, ...), custom_call_target="tpu_custom_call" | custom-call | flops 1000000 | bytes 1000000 | tf_op jit(solution)/shard_map/attention_in/pallas_call | solution.py:270
  101.5 24.3 %collective-permute-done.26.refs_3_ = bf16[3,192,1536]{2,1,0:T(8,128)(2,1)} collective-permute-done((bf16[3,192,1536]{2,1,0:T(8,128)(2,1)}, bf16[3,192,1536]{2,1,0:T(8,128)(2,1)}, u32[]{:S(2)}, u32[]{:S(2)}) %collective-permute-start.26) | collective-permute-done | bytes 1769504 | tf_op jit(solution)/shard_map/ppermute | solution.py:738
  131.6 15.0 %collective-permute-start.14 = (bf16[3,192,768]{2,1,0:T(8,128)(2,1)}, bf16[3,192,768]{2,1,0:T(8,128)(2,1)}, u32[]{:S(2)}, u32[]{:S(2)}) collective-permute-start(bf16[3,192,768]{2,1,0:T(8,128)(2,1)} %cut_columns.6), channel_id=1, source_target_pairs={{0,1},{2,3},{4,5},{6,7},{9,8},{11,10},{13,12},{15,14},{16,17},{18,... | collective-permute-start | bytes 2654216 | tf_op jit(solution)/shard_map/ppermute | solution.py:735
  152.9 3.3 collective-permute-start.23
  157.5 4.0 cut_columns.7
  161.6 10.4 %collective-permute-done.27.refs_5_ = bf16[3,192,1536]{2,1,0:T(8,128)(2,1)} collective-permute-done((bf16[3,192,1536]{2,1,0:T(8,128)(2,1)}, bf16[3,192,1536]{2,1,0:T(8,128)(2,1)}, u32[]{:S(2)}, u32[]{:S(2)}) %collective-permute-start.27) | collective-permute-done | bytes 1769504 | tf_op jit(solution)/shard_map/ppermute | solution.py:741
  175.5 3.2 collective-permute-start.32
  180.8 22.4 %collective-permute-done.22.refs_12_ = bf16[256,768]{1,0:T(8,128)(2,1)S(1)} collective-permute-done((bf16[256,768]{1,0:T(8,128)(2,1)S(1)}, bf16[256,768]{1,0:T(8,128)(2,1)S(1)}, u32[]{:S(2)}, u32[]{:S(2)}) %collective-permute-start.22) | collective-permute-done | bytes 393248 | tf_op jit(solution)/shard_map/ppermute | solution.py:726
  207.3 23.2 %collective-permute-done.24.refs_14_ = bf16[2,256,768]{2,1,0:T(8,128)(2,1)} collective-permute-done((bf16[2,256,768]{2,1,0:T(8,128)(2,1)S(1)}, bf16[2,256,768]{2,1,0:T(8,128)(2,1)}, u32[]{:S(2)}, u32[]{:S(2)}) %collective-permute-start.24) | collective-permute-done | bytes 786464 | tf_op jit(solution)/shard_map/ppermute | solution.py:732
  230.5 56.4 %feed_forward.2 = (bf16[3,2,384,1536]{3,2,1,0:T(8,128)(2,1)}, bf16[3,2,384,1536]{3,2,1,0:T(8,128)(2,1)}, bf16[1536,1024]{1,0:T(8,128)(2,1)}, bf16[1536,1024]{1,0...) custom-call(s32[4]{0:T(128)} %gather_fusion, s32[1]{0:T(128)} %bitcast.13.refs_1_, ...), custom_call_target="tpu_custom_call" | custom-call | flops 1000000 | bytes 1000000 | tf_op jit(solution)/shard_map/feed_forward/pallas_call | solution.py:696
  287.5 7.9 %collective-permute-done.18.refs_6_ = bf16[3,192,768]{2,1,0:T(8,128)(2,1)S(1)} collective-permute-done((bf16[3,192,768]{2,1,0:T(8,128)(2,1)S(1)}, bf16[3,192,768]{2,1,0:T(8,128)(2,1)S(1)}, u32[]{:S(2)}, u32[]{:S(2)}) %collective-permute-start.18) | collective-permute-done | bytes 884768 | tf_op jit(solution)/shard_map/ppermute | solution.py:729
  304.8 6.2 %fusion.6 = (bf16[3,2,96,1536]{3,2,1,0:T(8,128)(2,1)}, bf16[3,2,96,1536]{3,2,1,0:T(8,128)(2,1)}) fusion(bf16[3,2,4,96,1536]{4,3,2,1,0:T(8,128)(2,1)} %bitcast.23, s32[]{:T(128)S(6)} %select_n.299, bf16[3,2,4,96,1536]{4,3,2,1,0:T(8,128)(2,1)} %bitcast.303, s32[]{:T(128)S(6)} %select_n.296), kind=kLoop, calls=%fused_computation.20 | loop fusion | flops 7077888 | bytes 10616840 | tf_op jit(solution)/shard_map/convert_element_type | solution.py:917
  312.9 13.1 %collective-permute-done.17.refs_5_ = bf16[3,192,768]{2,1,0:T(8,128)(2,1)S(1)} collective-permute-done((bf16[3,192,768]{2,1,0:T(8,128)(2,1)}, bf16[3,192,768]{2,1,0:T(8,128)(2,1)S(1)}, u32[]{:S(2)}, u32[]{:S(2)}) %collective-permute-start.17) | collective-permute-done | bytes 884768 | tf_op jit(solution)/shard_map/ppermute | solution.py:741
  330.2 33.8 %feed_forward.3 = (bf16[3,2,384,768]{3,2,1,0:T(8,128)(2,1)}, bf16[3,2,384,768]{3,2,1,0:T(8,128)(2,1)}, bf16[2,256,768]{2,1,0:T(8,128)(2,1)}, bf16[2,256,768]{2,1...) custom-call(s32[4]{0:T(128)} %gather_fusion, ...), custom_call_target="tpu_custom_call" | custom-call | flops 1000000 | bytes 1000000 | tf_op jit(solution)/shard_map/feed_forward/pallas_call | solution.py:696
  368.4 4.5 fusion.2
  372.9 11.0 %collective-permute-done.36 = bf16[2,256,768]{2,1,0:T(8,128)(2,1)S(1)} collective-permute-done((bf16[2,256,768]{2,1,0:T(8,128)(2,1)}, bf16[2,256,768]{2,1,0:T(8,128)(2,1)S(1)}, u32[]{:S(2)}, u32[]{:S(2)}) %collective-permute-start.36) | collective-permute-done | bytes 786464 | tf_op jit(solution)/shard_map/ppermute | solution.py:726
  389.8 6.7 %collective-permute-done.37 = bf16[256,768]{1,0:T(8,128)(2,1)S(1)} collective-permute-done((bf16[256,768]{1,0:T(8,128)(2,1)S(1)}, bf16[256,768]{1,0:T(8,128)(2,1)S(1)}, u32[]{:S(2)}, u32[]{:S(2)}) %collective-permute-start.37) | collective-permute-done | bytes 393248 | tf_op jit(solution)/shard_map/ppermute | solution.py:726
  401.1 2.5 collective-permute-start.45
  403.6 14.2 %collective-permute-done.39.far = bf16[256,1536]{1,0:T(8,128)(2,1)S(1)} collective-permute-done((bf16[256,1536]{1,0:T(8,128)(2,1)S(1)}, bf16[256,1536]{1,0:T(8,128)(2,1)S(1)}, u32[]{:S(2)}, u32[]{:S(2)}) %collective-permute-start.39) | collective-permute-done | bytes 786464 | tf_op jit(solution)/shard_map/ppermute | solution.py:726
  424.7 10.8 %collective-permute-done.41 = bf16[2,256,768]{2,1,0:T(8,128)(2,1)} collective-permute-done((bf16[2,256,768]{2,1,0:T(8,128)(2,1)}, bf16[2,256,768]{2,1,0:T(8,128)(2,1)}, u32[]{:S(2)}, u32[]{:S(2)}) %collective-permute-start.41) | collective-permute-done | bytes 786464 | tf_op jit(solution)/shard_map/ppermute | solution.py:726
  438.3 3.2 fusion.19
  447.1 7.6 %collective-permute-done.42 = bf16[256,768]{1,0:T(8,128)(2,1)S(1)} collective-permute-done((bf16[256,768]{1,0:T(8,128)(2,1)S(1)}, bf16[256,768]{1,0:T(8,128)(2,1)S(1)}, u32[]{:S(2)}, u32[]{:S(2)}) %collective-permute-start.42) | collective-permute-done | bytes 393248 | tf_op jit(solution)/shard_map/ppermute | solution.py:726
  459.7 18.5 %attention_out.1 = (bf16[1024,384]{1,0:T(8,128)(2,1)}, bf16[2,1024,128]{2,1,0:T(8,128)(2,1)}, bf16[1024,1536]{1,0:T(8,128)(2,1)}) custom-call(s32[2]{0:T(128)} %pad_add_fusion.refs_1_.own, bf16[256,1536]{1,0:T(8,128)(2,1)} %copy-done.9, bf16[256,1536]{1,0:T(8,128)(2,1)} %copy-done.17, bf16[2,256,1536]{2,1,0:T(8,128)(2,1)} %collective-permute-done.46.other, ...), custom_call_target="tpu_custom_call" | custom-call | flops 1000000 | bytes 1000000 | tf_op jit(solution)/shard_map/attention_out/pallas_call | solution.py:349
  478.3 2.7 collective-permute-done.47
  480.9 3.9 convolution_convert_fusion
  486.8 4.0 fusion.1
  490.8 10.0 %collective-permute-done.58 = bf16[2,2,4,48,384]{4,3,1,0,2:T(8,128)(2,1)S(1)} collective-permute-done((bf16[2,2,4,48,384]{4,3,1,0,2:T(8,128)(2,1)S(1)}, bf16[2,2,4,48,384]{4,3,1,0,2:T(8,128)(2,1)S(1)}, u32[]{:S(2)}, u32[]{:S(2)}) %collective-permute-start.58) | collective-permute-done | bytes 589856 | tf_op jit(solution)/shard_map/ppermute | solution.py:732
  500.8 3.5 collective-permute-start.60
  506.8 13.4 %collective-permute-done.60 = bf16[2,2,48,384]{3,2,1,0:T(8,128)(2,1)S(1)} collective-permute-done((bf16[2,2,48,384]{3,2,1,0:T(8,128)(2,1)S(1)}, bf16[2,2,48,384]{3,2,1,0:T(8,128)(2,1)S(1)}, u32[]{:S(2)}, u32[]{:S(2)}) %collective-permute-start.60) | collective-permute-done | bytes 147488 | tf_op jit(solution)/shard_map/ppermute | solution.py:741
  523.3 3.0 fusion.9
  527.0 11.5 %projection_out.1 = (bf16[1536,640]{1,0:T(8,128)(2,1)}, bf16[2,256,1536]{2,1,0:T(8,128)(2,1)}, bf16[2,256,1536]{2,1,0:T(8,128)(2,1)}) custom-call(s32[2]{0:T(128)} %pad_add_fusion.refs_1_.own, bf16[1024,384]{1,0:T(8,128)(2,1)} %get-tuple-element.211.grad_q, bf16[2,1024,128]{2,1,0:T(8,128)(2,1)} %get-tuple-element.212.ours, ...), custom_call_target="tpu_custom_call" | custom-call | flops 1000000 | bytes 1000000 | tf_op jit(solution)/shard_map/projection_out/pallas_call | solution.py:439
  538.5 10.9 %collective-permute-done.59 = bf16[2,2,48,384]{3,2,1,0:T(8,128)(2,1)} collective-permute-done((bf16[2,2,48,384]{3,2,1,0:T(8,128)(2,1)S(1)}, bf16[2,2,48,384]{3,2,1,0:T(8,128)(2,1)}, u32[]{:S(2)}, u32[]{:S(2)}) %collective-permute-start.59) | collective-permute-done | bytes 147488 | tf_op jit(solution)/shard_map/ppermute | solution.py:738
  564.2 15.7 %collective-permute-done.52 = bf16[2,2,4,48,640]{4,3,1,0,2:T(8,128)(2,1)S(1)} collective-permute-done((bf16[2,2,4,48,640]{4,3,1,0,2:T(8,128)(2,1)S(1)}, bf16[2,2,4,48,640]{4,3,1,0,2:T(8,128)(2,1)S(1)}, u32[]{:S(2)}, u32[]{:S(2)}) %collective-permute-start.52) | collective-permute-done | bytes 983072 | tf_op jit(solution)/shard_map/ppermute | solution.py:732
  582.0 4.2 collective-permute-done.54
  591.3 6.2 collective-permute-done.53
  601.4 5.7 collective-permute-done.65
  611.0 4.4 copy.87
  (313 shorter events, 127.7 us)
Async XLA Ops:
  7.9 35.5 %collective-permute-start.9 = (bf16[3,192,1536]{2,1,0:T(8,128)(2,1)}, bf16[3,192,1536]{2,1,0:T(8,128)(2,1)}, u32[]{:S(2)}, u32[]{:S(2)}) collective-permute-start(bf16[3,192,1536]{2,1,0:T(8,128)(2,1)} %cut_columns.4), channel_id=1, source_target_pairs={{0,1},{2,3},{4,5},{6,7},{9,8},{11,10},{13,12},{15,14},{16,17},{18,... | collective-permute-start | bytes 5308424 | tf_op jit(solution)/shard_map/ppermute | solution.py:735
  14.0 26.9 %collective-permute-start.7 = (bf16[256,1536]{1,0:T(8,128)(2,1)S(1)}, bf16[256,1536]{1,0:T(8,128)(2,1)S(1)}, u32[]{:S(2)}, u32[]{:S(2)}) collective-permute-start(bf16[256,1536]{1,0:T(8,128)(2,1)S(1)} %bitcast.298), channel_id=1, source_target_pairs={{0,16},{8,24},{16,0},{24,8},{1,17},{9,25},{17,1},{25,9},{2,18},{10... | collective-permute-start | bytes 2359304 | tf_op jit(solution)/shard_map/ppermute | solution.py:726
  19.5 22.8 %collective-permute-start = (bf16[208,1024]{1,0:T(8,128)(2,1)S(1)}, bf16[208,1024]{1,0:T(8,128)(2,1)}, u32[]{:S(2)}, u32[]{:S(2)}) collective-permute-start(bf16[208,1024]{1,0:T(8,128)(2,1)S(1)} %fusion.38.refs_2_), channel_id=1, source_target_pairs={{0,2},{1,3},{2,6},{3,7},{4,0},{5,1},{6,4},{7,5},{8,10},{9,11},{10,... | collective-permute-start | bytes 1277960 | tf_op jit(solution)/shard_map/ppermute | solution.py:738
  19.5 22.8 %collective-permute-start.3 = (bf16[208,1024]{1,0:T(8,128)(2,1)S(1)}, bf16[208,1024]{1,0:T(8,128)(2,1)}, u32[]{:S(2)}, u32[]{:S(2)}) collective-permute-start(bf16[208,1024]{1,0:T(8,128)(2,1)S(1)} %fusion.38.refs_2_), channel_id=1, source_target_pairs={{0,1},{1,0},{2,3},{3,2},{4,5},{5,4},{6,7},{7,6},{8,9},{9,8},{10,11... | collective-permute-start | bytes 1277960 | tf_op jit(solution)/shard_map/ppermute | solution.py:732
  42.2 25.8 %collective-permute-start.8 = (bf16[2,256,1536]{2,1,0:T(8,128)(2,1)}, bf16[2,256,1536]{2,1,0:T(8,128)(2,1)}, u32[]{:S(2)}, u32[]{:S(2)}) collective-permute-start(bf16[2,256,1536]{2,1,0:T(8,128)(2,1)} %pad_maximum_fusion.3), channel_id=1, source_target_pairs={{0,8},{8,0},{16,24},{24,16},{1,9},{9,1},{17,25},{25,17},{2,10},{10... | collective-permute-start | bytes 4718600 | tf_op jit(solution)/shard_map/ppermute | solution.py:729
  44.9 56.6 %collective-permute-start.11 = (bf16[3,192,1536]{2,1,0:T(8,128)(2,1)}, bf16[3,192,1536]{2,1,0:T(8,128)(2,1)}, u32[]{:S(2)}, u32[]{:S(2)}) collective-permute-start(bf16[3,192,1536]{2,1,0:T(8,128)(2,1)} %broadcast_select_fusion.refs_2_), channel_id=1, source_target_pairs={{2,0},{3,1},{6,2},{7,3},{0,4},{1,5},{4,6},{5,7},{10,8},{11,9},{14,... | collective-permute-start | bytes 5308424 | tf_op jit(solution)/shard_map/ppermute | solution.py:741
  48.2 19.7 %collective-permute-start.10 = (bf16[256,1536]{1,0:T(8,128)(2,1)S(1)}, bf16[256,1536]{1,0:T(8,128)(2,1)S(1)}, u32[]{:S(2)}, u32[]{:S(2)}) collective-permute-start(bf16[256,1536]{1,0:T(8,128)(2,1)S(1)} %bitcast.301), channel_id=1, source_target_pairs={{0,16},{8,24},{16,0},{24,8},{1,17},{9,25},{17,1},{25,9},{2,18},{10... | collective-permute-start | bytes 2359304 | tf_op jit(solution)/shard_map/ppermute | solution.py:726
  55.9 21.4 %collective-permute-start.5 = (bf16[208,1024]{1,0:T(8,128)(2,1)}, bf16[208,1024]{1,0:T(8,128)(2,1)}, u32[]{:S(2)}, u32[]{:S(2)}) collective-permute-start(bf16[208,1024]{1,0:T(8,128)(2,1)} %collective-permute-done.1.refs_4_), channel_id=1, source_target_pairs={{0,1},{1,0},{2,3},{3,2},{4,5},{5,4},{6,7},{7,6},{8,9},{9,8},{10,11... | collective-permute-start | bytes 1277960 | tf_op jit(solution)/shard_map/ppermute | solution.py:732
  68.0 57.8 %collective-permute-start.26 = (bf16[3,192,1536]{2,1,0:T(8,128)(2,1)}, bf16[3,192,1536]{2,1,0:T(8,128)(2,1)}, u32[]{:S(2)}, u32[]{:S(2)}) collective-permute-start(bf16[3,192,1536]{2,1,0:T(8,128)(2,1)} %broadcast_select_fusion.refs_2_), channel_id=1, source_target_pairs={{0,2},{1,3},{2,6},{3,7},{4,0},{5,1},{6,4},{7,5},{8,10},{9,11},{10,... | collective-permute-start | bytes 5308424 | tf_op jit(solution)/shard_map/ppermute | solution.py:738
  68.0 57.8 %collective-permute-start.28 = (bf16[3,192,1536]{2,1,0:T(8,128)(2,1)}, bf16[3,192,1536]{2,1,0:T(8,128)(2,1)}, u32[]{:S(2)}, u32[]{:S(2)}) collective-permute-start(bf16[3,192,1536]{2,1,0:T(8,128)(2,1)} %broadcast_select_fusion.refs_2_), channel_id=1, source_target_pairs={{0,8},{8,0},{16,24},{24,16},{1,9},{9,1},{17,25},{25,17},{2,10},{10... | collective-permute-start | bytes 5308424 | tf_op jit(solution)/shard_map/ppermute | solution.py:729
  101.4 24.4 %collective-permute-start.12 = (bf16[2,256,1536]{2,1,0:T(8,128)(2,1)}, bf16[2,256,1536]{2,1,0:T(8,128)(2,1)S(1)}, u32[]{:S(2)}, u32[]{:S(2)}) collective-permute-start(bf16[2,256,1536]{2,1,0:T(8,128)(2,1)} %get-tuple-element.141), channel_id=1, source_target_pairs={{0,8},{8,0},{16,24},{24,16},{1,9},{9,1},{17,25},{25,17},{2,10},{10... | collective-permute-start | bytes 4718600 | tf_op jit(solution)/shard_map/ppermute | solution.py:729
  129.4 20.1 %collective-permute-start.13 = (bf16[256,1536]{1,0:T(8,128)(2,1)S(1)}, bf16[256,1536]{1,0:T(8,128)(2,1)}, u32[]{:S(2)}, u32[]{:S(2)}) collective-permute-start(bf16[256,1536]{1,0:T(8,128)(2,1)S(1)} %fusion.21), channel_id=1, source_target_pairs={{0,16},{8,24},{16,0},{24,8},{1,17},{9,25},{17,1},{25,9},{2,18},{10... | collective-permute-start | bytes 2359304 | tf_op jit(solution)/shard_map/ppermute | solution.py:726
  131.0 41.0 %collective-permute-start.27 = (bf16[3,192,1536]{2,1,0:T(8,128)(2,1)}, bf16[3,192,1536]{2,1,0:T(8,128)(2,1)}, u32[]{:S(2)}, u32[]{:S(2)}) collective-permute-start(bf16[3,192,1536]{2,1,0:T(8,128)(2,1)} %collective-permute-done.11.refs_4_), channel_id=1, source_target_pairs={{2,0},{3,1},{6,2},{7,3},{0,4},{1,5},{4,6},{5,7},{10,8},{11,9},{14,... | collective-permute-start | bytes 5308424 | tf_op jit(solution)/shard_map/ppermute | solution.py:741
  131.6 40.4 %collective-permute-start.30 = (bf16[3,192,1536]{2,1,0:T(8,128)(2,1)}, bf16[3,192,1536]{2,1,0:T(8,128)(2,1)}, u32[]{:S(2)}, u32[]{:S(2)}) collective-permute-start(bf16[3,192,1536]{2,1,0:T(8,128)(2,1)} %collective-permute-done.11.refs_4_), channel_id=1, source_target_pairs={{0,8},{8,0},{16,24},{24,16},{1,9},{9,1},{17,25},{25,17},{2,10},{10... | collective-permute-start | bytes 5308424 | tf_op jit(solution)/shard_map/ppermute | solution.py:729
  131.6 40.4 %collective-permute-start.14 = (bf16[3,192,768]{2,1,0:T(8,128)(2,1)}, bf16[3,192,768]{2,1,0:T(8,128)(2,1)}, u32[]{:S(2)}, u32[]{:S(2)}) collective-permute-start(bf16[3,192,768]{2,1,0:T(8,128)(2,1)} %cut_columns.6), channel_id=1, source_target_pairs={{0,1},{2,3},{4,5},{6,7},{9,8},{11,10},{13,12},{15,14},{16,17},{18,... | collective-permute-start | bytes 2654216 | tf_op jit(solution)/shard_map/ppermute | solution.py:735
  152.9 20.4 %collective-permute-start.23 = (bf16[256,768]{1,0:T(8,128)(2,1)S(1)}, bf16[256,768]{1,0:T(8,128)(2,1)}, u32[]{:S(2)}, u32[]{:S(2)}) collective-permute-start(bf16[256,768]{1,0:T(8,128)(2,1)S(1)} %get-tuple-element.166.refs_11_), channel_id=1, source_target_pairs={{0,1},{1,0},{2,3},{3,2},{4,5},{5,4},{6,7},{7,6},{8,9},{9,8},{10,11... | collective-permute-start | bytes 1179656 | tf_op jit(solution)/shard_map/ppermute | solution.py:732
  172.0 58.5 %collective-permute-start.31 = (bf16[3,192,1536]{2,1,0:T(8,128)(2,1)}, bf16[3,192,1536]{2,1,0:T(8,128)(2,1)}, u32[]{:S(2)}, u32[]{:S(2)}) collective-permute-start(bf16[3,192,1536]{2,1,0:T(8,128)(2,1)} %collective-permute-done.27.refs_5_), channel_id=1, source_target_pairs={{0,8},{8,0},{16,24},{24,16},{1,9},{9,1},{17,25},{25,17},{2,10},{10... | collective-permute-start | bytes 5308424 | tf_op jit(solution)/shard_map/ppermute | solution.py:729
  174.8 30.0 %collective-permute-start.25 = (bf16[2,256,768]{2,1,0:T(8,128)(2,1)S(1)}, bf16[2,256,768]{2,1,0:T(8,128)(2,1)}, u32[]{:S(2)}, u32[]{:S(2)}) collective-permute-start(bf16[2,256,768]{2,1,0:T(8,128)(2,1)S(1)} %pad_maximum_fusion.9), channel_id=1, source_target_pairs={{0,16},{8,24},{16,0},{24,8},{1,17},{9,25},{17,1},{25,9},{2,18},{10... | collective-permute-start | bytes 2359304 | tf_op jit(solution)/shard_map/ppermute | solution.py:726
  175.5 55.0 %collective-permute-start.32 = (bf16[2,256,1536]{2,1,0:T(8,128)(2,1)S(1)}, bf16[2,256,1536]{2,1,0:T(8,128)(2,1)}, u32[]{:S(2)}, u32[]{:S(2)}) collective-permute-start(bf16[2,256,1536]{2,1,0:T(8,128)(2,1)S(1)} %copy-done.21), channel_id=1, source_target_pairs={{0,1},{1,0},{2,3},{3,2},{4,5},{5,4},{6,7},{7,6},{8,9},{9,8},{10,11... | collective-permute-start | bytes 4718600 | tf_op jit(solution)/shard_map/ppermute | solution.py:732
  178.7 24.5 %collective-permute-start.22 = (bf16[256,768]{1,0:T(8,128)(2,1)S(1)}, bf16[256,768]{1,0:T(8,128)(2,1)S(1)}, u32[]{:S(2)}, u32[]{:S(2)}) collective-permute-start(bf16[256,768]{1,0:T(8,128)(2,1)S(1)} %copy-done.13), channel_id=1, source_target_pairs={{0,16},{8,24},{16,0},{24,8},{1,17},{9,25},{17,1},{25,9},{2,18},{10... | collective-permute-start | bytes 1179656 | tf_op jit(solution)/shard_map/ppermute | solution.py:726
  179.3 107.6 %collective-permute-start.15 = (bf16[3,192,768]{2,1,0:T(8,128)(2,1)S(1)}, bf16[3,192,768]{2,1,0:T(8,128)(2,1)}, u32[]{:S(2)}, u32[]{:S(2)}) collective-permute-start(bf16[3,192,768]{2,1,0:T(8,128)(2,1)S(1)} %broadcast_select_fusion.1.refs_2_), channel_id=1, source_target_pairs={{0,2},{1,3},{2,6},{3,7},{4,0},{5,1},{6,4},{7,5},{8,10},{9,11},{10,... | collective-permute-start | bytes 2654216 | tf_op jit(solution)/shard_map/ppermute | solution.py:738
  203.3 83.7 %collective-permute-start.16 = (bf16[3,192,768]{2,1,0:T(8,128)(2,1)S(1)}, bf16[3,192,768]{2,1,0:T(8,128)(2,1)}, u32[]{:S(2)}, u32[]{:S(2)}) collective-permute-start(bf16[3,192,768]{2,1,0:T(8,128)(2,1)S(1)} %broadcast_select_fusion.1.refs_2_), channel_id=1, source_target_pairs={{2,0},{3,1},{6,2},{7,3},{0,4},{1,5},{4,6},{5,7},{10,8},{11,9},{14,... | collective-permute-start | bytes 2654216 | tf_op jit(solution)/shard_map/ppermute | solution.py:741
  204.9 25.6 %collective-permute-start.24 = (bf16[2,256,768]{2,1,0:T(8,128)(2,1)S(1)}, bf16[2,256,768]{2,1,0:T(8,128)(2,1)}, u32[]{:S(2)}, u32[]{:S(2)}) collective-permute-start(bf16[2,256,768]{2,1,0:T(8,128)(2,1)S(1)} %pad_maximum_fusion.8), channel_id=1, source_target_pairs={{0,1},{1,0},{2,3},{3,2},{4,5},{5,4},{6,7},{7,6},{8,9},{9,8},{10,11... | collective-permute-start | bytes 2359304 | tf_op jit(solution)/shard_map/ppermute | solution.py:732
  286.9 17.8 %collective-permute-start.33 = (bf16[3,2,384,1536]{3,2,1,0:T(8,128)(2,1)}, bf16[3,2,384,1536]{3,2,1,0:T(8,128)(2,1)}, u32[]{:S(2)}, u32[]{:S(2)}) collective-permute-start(bf16[3,2,384,1536]{3,2,1,0:T(8,128)(2,1)} %get-tuple-element.164), channel_id=1, source_target_pairs={{0,8},{8,0},{16,24},{24,16},{1,9},{9,1},{17,25},{25,17},{2,10},{10... | collective-permute-start | bytes 21233672 | tf_op jit(solution)/shard_map/ppermute | solution.py:729
  303.2 22.8 %collective-permute-start.17 = (bf16[3,192,768]{2,1,0:T(8,128)(2,1)}, bf16[3,192,768]{2,1,0:T(8,128)(2,1)S(1)}, u32[]{:S(2)}, u32[]{:S(2)}) collective-permute-start(bf16[3,192,768]{2,1,0:T(8,128)(2,1)} %collective-permute-done.16.refs_4_), channel_id=1, source_target_pairs={{2,0},{3,1},{6,2},{7,3},{0,4},{1,5},{4,6},{5,7},{10,8},{11,9},{14,... | collective-permute-start | bytes 2654216 | tf_op jit(solution)/shard_map/ppermute | solution.py:741
  304.8 21.2 %collective-permute-start.20 = (bf16[3,192,768]{2,1,0:T(8,128)(2,1)}, bf16[3,192,768]{2,1,0:T(8,128)(2,1)S(1)}, u32[]{:S(2)}, u32[]{:S(2)}) collective-permute-start(bf16[3,192,768]{2,1,0:T(8,128)(2,1)} %collective-permute-done.16.refs_4_), channel_id=1, source_target_pairs={{0,8},{8,0},{16,24},{24,16},{1,9},{9,1},{17,25},{25,17},{2,10},{10... | collective-permute-start | bytes 2654216 | tf_op jit(solution)/shard_map/ppermute | solution.py:729
  311.0 53.0 %collective-permute-start.34 = (bf16[3,2,96,1536]{3,2,1,0:T(8,128)(2,1)}, bf16[3,2,96,1536]{3,2,1,0:T(8,128)(2,1)}, u32[]{:S(2)}, u32[]{:S(2)}) collective-permute-start(bf16[3,2,96,1536]{3,2,1,0:T(8,128)(2,1)} %get-tuple-element.274), channel_id=1, source_target_pairs={{2,0},{3,1},{6,2},{7,3},{0,4},{1,5},{4,6},{5,7},{10,8},{11,9},{14,... | collective-permute-start | bytes 5308424 | tf_op jit(solution)/shard_map/ppermute | solution.py:741
  364.0 19.9 %collective-permute-start.36 = (bf16[2,256,768]{2,1,0:T(8,128)(2,1)}, bf16[2,256,768]{2,1,0:T(8,128)(2,1)S(1)}, u32[]{:S(2)}, u32[]{:S(2)}) collective-permute-start(bf16[2,256,768]{2,1,0:T(8,128)(2,1)} %get-tuple-element.192), channel_id=1, source_target_pairs={{0,16},{8,24},{16,0},{24,8},{1,17},{9,25},{17,1},{25,9},{2,18},{10... | collective-permute-start | bytes 2359304 | tf_op jit(solution)/shard_map/ppermute | solution.py:726
  366.6 19.6 %collective-permute-start.35 = (bf16[2,256,768]{2,1,0:T(8,128)(2,1)}, bf16[2,256,768]{2,1,0:T(8,128)(2,1)S(1)}, u32[]{:S(2)}, u32[]{:S(2)}) collective-permute-start(bf16[2,256,768]{2,1,0:T(8,128)(2,1)} %get-tuple-element.190), channel_id=1, source_target_pairs={{0,1},{1,0},{2,3},{3,2},{4,5},{5,4},{6,7},{7,6},{8,9},{9,8},{10,11... | collective-permute-start | bytes 2359304 | tf_op jit(solution)/shard_map/ppermute | solution.py:732
  389.8 48.5 %collective-permute-start.44 = (bf16[3,2,384,768]{3,2,1,0:T(8,128)(2,1)}, bf16[3,2,384,768]{3,2,1,0:T(8,128)(2,1)}, u32[]{:S(2)}, u32[]{:S(2)}) collective-permute-start(bf16[3,2,384,768]{3,2,1,0:T(8,128)(2,1)} %get-tuple-element.202), channel_id=1, source_target_pairs={{0,8},{8,0},{16,24},{24,16},{1,9},{9,1},{17,25},{25,17},{2,10},{10... | collective-permute-start | bytes 10616840 | tf_op jit(solution)/shard_map/ppermute | solution.py:729
  400.6 17.2 %collective-permute-start.39 = (bf16[256,1536]{1,0:T(8,128)(2,1)S(1)}, bf16[256,1536]{1,0:T(8,128)(2,1)S(1)}, u32[]{:S(2)}, u32[]{:S(2)}) collective-permute-start(bf16[256,1536]{1,0:T(8,128)(2,1)S(1)} %get-tuple-element.270.near), channel_id=1, source_target_pairs={{0,16},{8,24},{16,0},{24,8},{1,17},{9,25},{17,1},{25,9},{2,18},{10... | collective-permute-start | bytes 2359304 | tf_op jit(solution)/shard_map/ppermute | solution.py:726
  401.1 41.9 %collective-permute-start.45 = (bf16[3,2,96,1536]{3,2,1,0:T(8,128)(2,1)}, bf16[3,2,96,1536]{3,2,1,0:T(8,128)(2,1)}, u32[]{:S(2)}, u32[]{:S(2)}) collective-permute-start(bf16[3,2,96,1536]{3,2,1,0:T(8,128)(2,1)} %get-tuple-element.275), channel_id=1, source_target_pairs={{0,2},{1,3},{2,6},{3,7},{4,0},{5,1},{6,4},{7,5},{8,10},{9,11},{10,... | collective-permute-start | bytes 5308424 | tf_op jit(solution)/shard_map/ppermute | solution.py:738
  418.7 16.7 %collective-permute-start.41 = (bf16[2,256,768]{2,1,0:T(8,128)(2,1)}, bf16[2,256,768]{2,1,0:T(8,128)(2,1)}, u32[]{:S(2)}, u32[]{:S(2)}) collective-permute-start(bf16[2,256,768]{2,1,0:T(8,128)(2,1)} %get-tuple-element.198), channel_id=1, source_target_pairs={{0,16},{8,24},{16,0},{24,8},{1,17},{9,25},{17,1},{25,9},{2,18},{10... | collective-permute-start | bytes 2359304 | tf_op jit(solution)/shard_map/ppermute | solution.py:726
  419.3 17.7 %collective-permute-start.40 = (bf16[2,256,768]{2,1,0:T(8,128)(2,1)}, bf16[2,256,768]{2,1,0:T(8,128)(2,1)}, u32[]{:S(2)}, u32[]{:S(2)}) collective-permute-start(bf16[2,256,768]{2,1,0:T(8,128)(2,1)} %get-tuple-element.196), channel_id=1, source_target_pairs={{0,1},{1,0},{2,3},{3,2},{4,5},{5,4},{6,7},{7,6},{8,9},{9,8},{10,11... | collective-permute-start | bytes 2359304 | tf_op jit(solution)/shard_map/ppermute | solution.py:732
  421.0 59.9 %collective-permute-start.47 = (bf16[3,2,96,1536]{3,2,1,0:T(8,128)(2,1)}, bf16[3,2,96,1536]{3,2,1,0:T(8,128)(2,1)}, u32[]{:S(2)}, u32[]{:S(2)}) collective-permute-start(bf16[3,2,96,1536]{3,2,1,0:T(8,128)(2,1)} %fusion.2), channel_id=1, source_target_pairs={{2,0},{3,1},{6,2},{7,3},{0,4},{1,5},{4,6},{5,7},{10,8},{11,9},{14,... | collective-permute-start | bytes 5308424 | tf_op jit(solution)/shard_map/ppermute | solution.py:741
  457.2 63.8 %collective-permute-start.49 = (bf16[3,2,96,768]{3,2,1,0:T(8,128)(2,1)}, bf16[3,2,96,768]{3,2,1,0:T(8,128)(2,1)}, u32[]{:S(2)}, u32[]{:S(2)}) collective-permute-start(bf16[3,2,96,768]{3,2,1,0:T(8,128)(2,1)} %get-tuple-element.276), channel_id=1, source_target_pairs={{2,0},{3,1},{6,2},{7,3},{0,4},{1,5},{4,6},{5,7},{10,8},{11,9},{14,... | collective-permute-start | bytes 2654216 | tf_op jit(solution)/shard_map/ppermute | solution.py:741
  459.5 101.8 %collective-permute-start.66 = (bf16[3,2,96,768]{3,2,1,0:T(8,128)(2,1)}, bf16[3,2,96,768]{3,2,1,0:T(8,128)(2,1)}, u32[]{:S(2)}, u32[]{:S(2)}) collective-permute-start(bf16[3,2,96,768]{3,2,1,0:T(8,128)(2,1)} %get-tuple-element.277), channel_id=1, source_target_pairs={{0,2},{1,3},{2,6},{3,7},{4,0},{5,1},{6,4},{7,5},{8,10},{9,11},{10,... | collective-permute-start | bytes 2654216 | tf_op jit(solution)/shard_map/ppermute | solution.py:738
  480.9 45.4 %collective-permute-start.48 = (bf16[2,1024,128]{2,1,0:T(8,128)(2,1)}, bf16[2,1024,128]{2,1,0:T(8,128)(2,1)}, u32[]{:S(2)}, u32[]{:S(2)}) collective-permute-start(bf16[2,1024,128]{2,1,0:T(8,128)(2,1)} %get-tuple-element.212.ours), channel_id=1, source_target_pairs={{0,8},{8,0},{16,24},{24,16},{1,9},{9,1},{17,25},{25,17},{2,10},{10... | collective-permute-start | bytes 1572872 | tf_op jit(solution)/shard_map/ppermute | solution.py:729
  500.8 19.4 %collective-permute-start.60 = (bf16[2,2,48,384]{3,2,1,0:T(8,128)(2,1)S(1)}, bf16[2,2,48,384]{3,2,1,0:T(8,128)(2,1)S(1)}, u32[]{:S(2)}, u32[]{:S(2)}) collective-permute-start(bf16[2,2,48,384]{3,2,1,0:T(8,128)(2,1)S(1)} %fusion.43), channel_id=1, source_target_pairs={{2,0},{3,1},{6,2},{7,3},{0,4},{1,5},{4,6},{5,7},{10,8},{11,9},{14,... | collective-permute-start | bytes 442376 | tf_op jit(solution)/shard_map/ppermute | solution.py:741
  505.3 51.7 %collective-permute-start.64 = (bf16[3,2,48,1536]{3,2,1,0:T(8,128)(2,1)}, bf16[3,2,48,1536]{3,2,1,0:T(8,128)(2,1)S(1)}, u32[]{:S(2)}, u32[]{:S(2)}) collective-permute-start(bf16[3,2,48,1536]{3,2,1,0:T(8,128)(2,1)} %get-tuple-element.288), channel_id=1, source_target_pairs={{0,16},{8,24},{16,0},{24,8},{1,17},{9,25},{17,1},{25,9},{2,18},{10... | collective-permute-start | bytes 2654216 | tf_op jit(solution)/shard_map/ppermute | solution.py:726
  520.3 29.0 %collective-permute-start.59 = (bf16[2,2,48,384]{3,2,1,0:T(8,128)(2,1)S(1)}, bf16[2,2,48,384]{3,2,1,0:T(8,128)(2,1)}, u32[]{:S(2)}, u32[]{:S(2)}) collective-permute-start(bf16[2,2,48,384]{3,2,1,0:T(8,128)(2,1)S(1)} %get-tuple-element.290), channel_id=1, source_target_pairs={{0,2},{1,3},{2,6},{3,7},{4,0},{5,1},{6,4},{7,5},{8,10},{9,11},{10,... | collective-permute-start | bytes 442376 | tf_op jit(solution)/shard_map/ppermute | solution.py:738
  521.0 28.3 %collective-permute-start.61 = (bf16[2,2,48,384]{3,2,1,0:T(8,128)(2,1)S(1)}, bf16[2,2,48,384]{3,2,1,0:T(8,128)(2,1)}, u32[]{:S(2)}, u32[]{:S(2)}) collective-permute-start(bf16[2,2,48,384]{3,2,1,0:T(8,128)(2,1)S(1)} %get-tuple-element.289), channel_id=1, source_target_pairs={{2,0},{3,1},{6,2},{7,3},{0,4},{1,5},{4,6},{5,7},{10,8},{11,9},{14,... | collective-permute-start | bytes 442376 | tf_op jit(solution)/shard_map/ppermute | solution.py:741
  526.3 35.0 %collective-permute-start.67 = (bf16[3,2,96,768]{3,2,1,0:T(8,128)(2,1)}, bf16[3,2,96,768]{3,2,1,0:T(8,128)(2,1)}, u32[]{:S(2)}, u32[]{:S(2)}) collective-permute-start(bf16[3,2,96,768]{3,2,1,0:T(8,128)(2,1)} %fusion.9), channel_id=1, source_target_pairs={{2,0},{3,1},{6,2},{7,3},{0,4},{1,5},{4,6},{5,7},{10,8},{11,9},{14,... | collective-permute-start | bytes 2654216 | tf_op jit(solution)/shard_map/ppermute | solution.py:741
  555.3 24.7 %collective-permute-start.52 = (bf16[2,2,4,48,640]{4,3,1,0,2:T(8,128)(2,1)S(1)}, bf16[2,2,4,48,640]{4,3,1,0,2:T(8,128)(2,1)S(1)}, u32[]{:S(2)}, u32[]{:S(2)}) collective-permute-start(bf16[2,2,4,48,640]{4,3,1,0,2:T(8,128)(2,1)S(1)} %copy_bitcast_fusion), channel_id=1, source_target_pairs={{0,1},{1,0},{2,3},{3,2},{4,5},{5,4},{6,7},{7,6},{8,9},{9,8},{10,11... | collective-permute-start | bytes 2949128 | tf_op jit(solution)/shard_map/ppermute | solution.py:732
  559.8 37.8 %collective-permute-start.51 = (bf16[256,1536]{1,0:T(8,128)(2,1)S(1)}, bf16[256,1536]{1,0:T(8,128)(2,1)S(1)}, u32[]{:S(2)}, u32[]{:S(2)}) collective-permute-start(bf16[256,1536]{1,0:T(8,128)(2,1)S(1)} %fusion.22), channel_id=1, source_target_pairs={{0,16},{8,24},{16,0},{24,8},{1,17},{9,25},{17,1},{25,9},{2,18},{10... | collective-permute-start | bytes 2359304 | tf_op jit(solution)/shard_map/ppermute | solution.py:726
  563.9 25.8 %collective-permute-start.68 = (bf16[3,2,48,768]{3,2,0,1:T(8,128)(2,1)S(1)}, bf16[3,2,48,768]{3,2,0,1:T(8,128)(2,1)S(1)}, u32[]{:S(2)}, u32[]{:S(2)}) collective-permute-start(bf16[3,2,48,768]{3,2,0,1:T(8,128)(2,1)S(1)} %bitcast.327), channel_id=1, source_target_pairs={{0,1},{1,0},{2,3},{3,2},{4,5},{5,4},{6,7},{7,6},{8,9},{9,8},{10,11... | collective-permute-start | bytes 1327112 | tf_op jit(solution)/shard_map/ppermute | solution.py:732
  580.2 26.9 %collective-permute-start.65 = (bf16[3,2,48,1536]{3,2,1,0:T(8,128)(2,1)S(1)}, bf16[3,2,48,1536]{3,2,1,0:T(8,128)(2,1)S(1)}, u32[]{:S(2)}, u32[]{:S(2)}) collective-permute-start(bf16[3,2,48,1536]{3,2,1,0:T(8,128)(2,1)S(1)} %get-tuple-element.286), channel_id=1, source_target_pairs={{0,1},{1,0},{2,3},{3,2},{4,5},{5,4},{6,7},{7,6},{8,9},{9,8},{10,11... | collective-permute-start | bytes 2654216 | tf_op jit(solution)/shard_map/ppermute | solution.py:732
  589.7 18.3 %collective-permute-start.69 = (bf16[3,2,48,768]{3,2,0,1:T(8,128)(2,1)S(1)}, bf16[3,2,48,768]{3,2,0,1:T(8,128)(2,1)S(1)}, u32[]{:S(2)}, u32[]{:S(2)}) collective-permute-start(bf16[3,2,48,768]{3,2,0,1:T(8,128)(2,1)S(1)} %get-tuple-element.294), channel_id=1, source_target_pairs={{0,16},{8,24},{16,0},{24,8},{1,17},{9,25},{17,1},{25,9},{2,18},{10... | collective-permute-start | bytes 1327112 | tf_op jit(solution)/shard_map/ppermute | solution.py:726
  (67 other events, 818.0 us)

commit v3 on v2

v3 whole, which is shorter than its diff:
```python
import functools

import jax
import jax.numpy as jnp
from jax import lax
from jax.experimental import pallas as pl
from jax.experimental.pallas import tpu as pltpu
from jax.sharding import PartitionSpec as P

D = 1536
HEADS = 12
KV = 2
HD = 128
FF = 8960
LANE = 128

epsilon = 1e-06
rope_base = 1000000.0
masked_value = -1e30
BF = jnp.bfloat16
F32 = jnp.float32
VMEM_BYTES = 60 * 1024 * 1024

CHIP_STARTS = (0, 18, 36, 52)
CHIP_VALID = ((0, 18), (0, 18), (0, 17), (1, 18))
TILE = 256
CHUNKS = ((0, 1280), (1280, 2304))
QUERY_ROWS = 256

anywhere = pl.BlockSpec(memory_space=pl.ANY)
in_vmem = pl.BlockSpec(memory_space=pltpu.VMEM)
in_smem = pl.BlockSpec(memory_space=pltpu.SMEM)


def rope_tables(positions):
    ladder = jnp.arange(HD // 2, dtype=F32)
    inverse = rope_base ** (-2.0 * ladder / HD)
    angles = positions.astype(F32)[:, None] * inverse[None, :]
    cosine, sine = jnp.cos(angles), jnp.sin(angles)
    return (
        jnp.concatenate([cosine, cosine], axis=-1),
        jnp.concatenate([-sine, sine], axis=-1),
    )


def rms_factor(value):
    return lax.rsqrt(jnp.mean(value * value, axis=-1, keepdims=True) + epsilon)


def rms_backward(value, factor, gain, grad):
    unit = value * factor
    weighted = grad * gain
    grad_gain = jnp.sum(grad * unit, axis=0)
    inner = jnp.mean(weighted * unit, axis=-1, keepdims=True)
    return (factor * (weighted - unit * inner), grad_gain)


def dot(left, right):
    return jnp.dot(left, right, preferred_element_type=F32)


def dot_t(left, right):
    return lax.dot_general(left, right, (((1,), (1,)), ((), ())), preferred_element_type=F32)


def t_dot(left, right):
    return lax.dot_general(left, right, (((0,), (0,)), ((), ())), preferred_element_type=F32)


def pick(array, index, axis=0):
    return lax.dynamic_index_in_dim(array, index, axis, keepdims=False)


def tie(value, *others):
    return lax.optimization_barrier((value, *others))[0] if jax.tree.leaves(others) else value


def kernel_params():
    return pltpu.CompilerParams(vmem_limit_bytes=VMEM_BYTES)


KERNEL_COST = pl.CostEstimate(flops=1_000_000, bytes_accessed=1_000_000, transcendentals=0)


def cut_body(place, gate_up, down, target, pairs, sems):
    cols = pl.ds(pl.multiple_of(place[0], LANE), target.shape[2])
    copies = [
        pltpu.make_async_copy(gate_up.at[:, :, cols], pairs, sems.at[0]),
        pltpu.make_async_copy(down.at[:, cols], target.at[2], sems.at[1]),
    ]
    for copy in copies:
        copy.start()
    copies[0].wait()
    target[0] = pairs[:, 0, :]
    target[1] = pairs[:, 1, :]
    copies[1].wait()
    empty = jnp.zeros((3, target.shape[1], LANE), BF)

    @pl.when(place[1] == 1)
    def _():
        target[:, :, 0:LANE] = empty

    @pl.when(place[1] == 2)
    def _():
        target[:, :, target.shape[2] - LANE :] = empty


def cut_columns(place, gate_up, down, cols):
    rows = down.shape[0]
    return pl.pallas_call(
        cut_body,
        out_shape=jax.ShapeDtypeStruct((3, rows, cols), BF),
        in_specs=[in_smem, anywhere, anywhere],
        out_specs=in_vmem,
        scratch_shapes=[pltpu.VMEM((rows, 2, cols), BF), pltpu.SemaphoreType.DMA((2,))],
        compiler_params=kernel_params(),
        cost_estimate=KERNEL_COST,
        name="cut_columns",
    )(place, gate_up, down)


def sequence_copies(s, sources, target, sems):
    near, far, other_near, other_far = sources
    rows = near.shape[0]
    x, c = s // 2, lax.rem(s, 2)
    copies = []
    for i, (source, owner) in enumerate(
        (
            (near, 2 * x + c),
            (far, 2 * (1 - x) + c),
            (other_near, 2 * x + 1 - c),
            (other_far, 2 * (1 - x) + 1 - c),
        )
    ):
        place = pl.multiple_of(owner * rows, LANE)
        copies.append(pltpu.make_async_copy(source, target.at[pl.ds(place, rows)], sems.at[i]))
    return copies


def split_store(s, block, value, targets):
    x, c = s // 2, lax.rem(s, 2)
    for i, target in enumerate(targets):
        far, away = i % 2, i // 2
        owner = 2 * (1 - x if far else x) + (1 - c if away else c)

        @pl.when(owner == block)
        def _():
            target[...] = value


def attention_in_body(planes, rows, *refs):
    places, own = refs[0], refs[1]
    mine = refs[2 : 2 + planes]
    theirs = refs[2 + planes : 2 + 2 * planes]
    sources = refs[2 + 2 * planes : 6 + 2 * planes]
    cosine, sine, starts = refs[6 + 2 * planes : 9 + 2 * planes]
    normed_t, queries, keys, values, attended_t = refs[9 + 2 * planes : 14 + 2 * planes]
    targets = refs[14 + 2 * planes : 18 + 2 * planes]
    weights, gains, tokens, small, sems, token_sems = refs[18 + 2 * planes :]
    length = tokens.shape[0]
    group_cols = queries.shape[1]
    blocks = 2 * planes
    s, y = own[0], own[1]
    copies = sequence_copies(s, sources, tokens, token_sems)
    for k in range(planes):
        for side, source in enumerate((mine[k], theirs[k])):
            block = places[k] * 2 + (y if side == 0 else 1 - y)
            first = pl.multiple_of(block * rows, 16)
            copies.append(
                pltpu.make_async_copy(
                    source.at[pl.ds(0, rows)], weights.at[pl.ds(first, rows)], sems.at[0, 2 * k + side]
                )
            )
            copies.append(
                pltpu.make_async_copy(
                    source.at[pl.ds(rows, 16)],
                    small.at[pl.ds(pl.multiple_of(block * 16, 16), 16)],
                    sems.at[1, 2 * k + side],
                )
            )
    for copy in copies:
        copy.start()
    for copy in copies:
        copy.wait()
    kv_own = KV * HD // blocks
    vectors = []
    for row, width in enumerate((rows, rows, rows, kv_own, kv_own)):
        vectors.append(
            jnp.concatenate(
                [small[pl.ds(16 * b + row, 1), 0:width].astype(F32) for b in range(blocks)], axis=1
            )
        )
    gains[0:1, :] = vectors[0]
    gains[1:2, :] = vectors[1]
    gains[2:3, :] = vectors[2]
    gains[3:4, 0 : KV * HD] = vectors[3]
    gains[4:5, 0 : KV * HD] = vectors[4]
    gain = gains[0:1, :]
    kv = s // 2
    bias = jnp.concatenate(
        [
            gains[2:3, pl.ds(pl.multiple_of(s * group_cols, LANE), group_cols)],
            gains[3:4, pl.ds(pl.multiple_of(kv * HD, LANE), HD)],
            gains[4:5, pl.ds(pl.multiple_of(kv * HD, LANE), HD)],
        ],
        axis=1,
    )
    wide = group_cols + 2 * HD
    heads = group_cols // HD
    for first in range(0, length, QUERY_ROWS):
        r = pl.ds(first, QUERY_ROWS)
        value = tokens[r, :].astype(F32)
        low = (value * rms_factor(value) * gain).astype(BF)
        normed_t[:, r] = low.T
        qkv = dot(low, weights[:, 0:wide]) + bias
        cos_rows, sin_rows = cosine[r, :], sine[r, :]
        for head in range(heads + 1):
            one = qkv[:, head * HD : (head + 1) * HD]
            turned = (one * cos_rows + pltpu.roll(one, HD // 2, 1) * sin_rows).astype(BF)
            if head < heads:
                queries[r, head * HD : (head + 1) * HD] = turned
            else:
                keys[r, :] = turned
        values[r, :] = qkv[:, group_cols + HD :].astype(BF)
    scaling = HD ** (-0.5)
    for first in range(0, length, QUERY_ROWS):
        r = pl.ds(first, QUERY_ROWS)
        reach = first + QUERY_ROWS
        query_place = first + lax.broadcasted_iota(jnp.int32, (QUERY_ROWS, reach), 0)
        key_place = lax.broadcasted_iota(jnp.int32, (QUERY_ROWS, reach), 1)
        allowed = (key_place <= query_place) & (key_place >= starts[r, :])
        outcomes = []
        for head in range(heads):
            cols = slice(head * HD, (head + 1) * HD)
            scores = dot_t(queries[r, cols], keys[0:reach, :]) * scaling
            scores = jnp.where(allowed, scores, masked_value)
            shifted = jnp.exp(scores - jnp.max(scores, axis=-1, keepdims=True))
            total = jnp.sum(shifted, axis=-1, keepdims=True)
            outcome = dot(shifted.astype(BF), values[0:reach, :])
            outcomes.append((outcome / total).astype(BF))
        attended = jnp.concatenate(outcomes, axis=1)
        attended_t[:, r] = attended.T
        term = dot_t(attended, weights[:, wide:]).astype(BF)
        split_store(s, first // QUERY_ROWS, term, targets)


def attention_in(places, own, mine, theirs, tokens, cosine, sine, starts, group_cols):
    planes = len(mine)
    rows = mine[0].shape[0] - 16
    length = cosine.shape[0]
    shapes = [
        jax.ShapeDtypeStruct((D, length), BF),
        jax.ShapeDtypeStruct((length, group_cols), BF),
        jax.ShapeDtypeStruct((length, HD), BF),
        jax.ShapeDtypeStruct((length, HD), BF),
        jax.ShapeDtypeStruct((group_cols, length), BF),
        *[jax.ShapeDtypeStruct((QUERY_ROWS, D), BF)] * 4,
        jax.ShapeDtypeStruct((D, mine[0].shape[1]), BF),
        jax.ShapeDtypeStruct((8, D), F32),
        jax.ShapeDtypeStruct((length, D), BF),
    ]
    return pl.pallas_call(
        functools.partial(attention_in_body, planes, rows),
        out_shape=shapes,
        in_specs=[in_smem, in_smem] + [anywhere] * (2 * planes + 4) + [in_vmem] * 3,
        out_specs=[in_vmem] * len(shapes),
        scratch_shapes=[
            pltpu.VMEM((2 * planes * 16, mine[0].shape[1]), BF),
            pltpu.SemaphoreType.DMA((2, 2 * planes)),
            pltpu.SemaphoreType.DMA((4,)),
        ],
        compiler_params=kernel_params(),
        cost_estimate=KERNEL_COST,
        name="attention_in",
    )(places, own, *mine, *theirs, *tokens, cosine, sine, starts)


def attention_out_body(
    own,
    near,
    far,
    other_near,
    other_far,
    weights,
    queries,
    keys,
    values,
    cosine,
    sine,
    starts,
    normed_t,
    attended_t,
    grad_q,
    grad_kv,
    d_early,
    grad,
    grad_k,
    grad_v,
    sems,
):
    copies = sequence_copies(own[0], (near, far, other_near, other_far), grad, sems)
    for copy in copies:
        copy.start()
    for copy in copies:
        copy.wait()
    length = grad.shape[0]
    group_cols = queries.shape[1]
    heads = group_cols // HD
    scaling = HD ** (-0.5)
    output = weights[:, group_cols + 2 * HD :]
    grad_k[...] = jnp.zeros_like(grad_k)
    grad_v[...] = jnp.zeros_like(grad_v)
    for first in range(0, length, QUERY_ROWS):
        r = pl.ds(first, QUERY_ROWS)
        reach = first + QUERY_ROWS
        grad_heads = dot(grad[r, :], output).astype(BF)
        query_place = first + lax.broadcasted_iota(jnp.int32, (QUERY_ROWS, reach), 0)
        key_place = lax.broadcasted_iota(jnp.int32, (QUERY_ROWS, reach), 1)
        allowed = (key_place <= query_place) & (key_place >= starts[r, :])
        cos_rows, sin_rows = cosine[r, :], sine[r, :]
        for head in range(heads):
            cols = slice(head * HD, (head + 1) * HD)
            one_query = queries[r, cols]
            one_grad = grad_heads[:, cols]
            scores = dot_t(one_query, keys[0:reach, :]) * scaling
            scores = jnp.where(allowed, scores, masked_value)
            shifted = jnp.exp(scores - jnp.max(scores, axis=-1, keepdims=True))
            probability = shifted * (1.0 / jnp.sum(shifted, axis=-1, keepdims=True))
            grad_prob = dot_t(one_grad, values[0:reach, :])
            weighted = probability * grad_prob
            inner = jnp.sum(weighted, axis=-1, keepdims=True)
            grad_low = (weighted - probability * inner).astype(BF)
            turned = (dot(grad_low, keys[0:reach, :]) * scaling).astype(BF).astype(F32)
            grad_q[r, cols] = (
                turned * cos_rows - pltpu.roll(turned, HD // 2, 1) * sin_rows
            ).astype(BF)
            grad_k[0:reach, :] += t_dot(grad_low, one_query)
            grad_v[0:reach, :] += t_dot(probability.astype(BF), one_grad)
    grad_kv[0] = (grad_k[...] * scaling).astype(BF)
    grad_kv[1] = grad_v[...].astype(BF)
    d_early[:, 0:group_cols] = dot(attended_t[...], grad[...]).astype(BF).T
    d_early[:, group_cols:] = dot(normed_t[...], grad_q[...]).astype(BF)


def attention_out(
    own, grad, weights, queries, keys, values, cosine, sine, starts, normed_t, attended_t
):
    length, group_cols = queries.shape
    return pl.pallas_call(
        attention_out_body,
        out_shape=[
            jax.ShapeDtypeStruct((length, group_cols), BF),
            jax.ShapeDtypeStruct((2, length, HD), BF),
            jax.ShapeDtypeStruct((D, 2 * group_cols), BF),
        ],
        in_specs=[in_smem] + [anywhere] * 4 + [in_vmem] * 9,
        out_specs=[in_vmem] * 3,
        scratch_shapes=[
            pltpu.VMEM((length, D), BF),
            pltpu.VMEM((length, HD), F32),
            pltpu.VMEM((length, HD), F32),
            pltpu.SemaphoreType.DMA((4,)),
        ],
        compiler_params=kernel_params(),
        cost_estimate=KERNEL_COST,
        name="attention_out",
    )(
        own,
        *grad,
        weights,
        queries,
        keys,
        values,
        cosine,
        sine,
        starts,
        normed_t,
        attended_t,
    )


def projection_out_body(
    own_rows,
    kv_rows,
    own,
    grad_q,
    ours,
    theirs,
    weights,
    normed_t,
    cosine,
    sine,
    tokens,
    gain_mlp,
    d_late,
    near,
    far,
    other_near,
    other_far,
    joined,
    sums,
):
    length, group_cols = grad_q.shape
    wide = group_cols + HD
    s = own[0]
    x, c = s // 2, lax.rem(s, 2)
    key_grad = ours[0].astype(F32) + theirs[0].astype(F32)
    key_grad = key_grad * cosine[...] - pltpu.roll(key_grad, HD // 2, 1) * sine[...]
    value_grad = ours[1].astype(F32) + theirs[1].astype(F32)
    joined[:, 0:group_cols] = grad_q[...]
    joined[:, group_cols:] = jnp.where(c == 0, key_grad, value_grad).astype(BF)
    one = jnp.where(
        c == 0,
        weights[:, group_cols : group_cols + HD],
        weights[:, group_cols + HD : group_cols + 2 * HD],
    )
    sums[...] = jnp.zeros_like(sums)
    gain_sum = jnp.zeros((1, D), F32)
    for first in range(0, length, QUERY_ROWS):
        r = pl.ds(first, QUERY_ROWS)
        term = dot_t(joined[r, 0:group_cols], weights[:, 0:group_cols]) + dot_t(
            joined[r, group_cols:], one
        )
        value = tokens[r, :].astype(F32)
        gain_sum += jnp.sum(term * (value * rms_factor(value)), axis=0, keepdims=True)
        split_store(
            s, first // QUERY_ROWS, term.astype(BF), (near, far, other_near, other_far)
        )

    bias = jnp.sum(joined[...].astype(F32), axis=0, keepdims=True)
    lane = lax.broadcasted_iota(jnp.int32, (HD, D // 2), 1)
    feature = lax.broadcasted_iota(jnp.int32, (HD, D // 2), 0)
    core, inner = lax.div(lane, D // 4), lax.rem(lane, D // 4)
    owner, row = lax.div(inner, own_rows), lax.rem(inner, own_rows)
    spot = core * (HD // 2) + owner * kv_rows + row
    chosen = jnp.where((spot == feature) & (row < kv_rows), 1.0, 0.0).astype(BF)
    spread = dot(bias[:, group_cols:].astype(BF), chosen)
    sums[0:1, :] = gain_sum
    sums[1:2, :] = gain_mlp[...]
    sums[2:3, pl.ds(pl.multiple_of(s * group_cols, LANE), group_cols)] = bias[:, 0:group_cols]
    sums[3:4, pl.ds(pl.multiple_of(x * (D // 2), LANE), D // 2)] = spread
    d_late[:, 0:HD] = dot(normed_t[...], joined[:, group_cols:]).astype(BF)
    d_late[:, HD:] = sums[...].T.astype(BF)


def projection_out(
    own_rows,
    kv_rows,
    own,
    grad_q,
    ours,
    theirs,
    weights,
    normed_t,
    cosine,
    sine,
    tokens,
    gain_mlp,
):
    length, group_cols = grad_q.shape
    wide = group_cols + HD
    return pl.pallas_call(
        functools.partial(projection_out_body, own_rows, kv_rows),
        out_shape=[
            jax.ShapeDtypeStruct((D, HD + LANE), BF),
            *[jax.ShapeDtypeStruct((QUERY_ROWS, D), BF)] * 4,
        ],
        in_specs=[in_smem] + [in_vmem] * 9,
        out_specs=[in_vmem] * 5,
        scratch_shapes=[pltpu.VMEM((length, wide), BF), pltpu.VMEM((LANE, D), F32)],
        compiler_params=kernel_params(),
        cost_estimate=KERNEL_COST,
        name="projection_out",
    )(own, grad_q, ours, theirs, weights, normed_t, cosine, sine, tokens, gain_mlp)


def plane_copies(chip, parts, target, sems, first):
    x, y = lax.div(chip, 2), lax.rem(chip, 2)
    copies = []
    for i, part in enumerate(parts):
        owner = 2 * (1 - x if i % 2 else x) + (1 - y if i // 2 else y)
        r = pl.ds(pl.multiple_of(owner * QUERY_ROWS, QUERY_ROWS), QUERY_ROWS)
        copies.append(pltpu.make_async_copy(part, target.at[r], sems.at[first + i]))
    return copies


def weight_terms(c, normed_t, cotangent_t, grad_gate, grad_up, activated, keep, send):
    owner_rows = D // 4
    for part in range(2):
        for targets, core in ((send, 1 - c), (keep, c)):
            r = pl.ds(pl.multiple_of((2 * part + core) * owner_rows, LANE), owner_rows)
            targets[0][part] = dot(normed_t[r, :], grad_gate[...]).astype(BF)
            targets[1][part] = dot(normed_t[r, :], grad_up[...]).astype(BF)
            targets[2][part] = dot(cotangent_t[r, :], activated[...]).astype(BF)


def last_weights_body(
    own, normed_t, cotangent_t, grad_gate, grad_up, activated, *targets
):
    weight_terms(
        own[0], normed_t, cotangent_t, grad_gate, grad_up, activated, targets[:3], targets[3:]
    )


def last_weights(own, turned, parts):
    tokens, cols = parts[0].shape
    owner_rows = D // 4
    piece = jax.ShapeDtypeStruct((2, owner_rows, cols), BF)
    piece_spec = pl.BlockSpec((2, owner_rows, TILE), lambda i: (0, 0, i))
    whole = pl.BlockSpec((D, tokens), lambda i: (0, 0), pipeline_mode=pl.Buffered(1))
    part = pl.BlockSpec((tokens, TILE), lambda i: (0, i))
    return pl.pallas_call(
        last_weights_body,
        grid=(cols // TILE,),
        out_shape=[piece] * 6,
        in_specs=[in_smem, whole, whole, part, part, part],
        out_specs=[piece_spec] * 6,
        compiler_params=kernel_params(),
        cost_estimate=KERNEL_COST,
        name="last_weights",
    )(own, *turned, *parts)


def feed_forward_body(planes, rows, first, last, *refs):
    places, own = refs[0], refs[1]
    mine = refs[2 : 2 + planes]
    theirs = refs[2 + planes : 2 + 2 * planes]
    rest = list(refs[2 + 2 * planes :])
    normed_parts, cot_parts = [[rest.pop(0) for _ in range(4)] for _ in range(2)]
    totals_in = [] if first else [rest.pop(0) for _ in range(2)]
    if last:
        grad_gate, grad_up, activated = [rest.pop(0) for _ in range(3)]
    else:
        keep, send = [rest.pop(0) for _ in range(2)]
    turned_out = [rest.pop(0) for _ in range(2)] if first else []
    totals_out = [rest.pop(0) for _ in range(2)]
    weights, grad_total, branch_total = [rest.pop(0) for _ in range(3)]
    normed, cotangent, weight_sems, sems = [rest.pop(0) for _ in range(4)]
    if last:
        low = rest
    else:
        grad_gate, grad_up, activated, normed_t, cotangent_t = rest
    step, steps = pl.program_id(0), pl.num_programs(0)
    tokens = normed.shape[0]
    c = own[0]
    normed_loads = plane_copies(own[1], normed_parts, normed, sems, 8)
    cot_loads = plane_copies(own[1], cot_parts, cotangent, sems, 12)
    turned_ends = [
        pltpu.make_async_copy(source, target, sems.at[16 + i])
        for i, (source, target) in enumerate(
            zip((normed_t, cotangent_t) if first else (), turned_out)
        )
    ]
    fills = [
        pltpu.make_async_copy(source, target, sems.at[i])
        for i, (source, target) in enumerate(zip(totals_in, (grad_total, branch_total)))
    ]
    if last:
        ends = [
            pltpu.make_async_copy(low[i], target, sems.at[i]) for i, target in enumerate(totals_out)
        ]
    else:
        ends = [
            pltpu.make_async_copy(source, target, sems.at[i])
            for i, (source, target) in enumerate(zip((grad_total, branch_total), totals_out))
        ]

    def weight_copies(at, slot):
        cols = pl.ds(pl.multiple_of(at * TILE, TILE), TILE)
        copies = []
        for k in range(planes):
            base = places[k] * (2 * rows)
            for side, source in enumerate((mine[k], theirs[k])):
                start = base + (c if side == 0 else 1 - c) * rows
                copies.append(
                    pltpu.make_async_copy(
                        source.at[:, :, cols],
                        weights.at[slot, :, pl.ds(pl.multiple_of(start, 16), rows), :],
                        weight_sems.at[slot, 2 * k + side],
                    )
                )
        return copies

    slot = lax.rem(step, 2)

    @pl.when(step == 0)
    def _():
        for load in normed_loads:
            load.start()
        for copy in weight_copies(0, 0):
            copy.start()
        for load in cot_loads + fills:
            load.start()

    @pl.when(step + 1 < steps)
    def _():
        for copy in weight_copies(step + 1, 1 - slot):
            copy.start()

    if first:

        @pl.when(step == 0)
        def _():
            grad_total[...] = jnp.zeros_like(grad_total)
            branch_total[...] = jnp.zeros_like(branch_total)

    @pl.when(step == 0)
    def _():
        for load in normed_loads:
            load.wait()

    for copy in weight_copies(step, slot):
        copy.wait()

    @pl.when(step == 0)
    def _():
        for load in cot_loads:
            load.wait()

    block = min(256, tokens)
    for start in range(0, tokens, block):
        r = pl.ds(start, block)
        some = normed[r, :]
        gate = dot(some, weights[slot, 0])
        up = dot(some, weights[slot, 1])
        grad_act = dot(cotangent[r, :], weights[slot, 2])
        sigma = jax.nn.sigmoid(gate)
        silu = gate * sigma
        activated[r, :] = (silu * up).astype(BF)
        grad_gate[r, :] = (grad_act * up * (sigma + silu * (1.0 - sigma))).astype(BF)
        grad_up[r, :] = (grad_act * silu).astype(BF)

    @pl.when(step == 0)
    def _():
        for fill in fills:
            fill.wait()

    for start in range(0, tokens, block):
        r = pl.ds(start, block)
        grad_total[r, :] += dot_t(grad_gate[r, :], weights[slot, 0]) + dot_t(
            grad_up[r, :], weights[slot, 1]
        )
        branch_total[r, :] += dot_t(activated[r, :], weights[slot, 2])

    @pl.when(step == steps - 1)
    def _():
        if last:
            low[0][...] = grad_total[...].astype(BF)
            low[1][...] = branch_total[...].astype(BF)
        for end in ends:
            end.start()

    if not last:

        @pl.when(step == 0)
        def _():
            for source, target in ((normed, normed_t), (cotangent, cotangent_t)):
                for start in range(0, D, TILE):
                    cols = pl.ds(start, TILE)
                    target[cols, :] = source[:, cols].T
            for end in turned_ends:
                end.start()

        keep, send = [[piece.at[kind] for kind in range(3)] for piece in (keep, send)]
        weight_terms(c, normed_t, cotangent_t, grad_gate, grad_up, activated, keep, send)

    @pl.when(step == steps - 1)
    def _():
        for end in ends + turned_ends:
            end.wait()


def feed_forward(places, own, mine, theirs, normed, cotangent, totals, last):
    planes = len(mine)
    rows, cols = mine[0].shape[1:]
    tokens = 4 * QUERY_ROWS
    first = totals is None
    totals = () if first else totals
    if last:
        shapes = [jax.ShapeDtypeStruct((tokens, cols), BF)] * 3
        specs = [pl.BlockSpec((tokens, TILE), lambda i, *_: (0, i))] * 3
    else:
        owner_rows = D // 4
        shapes = [jax.ShapeDtypeStruct((3, 2, owner_rows, cols), BF)] * 2
        specs = [pl.BlockSpec((3, 2, owner_rows, TILE), lambda i, *_: (0, 0, 0, i))] * 2
    blocks = len(shapes)
    if first:
        shapes += [jax.ShapeDtypeStruct((D, tokens), BF)] * 2
    if last:
        shapes += [jax.ShapeDtypeStruct((tokens, D), BF)] * 2
    else:
        shapes += [jax.ShapeDtypeStruct((tokens, D), F32)] * 2
    scratch = [pltpu.VMEM((2, 3, D, TILE), BF)]
    scratch += [pltpu.VMEM((tokens, D), F32)] * 2
    scratch += [pltpu.VMEM((tokens, D), BF)] * 2
    scratch += [pltpu.SemaphoreType.DMA((2, 2 * planes)), pltpu.SemaphoreType.DMA((18,))]
    if last:
        scratch += [pltpu.VMEM((tokens, D), BF)] * 2
    else:
        scratch += [pltpu.VMEM((tokens, TILE), BF)] * 3 + [pltpu.VMEM((D, tokens), BF)] * 2
    inputs = [*mine, *theirs, *normed, *cotangent, *totals]
    return pl.pallas_call(
        functools.partial(feed_forward_body, planes, rows, first, last),
        grid=(cols // TILE,),
        out_shape=shapes,
        in_specs=[in_smem, in_smem] + [anywhere] * len(inputs),
        out_specs=specs + [anywhere] * (len(shapes) - blocks),
        scratch_shapes=scratch,
        compiler_params=kernel_params(),
        cost_estimate=KERNEL_COST,
        name="feed_forward",
    )(places, own, *inputs)


def assemble_body(*refs):
    parts, gate_up, down = refs[:-2], refs[-2], refs[-1]
    for chip, (start, (first, end)) in enumerate(zip(CHIP_STARTS, CHIP_VALID)):
        for part, (low, high) in zip(parts, CHUNKS):
            from_col = max(first * LANE, low)
            to_col = min(end * LANE, high)
            here = slice(from_col - low, to_col - low)
            there = slice(start * LANE + from_col, start * LANE + to_col)
            for kind in range(2):
                gate_up[:, kind, there] = part[chip, kind, :, here].astype(F32)
            down[:, there] = part[chip, 2, :, here].astype(F32)


def assemble(parts):
    rows = parts[0].shape[2]
    return pl.pallas_call(
        assemble_body,
        out_shape=[
            jax.ShapeDtypeStruct((rows, 2, FF), F32),
            jax.ShapeDtypeStruct((rows, FF), F32),
        ],
        in_specs=[in_vmem] * len(parts),
        out_specs=[in_vmem] * 2,
        compiler_params=kernel_params(),
        cost_estimate=KERNEL_COST,
        name="assemble",
    )(*parts)


def build(seq_count, fsdp_count):
    planes = fsdp_count // 2
    order = list(range(0, 1)) + list(range(1, planes, 2)) + list(range(2, planes, 2))[::-1]
    place = [order.index(plane) for plane in range(planes)]
    after = {order[i]: order[(i + 1) % planes] for i in range(planes)}
    ring_perm = [(z, after[z]) for z in range(planes)]
    other = [(0, 1), (1, 0)]
    rows_perm = [(0, 1), (3, 2)]

    def swap_x(value):
        return lax.ppermute(value, "x", other)

    def swap_c(value):
        return lax.ppermute(value, "c", other)

    def swap_y(value):
        return lax.ppermute(value, "y", other)

    def swap_xy(value):
        return lax.ppermute(value, ("x", "y"), [(i, 3 - i) for i in range(4)])

    def send_rows(value):
        return lax.ppermute(value, ("c", "y"), rows_perm)

    def ring(value):
        return lax.ppermute(value, "z", ring_perm)

    def ring_back(value):
        return lax.ppermute(value, "z", [(j, i) for i, j in ring_perm])

    def trade(blocks, axes):
        return lax.all_to_all(blocks, axes, split_axis=0, concat_axis=0, tiled=True)

    along = (planes - 1) // 2
    against = planes - 1 - along
    steps_behind = list(range(along + 1)) + [-i for i in range(1, against + 1)]

    def local(
        tokens,
        positions,
        w_query,
        w_key,
        w_value,
        w_output,
        gate_up,
        w_down,
        bias_query,
        bias_key,
        bias_value,
        gain_attn,
        gain_mlp,
        cotangent,
    ):
        x, c, z, y = [lax.axis_index(axis) for axis in ("x", "c", "z", "y")]
        s = 2 * x + c
        ring_order = jnp.array(order, jnp.int32)
        ring_place = jnp.array(place, jnp.int32)
        behind = ring_order[(ring_place[z] - jnp.array(steps_behind)) % planes].astype(jnp.int32)

        def ring_gather(piece, then=()):
            ahead, back = [piece], [piece]
            for _ in range(along):
                ahead.append(ring(ahead[-1]))
            for step in range(against):
                back.append(ring_back(tie(back[-1], then) if step else back[-1]))
            return ahead + back[1:]
        core = jnp.stack([c, 2 * x + y]).astype(jnp.int32)
        own_place = jnp.stack([s, y]).astype(jnp.int32)

        tok_rows = tokens.shape[1]
        length = tok_rows * seq_count
        per_group = HEADS // seq_count
        group_cols = per_group * HD
        w_rows = w_query.shape[0]
        own_rows = D // (seq_count * fsdp_count)

        def gather_sequence(own, then=()):
            far = swap_x(own)
            theirs = swap_c(own)
            return [own, far, theirs, swap_c(tie(far, theirs, then))]

        def gather_plane(own):
            return [own, swap_x(own), swap_y(own), swap_xy(own)]

        def scatter_plane(terms, then=()):
            came = trade(terms.reshape(4, tok_rows, D), ("x", "y"))
            return jnp.sum(tie(came, then).astype(F32), axis=0)

        wide = group_cols + 2 * HD
        small_rows = jnp.stack(
            [
                jnp.pad(vector, (0, wide + group_cols - vector.shape[0]))
                for vector in (gain_attn, gain_mlp, bias_query, bias_key, bias_value)
            ]
        )
        small_rows = jnp.pad(small_rows, ((0, 11), (0, 0)))
        attn_own = jnp.concatenate(
            [
                lax.dynamic_slice_in_dim(w_query, s * group_cols, group_cols, 1),
                lax.dynamic_slice_in_dim(w_key, x * HD, HD, 1),
                lax.dynamic_slice_in_dim(w_value, x * HD, HD, 1),
                lax.dynamic_slice_in_dim(w_output, s * group_cols, group_cols, 1),
            ],
            axis=1,
        )
        attn_payload = jnp.concatenate([attn_own, small_rows], axis=0)
        chunk_places = []
        for low, high in CHUNKS:
            table = []
            for start, (first, end) in zip(CHIP_STARTS, CHIP_VALID):
                edge = 1 if low == 0 and first > 0 else 0
                edge = 2 if high > end * LANE else edge
                table.append((start * LANE + low, edge))
            table = jnp.array(table, jnp.int32)
            chunk_places.append((table[2 * x + y], table[2 * x + 1 - y]))

        def cut(chunk, whose, then):
            low, high = CHUNKS[chunk]
            return cut_columns(tie(chunk_places[chunk][whose], then), gate_up, w_down, high - low)

        sent = cut(0, 1, ())
        attn_payload = tie(attn_payload, sent)
        token_far = swap_x(tokens[0])
        token_pieces = [tokens[0], token_far, swap_c(tokens[0])]
        attn_pieces = ring_gather(attn_payload, token_pieces[2])
        first_back = along + 1
        attn_theirs = [swap_y(tie(attn_pieces[0], attn_pieces[1]))]
        attn_theirs += [swap_y(piece) for piece in attn_pieces[1:-1]]

        came, kept = send_rows(sent), cut(0, 0, attn_payload)
        kept, came = tie((kept, came), attn_pieces[1:], attn_theirs[first_back], token_pieces[1:3])
        payloads = [jnp.where(c == y, kept, came)]
        token_pieces.append(swap_c(tie(token_far, payloads[0])))
        after = (payloads[0], token_pieces[3])
        cuts = [(cut(1, 1, after), cut(1, 0, after))]
        attn_theirs.append(swap_y(tie(attn_pieces[-1], cuts)))
        own_swapped = swap_c(tie(payloads[0], attn_theirs))
        for sent, kept in cuts:
            came = send_rows(tie(sent, attn_theirs))
            payloads.append(jnp.where(c == y, kept, came))
        chunk_pieces = [ring_gather(payloads[0])]
        cot_x = swap_x(tie(cotangent[0], cuts))
        cot_y = swap_y(tie(cotangent[0], attn_theirs))

        seq_positions = positions[0]
        cosine, sine = rope_tables(seq_positions)
        first_keys = (jnp.arange(length, dtype=jnp.int32) - seq_positions)[:, None]
        (
            normed_attn_t,
            queries,
            keys,
            values,
            attended_t,
            *out_terms,
            attn_weights,
            gains,
            tokens_all,
        ) = attention_in(
            behind,
            own_place,
            attn_pieces,
            attn_theirs,
            tie(token_pieces, cot_x),
            cosine,
            sine,
            first_keys,
            group_cols,
        )
        inputs = tokens[0].astype(F32)
        out_terms, queries, keys, values, attended_t, gains = tie(
            (out_terms, queries, keys, values, attended_t, gains),
            chunk_pieces[0][1 : along + 2],
            came,
            cot_y,
            own_swapped,
        )

        def scatter_sequence(near, far, other_near, other_far, then=()):
            leaves = (far.astype(F32) + swap_c(other_far).astype(F32)).astype(BF)
            leaves = tie(leaves, *then)
            back = swap_x(leaves)
            stays = near.astype(F32) + swap_c(other_near).astype(F32)
            return stays + back.astype(F32), leaves, back

        gain_a, gain_m = gains[0], gains[1]
        branch_attn, out_leaves, _ = scatter_sequence(*out_terms)
        cot_pieces = [cotangent[0], cot_x, cot_y, swap_y(tie(cot_x, out_terms))]
        hidden = inputs + tie(branch_attn, cot_pieces[3])
        factor_mlp = rms_factor(hidden)
        normed_own = (hidden * factor_mlp * gain_m).astype(BF)
        normed = gather_plane(normed_own)
        chunk_theirs = [[own_swapped] + [swap_c(piece) for piece in chunk_pieces[0][1:-1]], []]
        chunk_theirs[0].append(swap_c(tie(chunk_pieces[0][-1], normed[1:])))
        chunk_pieces.append(ring_gather(tie(payloads[1], normed_own)))

        def plane_ahead(steps):
            return ring_order[(ring_place[z] + steps) % planes]

        class RingScatter:
            def __init__(self, block):
                self.block = block
                self.own = block(z)
                self.first = [
                    block(plane_ahead(sign * steps)).astype(BF)
                    for steps, sign in ((along, 1), (against, -1))
                    if steps
                ]

            def go(self, then=()):
                self.arrived, self.second, self.last = [], [], []
                firsts = list(self.first)
                for steps, sign, move in ((along, 1, ring), (against, -1, ring_back)):
                    if steps:
                        running = firsts.pop(0)
                        for left in range(steps - 1, 0, -1):
                            came = tie(move(running), then)
                            self.arrived.append(came)
                            running = self.block(plane_ahead(sign * left)) + came.astype(F32)
                            running = running.astype(BF)
                            self.second.append(running)
                        came = move(running)
                        self.arrived.append(came)
                        self.last.append(came)
                return self

            def total(self, then=()):
                total = self.own
                for came in tie(self.last, then):
                    total = total + came.astype(F32)
                return total.astype(BF)

        def chunk_scatter(keep, send, then):
            def by_plane(piece):
                return piece.reshape(piece.shape[:-2] + (planes, 2 * own_rows, piece.shape[-1]))

            if isinstance(send, (list, tuple)):
                away = [by_plane(swap_c(piece)) for piece in send]
                keep = [by_plane(piece) for piece in keep]

                def block(plane):
                    return jnp.stack(
                        [
                            pick(ours, plane, 1).astype(F32) + pick(theirs, plane, 1).astype(F32)
                            for ours, theirs in zip(keep, away)
                        ]
                    )

            else:
                away = by_plane(tie(swap_c(send), then))
                keep = by_plane(keep)

                def block(plane):
                    return pick(keep, plane, 2).astype(F32) + pick(away, plane, 2).astype(F32)

            return RingScatter(block)

        before = [(), None]
        beside = [chunk_pieces[1][1 : along + 2]]
        totals = None
        scatters = []
        for chunk in range(len(CHUNKS)):
            last = chunk == len(CHUNKS) - 1
            results = feed_forward(
                behind,
                core,
                chunk_pieces[chunk],
                chunk_theirs[chunk],
                tie(normed, before[chunk]),
                cot_pieces,
                totals,
                last,
            )
            if last:
                results = tie(results, scatters[0].arrived[along])
                totals = results[3:]
                pieces = last_weights(core, turned, results[:3])
                keep, send = pieces[:3], pieces[3:]
            else:
                results = tie(results, beside[chunk])
                keep, send = results[:2]
                turned, totals = results[2:4], results[4:]
                own = tie(chunk_pieces[1][0], send)
                chunk_theirs[1] = [swap_c(piece) for piece in [own] + chunk_pieces[1][1:]]
            then = () if last else chunk_theirs[1][:-1]
            scatters.append(chunk_scatter(keep, send, then))
            if not last:
                scatters[0].go()
                before[1] = scatters[0].first
        last_sent = (keep, send)

        grad_out = cotangent[0].astype(F32)
        grad_hidden_norm, grad_gain_mlp = rms_backward(
            hidden, factor_mlp, gain_m, scatter_plane(totals[0], (last_sent, scatters[0].last[0], scatters[0].second))
        )
        grad_hidden = grad_out + grad_hidden_norm
        grad_pieces = gather_sequence(
            grad_hidden.astype(BF)
        )
        grad_q, grad_kv, d_early = attention_out(
            own_place,
            tie(grad_pieces, scatters[1].first),
            attn_weights,
            queries,
            keys,
            values,
            cosine,
            sine,
            first_keys,
            normed_attn_t,
            attended_t,
        )
        scatters[1].go()
        grad_q, grad_kv, d_early = tie(
            (grad_q, grad_kv, d_early), scatters[1].arrived[along], scatters[0].last[-1]
        )

        branch = trade(tie(totals[1], grad_pieces[1]).reshape(4, tok_rows, D), ("x", "y"))

        def owner_rows(partial):
            rows = partial.reshape(2, 2, planes, 2, own_rows, partial.shape[1])
            return pick(rows, 1 - y, 3), pick(rows, y, 3)

        grad_kv_theirs = swap_c(grad_kv)
        early_rows = owner_rows(d_early)
        kv_rows = KV * HD // (seq_count * fsdp_count)
        d_late, *in_terms = projection_out(
            own_rows,
            kv_rows,
            own_place,
            tie(grad_q, early_rows[0], scatters[1].second, branch),
            grad_kv,
            grad_kv_theirs,
            attn_weights,
            normed_attn_t,
            cosine,
            sine,
            tokens_all,
            grad_gain_mlp[None],
        )
        def owner_scatter(away, stays, then=()):
            def block(plane):
                return pick(stays, plane, 2).astype(F32) + pick(away, plane, 2).astype(F32)

            return RingScatter(block).go(then)

        def chunk_sum(scatter, then):
            total = scatter.total(then).reshape(3, 2, 2, own_rows, -1)
            return total.transpose(1, 2, 0, 3, 4).reshape(4, 3, own_rows, -1)

        early_away = tie(swap_y(early_rows[0]), d_late)
        late_leaves, late_stays = owner_rows(d_late)
        grad_normed_attn, in_leaves, in_back = scatter_sequence(*in_terms, (early_away, late_leaves))
        grad_input_norm, _ = rms_backward(
            inputs,
            rms_factor(inputs),
            gain_a,
            grad_normed_attn,
        )
        grad_input = grad_hidden + grad_input_norm
        result = hidden + jnp.sum(tie(branch, in_leaves).astype(F32), axis=0)
        result = result.astype(BF)
        first_sum = chunk_sum(scatters[0], in_leaves)
        gathered = [trade(first_sum, ("x", "y"))]

        late_away = tie(swap_y(late_leaves), in_back)
        early = owner_scatter(early_away, early_rows[1], (in_back, gathered))
        late = owner_scatter(late_away, late_stays)
        second_sum = chunk_sum(scatters[1], (early.first, late.first))
        gathered.append(trade(second_sum, ("x", "y")))
        d_gate_up, d_w_down = assemble(gathered)
        owned = [early.total(second_sum), late.total(second_sum)]
        owned = jnp.concatenate(owned, axis=-1).reshape(4, own_rows, -1)
        owned = trade(owned, ("x", "c")).astype(F32)
        early, late = owned[..., : 2 * group_cols], owned[..., 2 * group_cols :]
        d_w_output = jnp.concatenate([early[i, :, :group_cols] for i in range(4)], axis=1)
        d_w_query = jnp.concatenate([early[i, :, group_cols:] for i in range(4)], axis=1)
        d_w_key = jnp.concatenate([late[0, :, :HD], late[2, :, :HD]], axis=1)
        d_w_value = jnp.concatenate([late[1, :, :HD], late[3, :, :HD]], axis=1)
        sums = jnp.sum(late[:, :, HD:], axis=0)
        d_gain_attn, d_gain_mlp, d_bias_query = sums[:, 0], sums[:, 1], sums[:, 2]
        kv_sums = late[:, :kv_rows, HD + 3]
        d_bias_key = kv_sums[0] + kv_sums[2]
        d_bias_value = kv_sums[1] + kv_sums[3]
        return (
            result[None],
            grad_input[None],
            d_w_query,
            d_w_key,
            d_w_value,
            d_w_output,
            d_gate_up,
            d_w_down,
            d_bias_query,
            d_bias_key,
            d_bias_value,
            d_gain_attn,
            d_gain_mlp,
        )

    return local


def solution(mesh):
    seq, fsdp = mesh.shape["seq"], mesh.shape["fsdp"]
    grid = jax.sharding.Mesh(mesh.devices.reshape(seq // 2, 2, fsdp // 2, 2), ("x", "c", "z", "y"))
    by_rows, by_owner = ("z", "y"), ("x", "c", "z", "y")
    tokens = P(by_rows, ("x", "c"), None)
    rows, vector = P(by_rows, None), P(by_rows)
    owner, owner_vector = P(by_owner, None), P(by_owner)
    return jax.shard_map(
        build(seq, fsdp),
        mesh=grid,
        in_specs=(
            tokens,
            rows,
            rows,
            rows,
            rows,
            rows,
            P(by_rows, None, None),
            rows,
            vector,
            vector,
            vector,
            vector,
            vector,
            tokens,
        ),
        out_specs=(
            tokens,
            tokens,
            owner,
            owner,
            owner,
            owner,
            P(by_owner, None, None),
            owner,
            owner_vector,
            owner_vector,
            owner_vector,
            owner_vector,
            owner_vector,
        ),
        check_vma=False,
    )
```

time: 629 us -> 569 us (0.905)
  waiting for transfers between devices: 259 us -> 196 us
  starting transfers between devices: 102 us -> 79 us
  Pallas kernels: 161 us -> 183 us
  other arithmetic: 58.6 us -> 73 us
    ppermute x70 -> x60, waiting for transfers between devices: 259 us -> 181 us  [the longest x14 71.5 us: ring_back(): return lax.ppermute(value, 'z', [(j, i) for i, j in ring_perm])]
    ppermute x70 -> x60, starting transfers between devices: 102 us -> 58.4 us  [the longest x14 23.4 us: ring_back(): return lax.ppermute(value, 'z', [(j, i) for i, j in ring_perm])]
    all_to_all x0 -> x5, starting transfers between devices: none -> 20.6 us  [trade(): return lax.all_to_all(blocks, axes, split_axis=0, concat_axis=0, tiled=True)]
    pallas_call x0 -> x2, Pallas kernels: none -> 20.1 us  [the longest x1 15.3 us: last_weights(): pl.pallas_call(last_weights_body, grid=(cols // TILE,), out_shape=[piece]...]
    all_to_all x0 -> x5, waiting for transfers between devices: none -> 15.1 us  [trade(): return lax.all_to_all(blocks, axes, split_axis=0, concat_axis=0, tiled=True)]
    pallas_call x2, Pallas kernels: 90.2 us -> 79.9 us  [feed_forward(): pl.pallas_call(functools.partial(feed_forward_body, planes, rows, first,...]
    pallas_call x1, Pallas kernels: 20.6 us -> 30.9 us  [attention_in(): pl.pallas_call(functools.partial(attention_in_body, planes, rows), out_sh...]
    unnamed x95 -> x96, local copies, waits for them, and re-layouts: 11.6 us -> 3.04 us
  transfers between devices with their start and end apart: 70 -> 65, of which waited for: 32 -> 30; matrix products, arithmetic and copies ran while one was open for 12% -> 15% of each run, Pallas kernels for 25% -> 31%
where the time goes in v3:
time: 569 us; the launch traced here: 560 us
  waiting for transfers between devices  196 us (34%)
  Pallas kernels  183 us (32%)
  starting transfers between devices  79 us (14%)
  other arithmetic  73 us (13%)
  local copies, waits for them, and re-layouts  18.9 us (3%)
  between operations  9.83 us (2%)
    pallas_call x2, Pallas kernels, feed_forward(): pl.pallas_call(functools.partial(feed_forward_body, planes, rows, first,...  79.9 us
    ppermute x14, waiting for transfers between devices, ring_back(): return lax.ppermute(value, 'z', [(j, i) for i, j in ring_perm])  71.5 us
    ppermute x6, waiting for transfers between devices, swap_x(): return lax.ppermute(value, 'x', other)  39.6 us
    ppermute x9, waiting for transfers between devices, swap_y(): return lax.ppermute(value, 'y', other)  38 us
    pallas_call x1, Pallas kernels, attention_in(): pl.pallas_call(functools.partial(attention_in_body, planes, rows), out_sh...  30.9 us
    ppermute x14, starting transfers between devices, ring_back(): return lax.ppermute(value, 'z', [(j, i) for i, j in ring_perm])  23.4 us
    pallas_call x1, Pallas kernels, attention_out(): pl.pallas_call(attention_out_body, out_shape=[jax.ShapeDtypeStruct((lengt...  21.9 us
    all_to_all x5, starting transfers between devices, trade(): return lax.all_to_all(blocks, axes, split_axis=0, concat_axis=0, tiled=True)  20.6 us
  transfers between devices with their start and end apart: 65, of which 30 were waited for; matrix products, arithmetic and copies ran while one was open for 15% of the time, Pallas kernels for 31%

profile of v3, /device:TPU:0, one launch (start us, length us, event | category | flops | bytes accessed | tf_op | source)
XLA Modules:
  0.0 559.5 jit_solution(16191061536293381040)
XLA Ops:
  2.0 5.3 cut_columns.4
  7.3 5.0 collective-permute-start.7
  18.6 9.0 %collective-permute-done.1.refs_4_ = bf16[208,1024]{1,0:T(8,128)(2,1)S(1)} collective-permute-done((bf16[208,1024]{1,0:T(8,128)(2,1)}, bf16[208,1024]{1,0:T(8,128)(2,1)S(1)}, u32[]{:S(2)}, u32[]{:S(2)}) %collective-permute-start.1) | collective-permute-done | bytes 426016 | tf_op jit(solution)/shard_map/ppermute | solution.py:772
  27.7 3.3 collective-permute-start.3
  30.9 5.1 cut_columns.5
  38.7 8.5 %collective-permute-done.3.refs_5_ = bf16[208,1024]{1,0:T(8,128)(2,1)} collective-permute-done((bf16[208,1024]{1,0:T(8,128)(2,1)S(1)}, bf16[208,1024]{1,0:T(8,128)(2,1)}, u32[]{:S(2)}, u32[]{:S(2)}) %collective-permute-start.3) | collective-permute-done | bytes 426016 | tf_op jit(solution)/shard_map/ppermute | solution.py:772
  51.5 4.6 cut_columns.7
  56.2 4.7 cut_columns.6
  65.5 6.1 %collective-permute-done.5.refs_7_ = bf16[208,1024]{1,0:T(8,128)(2,1)} collective-permute-done((bf16[208,1024]{1,0:T(8,128)(2,1)}, bf16[208,1024]{1,0:T(8,128)(2,1)}, u32[]{:S(2)}, u32[]{:S(2)}) %collective-permute-start.5) | collective-permute-done | bytes 426016 | tf_op jit(solution)/shard_map/ppermute | solution.py:760
  71.6 8.4 %collective-permute-done.10.refs_9_ = bf16[208,1024]{1,0:T(8,128)(2,1)S(1)} collective-permute-done((bf16[208,1024]{1,0:T(8,128)(2,1)}, bf16[208,1024]{1,0:T(8,128)(2,1)S(1)}, u32[]{:S(2)}, u32[]{:S(2)}) %collective-permute-start.10) | collective-permute-done | bytes 426016 | tf_op jit(solution)/shard_map/ppermute | solution.py:760
  81.3 3.4 collective-permute-start.14
  92.5 30.9 %attention_in.1 = (bf16[1536,1024]{1,0:T(8,128)(2,1)}, bf16[1024,384]{1,0:T(8,128)(2,1)}, bf16[1024,128]{1,0:T(8,128)(2,1)}, bf16[1024,128]{1,0:T(8,128)(2,1)}, ...) custom-call(s32[4]{0:T(128)} %gather_fusion, ...), custom_call_target="tpu_custom_call" | custom-call | flops 1000000 | bytes 1000000 | tf_op jit(solution)/shard_map/attention_in/pallas_call | solution.py:262
  123.4 5.7 %collective-permute-done.13.refs_4_ = bf16[3,192,1280]{2,1,0:T(8,128)(2,1)} collective-permute-done((bf16[3,192,1280]{2,1,0:T(8,128)(2,1)S(1)}, bf16[3,192,1280]{2,1,0:T(8,128)(2,1)}, u32[]{:S(2)}, u32[]{:S(2)}) %collective-permute-start.13) | collective-permute-done | bytes 1474592 | tf_op jit(solution)/shard_map/ppermute | solution.py:772
  137.4 15.2 %collective-permute-done.19 = bf16[256,1536]{1,0:T(8,128)(2,1)S(1)} collective-permute-done((bf16[256,1536]{1,0:T(8,128)(2,1)S(1)}, bf16[256,1536]{1,0:T(8,128)(2,1)S(1)}, u32[]{:S(2)}, u32[]{:S(2)}) %collective-permute-start.19) | collective-permute-done | bytes 786464 | tf_op jit(solution)/shard_map/ppermute | solution.py:754
  157.7 11.5 %collective-permute-done.24.refs_5_ = bf16[3,192,1280]{2,1,0:T(8,128)(2,1)S(1)} collective-permute-done((bf16[3,192,1280]{2,1,0:T(8,128)(2,1)}, bf16[3,192,1280]{2,1,0:T(8,128)(2,1)S(1)}, u32[]{:S(2)}, u32[]{:S(2)}) %collective-permute-start.24) | collective-permute-done | bytes 1474592 | tf_op jit(solution)/shard_map/ppermute | solution.py:772
  169.2 5.5 collective-permute-done.27.refs_11_
  174.7 15.1 %collective-permute-done.28.refs_12_ = bf16[256,1536]{1,0:T(8,128)(2,1)S(1)} collective-permute-done((bf16[256,1536]{1,0:T(8,128)(2,1)S(1)}, bf16[256,1536]{1,0:T(8,128)(2,1)S(1)}, u32[]{:S(2)}, u32[]{:S(2)}) %collective-permute-start.28) | collective-permute-done | bytes 786464 | tf_op jit(solution)/shard_map/ppermute | solution.py:760
  195.6 48.6 %feed_forward.2 = (bf16[3,2,384,1280]{3,2,1,0:T(8,128)(2,1)}, bf16[3,2,384,1280]{3,2,1,0:T(8,128)(2,1)}, bf16[1536,1024]{1,0:T(8,128)(2,1)}, bf16[1536,1024]{1,0...) custom-call(s32[4]{0:T(128)} %gather_fusion, s32[2]{0:T(128)} %pad_add_fusion.1.refs_1_.own, ...), custom_call_target="tpu_custom_call" | custom-call | flops 1000000 | bytes 1000000 | tf_op jit(solution)/shard_map/feed_forward/pallas_call | solution.py:702
  254.9 5.3 collective-permute-done.32.refs_7_
  261.8 4.6 fusion.15
  267.5 9.5 %collective-permute-done.23.refs_5_ = bf16[3,192,1024]{2,1,0:T(8,128)(2,1)} collective-permute-done((bf16[3,192,1024]{2,1,0:T(8,128)(2,1)}, bf16[3,192,1024]{2,1,0:T(8,128)(2,1)}, u32[]{:S(2)}, u32[]{:S(2)}) %collective-permute-start.23) | collective-permute-done | bytes 1179680 | tf_op jit(solution)/shard_map/ppermute | solution.py:772
  277.0 3.2 collective-permute-done.34.refs_9_
  280.1 31.3 %feed_forward.3 = (bf16[1024,1024]{1,0:T(8,128)(2,1)}, bf16[1024,1024]{1,0:T(8,128)(2,1)}, bf16[1024,1024]{1,0:T(8,128)(2,1)}, bf16[1024,1536]{1,0:T(8,128)(2,1)}, bf16[1024,1536]{1,0:T(8,128)(2,1)}) custom-call(s32[4]{0:T(128)} %gather_fusion, s32[2]{0:T(128)} %pad_add_fusion.1.refs_1_.own, bf16[3,192,1024]{2,1,0:T(8,128)(2,1)} %copy-done.8, ...), custom_call_target="tpu_custom_call" | custom-call | flops 1000000 | bytes 1000000 | tf_op jit(solution)/shard_map/feed_forward/pallas_call | solution.py:702
  311.4 4.7 all-to-all-start
  319.0 15.3 %last_weights.1 = (bf16[2,384,1024]{2,1,0:T(8,128)(2,1)}, bf16[2,384,1024]{2,1,0:T(8,128)(2,1)}, bf16[2,384,1024]{2,1,0:T(8,128)(2,1)}, bf16[2,384,1024]{2,1,0:T...) custom-call(s32[2]{0:T(128)} %pad_add_fusion.1.refs_1_.own, ...), custom_call_target="tpu_custom_call" | custom-call | flops 1000000 | bytes 1000000 | tf_op jit(solution)/shard_map/last_weights/pallas_call | solution.py:512
  335.0 3.9 fusion.2
  338.9 12.6 %collective-permute-done.37 = bf16[3,2,96,1280]{3,2,1,0:T(8,128)(2,1)} collective-permute-done((bf16[3,2,96,1280]{3,2,1,0:T(8,128)(2,1)S(1)}, bf16[3,2,96,1280]{3,2,1,0:T(8,128)(2,1)}, u32[]{:S(2)}, u32[]{:S(2)}) %collective-permute-start.37) | collective-permute-done | bytes 1474592 | tf_op jit(solution)/shard_map/ppermute | solution.py:769
  361.0 2.9 add_bitcast_fusion
  363.9 14.0 %collective-permute-done.38.far = bf16[256,1536]{1,0:T(8,128)(2,1)} collective-permute-done((bf16[256,1536]{1,0:T(8,128)(2,1)}, bf16[256,1536]{1,0:T(8,128)(2,1)}, u32[]{:S(2)}, u32[]{:S(2)}) %collective-permute-start.38) | collective-permute-done | bytes 786464 | tf_op jit(solution)/shard_map/ppermute | solution.py:754
  377.9 4.6 all-to-all-start.1
  382.6 3.5 add_bitcast_fusion.1
  386.1 3.0 add_bitcast_fusion.2
  394.7 21.9 %attention_out.1 = (bf16[1024,384]{1,0:T(8,128)(2,1)}, bf16[2,1024,128]{2,1,0:T(8,128)(2,1)}, bf16[1536,768]{1,0:T(8,128)(2,1)}) custom-call(s32[2]{0:T(128)} %pad_add_fusion.refs_1_.own, bf16[256,1536]{1,0:T(8,128)(2,1)} %fusion.47.near, bf16[256,1536]{1,0:T(8,128)(2,1)} %collective-permute-done.38.far, ...), custom_call_target="tpu_custom_call" | custom-call | flops 1000000 | bytes 1000000 | tf_op jit(solution)/shard_map/attention_out/pallas_call | solution.py:349
  422.6 2.8 fusion.3
  425.4 10.3 %projection_out.1 = (bf16[1536,256]{1,0:T(8,128)(2,1)}, bf16[256,1536]{1,0:T(8,128)(2,1)}, bf16[256,1536]{1,0:T(8,128)(2,1)}, bf16[256,1536]{1,0:T(8,128)(2,1)}, bf16[256,1536]{1,0:T(8,128)(2,1)}) custom-call(s32[2]{0:T(128)} %pad_add_fusion.refs_1_.own, bf16[1024,384]{1,0:T(8,128)(2,1)} %get-tuple-element.212.grad_q, ...), custom_call_target="tpu_custom_call" | custom-call | flops 1000000 | bytes 1000000 | tf_op jit(solution)/shard_map/projection_out/pallas_call | solution.py:462
  439.7 8.2 %collective-permute-done.48 = bf16[2,2,4,48,768]{4,3,1,0,2:T(8,128)(2,1)} collective-permute-done((bf16[2,2,4,48,768]{4,3,1,0,2:T(8,128)(2,1)}, bf16[2,2,4,48,768]{4,3,1,0,2:T(8,128)(2,1)}, u32[]{:S(2)}, u32[]{:S(2)}) %collective-permute-start.48) | collective-permute-done | bytes 1179680 | tf_op jit(solution)/shard_map/ppermute | solution.py:760
  456.9 3.4 fusion.1
  461.6 4.3 all-to-all-start.2
  466.0 3.8 convert_reduce_fusion
  471.1 5.0 collective-permute-done.50
  481.2 18.3 %collective-permute-done.58 = bf16[2,2,48,256]{3,2,1,0:T(8,128)(2,1)S(1)} collective-permute-done((bf16[2,2,48,256]{3,2,1,0:T(8,128)(2,1)S(1)}, bf16[2,2,48,256]{3,2,1,0:T(8,128)(2,1)S(1)}, u32[]{:S(2)}, u32[]{:S(2)}) %collective-permute-start.58) | collective-permute-done | bytes 98336 | tf_op jit(solution)/shard_map/ppermute | solution.py:772
  513.6 3.3 collective-permute-done.51
  516.9 4.8 collective-permute-done.53
  523.8 3.5 all-to-all-start.3
  527.2 5.0 fusion.12
  534.6 3.5 all-to-all-start.4
  542.5 10.8 %all-to-all-done.4.refs_1_ = bf16[4,3,48,1024]{3,2,1,0:T(8,128)(2,1)S(1)} async-done(((bf16[4,3,48,1024]{3,2,1,0:T(8,128)(2,1)}), bf16[4,3,48,1024]{3,2,1,0:T(8,128)(2,1)S(1)}, u32[]{:S(2)}, u32[]{:S(2)}) %all-to-all-start.4) | async-done | bytes 1179680 | tf_op jit(solution)/shard_map/all_to_all | solution.py:775
  554.3 4.8 assemble.1
  (268 shorter events, 121.9 us)
Async XLA Ops:
  7.3 39.9 %collective-permute-start.7 = (bf16[3,192,1280]{2,1,0:T(8,128)(2,1)}, bf16[3,192,1280]{2,1,0:T(8,128)(2,1)S(1)}, u32[]{:S(2)}, u32[]{:S(2)}) collective-permute-start(bf16[3,192,1280]{2,1,0:T(8,128)(2,1)} %cut_columns.4), channel_id=1, source_target_pairs={{0,1},{9,8},{2,3},{11,10},{4,5},{13,12},{6,7},{15,14},{16,17},{25,... | collective-permute-start | bytes 4423688 | tf_op jit(solution)/shard_map/ppermute | solution.py:766
  12.3 15.4 %collective-permute-start.2 = (bf16[256,1536]{1,0:T(8,128)(2,1)S(1)}, bf16[256,1536]{1,0:T(8,128)(2,1)S(1)}, u32[]{:S(2)}, u32[]{:S(2)}) collective-permute-start(bf16[256,1536]{1,0:T(8,128)(2,1)S(1)} %bitcast.250), channel_id=1, source_target_pairs={{0,8},{8,0},{1,9},{9,1},{2,10},{10,2},{3,11},{11,3},{4,12},{12,4},... | collective-permute-start | bytes 2359304 | tf_op jit(solution)/shard_map/ppermute | solution.py:757
  17.1 21.4 %collective-permute-start.8 = (bf16[256,1536]{1,0:T(8,128)(2,1)S(1)}, bf16[256,1536]{1,0:T(8,128)(2,1)}, u32[]{:S(2)}, u32[]{:S(2)}) collective-permute-start(bf16[256,1536]{1,0:T(8,128)(2,1)S(1)} %bitcast.251), channel_id=1, source_target_pairs={{0,16},{16,0},{1,17},{17,1},{2,18},{18,2},{3,19},{19,3},{4,20},{20... | collective-permute-start | bytes 2359304 | tf_op jit(solution)/shard_map/ppermute | solution.py:754
  18.6 19.9 %collective-permute-start = (bf16[208,1024]{1,0:T(8,128)(2,1)}, bf16[208,1024]{1,0:T(8,128)(2,1)}, u32[]{:S(2)}, u32[]{:S(2)}) collective-permute-start(bf16[208,1024]{1,0:T(8,128)(2,1)} %fusion.25.refs_2_), channel_id=1, source_target_pairs={{0,2},{2,6},{4,0},{6,4},{1,3},{3,7},{5,1},{7,5},{8,10},{10,14},{12... | collective-permute-start | bytes 1277960 | tf_op jit(solution)/shard_map/ppermute | solution.py:769
  27.7 19.5 %collective-permute-start.3 = (bf16[208,1024]{1,0:T(8,128)(2,1)S(1)}, bf16[208,1024]{1,0:T(8,128)(2,1)}, u32[]{:S(2)}, u32[]{:S(2)}) collective-permute-start(bf16[208,1024]{1,0:T(8,128)(2,1)S(1)} %collective-permute-done.1.refs_4_), channel_id=1, source_target_pairs={{2,0},{6,2},{0,4},{4,6},{3,1},{7,3},{1,5},{5,7},{10,8},{14,10},{8,... | collective-permute-start | bytes 1277960 | tf_op jit(solution)/shard_map/ppermute | solution.py:772
  49.4 22.1 %collective-permute-start.5 = (bf16[208,1024]{1,0:T(8,128)(2,1)}, bf16[208,1024]{1,0:T(8,128)(2,1)}, u32[]{:S(2)}, u32[]{:S(2)}) collective-permute-start(bf16[208,1024]{1,0:T(8,128)(2,1)} %collective-permute-done.refs_3_), channel_id=1, source_target_pairs={{0,1},{1,0},{2,3},{3,2},{4,5},{5,4},{6,7},{7,6},{8,9},{9,8},{10,11... | collective-permute-start | bytes 1277960 | tf_op jit(solution)/shard_map/ppermute | solution.py:760
  60.9 19.1 %collective-permute-start.10 = (bf16[208,1024]{1,0:T(8,128)(2,1)}, bf16[208,1024]{1,0:T(8,128)(2,1)S(1)}, u32[]{:S(2)}, u32[]{:S(2)}) collective-permute-start(bf16[208,1024]{1,0:T(8,128)(2,1)} %collective-permute-done.3.refs_5_), channel_id=1, source_target_pairs={{0,1},{1,0},{2,3},{3,2},{4,5},{5,4},{6,7},{7,6},{8,9},{9,8},{10,11... | collective-permute-start | bytes 1277960 | tf_op jit(solution)/shard_map/ppermute | solution.py:760
  60.9 24.5 %collective-permute-start.11 = (bf16[256,1536]{1,0:T(8,128)(2,1)S(1)}, bf16[256,1536]{1,0:T(8,128)(2,1)S(1)}, u32[]{:S(2)}, u32[]{:S(2)}) collective-permute-start(bf16[256,1536]{1,0:T(8,128)(2,1)S(1)} %bitcast.247), channel_id=1, source_target_pairs={{0,16},{16,0},{1,17},{17,1},{2,18},{18,2},{3,19},{19,3},{4,20},{20... | collective-permute-start | bytes 2359304 | tf_op jit(solution)/shard_map/ppermute | solution.py:754
  62.5 60.9 %collective-permute-start.12 = (bf16[3,192,1280]{2,1,0:T(8,128)(2,1)S(1)}, bf16[3,192,1280]{2,1,0:T(8,128)(2,1)}, u32[]{:S(2)}, u32[]{:S(2)}) collective-permute-start(bf16[3,192,1280]{2,1,0:T(8,128)(2,1)S(1)} %broadcast_select_fusion.refs_2_), channel_id=1, source_target_pairs={{0,2},{2,6},{4,0},{6,4},{1,3},{3,7},{5,1},{7,5},{8,10},{10,14},{12... | collective-permute-start | bytes 4423688 | tf_op jit(solution)/shard_map/ppermute | solution.py:769
  63.1 65.9 %collective-permute-start.13 = (bf16[3,192,1280]{2,1,0:T(8,128)(2,1)S(1)}, bf16[3,192,1280]{2,1,0:T(8,128)(2,1)}, u32[]{:S(2)}, u32[]{:S(2)}) collective-permute-start(bf16[3,192,1280]{2,1,0:T(8,128)(2,1)S(1)} %broadcast_select_fusion.refs_2_), channel_id=1, source_target_pairs={{2,0},{6,2},{0,4},{4,6},{3,1},{7,3},{1,5},{5,7},{10,8},{14,10},{8,... | collective-permute-start | bytes 4423688 | tf_op jit(solution)/shard_map/ppermute | solution.py:772
  80.8 48.4 %collective-permute-start.16 = (bf16[3,192,1280]{2,1,0:T(8,128)(2,1)S(1)}, bf16[3,192,1280]{2,1,0:T(8,128)(2,1)}, u32[]{:S(2)}, u32[]{:S(2)}) collective-permute-start(bf16[3,192,1280]{2,1,0:T(8,128)(2,1)S(1)} %broadcast_select_fusion.refs_2_), channel_id=1, source_target_pairs={{0,8},{8,0},{1,9},{9,1},{2,10},{10,2},{3,11},{11,3},{4,12},{12,4},... | collective-permute-start | bytes 4423688 | tf_op jit(solution)/shard_map/ppermute | solution.py:757
  81.3 47.8 %collective-permute-start.14 = (bf16[3,192,1024]{2,1,0:T(8,128)(2,1)}, bf16[3,192,1024]{2,1,0:T(8,128)(2,1)}, u32[]{:S(2)}, u32[]{:S(2)}) collective-permute-start(bf16[3,192,1024]{2,1,0:T(8,128)(2,1)} %cut_columns.6), channel_id=1, source_target_pairs={{0,1},{9,8},{2,3},{11,10},{4,5},{13,12},{6,7},{15,14},{16,17},{25,... | collective-permute-start | bytes 3538952 | tf_op jit(solution)/shard_map/ppermute | solution.py:766
  85.5 43.6 %collective-permute-start.15 = (bf16[256,1536]{1,0:T(8,128)(2,1)S(1)}, bf16[256,1536]{1,0:T(8,128)(2,1)}, u32[]{:S(2)}, u32[]{:S(2)}) collective-permute-start(bf16[256,1536]{1,0:T(8,128)(2,1)S(1)} %bitcast.248), channel_id=1, source_target_pairs={{0,1},{1,0},{2,3},{3,2},{4,5},{5,4},{6,7},{7,6},{8,9},{9,8},{10,11... | collective-permute-start | bytes 2359304 | tf_op jit(solution)/shard_map/ppermute | solution.py:760
  133.0 19.6 %collective-permute-start.19 = (bf16[256,1536]{1,0:T(8,128)(2,1)S(1)}, bf16[256,1536]{1,0:T(8,128)(2,1)S(1)}, u32[]{:S(2)}, u32[]{:S(2)}) collective-permute-start(bf16[256,1536]{1,0:T(8,128)(2,1)S(1)} %add_convert_fusion.4), channel_id=1, source_target_pairs={{0,16},{16,0},{1,17},{17,1},{2,18},{18,2},{3,19},{19,3},{4,20},{20... | collective-permute-start | bytes 2359304 | tf_op jit(solution)/shard_map/ppermute | solution.py:754
  133.6 19.4 %collective-permute-start.20 = (bf16[256,1536]{1,0:T(8,128)(2,1)S(1)}, bf16[256,1536]{1,0:T(8,128)(2,1)S(1)}, u32[]{:S(2)}, u32[]{:S(2)}) collective-permute-start(bf16[256,1536]{1,0:T(8,128)(2,1)S(1)} %collective-permute-done.11.refs_15_), channel_id=1, source_target_pairs={{0,1},{1,0},{2,3},{3,2},{4,5},{5,4},{6,7},{7,6},{8,9},{9,8},{10,11... | collective-permute-start | bytes 2359304 | tf_op jit(solution)/shard_map/ppermute | solution.py:760
  135.2 34.0 %collective-permute-start.24 = (bf16[3,192,1280]{2,1,0:T(8,128)(2,1)}, bf16[3,192,1280]{2,1,0:T(8,128)(2,1)S(1)}, u32[]{:S(2)}, u32[]{:S(2)}) collective-permute-start(bf16[3,192,1280]{2,1,0:T(8,128)(2,1)} %collective-permute-done.13.refs_4_), channel_id=1, source_target_pairs={{2,0},{6,2},{0,4},{4,6},{3,1},{7,3},{1,5},{5,7},{10,8},{14,10},{8,... | collective-permute-start | bytes 4423688 | tf_op jit(solution)/shard_map/ppermute | solution.py:772
  154.1 20.5 %collective-permute-start.27 = (bf16[256,1536]{1,0:T(8,128)(2,1)S(1)}, bf16[256,1536]{1,0:T(8,128)(2,1)S(1)}, u32[]{:S(2)}, u32[]{:S(2)}) collective-permute-start(bf16[256,1536]{1,0:T(8,128)(2,1)S(1)} %multiply_convert_fusion.refs_10_), channel_id=1, source_target_pairs={{0,16},{16,0},{1,17},{17,1},{2,18},{18,2},{3,19},{19,3},{4,20},{20... | collective-permute-start | bytes 2359304 | tf_op jit(solution)/shard_map/ppermute | solution.py:754
  155.6 34.2 %collective-permute-start.28 = (bf16[256,1536]{1,0:T(8,128)(2,1)S(1)}, bf16[256,1536]{1,0:T(8,128)(2,1)S(1)}, u32[]{:S(2)}, u32[]{:S(2)}) collective-permute-start(bf16[256,1536]{1,0:T(8,128)(2,1)S(1)} %multiply_convert_fusion.refs_10_), channel_id=1, source_target_pairs={{0,1},{1,0},{2,3},{3,2},{4,5},{5,4},{6,7},{7,6},{8,9},{9,8},{10,11... | collective-permute-start | bytes 2359304 | tf_op jit(solution)/shard_map/ppermute | solution.py:760
  157.3 33.6 %collective-permute-start.29 = (bf16[256,1536]{1,0:T(8,128)(2,1)S(1)}, bf16[256,1536]{1,0:T(8,128)(2,1)S(1)}, u32[]{:S(2)}, u32[]{:S(2)}) collective-permute-start(bf16[256,1536]{1,0:T(8,128)(2,1)S(1)} %multiply_convert_fusion.refs_10_), channel_id=1, source_target_pairs={{0,17},{1,16},{16,1},{17,0},{2,19},{3,18},{18,3},{19,2},{4,21},{5,... | collective-permute-start | bytes 2359304 | tf_op jit(solution)/shard_map/ppermute | solution.py:763
  157.7 37.9 %collective-permute-start.25 = (bf16[3,192,1280]{2,1,0:T(8,128)(2,1)}, bf16[3,192,1280]{2,1,0:T(8,128)(2,1)}, u32[]{:S(2)}, u32[]{:S(2)}) collective-permute-start(bf16[3,192,1280]{2,1,0:T(8,128)(2,1)} %collective-permute-done.12.refs_3_), channel_id=1, source_target_pairs={{0,8},{8,0},{1,9},{9,1},{2,10},{10,2},{3,11},{11,3},{4,12},{12,4},... | collective-permute-start | bytes 4423688 | tf_op jit(solution)/shard_map/ppermute | solution.py:757
  169.2 26.4 %collective-permute-start.26 = (bf16[3,192,1280]{2,1,0:T(8,128)(2,1)}, bf16[3,192,1280]{2,1,0:T(8,128)(2,1)}, u32[]{:S(2)}, u32[]{:S(2)}) collective-permute-start(bf16[3,192,1280]{2,1,0:T(8,128)(2,1)} %collective-permute-done.13.refs_4_), channel_id=1, source_target_pairs={{0,8},{8,0},{1,9},{9,1},{2,10},{10,2},{3,11},{11,3},{4,12},{12,4},... | collective-permute-start | bytes 4423688 | tf_op jit(solution)/shard_map/ppermute | solution.py:757
  192.0 52.2 %collective-permute-start.21 = (bf16[3,192,1024]{2,1,0:T(8,128)(2,1)S(1)}, bf16[3,192,1024]{2,1,0:T(8,128)(2,1)}, u32[]{:S(2)}, u32[]{:S(2)}) collective-permute-start(bf16[3,192,1024]{2,1,0:T(8,128)(2,1)S(1)} %broadcast_select_fusion.1.refs_2_), channel_id=1, source_target_pairs={{0,2},{2,6},{4,0},{6,4},{1,3},{3,7},{5,1},{7,5},{8,10},{10,14},{12... | collective-permute-start | bytes 3538952 | tf_op jit(solution)/shard_map/ppermute | solution.py:769
  192.8 54.0 %collective-permute-start.22 = (bf16[3,192,1024]{2,1,0:T(8,128)(2,1)S(1)}, bf16[3,192,1024]{2,1,0:T(8,128)(2,1)}, u32[]{:S(2)}, u32[]{:S(2)}) collective-permute-start(bf16[3,192,1024]{2,1,0:T(8,128)(2,1)S(1)} %broadcast_select_fusion.1.refs_2_), channel_id=1, source_target_pairs={{2,0},{6,2},{0,4},{4,6},{3,1},{7,3},{1,5},{5,7},{10,8},{14,10},{8,... | collective-permute-start | bytes 3538952 | tf_op jit(solution)/shard_map/ppermute | solution.py:772
  246.8 15.0 %collective-permute-start.35 = (bf16[3,2,384,1280]{3,2,1,0:T(8,128)(2,1)}, bf16[3,2,384,1280]{3,2,1,0:T(8,128)(2,1)}, u32[]{:S(2)}, u32[]{:S(2)}) collective-permute-start(bf16[3,2,384,1280]{3,2,1,0:T(8,128)(2,1)} %get-tuple-element.166), channel_id=1, source_target_pairs={{0,8},{8,0},{1,9},{9,1},{2,10},{10,2},{3,11},{11,3},{4,12},{12,4},... | collective-permute-start | bytes 17694728 | tf_op jit(solution)/shard_map/ppermute | solution.py:757
  247.8 29.1 %collective-permute-start.23 = (bf16[3,192,1024]{2,1,0:T(8,128)(2,1)}, bf16[3,192,1024]{2,1,0:T(8,128)(2,1)}, u32[]{:S(2)}, u32[]{:S(2)}) collective-permute-start(bf16[3,192,1024]{2,1,0:T(8,128)(2,1)} %collective-permute-done.22.refs_4_), channel_id=1, source_target_pairs={{2,0},{6,2},{0,4},{4,6},{3,1},{7,3},{1,5},{5,7},{10,8},{14,10},{8,... | collective-permute-start | bytes 3538952 | tf_op jit(solution)/shard_map/ppermute | solution.py:772
  266.4 45.0 %collective-permute-start.36 = (bf16[3,2,96,1280]{3,2,1,0:T(8,128)(2,1)}, bf16[3,2,96,1280]{3,2,1,0:T(8,128)(2,1)}, u32[]{:S(2)}, u32[]{:S(2)}) collective-permute-start(bf16[3,2,96,1280]{3,2,1,0:T(8,128)(2,1)} %get-tuple-element.246), channel_id=1, source_target_pairs={{2,0},{6,2},{0,4},{4,6},{3,1},{7,3},{1,5},{5,7},{10,8},{14,10},{8,... | collective-permute-start | bytes 4423688 | tf_op jit(solution)/shard_map/ppermute | solution.py:772
  311.4 42.0 %all-to-all-start = ((bf16[4,256,1536]{2,1,0:T(8,128)(2,1)}), bf16[4,256,1536]{2,1,0:T(8,128)(2,1)}, u32[]{:S(2)}, u32[]{:S(2)}) async-start(bf16[4,256,1536]{2,1,0:T(8,128)(2,1)} %bitcast.260), calls=%async_computation | async-start | bytes 6291456 | tf_op jit(solution)/shard_map/all_to_all | solution.py:775
  316.1 35.4 %collective-permute-start.37 = (bf16[3,2,96,1280]{3,2,1,0:T(8,128)(2,1)S(1)}, bf16[3,2,96,1280]{3,2,1,0:T(8,128)(2,1)}, u32[]{:S(2)}, u32[]{:S(2)}) collective-permute-start(bf16[3,2,96,1280]{3,2,1,0:T(8,128)(2,1)S(1)} %get-tuple-element.247), channel_id=1, source_target_pairs={{0,2},{2,6},{4,0},{6,4},{1,3},{3,7},{5,1},{7,5},{8,10},{10,14},{12... | collective-permute-start | bytes 4423688 | tf_op jit(solution)/shard_map/ppermute | solution.py:769
  334.3 26.7 %collective-permute-start.43 = (bf16[2,384,1024]{2,1,0:T(8,128)(2,1)}, bf16[2,384,1024]{2,1,0:T(8,128)(2,1)}, u32[]{:S(2)}, u32[]{:S(2)}) collective-permute-start(bf16[2,384,1024]{2,1,0:T(8,128)(2,1)} %get-tuple-element.193), channel_id=1, source_target_pairs={{0,8},{8,0},{1,9},{9,1},{2,10},{10,2},{3,11},{11,3},{4,12},{12,4},... | collective-permute-start | bytes 4718600 | tf_op jit(solution)/shard_map/ppermute | solution.py:757
  334.4 48.2 %collective-permute-start.42 = (bf16[2,384,1024]{2,1,0:T(8,128)(2,1)}, bf16[2,384,1024]{2,1,0:T(8,128)(2,1)}, u32[]{:S(2)}, u32[]{:S(2)}) collective-permute-start(bf16[2,384,1024]{2,1,0:T(8,128)(2,1)} %get-tuple-element.192), channel_id=1, source_target_pairs={{0,8},{8,0},{1,9},{9,1},{2,10},{10,2},{3,11},{11,3},{4,12},{12,4},... | collective-permute-start | bytes 4718600 | tf_op jit(solution)/shard_map/ppermute | solution.py:757
  334.9 51.2 %collective-permute-start.41 = (bf16[2,384,1024]{2,1,0:T(8,128)(2,1)}, bf16[2,384,1024]{2,1,0:T(8,128)(2,1)}, u32[]{:S(2)}, u32[]{:S(2)}) collective-permute-start(bf16[2,384,1024]{2,1,0:T(8,128)(2,1)} %get-tuple-element.191), channel_id=1, source_target_pairs={{0,8},{8,0},{1,9},{9,1},{2,10},{10,2},{3,11},{11,3},{4,12},{12,4},... | collective-permute-start | bytes 4718600 | tf_op jit(solution)/shard_map/ppermute | solution.py:757
  358.4 19.5 %collective-permute-start.38 = (bf16[256,1536]{1,0:T(8,128)(2,1)}, bf16[256,1536]{1,0:T(8,128)(2,1)}, u32[]{:S(2)}, u32[]{:S(2)}) collective-permute-start(bf16[256,1536]{1,0:T(8,128)(2,1)} %fusion.47.near), channel_id=1, source_target_pairs={{0,16},{16,0},{1,17},{17,1},{2,18},{18,2},{3,19},{19,3},{4,20},{20... | collective-permute-start | bytes 2359304 | tf_op jit(solution)/shard_map/ppermute | solution.py:754
  359.3 57.4 %collective-permute-start.45 = (bf16[3,2,96,1280]{3,2,1,0:T(8,128)(2,1)}, bf16[3,2,96,1280]{3,2,1,0:T(8,128)(2,1)}, u32[]{:S(2)}, u32[]{:S(2)}) collective-permute-start(bf16[3,2,96,1280]{3,2,1,0:T(8,128)(2,1)} %fusion.2), channel_id=1, source_target_pairs={{2,0},{6,2},{0,4},{4,6},{3,1},{7,3},{1,5},{5,7},{10,8},{14,10},{8,... | collective-permute-start | bytes 4423688 | tf_op jit(solution)/shard_map/ppermute | solution.py:772
  363.9 28.1 %collective-permute-start.39 = (bf16[256,1536]{1,0:T(8,128)(2,1)}, bf16[256,1536]{1,0:T(8,128)(2,1)}, u32[]{:S(2)}, u32[]{:S(2)}) collective-permute-start(bf16[256,1536]{1,0:T(8,128)(2,1)} %fusion.47.near), channel_id=1, source_target_pairs={{0,8},{8,0},{1,9},{9,1},{2,10},{10,2},{3,11},{11,3},{4,12},{12,4},... | collective-permute-start | bytes 2359304 | tf_op jit(solution)/shard_map/ppermute | solution.py:757
  377.9 47.5 %all-to-all-start.1 = ((bf16[4,256,1536]{2,1,0:T(8,128)(2,1)}), bf16[4,256,1536]{2,1,0:T(8,128)(2,1)}, u32[]{:S(2)}, u32[]{:S(2)}) async-start(bf16[4,256,1536]{2,1,0:T(8,128)(2,1)} %bitcast.259), calls=%async_computation.1 | async-start | bytes 6291456 | tf_op jit(solution)/shard_map/all_to_all | solution.py:775
  390.2 28.1 %collective-permute-start.44 = (bf16[3,2,96,1024]{3,2,1,0:T(8,128)(2,1)}, bf16[3,2,96,1024]{3,2,1,0:T(8,128)(2,1)}, u32[]{:S(2)}, u32[]{:S(2)}) collective-permute-start(bf16[3,2,96,1024]{3,2,1,0:T(8,128)(2,1)} %pad_maximum_fusion.1), channel_id=1, source_target_pairs={{2,0},{6,2},{0,4},{4,6},{3,1},{7,3},{1,5},{5,7},{10,8},{14,10},{8,... | collective-permute-start | bytes 3538952 | tf_op jit(solution)/shard_map/ppermute | solution.py:772
  420.7 27.2 %collective-permute-start.48 = (bf16[2,2,4,48,768]{4,3,1,0,2:T(8,128)(2,1)}, bf16[2,2,4,48,768]{4,3,1,0,2:T(8,128)(2,1)}, u32[]{:S(2)}, u32[]{:S(2)}) collective-permute-start(bf16[2,2,4,48,768]{4,3,1,0,2:T(8,128)(2,1)} %copy_bitcast_fusion), channel_id=1, source_target_pairs={{0,1},{1,0},{2,3},{3,2},{4,5},{5,4},{6,7},{7,6},{8,9},{9,8},{10,11... | collective-permute-start | bytes 3538952 | tf_op jit(solution)/shard_map/ppermute | solution.py:760
  435.7 17.6 %collective-permute-start.47 = (bf16[256,1536]{1,0:T(8,128)(2,1)}, bf16[256,1536]{1,0:T(8,128)(2,1)}, u32[]{:S(2)}, u32[]{:S(2)}) collective-permute-start(bf16[256,1536]{1,0:T(8,128)(2,1)} %get-tuple-element.216), channel_id=1, source_target_pairs={{0,8},{8,0},{1,9},{9,1},{2,10},{10,2},{3,11},{11,3},{4,12},{12,4},... | collective-permute-start | bytes 2359304 | tf_op jit(solution)/shard_map/ppermute | solution.py:757
  436.8 69.8 %collective-permute-start.54 = (bf16[3,2,96,1024]{3,2,1,0:T(8,128)(2,1)}, bf16[3,2,96,1024]{3,2,1,0:T(8,128)(2,1)}, u32[]{:S(2)}, u32[]{:S(2)}) collective-permute-start(bf16[3,2,96,1024]{3,2,1,0:T(8,128)(2,1)} %pad_maximum_fusion), channel_id=1, source_target_pairs={{0,2},{2,6},{4,0},{6,4},{1,3},{3,7},{5,1},{7,5},{8,10},{10,14},{12... | collective-permute-start | bytes 3538952 | tf_op jit(solution)/shard_map/ppermute | solution.py:769
  439.1 67.5 %collective-permute-start.55 = (bf16[3,2,96,1024]{3,2,1,0:T(8,128)(2,1)}, bf16[3,2,96,1024]{3,2,1,0:T(8,128)(2,1)}, u32[]{:S(2)}, u32[]{:S(2)}) collective-permute-start(bf16[3,2,96,1024]{3,2,1,0:T(8,128)(2,1)} %fusion.3), channel_id=1, source_target_pairs={{2,0},{6,2},{0,4},{4,6},{3,1},{7,3},{1,5},{5,7},{10,8},{14,10},{8,... | collective-permute-start | bytes 3538952 | tf_op jit(solution)/shard_map/ppermute | solution.py:772
  447.8 30.7 %collective-permute-start.49 = (bf16[256,1536]{1,0:T(8,128)(2,1)}, bf16[256,1536]{1,0:T(8,128)(2,1)}, u32[]{:S(2)}, u32[]{:S(2)}) collective-permute-start(bf16[256,1536]{1,0:T(8,128)(2,1)} %get-tuple-element.222), channel_id=1, source_target_pairs={{0,8},{8,0},{1,9},{9,1},{2,10},{10,2},{3,11},{11,3},{4,12},{12,4},... | collective-permute-start | bytes 2359304 | tf_op jit(solution)/shard_map/ppermute | solution.py:757
  449.7 20.1 %collective-permute-start.56 = (bf16[2,2,4,48,256]{4,3,1,0,2:T(8,128)(2,1)}, bf16[2,2,4,48,256]{4,3,1,0,2:T(8,128)(2,1)S(1)}, u32[]{:S(2)}, u32[]{:S(2)}) collective-permute-start(bf16[2,2,4,48,256]{4,3,1,0,2:T(8,128)(2,1)} %copy_bitcast_fusion.1), channel_id=1, source_target_pairs={{0,1},{1,0},{2,3},{3,2},{4,5},{5,4},{6,7},{7,6},{8,9},{9,8},{10,11... | collective-permute-start | bytes 1179656 | tf_op jit(solution)/shard_map/ppermute | solution.py:760
  455.4 20.7 %collective-permute-start.50 = (bf16[256,1536]{1,0:T(8,128)(2,1)}, bf16[256,1536]{1,0:T(8,128)(2,1)}, u32[]{:S(2)}, u32[]{:S(2)}) collective-permute-start(bf16[256,1536]{1,0:T(8,128)(2,1)} %add_convert_fusion.3), channel_id=1, source_target_pairs={{0,16},{16,0},{1,17},{17,1},{2,18},{18,2},{3,19},{19,3},{4,20},{20... | collective-permute-start | bytes 2359304 | tf_op jit(solution)/shard_map/ppermute | solution.py:754
  461.6 42.5 %all-to-all-start.2 = ((bf16[4,3,48,1280]{3,2,1,0:T(8,128)(2,1)}), bf16[4,3,48,1280]{3,2,1,0:T(8,128)(2,1)}, u32[]{:S(2)}, u32[]{:S(2)}) async-start(bf16[4,3,48,1280]{3,2,1,0:T(8,128)(2,1)} %bitcast.252), calls=%async_computation.2 | async-start | bytes 2949120 | tf_op jit(solution)/shard_map/all_to_all | solution.py:775
  469.7 34.4 %collective-permute-start.52 = (bf16[2,2,48,768]{3,2,1,0:T(8,128)(2,1)S(1)}, bf16[2,2,48,768]{3,2,1,0:T(8,128)(2,1)}, u32[]{:S(2)}, u32[]{:S(2)}) collective-permute-start(bf16[2,2,48,768]{3,2,1,0:T(8,128)(2,1)S(1)} %copy-done.33), channel_id=1, source_target_pairs={{2,0},{6,2},{0,4},{4,6},{3,1},{7,3},{1,5},{5,7},{10,8},{14,10},{8,... | collective-permute-start | bytes 884744 | tf_op jit(solution)/shard_map/ppermute | solution.py:772
  477.1 22.4 %collective-permute-start.58 = (bf16[2,2,48,256]{3,2,1,0:T(8,128)(2,1)S(1)}, bf16[2,2,48,256]{3,2,1,0:T(8,128)(2,1)S(1)}, u32[]{:S(2)}, u32[]{:S(2)}) collective-permute-start(bf16[2,2,48,256]{3,2,1,0:T(8,128)(2,1)S(1)} %fusion.37), channel_id=1, source_target_pairs={{2,0},{6,2},{0,4},{4,6},{3,1},{7,3},{1,5},{5,7},{10,8},{14,10},{8,... | collective-permute-start | bytes 294920 | tf_op jit(solution)/shard_map/ppermute | solution.py:772
  506.6 15.2 %collective-permute-start.53 = (bf16[2,2,48,768]{3,2,1,0:T(8,128)(2,1)S(1)}, bf16[2,2,48,768]{3,2,1,0:T(8,128)(2,1)S(1)}, u32[]{:S(2)}, u32[]{:S(2)}) collective-permute-start(bf16[2,2,48,768]{3,2,1,0:T(8,128)(2,1)S(1)} %get-tuple-element.248), channel_id=1, source_target_pairs={{2,0},{6,2},{0,4},{4,6},{3,1},{7,3},{1,5},{5,7},{10,8},{14,10},{8,... | collective-permute-start | bytes 884744 | tf_op jit(solution)/shard_map/ppermute | solution.py:772
  534.6 18.6 %all-to-all-start.4 = ((bf16[4,3,48,1024]{3,2,1,0:T(8,128)(2,1)}), bf16[4,3,48,1024]{3,2,1,0:T(8,128)(2,1)S(1)}, u32[]{:S(2)}, u32[]{:S(2)}) async-start(bf16[4,3,48,1024]{3,2,1,0:T(8,128)(2,1)} %bitcast.257), calls=%async_computation.4 | async-start | bytes 2359296 | tf_op jit(solution)/shard_map/all_to_all | solution.py:775
  (65 other events, 789.5 us)

commit v4 on v3

--- a/solution.py
+++ b/solution.py
@@ -156,12 +156,12 @@
     cosine, sine, starts = refs[6 + 2 * planes : 9 + 2 * planes]
     normed_t, queries, keys, values, attended_t = refs[9 + 2 * planes : 14 + 2 * planes]
     targets = refs[14 + 2 * planes : 18 + 2 * planes]
-    weights, gains, tokens, small, sems, token_sems = refs[18 + 2 * planes :]
+    weights, gains, tokens, small, attended, sems = refs[18 + 2 * planes :]
     length = tokens.shape[0]
     group_cols = queries.shape[1]
     blocks = 2 * planes
     s, y = own[0], own[1]
-    copies = sequence_copies(s, sources, tokens, token_sems)
+    copies = []
     for k in range(planes):
         for side, source in enumerate((mine[k], theirs[k])):
             block = places[k] * 2 + (y if side == 0 else 1 - y)
@@ -207,8 +207,14 @@
     )
     wide = group_cols + 2 * HD
     heads = group_cols // HD
-    for first in range(0, length, QUERY_ROWS):
-        r = pl.ds(first, QUERY_ROWS)
+    x, c = s // 2, lax.rem(s, 2)
+    owners = (2 * x + c, 2 * (1 - x) + c, 2 * x + 1 - c, 2 * (1 - x) + 1 - c)
+    for source, owner in zip(sources, owners):
+        r = pl.ds(pl.multiple_of(owner * QUERY_ROWS, QUERY_ROWS), QUERY_ROWS)
+        tokens[r, :] = source[...]
+
+    def project(at, carry):
+        r = pl.ds(pl.multiple_of(at * QUERY_ROWS, QUERY_ROWS), QUERY_ROWS)
         value = tokens[r, :].astype(F32)
         low = (value * rms_factor(value) * gain).astype(BF)
         normed_t[:, r] = low.T
@@ -222,6 +228,9 @@
             else:
                 keys[r, :] = turned
         values[r, :] = qkv[:, group_cols + HD :].astype(BF)
+        return carry
+
+    lax.fori_loop(0, length // QUERY_ROWS, project, 0)
     scaling = HD ** (-0.5)
     for first in range(0, length, QUERY_ROWS):
         r = pl.ds(first, QUERY_ROWS)
@@ -229,18 +238,20 @@
         query_place = first + lax.broadcasted_iota(jnp.int32, (QUERY_ROWS, reach), 0)
         key_place = lax.broadcasted_iota(jnp.int32, (QUERY_ROWS, reach), 1)
         allowed = (key_place <= query_place) & (key_place >= starts[r, :])
-        outcomes = []
-        for head in range(heads):
-            cols = slice(head * HD, (head + 1) * HD)
-            scores = dot_t(queries[r, cols], keys[0:reach, :]) * scaling
-            scores = jnp.where(allowed, scores, masked_value)
+        hidden_keys = jnp.where(allowed, 0.0, masked_value)
+
+        def attend(head, carry):
+            cols = pl.ds(pl.multiple_of(head * HD, HD), HD)
+            scores = dot_t(queries[r, cols], keys[0:reach, :]) * scaling + hidden_keys
             shifted = jnp.exp(scores - jnp.max(scores, axis=-1, keepdims=True))
             total = jnp.sum(shifted, axis=-1, keepdims=True)
             outcome = dot(shifted.astype(BF), values[0:reach, :])
-            outcomes.append((outcome / total).astype(BF))
-        attended = jnp.concatenate(outcomes, axis=1)
-        attended_t[:, r] = attended.T
-        term = dot_t(attended, weights[:, wide:]).astype(BF)
+            attended[:, cols] = (outcome / total).astype(BF)
+            return carry
+
+        lax.fori_loop(0, heads, attend, 0)
+        attended_t[:, r] = attended[...].T
+        term = dot_t(attended[...], weights[:, wide:]).astype(BF)
         split_store(s, first // QUERY_ROWS, term, targets)
 
 
@@ -262,12 +273,12 @@
     return pl.pallas_call(
         functools.partial(attention_in_body, planes, rows),
         out_shape=shapes,
-        in_specs=[in_smem, in_smem] + [anywhere] * (2 * planes + 4) + [in_vmem] * 3,
+        in_specs=[in_smem, in_smem] + [anywhere] * (2 * planes) + [in_vmem] * 7,
         out_specs=[in_vmem] * len(shapes),
         scratch_shapes=[
             pltpu.VMEM((2 * planes * 16, mine[0].shape[1]), BF),
+            pltpu.VMEM((QUERY_ROWS, group_cols), BF),
             pltpu.SemaphoreType.DMA((2, 2 * planes)),
-            pltpu.SemaphoreType.DMA((4,)),
         ],
         compiler_params=kernel_params(),
         cost_estimate=KERNEL_COST,
@@ -536,15 +547,14 @@
     totals_out = [rest.pop(0) for _ in range(2)]
     weights, grad_total, branch_total = [rest.pop(0) for _ in range(3)]
     normed, cotangent, weight_sems, sems = [rest.pop(0) for _ in range(4)]
-    if last:
-        low = rest
-    else:
+    low = [rest.pop(0) for _ in range(2)]
+    if not last:
         grad_gate, grad_up, activated, normed_t, cotangent_t = rest
     step, steps = pl.program_id(0), pl.num_programs(0)
     tokens = normed.shape[0]
-    c = own[0]
-    normed_loads = plane_copies(own[1], normed_parts, normed, sems, 8)
-    cot_loads = plane_copies(own[1], cot_parts, cotangent, sems, 12)
+    c, chip = own[0], own[1]
+    normed_loads = plane_copies(chip, normed_parts, normed, sems, 8)
+    cot_loads = plane_copies(chip, cot_parts, cotangent, sems, 12)
     turned_ends = [
         pltpu.make_async_copy(source, target, sems.at[16 + i])
         for i, (source, target) in enumerate(
@@ -553,17 +563,12 @@
     ]
     fills = [
         pltpu.make_async_copy(source, target, sems.at[i])
-        for i, (source, target) in enumerate(zip(totals_in, (grad_total, branch_total)))
+        for i, (source, target) in enumerate(zip(totals_in, low))
     ]
-    if last:
-        ends = [
-            pltpu.make_async_copy(low[i], target, sems.at[i]) for i, target in enumerate(totals_out)
-        ]
-    else:
-        ends = [
-            pltpu.make_async_copy(source, target, sems.at[i])
-            for i, (source, target) in enumerate(zip((grad_total, branch_total), totals_out))
-        ]
+    ends = [
+        pltpu.make_async_copy(source, target, sems.at[2 + i])
+        for i, (source, target) in enumerate(zip(low, totals_out))
+    ]
 
     def weight_copies(at, slot):
         cols = pl.ds(pl.multiple_of(at * TILE, TILE), TILE)
@@ -597,25 +602,15 @@
         for copy in weight_copies(step + 1, 1 - slot):
             copy.start()
 
-    if first:
-
-        @pl.when(step == 0)
-        def _():
-            grad_total[...] = jnp.zeros_like(grad_total)
-            branch_total[...] = jnp.zeros_like(branch_total)
-
     @pl.when(step == 0)
     def _():
+        grad_total[...] = jnp.zeros_like(grad_total)
+        branch_total[...] = jnp.zeros_like(branch_total)
         for load in normed_loads:
             load.wait()
 
     for copy in weight_copies(step, slot):
         copy.wait()
-
-    @pl.when(step == 0)
-    def _():
-        for load in cot_loads:
-            load.wait()
 
     block = min(256, tokens)
     for start in range(0, tokens, block):
@@ -623,6 +618,13 @@
         some = normed[r, :]
         gate = dot(some, weights[slot, 0])
         up = dot(some, weights[slot, 1])
+        if start == 0:
+
+            @pl.when(step == 0)
+            def _():
+                for load in cot_loads:
+                    load.wait()
+
         grad_act = dot(cotangent[r, :], weights[slot, 2])
         sigma = jax.nn.sigmoid(gate)
         silu = gate * sigma
@@ -630,11 +632,6 @@
         grad_gate[r, :] = (grad_act * up * (sigma + silu * (1.0 - sigma))).astype(BF)
         grad_up[r, :] = (grad_act * silu).astype(BF)
 
-    @pl.when(step == 0)
-    def _():
-        for fill in fills:
-            fill.wait()
-
     for start in range(0, tokens, block):
         r = pl.ds(start, block)
         grad_total[r, :] += dot_t(grad_gate[r, :], weights[slot, 0]) + dot_t(
@@ -644,9 +641,11 @@
 
     @pl.when(step == steps - 1)
     def _():
-        if last:
-            low[0][...] = grad_total[...].astype(BF)
-            low[1][...] = branch_total[...].astype(BF)
+        for fill in fills:
+            fill.wait()
+        for target, total in zip(low, (grad_total, branch_total)):
+            value = total[...]
+            target[...] = (value if first else value + target[...].astype(F32)).astype(BF)
         for end in ends:
             end.start()
 
@@ -686,17 +685,13 @@
     blocks = len(shapes)
     if first:
         shapes += [jax.ShapeDtypeStruct((D, tokens), BF)] * 2
-    if last:
-        shapes += [jax.ShapeDtypeStruct((tokens, D), BF)] * 2
-    else:
-        shapes += [jax.ShapeDtypeStruct((tokens, D), F32)] * 2
+    shapes += [jax.ShapeDtypeStruct((tokens, D), BF)] * 2
     scratch = [pltpu.VMEM((2, 3, D, TILE), BF)]
     scratch += [pltpu.VMEM((tokens, D), F32)] * 2
     scratch += [pltpu.VMEM((tokens, D), BF)] * 2
     scratch += [pltpu.SemaphoreType.DMA((2, 2 * planes)), pltpu.SemaphoreType.DMA((18,))]
-    if last:
-        scratch += [pltpu.VMEM((tokens, D), BF)] * 2
-    else:
+    scratch += [pltpu.VMEM((tokens, D), BF)] * 2
+    if not last:
         scratch += [pltpu.VMEM((tokens, TILE), BF)] * 3 + [pltpu.VMEM((D, tokens), BF)] * 2
     inputs = [*mine, *theirs, *normed, *cotangent, *totals]
     return pl.pallas_call(
@@ -710,6 +705,48 @@
         cost_estimate=KERNEL_COST,
         name="feed_forward",
     )(places, own, *inputs)
+
+
+def add_planes_body(kinds, count, rows, where, *refs):
+    ours, theirs = refs[:kinds], refs[kinds : 2 * kinds]
+    targets = refs[2 * kinds : 2 * kinds + count]
+    held, sems = refs[2 * kinds + count :]
+    copies = []
+    for i in range(count):
+        r = pl.ds(pl.multiple_of(where[i] * rows, 16), rows)
+        for kind in range(3):
+            for side, sources in enumerate((ours, theirs)):
+                source = sources[kind] if kinds == 3 else sources[0].at[kind]
+                copies.append(
+                    pltpu.make_async_copy(
+                        source.at[:, r, :], held.at[i, kind, side], sems.at[i, kind, side]
+                    )
+                )
+    for copy in copies:
+        copy.start()
+    for i in range(count):
+        for kind in range(3):
+            for side in range(2):
+                copies[(i * 3 + kind) * 2 + side].wait()
+            total = held[i, kind, 0].astype(F32) + held[i, kind, 1].astype(F32)
+            targets[i][kind] = total.astype(BF)
+
+
+def add_planes(ours, theirs, rows, where):
+    count, cols = where.shape[0], ours[0].shape[-1]
+    return pl.pallas_call(
+        functools.partial(add_planes_body, len(ours), count, rows),
+        out_shape=[jax.ShapeDtypeStruct((3, 2, rows, cols), BF)] * count,
+        in_specs=[in_smem] + [anywhere] * (2 * len(ours)),
+        out_specs=[in_vmem] * count,
+        scratch_shapes=[
+            pltpu.VMEM((count, 3, 2, 2, rows, cols), BF),
+            pltpu.SemaphoreType.DMA((count, 3, 2)),
+        ],
+        compiler_params=kernel_params(),
+        cost_estimate=KERNEL_COST,
+        name="add_planes",
+    )(where, *ours, *theirs)
 
 
 def assemble_body(*refs):
@@ -871,12 +908,13 @@
         attn_theirs += [swap_y(piece) for piece in attn_pieces[1:-1]]
 
         came, kept = send_rows(sent), cut(0, 0, attn_payload)
-        kept, came = tie((kept, came), attn_pieces[1:], attn_theirs[first_back], token_pieces[1:3])
+        cuts = [(cut(1, 1, kept), cut(1, 0, kept))]
+        kept, came = tie(
+            (kept, came), attn_pieces[1:], attn_theirs[first_back], token_pieces[1:3], cuts
+        )
         payloads = [jnp.where(c == y, kept, came)]
         token_pieces.append(swap_c(tie(token_far, payloads[0])))
-        after = (payloads[0], token_pieces[3])
-        cuts = [(cut(1, 1, after), cut(1, 0, after))]
-        attn_theirs.append(swap_y(tie(attn_pieces[-1], cuts)))
+        attn_theirs.append(swap_y(tie(attn_pieces[-1], payloads[0])))
         own_swapped = swap_c(tie(payloads[0], attn_theirs))
         for sent, kept in cuts:
             came = send_rows(tie(sent, attn_theirs))
@@ -940,19 +978,20 @@
             return ring_order[(ring_place[z] + steps) % planes]
 
         class RingScatter:
-            def __init__(self, block):
+            def __init__(self, block, first=None):
                 self.block = block
                 self.own = block(z)
-                self.first = [
+                self.first = first or [
                     block(plane_ahead(sign * steps)).astype(BF)
                     for steps, sign in ((along, 1), (against, -1))
                     if steps
                 ]
 
-            def go(self, then=()):
+            def go(self, then=(), together=False):
                 self.arrived, self.second, self.last = [], [], []
                 firsts = list(self.first)
                 for steps, sign, move in ((along, 1, ring), (against, -1, ring_back)):
+                    then = (then, self.last) if together else then
                     if steps:
                         running = firsts.pop(0)
                         for left in range(steps - 1, 0, -1):
@@ -977,7 +1016,12 @@
                 return piece.reshape(piece.shape[:-2] + (planes, 2 * own_rows, piece.shape[-1]))
 
             if isinstance(send, (list, tuple)):
-                away = [by_plane(swap_c(piece)) for piece in send]
+                away = [swap_c(piece) for piece in send]
+                first = None
+                if along and against and 2 * own_rows % 16 == 0:
+                    where = jnp.stack([plane_ahead(along), plane_ahead(-against)]).astype(jnp.int32)
+                    first = add_planes(keep, away, 2 * own_rows, where)
+                away = [by_plane(piece) for piece in away]
                 keep = [by_plane(piece) for piece in keep]
 
                 def block(plane):
@@ -989,13 +1033,14 @@
                     )
 
             else:
+                first = None
                 away = by_plane(tie(swap_c(send), then))
                 keep = by_plane(keep)
 
                 def block(plane):
                     return pick(keep, plane, 2).astype(F32) + pick(away, plane, 2).astype(F32)
 
-            return RingScatter(block)
+            return RingScatter(block, first)
 
         before = [(), None]
         beside = [chunk_pieces[1][1 : along + 2]]
@@ -1053,9 +1098,7 @@
             attended_t,
         )
         scatters[1].go()
-        grad_q, grad_kv, d_early = tie(
-            (grad_q, grad_kv, d_early), scatters[1].arrived[along], scatters[0].last[-1]
-        )
+        d_early = tie(d_early, scatters[0].last[-1])
 
         branch = trade(tie(totals[1], grad_pieces[1]).reshape(4, tok_rows, D), ("x", "y"))
 
@@ -1070,7 +1113,7 @@
             own_rows,
             kv_rows,
             own_place,
-            tie(grad_q, early_rows[0], scatters[1].second, branch),
+            tie(grad_q, branch),
             grad_kv,
             grad_kv_theirs,
             attn_weights,
@@ -1084,13 +1127,14 @@
             def block(plane):
                 return pick(stays, plane, 2).astype(F32) + pick(away, plane, 2).astype(F32)
 
-            return RingScatter(block).go(then)
+            return RingScatter(block).go(then, True)
 
         def chunk_sum(scatter, then):
             total = scatter.total(then).reshape(3, 2, 2, own_rows, -1)
             return total.transpose(1, 2, 0, 3, 4).reshape(4, 3, own_rows, -1)
 
         early_away = tie(swap_y(early_rows[0]), d_late)
+        d_late, in_terms = tie((d_late, in_terms), scatters[1].arrived[along])
         late_leaves, late_stays = owner_rows(d_late)
         grad_normed_attn, in_leaves, in_back = scatter_sequence(*in_terms, (early_away, late_leaves))
         grad_input_norm, _ = rms_backward(
@@ -1105,13 +1149,13 @@
         first_sum = chunk_sum(scatters[0], in_leaves)
         gathered = [trade(first_sum, ("x", "y"))]
 
-        late_away = tie(swap_y(late_leaves), in_back)
-        early = owner_scatter(early_away, early_rows[1], (in_back, gathered))
+        late_away = tie(swap_y(late_leaves), in_back, scatters[1].last[-1])
+        early = owner_scatter(early_away, early_rows[1], (in_back, gathered[0], scatters[1].last[0]))
         late = owner_scatter(late_away, late_stays)
         second_sum = chunk_sum(scatters[1], (early.first, late.first))
         gathered.append(trade(second_sum, ("x", "y")))
         d_gate_up, d_w_down = assemble(gathered)
-        owned = [early.total(second_sum), late.total(second_sum)]
+        owned = [early.total(gathered), late.total(gathered)]
         owned = jnp.concatenate(owned, axis=-1).reshape(4, own_rows, -1)
         owned = trade(owned, ("x", "c")).astype(F32)
         early, late = owned[..., : 2 * group_cols], owned[..., 2 * group_cols :]

time: 569 us -> 550 us (0.967)
  waiting for transfers between devices: 196 us -> 185 us
  other arithmetic: 73 us -> 66.9 us
    all_to_all x5, waiting for transfers between devices: 15.1 us -> 2.26 us  [trade(): return lax.all_to_all(blocks, axes, split_axis=0, concat_axis=0, tiled=True)]
    ppermute x7, waiting for transfers between devices: 18.3 us -> 29.5 us  [ring(): return lax.ppermute(value, 'z', ring_perm)]
    ppermute x14, waiting for transfers between devices: 71.5 us -> 62.9 us  [ring_back(): return lax.ppermute(value, 'z', [(j, i) for i, j in ring_perm])]
    pallas_call x1, Pallas kernels: 30.9 us -> 23.9 us  [attention_in(): pl.pallas_call(functools.partial(attention_in_body, planes, rows), out_sh...]
  transfers between devices with their start and end apart: 65 -> 65, of which waited for: 30 -> 28; matrix products, arithmetic and copies ran while one was open for 15% -> 13% of each run, Pallas kernels for 31% -> 32%
where the time goes in v4:
time: 550 us; the launch traced here: 541 us
  waiting for transfers between devices  185 us (34%)
  Pallas kernels  178 us (32%)
  starting transfers between devices  82.3 us (15%)
  other arithmetic  66.9 us (12%)
  local copies, waits for them, and re-layouts  18.5 us (3%)
  between operations  9.51 us (2%)
    pallas_call x2, Pallas kernels, feed_forward(): pl.pallas_call(functools.partial(feed_forward_body, planes, rows, first,...  77.8 us
    ppermute x14, waiting for transfers between devices, ring_back(): return lax.ppermute(value, 'z', [(j, i) for i, j in ring_perm])  62.9 us
    ppermute x6, waiting for transfers between devices, swap_x(): return lax.ppermute(value, 'x', other)  39.8 us
    ppermute x9, waiting for transfers between devices, swap_y(): return lax.ppermute(value, 'y', other)  36.6 us
    ppermute x7, waiting for transfers between devices, ring(): return lax.ppermute(value, 'z', ring_perm)  29.5 us
    pallas_call x1, Pallas kernels, attention_in(): pl.pallas_call(functools.partial(attention_in_body, planes, rows), out_sh...  23.9 us
    ppermute x14, starting transfers between devices, ring_back(): return lax.ppermute(value, 'z', [(j, i) for i, j in ring_perm])  23.3 us
    pallas_call x1, Pallas kernels, attention_out(): pl.pallas_call(attention_out_body, out_shape=[jax.ShapeDtypeStruct((lengt...  22 us
  transfers between devices with their start and end apart: 65, of which 28 were waited for; matrix products, arithmetic and copies ran while one was open for 13% of the time, Pallas kernels for 32%

profile of v4, /device:TPU:0, one launch (start us, length us, event | category | flops | bytes accessed | tf_op | source)
XLA Modules:
  0.0 540.8 jit_solution(17428567872822888254)
XLA Ops:
  2.0 5.3 cut_columns.4
  7.3 6.0 %collective-permute-start.7 = (bf16[3,192,1280]{2,1,0:T(8,128)(2,1)}, bf16[3,192,1280]{2,1,0:T(8,128)(2,1)}, u32[]{:S(2)}, u32[]{:S(2)}) collective-permute-start(bf16[3,192,1280]{2,1,0:T(8,128)(2,1)} %cut_columns.4), channel_id=1, source_target_pairs={{0,1},{9,8},{2,3},{11,10},{4,5},{13,12},{6,7},{15,14},{16,17},{25,... | collective-permute-start | bytes 4423688 | tf_op jit(solution)/shard_map/ppermute | solution.py:803
  14.7 2.6 collective-permute-start.1
  18.8 8.7 %collective-permute-done.1.refs_4_ = bf16[208,1024]{1,0:T(8,128)(2,1)} collective-permute-done((bf16[208,1024]{1,0:T(8,128)(2,1)S(1)}, bf16[208,1024]{1,0:T(8,128)(2,1)}, u32[]{:S(2)}, u32[]{:S(2)}) %collective-permute-start.1) | collective-permute-done | bytes 426016 | tf_op jit(solution)/shard_map/ppermute | solution.py:809
  27.6 3.5 collective-permute-start.3
  31.1 5.1 cut_columns.5
  36.3 4.6 cut_columns.6
  40.9 4.7 cut_columns.7
  50.6 3.3 collective-permute-start.9
  53.9 6.2 %collective-permute-done.4.refs_6_ = bf16[208,1024]{1,0:T(8,128)(2,1)S(1)} collective-permute-done((bf16[208,1024]{1,0:T(8,128)(2,1)S(1)}, bf16[208,1024]{1,0:T(8,128)(2,1)S(1)}, u32[]{:S(2)}, u32[]{:S(2)}) %collective-permute-start.4) | collective-permute-done | bytes 426016 | tf_op jit(solution)/shard_map/ppermute | solution.py:797
  60.8 8.5 %collective-permute-done.5.refs_7_ = bf16[208,1024]{1,0:T(8,128)(2,1)} collective-permute-done((bf16[208,1024]{1,0:T(8,128)(2,1)}, bf16[208,1024]{1,0:T(8,128)(2,1)}, u32[]{:S(2)}, u32[]{:S(2)}) %collective-permute-start.5) | collective-permute-done | bytes 426016 | tf_op jit(solution)/shard_map/ppermute | solution.py:797
  69.5 6.4 %collective-permute-done.9.refs_9_ = bf16[208,1024]{1,0:T(8,128)(2,1)S(1)} collective-permute-done((bf16[208,1024]{1,0:T(8,128)(2,1)}, bf16[208,1024]{1,0:T(8,128)(2,1)S(1)}, u32[]{:S(2)}, u32[]{:S(2)}) %collective-permute-start.9) | collective-permute-done | bytes 426016 | tf_op jit(solution)/shard_map/ppermute | solution.py:797
  76.6 4.8 collective-permute-start.14
  89.1 23.9 %attention_in.1 = (bf16[1536,1024]{1,0:T(8,128)(2,1)}, bf16[1024,384]{1,0:T(8,128)(2,1)}, bf16[1024,128]{1,0:T(8,128)(2,1)}, bf16[1024,128]{1,0:T(8,128)(2,1)}, ...) custom-call(s32[4]{0:T(128)} %gather_fusion, ...), custom_call_target="tpu_custom_call" | custom-call | flops 1000000 | bytes 1000000 | tf_op jit(solution)/shard_map/attention_in/pallas_call | solution.py:273
  113.1 10.3 %collective-permute-done.12.refs_3_ = bf16[3,192,1280]{2,1,0:T(8,128)(2,1)} collective-permute-done((bf16[3,192,1280]{2,1,0:T(8,128)(2,1)}, bf16[3,192,1280]{2,1,0:T(8,128)(2,1)}, u32[]{:S(2)}, u32[]{:S(2)}) %collective-permute-start.12) | collective-permute-done | bytes 1474592 | tf_op jit(solution)/shard_map/ppermute | solution.py:806
  131.1 15.8 %collective-permute-done.19 = bf16[256,1536]{1,0:T(8,128)(2,1)S(1)} collective-permute-done((bf16[256,1536]{1,0:T(8,128)(2,1)S(1)}, bf16[256,1536]{1,0:T(8,128)(2,1)S(1)}, u32[]{:S(2)}, u32[]{:S(2)}) %collective-permute-start.19) | collective-permute-done | bytes 786464 | tf_op jit(solution)/shard_map/ppermute | solution.py:791
  152.2 11.2 %collective-permute-done.24.refs_5_ = bf16[3,192,1280]{2,1,0:T(8,128)(2,1)S(1)} collective-permute-done((bf16[3,192,1280]{2,1,0:T(8,128)(2,1)}, bf16[3,192,1280]{2,1,0:T(8,128)(2,1)S(1)}, u32[]{:S(2)}, u32[]{:S(2)}) %collective-permute-start.24) | collective-permute-done | bytes 1474592 | tf_op jit(solution)/shard_map/ppermute | solution.py:809
  163.3 5.8 %collective-permute-done.27.refs_11_ = bf16[256,1536]{1,0:T(8,128)(2,1)S(1)} collective-permute-done((bf16[256,1536]{1,0:T(8,128)(2,1)S(1)}, bf16[256,1536]{1,0:T(8,128)(2,1)S(1)}, u32[]{:S(2)}, u32[]{:S(2)}) %collective-permute-start.27) | collective-permute-done | bytes 786464 | tf_op jit(solution)/shard_map/ppermute | solution.py:791
  169.1 15.0 %collective-permute-done.28.refs_12_ = bf16[256,1536]{1,0:T(8,128)(2,1)S(1)} collective-permute-done((bf16[256,1536]{1,0:T(8,128)(2,1)S(1)}, bf16[256,1536]{1,0:T(8,128)(2,1)S(1)}, u32[]{:S(2)}, u32[]{:S(2)}) %collective-permute-start.28) | collective-permute-done | bytes 786464 | tf_op jit(solution)/shard_map/ppermute | solution.py:797
  190.2 47.9 %feed_forward.2 = (bf16[3,2,384,1280]{3,2,1,0:T(8,128)(2,1)}, bf16[3,2,384,1280]{3,2,1,0:T(8,128)(2,1)}, bf16[1536,1024]{1,0:T(8,128)(2,1)}, bf16[1536,1024]{1,0...) custom-call(s32[4]{0:T(128)} %gather_fusion, s32[2]{0:T(128)} %pad_add_fusion.1.refs_1_.own, ...), custom_call_target="tpu_custom_call" | custom-call | flops 1000000 | bytes 1000000 | tf_op jit(solution)/shard_map/feed_forward/pallas_call | solution.py:697
  249.4 4.8 collective-permute-done.32.refs_7_
  255.9 4.6 fusion.15
  261.8 9.1 %collective-permute-done.23.refs_5_ = bf16[3,192,1024]{2,1,0:T(8,128)(2,1)} collective-permute-done((bf16[3,192,1024]{2,1,0:T(8,128)(2,1)}, bf16[3,192,1024]{2,1,0:T(8,128)(2,1)}, u32[]{:S(2)}, u32[]{:S(2)}) %collective-permute-start.23) | collective-permute-done | bytes 1179680 | tf_op jit(solution)/shard_map/ppermute | solution.py:809
  270.9 3.2 collective-permute-done.34.refs_9_
  274.1 29.9 %feed_forward.3 = (bf16[1024,1024]{1,0:T(8,128)(2,1)}, bf16[1024,1024]{1,0:T(8,128)(2,1)}, bf16[1024,1024]{1,0:T(8,128)(2,1)}, bf16[1024,1536]{1,0:T(8,128)(2,1)}, bf16[1024,1536]{1,0:T(8,128)(2,1)}) custom-call(s32[4]{0:T(128)} %gather_fusion, s32[2]{0:T(128)} %pad_add_fusion.1.refs_1_.own, bf16[3,192,1024]{2,1,0:T(8,128)(2,1)} %copy-done.8, ...), custom_call_target="tpu_custom_call" | custom-call | flops 1000000 | bytes 1000000 | tf_op jit(solution)/shard_map/feed_forward/pallas_call | solution.py:697
  304.0 4.7 all-to-all-start
  311.2 15.3 %last_weights.1 = (bf16[2,384,1024]{2,1,0:T(8,128)(2,1)}, bf16[2,384,1024]{2,1,0:T(8,128)(2,1)}, bf16[2,384,1024]{2,1,0:T(8,128)(2,1)}, bf16[2,384,1024]{2,1,0:T...) custom-call(s32[2]{0:T(128)} %pad_add_fusion.1.refs_1_.own, ...), custom_call_target="tpu_custom_call" | custom-call | flops 1000000 | bytes 1000000 | tf_op jit(solution)/shard_map/last_weights/pallas_call | solution.py:523
  326.4 3.9 fusion.2
  330.4 13.7 %collective-permute-done.37 = bf16[3,2,96,1280]{3,2,1,0:T(8,128)(2,1)} collective-permute-done((bf16[3,2,96,1280]{3,2,1,0:T(8,128)(2,1)S(1)}, bf16[3,2,96,1280]{3,2,1,0:T(8,128)(2,1)}, u32[]{:S(2)}, u32[]{:S(2)}) %collective-permute-start.37) | collective-permute-done | bytes 1474592 | tf_op jit(solution)/shard_map/ppermute | solution.py:806
  352.6 18.1 %collective-permute-done.38.far = bf16[256,1536]{1,0:T(8,128)(2,1)S(1)} collective-permute-done((bf16[256,1536]{1,0:T(8,128)(2,1)S(1)}, bf16[256,1536]{1,0:T(8,128)(2,1)S(1)}, u32[]{:S(2)}, u32[]{:S(2)}) %collective-permute-start.38) | collective-permute-done | bytes 786464 | tf_op jit(solution)/shard_map/ppermute | solution.py:791
  371.6 4.7 all-to-all-start.1
  381.0 4.5 add_planes.1
  386.9 22.0 %attention_out.1 = (bf16[1024,384]{1,0:T(8,128)(2,1)}, bf16[2,1024,128]{2,1,0:T(8,128)(2,1)}, bf16[1536,768]{1,0:T(8,128)(2,1)}) custom-call(s32[2]{0:T(128)} %pad_add_fusion.refs_1_.own, bf16[256,1536]{1,0:T(8,128)(2,1)} %copy-done.16, bf16[256,1536]{1,0:T(8,128)(2,1)} %copy-done.25, bf16[256,1536]{1,0:T(8,128)(2,1)} %collective-permute-done.39.other_near, ...), custom_call_target="tpu_custom_call" | custom-call | flops 1000000 | bytes 1000000 | tf_op jit(solution)/shard_map/attention_out/pallas_call | solution.py:360
  408.9 3.0 collective-permute-done.47
  417.9 10.3 %projection_out.1 = (bf16[1536,256]{1,0:T(8,128)(2,1)}, bf16[256,1536]{1,0:T(8,128)(2,1)}, bf16[256,1536]{1,0:T(8,128)(2,1)}, bf16[256,1536]{1,0:T(8,128)(2,1)}, bf16[256,1536]{1,0:T(8,128)(2,1)}) custom-call(s32[2]{0:T(128)} %pad_add_fusion.refs_1_.own, bf16[1024,384]{1,0:T(8,128)(2,1)} %get-tuple-element.216.grad_q, ...), custom_call_target="tpu_custom_call" | custom-call | flops 1000000 | bytes 1000000 | tf_op jit(solution)/shard_map/projection_out/pallas_call | solution.py:473
  428.2 8.6 %collective-permute-done.45 = bf16[3,2,96,1024]{3,2,1,0:T(8,128)(2,1)} collective-permute-done((bf16[3,2,96,1024]{3,2,1,0:T(8,128)(2,1)}, bf16[3,2,96,1024]{3,2,1,0:T(8,128)(2,1)}, u32[]{:S(2)}, u32[]{:S(2)}) %collective-permute-start.45) | collective-permute-done | bytes 1179680 | tf_op jit(solution)/shard_map/ppermute | solution.py:809
  444.1 2.9 fusion.5
  452.8 3.4 fusion.1
  457.5 4.5 all-to-all-start.2
  466.7 3.8 convert_reduce_fusion
  470.5 17.4 %collective-permute-done.55 = bf16[3,2,96,1024]{3,2,1,0:T(8,128)(2,1)} collective-permute-done((bf16[3,2,96,1024]{3,2,1,0:T(8,128)(2,1)}, bf16[3,2,96,1024]{3,2,1,0:T(8,128)(2,1)}, u32[]{:S(2)}, u32[]{:S(2)}) %collective-permute-start.55) | collective-permute-done | bytes 1179680 | tf_op jit(solution)/shard_map/ppermute | solution.py:809
  492.6 3.1 collective-permute-start.58
  499.0 4.3 all-to-all-start.3
  505.8 2.8 collective-permute-done.57
  514.8 3.9 collective-permute-done.54
  523.0 3.5 all-to-all-start.4
  526.5 5.0 fusion.12
  531.5 4.8 assemble.1
  (253 shorter events, 112.0 us)
Async XLA Ops:
  7.3 42.0 %collective-permute-start.7 = (bf16[3,192,1280]{2,1,0:T(8,128)(2,1)}, bf16[3,192,1280]{2,1,0:T(8,128)(2,1)}, u32[]{:S(2)}, u32[]{:S(2)}) collective-permute-start(bf16[3,192,1280]{2,1,0:T(8,128)(2,1)} %cut_columns.4), channel_id=1, source_target_pairs={{0,1},{9,8},{2,3},{11,10},{4,5},{13,12},{6,7},{15,14},{16,17},{25,... | collective-permute-start | bytes 4423688 | tf_op jit(solution)/shard_map/ppermute | solution.py:803
  17.3 30.0 %collective-permute-start.8 = (bf16[256,1536]{1,0:T(8,128)(2,1)S(1)}, bf16[256,1536]{1,0:T(8,128)(2,1)}, u32[]{:S(2)}, u32[]{:S(2)}) collective-permute-start(bf16[256,1536]{1,0:T(8,128)(2,1)S(1)} %bitcast.215), channel_id=1, source_target_pairs={{0,16},{16,0},{1,17},{17,1},{2,18},{18,2},{3,19},{19,3},{4,20},{20... | collective-permute-start | bytes 2359304 | tf_op jit(solution)/shard_map/ppermute | solution.py:791
  18.8 26.9 %collective-permute-start = (bf16[208,1024]{1,0:T(8,128)(2,1)S(1)}, bf16[208,1024]{1,0:T(8,128)(2,1)}, u32[]{:S(2)}, u32[]{:S(2)}) collective-permute-start(bf16[208,1024]{1,0:T(8,128)(2,1)S(1)} %fusion.25.refs_2_), channel_id=1, source_target_pairs={{0,2},{2,6},{4,0},{6,4},{1,3},{3,7},{5,1},{7,5},{8,10},{10,14},{12... | collective-permute-start | bytes 1277960 | tf_op jit(solution)/shard_map/ppermute | solution.py:806
  27.5 21.7 %collective-permute-start.6 = (bf16[208,1024]{1,0:T(8,128)(2,1)}, bf16[208,1024]{1,0:T(8,128)(2,1)}, u32[]{:S(2)}, u32[]{:S(2)}) collective-permute-start(bf16[208,1024]{1,0:T(8,128)(2,1)} %collective-permute-done.1.refs_4_), channel_id=1, source_target_pairs={{0,1},{1,0},{2,3},{3,2},{4,5},{5,4},{6,7},{7,6},{8,9},{9,8},{10,11... | collective-permute-start | bytes 1277960 | tf_op jit(solution)/shard_map/ppermute | solution.py:797
  27.6 21.7 %collective-permute-start.3 = (bf16[208,1024]{1,0:T(8,128)(2,1)}, bf16[208,1024]{1,0:T(8,128)(2,1)}, u32[]{:S(2)}, u32[]{:S(2)}) collective-permute-start(bf16[208,1024]{1,0:T(8,128)(2,1)} %collective-permute-done.1.refs_4_), channel_id=1, source_target_pairs={{2,0},{6,2},{0,4},{4,6},{3,1},{7,3},{1,5},{5,7},{10,8},{14,10},{8,... | collective-permute-start | bytes 1277960 | tf_op jit(solution)/shard_map/ppermute | solution.py:809
  45.7 30.9 %collective-permute-start.11 = (bf16[256,1536]{1,0:T(8,128)(2,1)S(1)}, bf16[256,1536]{1,0:T(8,128)(2,1)}, u32[]{:S(2)}, u32[]{:S(2)}) collective-permute-start(bf16[256,1536]{1,0:T(8,128)(2,1)S(1)} %bitcast.211), channel_id=1, source_target_pairs={{0,16},{16,0},{1,17},{17,1},{2,18},{18,2},{3,19},{19,3},{4,20},{20... | collective-permute-start | bytes 2359304 | tf_op jit(solution)/shard_map/ppermute | solution.py:791
  49.2 20.1 %collective-permute-start.5 = (bf16[208,1024]{1,0:T(8,128)(2,1)}, bf16[208,1024]{1,0:T(8,128)(2,1)}, u32[]{:S(2)}, u32[]{:S(2)}) collective-permute-start(bf16[208,1024]{1,0:T(8,128)(2,1)} %collective-permute-done.refs_3_), channel_id=1, source_target_pairs={{0,1},{1,0},{2,3},{3,2},{4,5},{5,4},{6,7},{7,6},{8,9},{9,8},{10,11... | collective-permute-start | bytes 1277960 | tf_op jit(solution)/shard_map/ppermute | solution.py:797
  50.6 25.4 %collective-permute-start.9 = (bf16[208,1024]{1,0:T(8,128)(2,1)}, bf16[208,1024]{1,0:T(8,128)(2,1)S(1)}, u32[]{:S(2)}, u32[]{:S(2)}) collective-permute-start(bf16[208,1024]{1,0:T(8,128)(2,1)} %collective-permute-done.3.refs_5_), channel_id=1, source_target_pairs={{0,1},{1,0},{2,3},{3,2},{4,5},{5,4},{6,7},{7,6},{8,9},{9,8},{10,11... | collective-permute-start | bytes 1277960 | tf_op jit(solution)/shard_map/ppermute | solution.py:797
  53.9 28.2 %collective-permute-start.10 = (bf16[256,1536]{1,0:T(8,128)(2,1)}, bf16[256,1536]{1,0:T(8,128)(2,1)S(1)}, u32[]{:S(2)}, u32[]{:S(2)}) collective-permute-start(bf16[256,1536]{1,0:T(8,128)(2,1)} %collective-permute-done.8.refs_11_), channel_id=1, source_target_pairs={{0,8},{8,0},{1,9},{9,1},{2,10},{10,2},{3,11},{11,3},{4,12},{12,4},... | collective-permute-start | bytes 2359304 | tf_op jit(solution)/shard_map/ppermute | solution.py:794
  60.8 62.6 %collective-permute-start.12 = (bf16[3,192,1280]{2,1,0:T(8,128)(2,1)}, bf16[3,192,1280]{2,1,0:T(8,128)(2,1)}, u32[]{:S(2)}, u32[]{:S(2)}) collective-permute-start(bf16[3,192,1280]{2,1,0:T(8,128)(2,1)} %broadcast_select_fusion.refs_2_), channel_id=1, source_target_pairs={{0,2},{2,6},{4,0},{6,4},{1,3},{3,7},{5,1},{7,5},{8,10},{10,14},{12... | collective-permute-start | bytes 4423688 | tf_op jit(solution)/shard_map/ppermute | solution.py:806
  69.3 54.1 %collective-permute-start.13 = (bf16[3,192,1280]{2,1,0:T(8,128)(2,1)}, bf16[3,192,1280]{2,1,0:T(8,128)(2,1)}, u32[]{:S(2)}, u32[]{:S(2)}) collective-permute-start(bf16[3,192,1280]{2,1,0:T(8,128)(2,1)} %broadcast_select_fusion.refs_2_), channel_id=1, source_target_pairs={{2,0},{6,2},{0,4},{4,6},{3,1},{7,3},{1,5},{5,7},{10,8},{14,10},{8,... | collective-permute-start | bytes 4423688 | tf_op jit(solution)/shard_map/ppermute | solution.py:809
  76.0 47.4 %collective-permute-start.16 = (bf16[3,192,1280]{2,1,0:T(8,128)(2,1)}, bf16[3,192,1280]{2,1,0:T(8,128)(2,1)}, u32[]{:S(2)}, u32[]{:S(2)}) collective-permute-start(bf16[3,192,1280]{2,1,0:T(8,128)(2,1)} %broadcast_select_fusion.refs_2_), channel_id=1, source_target_pairs={{0,8},{8,0},{1,9},{9,1},{2,10},{10,2},{3,11},{11,3},{4,12},{12,4},... | collective-permute-start | bytes 4423688 | tf_op jit(solution)/shard_map/ppermute | solution.py:794
  76.6 46.8 %collective-permute-start.14 = (bf16[3,192,1024]{2,1,0:T(8,128)(2,1)}, bf16[3,192,1024]{2,1,0:T(8,128)(2,1)}, u32[]{:S(2)}, u32[]{:S(2)}) collective-permute-start(bf16[3,192,1024]{2,1,0:T(8,128)(2,1)} %cut_columns.6), channel_id=1, source_target_pairs={{0,1},{9,8},{2,3},{11,10},{4,5},{13,12},{6,7},{15,14},{16,17},{25,... | collective-permute-start | bytes 3538952 | tf_op jit(solution)/shard_map/ppermute | solution.py:803
  82.1 30.9 %collective-permute-start.15 = (bf16[256,1536]{1,0:T(8,128)(2,1)S(1)}, bf16[256,1536]{1,0:T(8,128)(2,1)S(1)}, u32[]{:S(2)}, u32[]{:S(2)}) collective-permute-start(bf16[256,1536]{1,0:T(8,128)(2,1)S(1)} %bitcast.212), channel_id=1, source_target_pairs={{0,1},{1,0},{2,3},{3,2},{4,5},{5,4},{6,7},{7,6},{8,9},{9,8},{10,11... | collective-permute-start | bytes 2359304 | tf_op jit(solution)/shard_map/ppermute | solution.py:797
  127.3 19.6 %collective-permute-start.19 = (bf16[256,1536]{1,0:T(8,128)(2,1)S(1)}, bf16[256,1536]{1,0:T(8,128)(2,1)S(1)}, u32[]{:S(2)}, u32[]{:S(2)}) collective-permute-start(bf16[256,1536]{1,0:T(8,128)(2,1)S(1)} %add_convert_fusion.4), channel_id=1, source_target_pairs={{0,16},{16,0},{1,17},{17,1},{2,18},{18,2},{3,19},{19,3},{4,20},{20... | collective-permute-start | bytes 2359304 | tf_op jit(solution)/shard_map/ppermute | solution.py:791
  127.9 19.5 %collective-permute-start.20 = (bf16[256,1536]{1,0:T(8,128)(2,1)}, bf16[256,1536]{1,0:T(8,128)(2,1)S(1)}, u32[]{:S(2)}, u32[]{:S(2)}) collective-permute-start(bf16[256,1536]{1,0:T(8,128)(2,1)} %collective-permute-done.11.refs_15_), channel_id=1, source_target_pairs={{0,1},{1,0},{2,3},{3,2},{4,5},{5,4},{6,7},{7,6},{8,9},{9,8},{10,11... | collective-permute-start | bytes 2359304 | tf_op jit(solution)/shard_map/ppermute | solution.py:797
  129.3 34.0 %collective-permute-start.24 = (bf16[3,192,1280]{2,1,0:T(8,128)(2,1)}, bf16[3,192,1280]{2,1,0:T(8,128)(2,1)S(1)}, u32[]{:S(2)}, u32[]{:S(2)}) collective-permute-start(bf16[3,192,1280]{2,1,0:T(8,128)(2,1)} %collective-permute-done.13.refs_4_), channel_id=1, source_target_pairs={{2,0},{6,2},{0,4},{4,6},{3,1},{7,3},{1,5},{5,7},{10,8},{14,10},{8,... | collective-permute-start | bytes 4423688 | tf_op jit(solution)/shard_map/ppermute | solution.py:809
  148.6 20.5 %collective-permute-start.27 = (bf16[256,1536]{1,0:T(8,128)(2,1)S(1)}, bf16[256,1536]{1,0:T(8,128)(2,1)S(1)}, u32[]{:S(2)}, u32[]{:S(2)}) collective-permute-start(bf16[256,1536]{1,0:T(8,128)(2,1)S(1)} %multiply_convert_fusion.refs_10_), channel_id=1, source_target_pairs={{0,16},{16,0},{1,17},{17,1},{2,18},{18,2},{3,19},{19,3},{4,20},{20... | collective-permute-start | bytes 2359304 | tf_op jit(solution)/shard_map/ppermute | solution.py:791
  150.2 34.0 %collective-permute-start.28 = (bf16[256,1536]{1,0:T(8,128)(2,1)S(1)}, bf16[256,1536]{1,0:T(8,128)(2,1)S(1)}, u32[]{:S(2)}, u32[]{:S(2)}) collective-permute-start(bf16[256,1536]{1,0:T(8,128)(2,1)S(1)} %multiply_convert_fusion.refs_10_), channel_id=1, source_target_pairs={{0,1},{1,0},{2,3},{3,2},{4,5},{5,4},{6,7},{7,6},{8,9},{9,8},{10,11... | collective-permute-start | bytes 2359304 | tf_op jit(solution)/shard_map/ppermute | solution.py:797
  151.7 33.5 %collective-permute-start.29 = (bf16[256,1536]{1,0:T(8,128)(2,1)S(1)}, bf16[256,1536]{1,0:T(8,128)(2,1)S(1)}, u32[]{:S(2)}, u32[]{:S(2)}) collective-permute-start(bf16[256,1536]{1,0:T(8,128)(2,1)S(1)} %multiply_convert_fusion.refs_10_), channel_id=1, source_target_pairs={{0,17},{1,16},{16,1},{17,0},{2,19},{3,18},{18,3},{19,2},{4,21},{5,... | collective-permute-start | bytes 2359304 | tf_op jit(solution)/shard_map/ppermute | solution.py:800
  152.2 38.0 %collective-permute-start.25 = (bf16[3,192,1280]{2,1,0:T(8,128)(2,1)}, bf16[3,192,1280]{2,1,0:T(8,128)(2,1)}, u32[]{:S(2)}, u32[]{:S(2)}) collective-permute-start(bf16[3,192,1280]{2,1,0:T(8,128)(2,1)} %collective-permute-done.12.refs_3_), channel_id=1, source_target_pairs={{0,8},{8,0},{1,9},{9,1},{2,10},{10,2},{3,11},{11,3},{4,12},{12,4},... | collective-permute-start | bytes 4423688 | tf_op jit(solution)/shard_map/ppermute | solution.py:794
  163.3 26.9 %collective-permute-start.26 = (bf16[3,192,1280]{2,1,0:T(8,128)(2,1)}, bf16[3,192,1280]{2,1,0:T(8,128)(2,1)}, u32[]{:S(2)}, u32[]{:S(2)}) collective-permute-start(bf16[3,192,1280]{2,1,0:T(8,128)(2,1)} %collective-permute-done.13.refs_4_), channel_id=1, source_target_pairs={{0,8},{8,0},{1,9},{9,1},{2,10},{10,2},{3,11},{11,3},{4,12},{12,4},... | collective-permute-start | bytes 4423688 | tf_op jit(solution)/shard_map/ppermute | solution.py:794
  186.2 54.4 %collective-permute-start.21 = (bf16[3,192,1024]{2,1,0:T(8,128)(2,1)S(1)}, bf16[3,192,1024]{2,1,0:T(8,128)(2,1)}, u32[]{:S(2)}, u32[]{:S(2)}) collective-permute-start(bf16[3,192,1024]{2,1,0:T(8,128)(2,1)S(1)} %broadcast_select_fusion.1.refs_2_), channel_id=1, source_target_pairs={{0,2},{2,6},{4,0},{6,4},{1,3},{3,7},{5,1},{7,5},{8,10},{10,14},{12... | collective-permute-start | bytes 3538952 | tf_op jit(solution)/shard_map/ppermute | solution.py:806
  187.5 53.2 %collective-permute-start.22 = (bf16[3,192,1024]{2,1,0:T(8,128)(2,1)S(1)}, bf16[3,192,1024]{2,1,0:T(8,128)(2,1)}, u32[]{:S(2)}, u32[]{:S(2)}) collective-permute-start(bf16[3,192,1024]{2,1,0:T(8,128)(2,1)S(1)} %broadcast_select_fusion.1.refs_2_), channel_id=1, source_target_pairs={{2,0},{6,2},{0,4},{4,6},{3,1},{7,3},{1,5},{5,7},{10,8},{14,10},{8,... | collective-permute-start | bytes 3538952 | tf_op jit(solution)/shard_map/ppermute | solution.py:809
  240.7 15.2 %collective-permute-start.35 = (bf16[3,2,384,1280]{3,2,1,0:T(8,128)(2,1)}, bf16[3,2,384,1280]{3,2,1,0:T(8,128)(2,1)}, u32[]{:S(2)}, u32[]{:S(2)}) collective-permute-start(bf16[3,2,384,1280]{3,2,1,0:T(8,128)(2,1)} %get-tuple-element.172), channel_id=1, source_target_pairs={{0,8},{8,0},{1,9},{9,1},{2,10},{10,2},{3,11},{11,3},{4,12},{12,4},... | collective-permute-start | bytes 17694728 | tf_op jit(solution)/shard_map/ppermute | solution.py:794
  241.8 29.1 %collective-permute-start.23 = (bf16[3,192,1024]{2,1,0:T(8,128)(2,1)}, bf16[3,192,1024]{2,1,0:T(8,128)(2,1)}, u32[]{:S(2)}, u32[]{:S(2)}) collective-permute-start(bf16[3,192,1024]{2,1,0:T(8,128)(2,1)} %collective-permute-done.22.refs_4_), channel_id=1, source_target_pairs={{2,0},{6,2},{0,4},{4,6},{3,1},{7,3},{1,5},{5,7},{10,8},{14,10},{8,... | collective-permute-start | bytes 3538952 | tf_op jit(solution)/shard_map/ppermute | solution.py:809
  260.5 43.5 %collective-permute-start.36 = (bf16[3,2,96,1280]{3,2,1,0:T(8,128)(2,1)}, bf16[3,2,96,1280]{3,2,1,0:T(8,128)(2,1)}, u32[]{:S(2)}, u32[]{:S(2)}) collective-permute-start(bf16[3,2,96,1280]{3,2,1,0:T(8,128)(2,1)} %get-tuple-element.258), channel_id=1, source_target_pairs={{2,0},{6,2},{0,4},{4,6},{3,1},{7,3},{1,5},{5,7},{10,8},{14,10},{8,... | collective-permute-start | bytes 4423688 | tf_op jit(solution)/shard_map/ppermute | solution.py:809
  304.0 42.3 %all-to-all-start = ((bf16[4,256,1536]{2,1,0:T(8,128)(2,1)}), bf16[4,256,1536]{2,1,0:T(8,128)(2,1)}, u32[]{:S(2)}, u32[]{:S(2)}) async-start(bf16[4,256,1536]{2,1,0:T(8,128)(2,1)} %bitcast.227), calls=%async_computation | async-start | bytes 6291456 | tf_op jit(solution)/shard_map/all_to_all | solution.py:812
  308.7 35.4 %collective-permute-start.37 = (bf16[3,2,96,1280]{3,2,1,0:T(8,128)(2,1)S(1)}, bf16[3,2,96,1280]{3,2,1,0:T(8,128)(2,1)}, u32[]{:S(2)}, u32[]{:S(2)}) collective-permute-start(bf16[3,2,96,1280]{3,2,1,0:T(8,128)(2,1)S(1)} %get-tuple-element.259), channel_id=1, source_target_pairs={{0,2},{2,6},{4,0},{6,4},{1,3},{3,7},{5,1},{7,5},{8,10},{10,14},{12... | collective-permute-start | bytes 4423688 | tf_op jit(solution)/shard_map/ppermute | solution.py:806
  351.3 19.3 %collective-permute-start.38 = (bf16[256,1536]{1,0:T(8,128)(2,1)S(1)}, bf16[256,1536]{1,0:T(8,128)(2,1)S(1)}, u32[]{:S(2)}, u32[]{:S(2)}) collective-permute-start(bf16[256,1536]{1,0:T(8,128)(2,1)S(1)} %fusion.41.near), channel_id=1, source_target_pairs={{0,16},{16,0},{1,17},{17,1},{2,18},{18,2},{3,19},{19,3},{4,20},{20... | collective-permute-start | bytes 2359304 | tf_op jit(solution)/shard_map/ppermute | solution.py:791
  352.0 29.0 %collective-permute-start.41 = (bf16[2,384,1024]{2,1,0:T(8,128)(2,1)}, bf16[2,384,1024]{2,1,0:T(8,128)(2,1)}, u32[]{:S(2)}, u32[]{:S(2)}) collective-permute-start(bf16[2,384,1024]{2,1,0:T(8,128)(2,1)} %get-tuple-element.197), channel_id=1, source_target_pairs={{0,8},{8,0},{1,9},{9,1},{2,10},{10,2},{3,11},{11,3},{4,12},{12,4},... | collective-permute-start | bytes 4718600 | tf_op jit(solution)/shard_map/ppermute | solution.py:794
  352.0 29.0 %collective-permute-start.42 = (bf16[2,384,1024]{2,1,0:T(8,128)(2,1)}, bf16[2,384,1024]{2,1,0:T(8,128)(2,1)}, u32[]{:S(2)}, u32[]{:S(2)}) collective-permute-start(bf16[2,384,1024]{2,1,0:T(8,128)(2,1)} %get-tuple-element.198), channel_id=1, source_target_pairs={{0,8},{8,0},{1,9},{9,1},{2,10},{10,2},{3,11},{11,3},{4,12},{12,4},... | collective-permute-start | bytes 4718600 | tf_op jit(solution)/shard_map/ppermute | solution.py:794
  352.6 28.5 %collective-permute-start.43 = (bf16[2,384,1024]{2,1,0:T(8,128)(2,1)}, bf16[2,384,1024]{2,1,0:T(8,128)(2,1)}, u32[]{:S(2)}, u32[]{:S(2)}) collective-permute-start(bf16[2,384,1024]{2,1,0:T(8,128)(2,1)} %get-tuple-element.199), channel_id=1, source_target_pairs={{0,8},{8,0},{1,9},{9,1},{2,10},{10,2},{3,11},{11,3},{4,12},{12,4},... | collective-permute-start | bytes 4718600 | tf_op jit(solution)/shard_map/ppermute | solution.py:794
  371.6 46.3 %all-to-all-start.1 = ((bf16[4,256,1536]{2,1,0:T(8,128)(2,1)}), bf16[4,256,1536]{2,1,0:T(8,128)(2,1)}, u32[]{:S(2)}, u32[]{:S(2)}) async-start(bf16[4,256,1536]{2,1,0:T(8,128)(2,1)} %bitcast.226), calls=%async_computation.1 | async-start | bytes 6291456 | tf_op jit(solution)/shard_map/all_to_all | solution.py:812
  376.4 35.5 %collective-permute-start.47 = (bf16[3,2,96,1280]{3,2,1,0:T(8,128)(2,1)}, bf16[3,2,96,1280]{3,2,1,0:T(8,128)(2,1)}, u32[]{:S(2)}, u32[]{:S(2)}) collective-permute-start(bf16[3,2,96,1280]{3,2,1,0:T(8,128)(2,1)} %fusion.2), channel_id=1, source_target_pairs={{2,0},{6,2},{0,4},{4,6},{3,1},{7,3},{1,5},{5,7},{10,8},{14,10},{8,... | collective-permute-start | bytes 4423688 | tf_op jit(solution)/shard_map/ppermute | solution.py:809
  385.5 51.2 %collective-permute-start.45 = (bf16[3,2,96,1024]{3,2,1,0:T(8,128)(2,1)}, bf16[3,2,96,1024]{3,2,1,0:T(8,128)(2,1)}, u32[]{:S(2)}, u32[]{:S(2)}) collective-permute-start(bf16[3,2,96,1024]{3,2,1,0:T(8,128)(2,1)} %get-tuple-element.204), channel_id=1, source_target_pairs={{2,0},{6,2},{0,4},{4,6},{3,1},{7,3},{1,5},{5,7},{10,8},{14,10},{8,... | collective-permute-start | bytes 3538952 | tf_op jit(solution)/shard_map/ppermute | solution.py:809
  414.2 34.8 %collective-permute-start.48 = (bf16[2,2,4,48,768]{4,3,1,0,2:T(8,128)(2,1)}, bf16[2,2,4,48,768]{4,3,1,0,2:T(8,128)(2,1)}, u32[]{:S(2)}, u32[]{:S(2)}) collective-permute-start(bf16[2,2,4,48,768]{4,3,1,0,2:T(8,128)(2,1)} %copy_bitcast_fusion), channel_id=1, source_target_pairs={{0,1},{1,0},{2,3},{3,2},{4,5},{5,4},{6,7},{7,6},{8,9},{9,8},{10,11... | collective-permute-start | bytes 3538952 | tf_op jit(solution)/shard_map/ppermute | solution.py:797
  416.1 76.5 %collective-permute-start.53 = (bf16[3,2,96,1024]{3,2,1,0:T(8,128)(2,1)}, bf16[3,2,96,1024]{3,2,1,0:T(8,128)(2,1)}, u32[]{:S(2)}, u32[]{:S(2)}) collective-permute-start(bf16[3,2,96,1024]{3,2,1,0:T(8,128)(2,1)} %get-tuple-element.203), channel_id=1, source_target_pairs={{0,2},{2,6},{4,0},{6,4},{1,3},{3,7},{5,1},{7,5},{8,10},{10,14},{12... | collective-permute-start | bytes 3538952 | tf_op jit(solution)/shard_map/ppermute | solution.py:806
  446.9 41.0 %collective-permute-start.55 = (bf16[3,2,96,1024]{3,2,1,0:T(8,128)(2,1)}, bf16[3,2,96,1024]{3,2,1,0:T(8,128)(2,1)}, u32[]{:S(2)}, u32[]{:S(2)}) collective-permute-start(bf16[3,2,96,1024]{3,2,1,0:T(8,128)(2,1)} %fusion.5), channel_id=1, source_target_pairs={{2,0},{6,2},{0,4},{4,6},{3,1},{7,3},{1,5},{5,7},{10,8},{14,10},{8,... | collective-permute-start | bytes 3538952 | tf_op jit(solution)/shard_map/ppermute | solution.py:809
  451.0 39.9 %collective-permute-start.50 = (bf16[256,1536]{1,0:T(8,128)(2,1)}, bf16[256,1536]{1,0:T(8,128)(2,1)}, u32[]{:S(2)}, u32[]{:S(2)}) collective-permute-start(bf16[256,1536]{1,0:T(8,128)(2,1)} %add_convert_fusion.3), channel_id=1, source_target_pairs={{0,16},{16,0},{1,17},{17,1},{2,18},{18,2},{3,19},{19,3},{4,20},{20... | collective-permute-start | bytes 2359304 | tf_op jit(solution)/shard_map/ppermute | solution.py:791
  457.5 41.6 %all-to-all-start.2 = ((bf16[4,3,48,1280]{3,2,1,0:T(8,128)(2,1)}), bf16[4,3,48,1280]{3,2,1,0:T(8,128)(2,1)}, u32[]{:S(2)}, u32[]{:S(2)}) async-start(bf16[4,3,48,1280]{3,2,1,0:T(8,128)(2,1)} %bitcast.216), calls=%async_computation.2 | async-start | bytes 2949120 | tf_op jit(solution)/shard_map/all_to_all | solution.py:812
  462.5 26.3 %collective-permute-start.56 = (bf16[2,2,4,48,256]{4,3,1,0,2:T(8,128)(2,1)}, bf16[2,2,4,48,256]{4,3,1,0,2:T(8,128)(2,1)S(1)}, u32[]{:S(2)}, u32[]{:S(2)}) collective-permute-start(bf16[2,2,4,48,256]{4,3,1,0,2:T(8,128)(2,1)} %copy_bitcast_fusion.1), channel_id=1, source_target_pairs={{0,1},{1,0},{2,3},{3,2},{4,5},{5,4},{6,7},{7,6},{8,9},{9,8},{10,11... | collective-permute-start | bytes 1179656 | tf_op jit(solution)/shard_map/ppermute | solution.py:797
  464.5 38.9 %collective-permute-start.49 = (bf16[256,1536]{1,0:T(8,128)(2,1)}, bf16[256,1536]{1,0:T(8,128)(2,1)}, u32[]{:S(2)}, u32[]{:S(2)}) collective-permute-start(bf16[256,1536]{1,0:T(8,128)(2,1)} %get-tuple-element.233), channel_id=1, source_target_pairs={{0,8},{8,0},{1,9},{9,1},{2,10},{10,2},{3,11},{11,3},{4,12},{12,4},... | collective-permute-start | bytes 2359304 | tf_op jit(solution)/shard_map/ppermute | solution.py:794
  487.9 20.8 %collective-permute-start.51 = (bf16[2,2,48,768]{3,2,1,0:T(8,128)(2,1)}, bf16[2,2,48,768]{3,2,1,0:T(8,128)(2,1)}, u32[]{:S(2)}, u32[]{:S(2)}) collective-permute-start(bf16[2,2,48,768]{3,2,1,0:T(8,128)(2,1)} %get-tuple-element.261), channel_id=1, source_target_pairs={{0,2},{2,6},{4,0},{6,4},{1,3},{3,7},{5,1},{7,5},{8,10},{10,14},{12... | collective-permute-start | bytes 884744 | tf_op jit(solution)/shard_map/ppermute | solution.py:806
  488.9 19.8 %collective-permute-start.52 = (bf16[2,2,48,768]{3,2,1,0:T(8,128)(2,1)}, bf16[2,2,48,768]{3,2,1,0:T(8,128)(2,1)}, u32[]{:S(2)}, u32[]{:S(2)}) collective-permute-start(bf16[2,2,48,768]{3,2,1,0:T(8,128)(2,1)} %get-tuple-element.260), channel_id=1, source_target_pairs={{2,0},{6,2},{0,4},{4,6},{3,1},{7,3},{1,5},{5,7},{10,8},{14,10},{8,... | collective-permute-start | bytes 884744 | tf_op jit(solution)/shard_map/ppermute | solution.py:809
  492.5 16.2 %collective-permute-start.57 = (bf16[2,2,48,256]{3,2,1,0:T(8,128)(2,1)}, bf16[2,2,48,256]{3,2,1,0:T(8,128)(2,1)}, u32[]{:S(2)}, u32[]{:S(2)}) collective-permute-start(bf16[2,2,48,256]{3,2,1,0:T(8,128)(2,1)} %get-tuple-element.271), channel_id=1, source_target_pairs={{0,2},{2,6},{4,0},{6,4},{1,3},{3,7},{5,1},{7,5},{8,10},{10,14},{12... | collective-permute-start | bytes 294920 | tf_op jit(solution)/shard_map/ppermute | solution.py:806
  492.6 16.1 %collective-permute-start.58 = (bf16[2,2,48,256]{3,2,1,0:T(8,128)(2,1)}, bf16[2,2,48,256]{3,2,1,0:T(8,128)(2,1)}, u32[]{:S(2)}, u32[]{:S(2)}) collective-permute-start(bf16[2,2,48,256]{3,2,1,0:T(8,128)(2,1)} %get-tuple-element.270), channel_id=1, source_target_pairs={{2,0},{6,2},{0,4},{4,6},{3,1},{7,3},{1,5},{5,7},{10,8},{14,10},{8,... | collective-permute-start | bytes 294920 | tf_op jit(solution)/shard_map/ppermute | solution.py:809
  499.0 19.6 %all-to-all-start.3 = ((bf16[4,3,48,1024]{3,2,1,0:T(8,128)(2,1)}), bf16[4,3,48,1024]{3,2,1,0:T(8,128)(2,1)}, u32[]{:S(2)}, u32[]{:S(2)}) async-start(bf16[4,3,48,1024]{3,2,1,0:T(8,128)(2,1)} %bitcast.221), calls=%async_computation.3 | async-start | bytes 2359296 | tf_op jit(solution)/shard_map/all_to_all | solution.py:812
  (58 other events, 792.0 us)

commit v5 on v4

--- a/solution.py
+++ b/solution.py
@@ -855,9 +855,9 @@
         own_rows = D // (seq_count * fsdp_count)
 
         def gather_sequence(own, then=()):
-            far = swap_x(own)
+            far = tie(swap_x(own), then)
             theirs = swap_c(own)
-            return [own, far, theirs, swap_c(tie(far, theirs, then))]
+            return [own, far, theirs, swap_c(tie(far, theirs))]
 
         def gather_plane(own):
             return [own, swap_x(own), swap_y(own), swap_xy(own)]
@@ -987,7 +987,7 @@
                     if steps
                 ]
 
-            def go(self, then=(), together=False):
+            def go(self, then=(), together=False, parts=False):
                 self.arrived, self.second, self.last = [], [], []
                 firsts = list(self.first)
                 for steps, sign, move in ((along, 1, ring), (against, -1, ring_back)):
@@ -1000,7 +1000,11 @@
                             running = self.block(plane_ahead(sign * left)) + came.astype(F32)
                             running = running.astype(BF)
                             self.second.append(running)
-                        came = move(running)
+                        if parts and sign < 0:
+                            self.parts = [move(running[:2]), move(running[2:])]
+                            came = self.parts
+                        else:
+                            came = move(running)
                         self.arrived.append(came)
                         self.last.append(came)
                 return self
@@ -1008,6 +1012,7 @@
             def total(self, then=()):
                 total = self.own
                 for came in tie(self.last, then):
+                    came = jnp.concatenate(came, axis=0) if isinstance(came, list) else came
                     total = total + came.astype(F32)
                 return total.astype(BF)
 
@@ -1072,17 +1077,17 @@
             then = () if last else chunk_theirs[1][:-1]
             scatters.append(chunk_scatter(keep, send, then))
             if not last:
-                scatters[0].go()
+                scatters[0].go(parts=True)
                 before[1] = scatters[0].first
         last_sent = (keep, send)
 
         grad_out = cotangent[0].astype(F32)
         grad_hidden_norm, grad_gain_mlp = rms_backward(
-            hidden, factor_mlp, gain_m, scatter_plane(totals[0], (last_sent, scatters[0].last[0], scatters[0].second))
+            hidden, factor_mlp, gain_m, scatter_plane(totals[0], (last_sent, scatters[0].second))
         )
         grad_hidden = grad_out + grad_hidden_norm
         grad_pieces = gather_sequence(
-            grad_hidden.astype(BF)
+            grad_hidden.astype(BF), (scatters[0].parts[0], scatters[0].last[0])
         )
         grad_q, grad_kv, d_early = attention_out(
             own_place,
@@ -1098,7 +1103,6 @@
             attended_t,
         )
         scatters[1].go()
-        d_early = tie(d_early, scatters[0].last[-1])
 
         branch = trade(tie(totals[1], grad_pieces[1]).reshape(4, tok_rows, D), ("x", "y"))
 

time: 550 us -> 544 us (0.989)
  waiting for transfers between devices: 185 us -> 174 us
    ppermute x6, waiting for transfers between devices: 39.8 us -> 25.1 us  [swap_x(): return lax.ppermute(value, 'x', other)]
    ppermute x7, waiting for transfers between devices: 29.5 us -> 15.7 us  [ring(): return lax.ppermute(value, 'z', ring_perm)]
    all_to_all x5, waiting for transfers between devices: 2.26 us -> 12.6 us  [trade(): return lax.all_to_all(blocks, axes, split_axis=0, concat_axis=0, tiled=True)]
    ppermute x14 -> x15, waiting for transfers between devices: 62.9 us -> 69.2 us  [ring_back(): return lax.ppermute(value, 'z', [(j, i) for i, j in ring_perm])]
    ppermute x14 -> x15, starting transfers between devices: 23.3 us -> 24.5 us  [ring_back(): return lax.ppermute(value, 'z', [(j, i) for i, j in ring_perm])]
  transfers between devices with their start and end apart: 65 -> 66, of which waited for: 28 -> 26; matrix products, arithmetic and copies ran while one was open for 13% -> 14% of each run, Pallas kernels for 32% -> 32%
where the time goes in v5:
time: 544 us; the launch traced here: 535 us
  Pallas kernels  178 us (33%)
  waiting for transfers between devices  174 us (32%)
  starting transfers between devices  83.8 us (15%)
  other arithmetic  65.8 us (12%)
  local copies, waits for them, and re-layouts  22.6 us (4%)
  between operations  9.54 us (2%)
    pallas_call x2, Pallas kernels, feed_forward(): pl.pallas_call(functools.partial(feed_forward_body, planes, rows, first,...  77.9 us
    ppermute x15, waiting for transfers between devices, ring_back(): return lax.ppermute(value, 'z', [(j, i) for i, j in ring_perm])  69.2 us
    ppermute x9, waiting for transfers between devices, swap_y(): return lax.ppermute(value, 'y', other)  36.5 us
    ppermute x6, waiting for transfers between devices, swap_x(): return lax.ppermute(value, 'x', other)  25.1 us
    ppermute x15, starting transfers between devices, ring_back(): return lax.ppermute(value, 'z', [(j, i) for i, j in ring_perm])  24.5 us
    pallas_call x1, Pallas kernels, attention_in(): pl.pallas_call(functools.partial(attention_in_body, planes, rows), out_sh...  23.9 us
    pallas_call x1, Pallas kernels, attention_out(): pl.pallas_call(attention_out_body, out_shape=[jax.ShapeDtypeStruct((lengt...  22 us
    all_to_all x5, starting transfers between devices, trade(): return lax.all_to_all(blocks, axes, split_axis=0, concat_axis=0, tiled=True)  21.5 us
  transfers between devices with their start and end apart: 66, of which 26 were waited for; matrix products, arithmetic and copies ran while one was open for 14% of the time, Pallas kernels for 32%

profile of v5, /device:TPU:0, one launch (start us, length us, event | category | flops | bytes accessed | tf_op | source)
XLA Modules:
  0.0 534.6 jit_solution(12265889417482898412)
XLA Ops:
  2.0 5.3 cut_columns.4
  7.3 6.0 %collective-permute-start.7 = (bf16[3,192,1280]{2,1,0:T(8,128)(2,1)}, bf16[3,192,1280]{2,1,0:T(8,128)(2,1)}, u32[]{:S(2)}, u32[]{:S(2)}) collective-permute-start(bf16[3,192,1280]{2,1,0:T(8,128)(2,1)} %cut_columns.4), channel_id=1, source_target_pairs={{0,1},{9,8},{2,3},{11,10},{4,5},{13,12},{6,7},{15,14},{16,17},{25,... | collective-permute-start | bytes 4423688 | tf_op jit(solution)/shard_map/ppermute | solution.py:803
  14.7 2.6 collective-permute-start.1
  18.8 8.7 %collective-permute-done.1.refs_4_ = bf16[208,1024]{1,0:T(8,128)(2,1)} collective-permute-done((bf16[208,1024]{1,0:T(8,128)(2,1)S(1)}, bf16[208,1024]{1,0:T(8,128)(2,1)}, u32[]{:S(2)}, u32[]{:S(2)}) %collective-permute-start.1) | collective-permute-done | bytes 426016 | tf_op jit(solution)/shard_map/ppermute | solution.py:809
  27.6 3.5 collective-permute-start.3
  31.1 5.1 cut_columns.5
  36.2 4.6 cut_columns.6
  40.9 4.7 cut_columns.7
  50.6 3.3 collective-permute-start.9
  53.9 6.2 %collective-permute-done.4.refs_6_ = bf16[208,1024]{1,0:T(8,128)(2,1)S(1)} collective-permute-done((bf16[208,1024]{1,0:T(8,128)(2,1)S(1)}, bf16[208,1024]{1,0:T(8,128)(2,1)S(1)}, u32[]{:S(2)}, u32[]{:S(2)}) %collective-permute-start.4) | collective-permute-done | bytes 426016 | tf_op jit(solution)/shard_map/ppermute | solution.py:797
  60.8 8.4 %collective-permute-done.5.refs_7_ = bf16[208,1024]{1,0:T(8,128)(2,1)} collective-permute-done((bf16[208,1024]{1,0:T(8,128)(2,1)}, bf16[208,1024]{1,0:T(8,128)(2,1)}, u32[]{:S(2)}, u32[]{:S(2)}) %collective-permute-start.5) | collective-permute-done | bytes 426016 | tf_op jit(solution)/shard_map/ppermute | solution.py:797
  69.5 6.4 %collective-permute-done.9.refs_9_ = bf16[208,1024]{1,0:T(8,128)(2,1)S(1)} collective-permute-done((bf16[208,1024]{1,0:T(8,128)(2,1)}, bf16[208,1024]{1,0:T(8,128)(2,1)S(1)}, u32[]{:S(2)}, u32[]{:S(2)}) %collective-permute-start.9) | collective-permute-done | bytes 426016 | tf_op jit(solution)/shard_map/ppermute | solution.py:797
  76.6 4.9 collective-permute-start.14
  89.2 23.9 %attention_in.1 = (bf16[1536,1024]{1,0:T(8,128)(2,1)}, bf16[1024,384]{1,0:T(8,128)(2,1)}, bf16[1024,128]{1,0:T(8,128)(2,1)}, bf16[1024,128]{1,0:T(8,128)(2,1)}, ...) custom-call(s32[4]{0:T(128)} %gather_fusion, ...), custom_call_target="tpu_custom_call" | custom-call | flops 1000000 | bytes 1000000 | tf_op jit(solution)/shard_map/attention_in/pallas_call | solution.py:273
  113.2 10.2 %collective-permute-done.12.refs_3_ = bf16[3,192,1280]{2,1,0:T(8,128)(2,1)} collective-permute-done((bf16[3,192,1280]{2,1,0:T(8,128)(2,1)}, bf16[3,192,1280]{2,1,0:T(8,128)(2,1)}, u32[]{:S(2)}, u32[]{:S(2)}) %collective-permute-start.12) | collective-permute-done | bytes 1474592 | tf_op jit(solution)/shard_map/ppermute | solution.py:806
  131.1 15.8 %collective-permute-done.19 = bf16[256,1536]{1,0:T(8,128)(2,1)S(1)} collective-permute-done((bf16[256,1536]{1,0:T(8,128)(2,1)S(1)}, bf16[256,1536]{1,0:T(8,128)(2,1)S(1)}, u32[]{:S(2)}, u32[]{:S(2)}) %collective-permute-start.19) | collective-permute-done | bytes 786464 | tf_op jit(solution)/shard_map/ppermute | solution.py:791
  152.2 11.2 %collective-permute-done.24.refs_5_ = bf16[3,192,1280]{2,1,0:T(8,128)(2,1)S(1)} collective-permute-done((bf16[3,192,1280]{2,1,0:T(8,128)(2,1)}, bf16[3,192,1280]{2,1,0:T(8,128)(2,1)S(1)}, u32[]{:S(2)}, u32[]{:S(2)}) %collective-permute-start.24) | collective-permute-done | bytes 1474592 | tf_op jit(solution)/shard_map/ppermute | solution.py:809
  163.4 5.8 %collective-permute-done.27.refs_11_ = bf16[256,1536]{1,0:T(8,128)(2,1)S(1)} collective-permute-done((bf16[256,1536]{1,0:T(8,128)(2,1)S(1)}, bf16[256,1536]{1,0:T(8,128)(2,1)S(1)}, u32[]{:S(2)}, u32[]{:S(2)}) %collective-permute-start.27) | collective-permute-done | bytes 786464 | tf_op jit(solution)/shard_map/ppermute | solution.py:791
  169.2 15.0 %collective-permute-done.28.refs_12_ = bf16[256,1536]{1,0:T(8,128)(2,1)S(1)} collective-permute-done((bf16[256,1536]{1,0:T(8,128)(2,1)S(1)}, bf16[256,1536]{1,0:T(8,128)(2,1)S(1)}, u32[]{:S(2)}, u32[]{:S(2)}) %collective-permute-start.28) | collective-permute-done | bytes 786464 | tf_op jit(solution)/shard_map/ppermute | solution.py:797
  190.3 47.8 %feed_forward.2 = (bf16[3,2,384,1280]{3,2,1,0:T(8,128)(2,1)}, bf16[3,2,384,1280]{3,2,1,0:T(8,128)(2,1)}, bf16[1536,1024]{1,0:T(8,128)(2,1)}, bf16[1536,1024]{1,0...) custom-call(s32[4]{0:T(128)} %gather_fusion, s32[2]{0:T(128)} %pad_add_fusion.1.refs_1_.own, ...), custom_call_target="tpu_custom_call" | custom-call | flops 1000000 | bytes 1000000 | tf_op jit(solution)/shard_map/feed_forward/pallas_call | solution.py:697
  249.5 4.8 collective-permute-done.32.refs_7_
  256.0 4.7 fusion.15
  262.0 9.0 %collective-permute-done.23.refs_5_ = bf16[3,192,1024]{2,1,0:T(8,128)(2,1)} collective-permute-done((bf16[3,192,1024]{2,1,0:T(8,128)(2,1)}, bf16[3,192,1024]{2,1,0:T(8,128)(2,1)}, u32[]{:S(2)}, u32[]{:S(2)}) %collective-permute-start.23) | collective-permute-done | bytes 1179680 | tf_op jit(solution)/shard_map/ppermute | solution.py:809
  270.9 3.2 collective-permute-done.34.refs_9_
  274.1 30.1 %feed_forward.3 = (bf16[1024,1024]{1,0:T(8,128)(2,1)}, bf16[1024,1024]{1,0:T(8,128)(2,1)}, bf16[1024,1024]{1,0:T(8,128)(2,1)}, bf16[1024,1536]{1,0:T(8,128)(2,1)}, bf16[1024,1536]{1,0:T(8,128)(2,1)}) custom-call(s32[4]{0:T(128)} %gather_fusion, s32[2]{0:T(128)} %pad_add_fusion.1.refs_1_.own, bf16[3,192,1024]{2,1,0:T(8,128)(2,1)} %copy-done.9, ...), custom_call_target="tpu_custom_call" | custom-call | flops 1000000 | bytes 1000000 | tf_op jit(solution)/shard_map/feed_forward/pallas_call | solution.py:697
  304.2 4.6 all-to-all-start
  311.4 2.8 fusion.2
  318.8 15.3 %last_weights.1 = (bf16[2,384,1024]{2,1,0:T(8,128)(2,1)}, bf16[2,384,1024]{2,1,0:T(8,128)(2,1)}, bf16[2,384,1024]{2,1,0:T(8,128)(2,1)}, bf16[2,384,1024]{2,1,0:T...) custom-call(s32[2]{0:T(128)} %pad_add_fusion.1.refs_1_.own, ...), custom_call_target="tpu_custom_call" | custom-call | flops 1000000 | bytes 1000000 | tf_op jit(solution)/shard_map/last_weights/pallas_call | solution.py:523
  334.1 12.6 %all-to-all-done = bf16[4,256,1536]{2,1,0:T(8,128)(2,1)} async-done(((bf16[4,256,1536]{2,1,0:T(8,128)(2,1)}), bf16[4,256,1536]{2,1,0:T(8,128)(2,1)}, u32[]{:S(2)}, u32[]{:S(2)}) %all-to-all-start) | async-done | bytes 3145760 | tf_op jit(solution)/shard_map/all_to_all | solution.py:812
  352.8 14.7 %collective-permute-done.38 = bf16[2,2,96,1280]{3,2,1,0:T(8,128)(2,1)} collective-permute-done((bf16[2,2,96,1280]{3,2,1,0:T(8,128)(2,1)}, bf16[2,2,96,1280]{3,2,1,0:T(8,128)(2,1)}, u32[]{:S(2)}, u32[]{:S(2)}) %collective-permute-start.38) | collective-permute-done | bytes 983072 | tf_op jit(solution)/shard_map/ppermute | solution.py:809
  367.5 3.5 collective-permute-done.37.far
  371.9 4.7 all-to-all-start.1
  381.3 4.5 add_planes.1
  387.1 22.0 %attention_out.1 = (bf16[1024,384]{1,0:T(8,128)(2,1)}, bf16[2,1024,128]{2,1,0:T(8,128)(2,1)}, bf16[1536,768]{1,0:T(8,128)(2,1)}) custom-call(s32[2]{0:T(128)} %pad_add_fusion.refs_1_.own, bf16[256,1536]{1,0:T(8,128)(2,1)} %copy-done.17, bf16[256,1536]{1,0:T(8,128)(2,1)} %copy-done.26, bf16[256,1536]{1,0:T(8,128)(2,1)} %collective-permute-done.40.other_near, ...), custom_call_target="tpu_custom_call" | custom-call | flops 1000000 | bytes 1000000 | tf_op jit(solution)/shard_map/attention_out/pallas_call | solution.py:360
  418.1 10.3 %projection_out.1 = (bf16[1536,256]{1,0:T(8,128)(2,1)}, bf16[256,1536]{1,0:T(8,128)(2,1)}, bf16[256,1536]{1,0:T(8,128)(2,1)}, bf16[256,1536]{1,0:T(8,128)(2,1)}, bf16[256,1536]{1,0:T(8,128)(2,1)}) custom-call(s32[2]{0:T(128)} %pad_add_fusion.refs_1_.own, bf16[1024,384]{1,0:T(8,128)(2,1)} %get-tuple-element.218.grad_q, ...), custom_call_target="tpu_custom_call" | custom-call | flops 1000000 | bytes 1000000 | tf_op jit(solution)/shard_map/projection_out/pallas_call | solution.py:473
  428.5 2.6 add_bitcast_fusion.5
  435.7 2.9 fusion.5
  444.2 3.5 fusion.1
  448.8 4.5 all-to-all-start.2
  458.0 3.8 convert_reduce_fusion
  461.8 19.2 %collective-permute-done.56 = bf16[3,2,96,1024]{3,2,1,0:T(8,128)(2,1)} collective-permute-done((bf16[3,2,96,1024]{3,2,1,0:T(8,128)(2,1)}, bf16[3,2,96,1024]{3,2,1,0:T(8,128)(2,1)}, u32[]{:S(2)}, u32[]{:S(2)}) %collective-permute-start.56) | collective-permute-done | bytes 1179680 | tf_op jit(solution)/shard_map/ppermute | solution.py:809
  485.6 3.1 collective-permute-start.59
  492.2 4.3 all-to-all-start.3
  498.9 2.9 collective-permute-done.58
  507.0 5.5 %collective-permute-done.55 = bf16[2,2,48,768]{3,2,1,0:T(8,128)(2,1)} collective-permute-done((bf16[2,2,48,768]{3,2,1,0:T(8,128)(2,1)S(1)}, bf16[2,2,48,768]{3,2,1,0:T(8,128)(2,1)}, u32[]{:S(2)}, u32[]{:S(2)}) %collective-permute-start.55) | collective-permute-done | bytes 294944 | tf_op jit(solution)/shard_map/ppermute | solution.py:809
  516.7 3.5 all-to-all-start.4
  520.2 5.0 fusion.12
  525.2 4.8 assemble.1
  (259 shorter events, 113.5 us)
Async XLA Ops:
  7.3 42.0 %collective-permute-start.7 = (bf16[3,192,1280]{2,1,0:T(8,128)(2,1)}, bf16[3,192,1280]{2,1,0:T(8,128)(2,1)}, u32[]{:S(2)}, u32[]{:S(2)}) collective-permute-start(bf16[3,192,1280]{2,1,0:T(8,128)(2,1)} %cut_columns.4), channel_id=1, source_target_pairs={{0,1},{9,8},{2,3},{11,10},{4,5},{13,12},{6,7},{15,14},{16,17},{25,... | collective-permute-start | bytes 4423688 | tf_op jit(solution)/shard_map/ppermute | solution.py:803
  17.3 30.0 %collective-permute-start.8 = (bf16[256,1536]{1,0:T(8,128)(2,1)S(1)}, bf16[256,1536]{1,0:T(8,128)(2,1)}, u32[]{:S(2)}, u32[]{:S(2)}) collective-permute-start(bf16[256,1536]{1,0:T(8,128)(2,1)S(1)} %bitcast.215), channel_id=1, source_target_pairs={{0,16},{16,0},{1,17},{17,1},{2,18},{18,2},{3,19},{19,3},{4,20},{20... | collective-permute-start | bytes 2359304 | tf_op jit(solution)/shard_map/ppermute | solution.py:791
  18.8 26.9 %collective-permute-start = (bf16[208,1024]{1,0:T(8,128)(2,1)S(1)}, bf16[208,1024]{1,0:T(8,128)(2,1)}, u32[]{:S(2)}, u32[]{:S(2)}) collective-permute-start(bf16[208,1024]{1,0:T(8,128)(2,1)S(1)} %fusion.25.refs_2_), channel_id=1, source_target_pairs={{0,2},{2,6},{4,0},{6,4},{1,3},{3,7},{5,1},{7,5},{8,10},{10,14},{12... | collective-permute-start | bytes 1277960 | tf_op jit(solution)/shard_map/ppermute | solution.py:806
  27.5 21.7 %collective-permute-start.6 = (bf16[208,1024]{1,0:T(8,128)(2,1)}, bf16[208,1024]{1,0:T(8,128)(2,1)}, u32[]{:S(2)}, u32[]{:S(2)}) collective-permute-start(bf16[208,1024]{1,0:T(8,128)(2,1)} %collective-permute-done.1.refs_4_), channel_id=1, source_target_pairs={{0,1},{1,0},{2,3},{3,2},{4,5},{5,4},{6,7},{7,6},{8,9},{9,8},{10,11... | collective-permute-start | bytes 1277960 | tf_op jit(solution)/shard_map/ppermute | solution.py:797
  27.6 21.7 %collective-permute-start.3 = (bf16[208,1024]{1,0:T(8,128)(2,1)}, bf16[208,1024]{1,0:T(8,128)(2,1)}, u32[]{:S(2)}, u32[]{:S(2)}) collective-permute-start(bf16[208,1024]{1,0:T(8,128)(2,1)} %collective-permute-done.1.refs_4_), channel_id=1, source_target_pairs={{2,0},{6,2},{0,4},{4,6},{3,1},{7,3},{1,5},{5,7},{10,8},{14,10},{8,... | collective-permute-start | bytes 1277960 | tf_op jit(solution)/shard_map/ppermute | solution.py:809
  45.7 30.9 %collective-permute-start.11 = (bf16[256,1536]{1,0:T(8,128)(2,1)S(1)}, bf16[256,1536]{1,0:T(8,128)(2,1)}, u32[]{:S(2)}, u32[]{:S(2)}) collective-permute-start(bf16[256,1536]{1,0:T(8,128)(2,1)S(1)} %bitcast.211), channel_id=1, source_target_pairs={{0,16},{16,0},{1,17},{17,1},{2,18},{18,2},{3,19},{19,3},{4,20},{20... | collective-permute-start | bytes 2359304 | tf_op jit(solution)/shard_map/ppermute | solution.py:791
  49.2 20.1 %collective-permute-start.5 = (bf16[208,1024]{1,0:T(8,128)(2,1)}, bf16[208,1024]{1,0:T(8,128)(2,1)}, u32[]{:S(2)}, u32[]{:S(2)}) collective-permute-start(bf16[208,1024]{1,0:T(8,128)(2,1)} %collective-permute-done.refs_3_), channel_id=1, source_target_pairs={{0,1},{1,0},{2,3},{3,2},{4,5},{5,4},{6,7},{7,6},{8,9},{9,8},{10,11... | collective-permute-start | bytes 1277960 | tf_op jit(solution)/shard_map/ppermute | solution.py:797
  50.6 25.4 %collective-permute-start.9 = (bf16[208,1024]{1,0:T(8,128)(2,1)}, bf16[208,1024]{1,0:T(8,128)(2,1)S(1)}, u32[]{:S(2)}, u32[]{:S(2)}) collective-permute-start(bf16[208,1024]{1,0:T(8,128)(2,1)} %collective-permute-done.3.refs_5_), channel_id=1, source_target_pairs={{0,1},{1,0},{2,3},{3,2},{4,5},{5,4},{6,7},{7,6},{8,9},{9,8},{10,11... | collective-permute-start | bytes 1277960 | tf_op jit(solution)/shard_map/ppermute | solution.py:797
  53.9 28.3 %collective-permute-start.10 = (bf16[256,1536]{1,0:T(8,128)(2,1)}, bf16[256,1536]{1,0:T(8,128)(2,1)S(1)}, u32[]{:S(2)}, u32[]{:S(2)}) collective-permute-start(bf16[256,1536]{1,0:T(8,128)(2,1)} %collective-permute-done.8.refs_11_), channel_id=1, source_target_pairs={{0,8},{8,0},{1,9},{9,1},{2,10},{10,2},{3,11},{11,3},{4,12},{12,4},... | collective-permute-start | bytes 2359304 | tf_op jit(solution)/shard_map/ppermute | solution.py:794
  60.8 62.6 %collective-permute-start.12 = (bf16[3,192,1280]{2,1,0:T(8,128)(2,1)}, bf16[3,192,1280]{2,1,0:T(8,128)(2,1)}, u32[]{:S(2)}, u32[]{:S(2)}) collective-permute-start(bf16[3,192,1280]{2,1,0:T(8,128)(2,1)} %broadcast_select_fusion.refs_2_), channel_id=1, source_target_pairs={{0,2},{2,6},{4,0},{6,4},{1,3},{3,7},{5,1},{7,5},{8,10},{10,14},{12... | collective-permute-start | bytes 4423688 | tf_op jit(solution)/shard_map/ppermute | solution.py:806
  69.3 54.1 %collective-permute-start.13 = (bf16[3,192,1280]{2,1,0:T(8,128)(2,1)}, bf16[3,192,1280]{2,1,0:T(8,128)(2,1)}, u32[]{:S(2)}, u32[]{:S(2)}) collective-permute-start(bf16[3,192,1280]{2,1,0:T(8,128)(2,1)} %broadcast_select_fusion.refs_2_), channel_id=1, source_target_pairs={{2,0},{6,2},{0,4},{4,6},{3,1},{7,3},{1,5},{5,7},{10,8},{14,10},{8,... | collective-permute-start | bytes 4423688 | tf_op jit(solution)/shard_map/ppermute | solution.py:809
  76.0 47.5 %collective-permute-start.16 = (bf16[3,192,1280]{2,1,0:T(8,128)(2,1)}, bf16[3,192,1280]{2,1,0:T(8,128)(2,1)}, u32[]{:S(2)}, u32[]{:S(2)}) collective-permute-start(bf16[3,192,1280]{2,1,0:T(8,128)(2,1)} %broadcast_select_fusion.refs_2_), channel_id=1, source_target_pairs={{0,8},{8,0},{1,9},{9,1},{2,10},{10,2},{3,11},{11,3},{4,12},{12,4},... | collective-permute-start | bytes 4423688 | tf_op jit(solution)/shard_map/ppermute | solution.py:794
  76.6 46.8 %collective-permute-start.14 = (bf16[3,192,1024]{2,1,0:T(8,128)(2,1)}, bf16[3,192,1024]{2,1,0:T(8,128)(2,1)}, u32[]{:S(2)}, u32[]{:S(2)}) collective-permute-start(bf16[3,192,1024]{2,1,0:T(8,128)(2,1)} %cut_columns.6), channel_id=1, source_target_pairs={{0,1},{9,8},{2,3},{11,10},{4,5},{13,12},{6,7},{15,14},{16,17},{25,... | collective-permute-start | bytes 3538952 | tf_op jit(solution)/shard_map/ppermute | solution.py:803
  82.2 30.9 %collective-permute-start.15 = (bf16[256,1536]{1,0:T(8,128)(2,1)S(1)}, bf16[256,1536]{1,0:T(8,128)(2,1)S(1)}, u32[]{:S(2)}, u32[]{:S(2)}) collective-permute-start(bf16[256,1536]{1,0:T(8,128)(2,1)S(1)} %bitcast.212), channel_id=1, source_target_pairs={{0,1},{1,0},{2,3},{3,2},{4,5},{5,4},{6,7},{7,6},{8,9},{9,8},{10,11... | collective-permute-start | bytes 2359304 | tf_op jit(solution)/shard_map/ppermute | solution.py:797
  127.3 19.6 %collective-permute-start.19 = (bf16[256,1536]{1,0:T(8,128)(2,1)S(1)}, bf16[256,1536]{1,0:T(8,128)(2,1)S(1)}, u32[]{:S(2)}, u32[]{:S(2)}) collective-permute-start(bf16[256,1536]{1,0:T(8,128)(2,1)S(1)} %add_convert_fusion.4), channel_id=1, source_target_pairs={{0,16},{16,0},{1,17},{17,1},{2,18},{18,2},{3,19},{19,3},{4,20},{20... | collective-permute-start | bytes 2359304 | tf_op jit(solution)/shard_map/ppermute | solution.py:791
  127.9 19.5 %collective-permute-start.20 = (bf16[256,1536]{1,0:T(8,128)(2,1)}, bf16[256,1536]{1,0:T(8,128)(2,1)S(1)}, u32[]{:S(2)}, u32[]{:S(2)}) collective-permute-start(bf16[256,1536]{1,0:T(8,128)(2,1)} %collective-permute-done.11.refs_15_), channel_id=1, source_target_pairs={{0,1},{1,0},{2,3},{3,2},{4,5},{5,4},{6,7},{7,6},{8,9},{9,8},{10,11... | collective-permute-start | bytes 2359304 | tf_op jit(solution)/shard_map/ppermute | solution.py:797
  129.4 34.0 %collective-permute-start.24 = (bf16[3,192,1280]{2,1,0:T(8,128)(2,1)}, bf16[3,192,1280]{2,1,0:T(8,128)(2,1)S(1)}, u32[]{:S(2)}, u32[]{:S(2)}) collective-permute-start(bf16[3,192,1280]{2,1,0:T(8,128)(2,1)} %collective-permute-done.13.refs_4_), channel_id=1, source_target_pairs={{2,0},{6,2},{0,4},{4,6},{3,1},{7,3},{1,5},{5,7},{10,8},{14,10},{8,... | collective-permute-start | bytes 4423688 | tf_op jit(solution)/shard_map/ppermute | solution.py:809
  148.6 20.5 %collective-permute-start.27 = (bf16[256,1536]{1,0:T(8,128)(2,1)S(1)}, bf16[256,1536]{1,0:T(8,128)(2,1)S(1)}, u32[]{:S(2)}, u32[]{:S(2)}) collective-permute-start(bf16[256,1536]{1,0:T(8,128)(2,1)S(1)} %multiply_convert_fusion.refs_10_), channel_id=1, source_target_pairs={{0,16},{16,0},{1,17},{17,1},{2,18},{18,2},{3,19},{19,3},{4,20},{20... | collective-permute-start | bytes 2359304 | tf_op jit(solution)/shard_map/ppermute | solution.py:791
  150.2 34.0 %collective-permute-start.28 = (bf16[256,1536]{1,0:T(8,128)(2,1)S(1)}, bf16[256,1536]{1,0:T(8,128)(2,1)S(1)}, u32[]{:S(2)}, u32[]{:S(2)}) collective-permute-start(bf16[256,1536]{1,0:T(8,128)(2,1)S(1)} %multiply_convert_fusion.refs_10_), channel_id=1, source_target_pairs={{0,1},{1,0},{2,3},{3,2},{4,5},{5,4},{6,7},{7,6},{8,9},{9,8},{10,11... | collective-permute-start | bytes 2359304 | tf_op jit(solution)/shard_map/ppermute | solution.py:797
  151.7 33.5 %collective-permute-start.29 = (bf16[256,1536]{1,0:T(8,128)(2,1)S(1)}, bf16[256,1536]{1,0:T(8,128)(2,1)S(1)}, u32[]{:S(2)}, u32[]{:S(2)}) collective-permute-start(bf16[256,1536]{1,0:T(8,128)(2,1)S(1)} %multiply_convert_fusion.refs_10_), channel_id=1, source_target_pairs={{0,17},{1,16},{16,1},{17,0},{2,19},{3,18},{18,3},{19,2},{4,21},{5,... | collective-permute-start | bytes 2359304 | tf_op jit(solution)/shard_map/ppermute | solution.py:800
  152.2 38.1 %collective-permute-start.25 = (bf16[3,192,1280]{2,1,0:T(8,128)(2,1)}, bf16[3,192,1280]{2,1,0:T(8,128)(2,1)}, u32[]{:S(2)}, u32[]{:S(2)}) collective-permute-start(bf16[3,192,1280]{2,1,0:T(8,128)(2,1)} %collective-permute-done.12.refs_3_), channel_id=1, source_target_pairs={{0,8},{8,0},{1,9},{9,1},{2,10},{10,2},{3,11},{11,3},{4,12},{12,4},... | collective-permute-start | bytes 4423688 | tf_op jit(solution)/shard_map/ppermute | solution.py:794
  163.3 26.9 %collective-permute-start.26 = (bf16[3,192,1280]{2,1,0:T(8,128)(2,1)}, bf16[3,192,1280]{2,1,0:T(8,128)(2,1)}, u32[]{:S(2)}, u32[]{:S(2)}) collective-permute-start(bf16[3,192,1280]{2,1,0:T(8,128)(2,1)} %collective-permute-done.13.refs_4_), channel_id=1, source_target_pairs={{0,8},{8,0},{1,9},{9,1},{2,10},{10,2},{3,11},{11,3},{4,12},{12,4},... | collective-permute-start | bytes 4423688 | tf_op jit(solution)/shard_map/ppermute | solution.py:794
  186.3 54.4 %collective-permute-start.21 = (bf16[3,192,1024]{2,1,0:T(8,128)(2,1)S(1)}, bf16[3,192,1024]{2,1,0:T(8,128)(2,1)}, u32[]{:S(2)}, u32[]{:S(2)}) collective-permute-start(bf16[3,192,1024]{2,1,0:T(8,128)(2,1)S(1)} %broadcast_select_fusion.1.refs_2_), channel_id=1, source_target_pairs={{0,2},{2,6},{4,0},{6,4},{1,3},{3,7},{5,1},{7,5},{8,10},{10,14},{12... | collective-permute-start | bytes 3538952 | tf_op jit(solution)/shard_map/ppermute | solution.py:806
  187.6 53.2 %collective-permute-start.22 = (bf16[3,192,1024]{2,1,0:T(8,128)(2,1)S(1)}, bf16[3,192,1024]{2,1,0:T(8,128)(2,1)}, u32[]{:S(2)}, u32[]{:S(2)}) collective-permute-start(bf16[3,192,1024]{2,1,0:T(8,128)(2,1)S(1)} %broadcast_select_fusion.1.refs_2_), channel_id=1, source_target_pairs={{2,0},{6,2},{0,4},{4,6},{3,1},{7,3},{1,5},{5,7},{10,8},{14,10},{8,... | collective-permute-start | bytes 3538952 | tf_op jit(solution)/shard_map/ppermute | solution.py:809
  241.9 29.1 %collective-permute-start.23 = (bf16[3,192,1024]{2,1,0:T(8,128)(2,1)}, bf16[3,192,1024]{2,1,0:T(8,128)(2,1)}, u32[]{:S(2)}, u32[]{:S(2)}) collective-permute-start(bf16[3,192,1024]{2,1,0:T(8,128)(2,1)} %collective-permute-done.22.refs_4_), channel_id=1, source_target_pairs={{2,0},{6,2},{0,4},{4,6},{3,1},{7,3},{1,5},{5,7},{10,8},{14,10},{8,... | collective-permute-start | bytes 3538952 | tf_op jit(solution)/shard_map/ppermute | solution.py:809
  260.7 43.6 %collective-permute-start.36 = (bf16[3,2,96,1280]{3,2,1,0:T(8,128)(2,1)S(1)}, bf16[3,2,96,1280]{3,2,1,0:T(8,128)(2,1)}, u32[]{:S(2)}, u32[]{:S(2)}) collective-permute-start(bf16[3,2,96,1280]{3,2,1,0:T(8,128)(2,1)S(1)} %get-tuple-element.260), channel_id=1, source_target_pairs={{2,0},{6,2},{0,4},{4,6},{3,1},{7,3},{1,5},{5,7},{10,8},{14,10},{8,... | collective-permute-start | bytes 4423688 | tf_op jit(solution)/shard_map/ppermute | solution.py:809
  304.2 42.4 %all-to-all-start = ((bf16[4,256,1536]{2,1,0:T(8,128)(2,1)}), bf16[4,256,1536]{2,1,0:T(8,128)(2,1)}, u32[]{:S(2)}, u32[]{:S(2)}) async-start(bf16[4,256,1536]{2,1,0:T(8,128)(2,1)} %bitcast.227), calls=%async_computation | async-start | bytes 6291456 | tf_op jit(solution)/shard_map/all_to_all | solution.py:812
  310.8 42.0 %collective-permute-start.39 = (bf16[3,2,96,1280]{3,2,1,0:T(8,128)(2,1)}, bf16[3,2,96,1280]{3,2,1,0:T(8,128)(2,1)}, u32[]{:S(2)}, u32[]{:S(2)}) collective-permute-start(bf16[3,2,96,1280]{3,2,1,0:T(8,128)(2,1)} %get-tuple-element.261), channel_id=1, source_target_pairs={{0,2},{2,6},{4,0},{6,4},{1,3},{3,7},{5,1},{7,5},{8,10},{10,14},{12... | collective-permute-start | bytes 4423688 | tf_op jit(solution)/shard_map/ppermute | solution.py:806
  316.4 51.2 %collective-permute-start.38 = (bf16[2,2,96,1280]{3,2,1,0:T(8,128)(2,1)}, bf16[2,2,96,1280]{3,2,1,0:T(8,128)(2,1)}, u32[]{:S(2)}, u32[]{:S(2)}) collective-permute-start(bf16[2,2,96,1280]{3,2,1,0:T(8,128)(2,1)} %slice.123), channel_id=1, source_target_pairs={{2,0},{6,2},{0,4},{4,6},{3,1},{7,3},{1,5},{5,7},{10,8},{14,10},{8,... | collective-permute-start | bytes 2949128 | tf_op jit(solution)/shard_map/ppermute | solution.py:809
  351.6 19.4 %collective-permute-start.37 = (bf16[256,1536]{1,0:T(8,128)(2,1)S(1)}, bf16[256,1536]{1,0:T(8,128)(2,1)S(1)}, u32[]{:S(2)}, u32[]{:S(2)}) collective-permute-start(bf16[256,1536]{1,0:T(8,128)(2,1)S(1)} %fusion.41.near), channel_id=1, source_target_pairs={{0,16},{16,0},{1,17},{17,1},{2,18},{18,2},{3,19},{19,3},{4,20},{20... | collective-permute-start | bytes 2359304 | tf_op jit(solution)/shard_map/ppermute | solution.py:791
  352.3 29.0 %collective-permute-start.42 = (bf16[2,384,1024]{2,1,0:T(8,128)(2,1)}, bf16[2,384,1024]{2,1,0:T(8,128)(2,1)}, u32[]{:S(2)}, u32[]{:S(2)}) collective-permute-start(bf16[2,384,1024]{2,1,0:T(8,128)(2,1)} %get-tuple-element.198), channel_id=1, source_target_pairs={{0,8},{8,0},{1,9},{9,1},{2,10},{10,2},{3,11},{11,3},{4,12},{12,4},... | collective-permute-start | bytes 4718600 | tf_op jit(solution)/shard_map/ppermute | solution.py:794
  352.3 29.0 %collective-permute-start.43 = (bf16[2,384,1024]{2,1,0:T(8,128)(2,1)}, bf16[2,384,1024]{2,1,0:T(8,128)(2,1)}, u32[]{:S(2)}, u32[]{:S(2)}) collective-permute-start(bf16[2,384,1024]{2,1,0:T(8,128)(2,1)} %get-tuple-element.199), channel_id=1, source_target_pairs={{0,8},{8,0},{1,9},{9,1},{2,10},{10,2},{3,11},{11,3},{4,12},{12,4},... | collective-permute-start | bytes 4718600 | tf_op jit(solution)/shard_map/ppermute | solution.py:794
  352.8 28.4 %collective-permute-start.44 = (bf16[2,384,1024]{2,1,0:T(8,128)(2,1)}, bf16[2,384,1024]{2,1,0:T(8,128)(2,1)}, u32[]{:S(2)}, u32[]{:S(2)}) collective-permute-start(bf16[2,384,1024]{2,1,0:T(8,128)(2,1)} %get-tuple-element.200), channel_id=1, source_target_pairs={{0,8},{8,0},{1,9},{9,1},{2,10},{10,2},{3,11},{11,3},{4,12},{12,4},... | collective-permute-start | bytes 4718600 | tf_op jit(solution)/shard_map/ppermute | solution.py:794
  371.9 46.2 %all-to-all-start.1 = ((bf16[4,256,1536]{2,1,0:T(8,128)(2,1)}), bf16[4,256,1536]{2,1,0:T(8,128)(2,1)}, u32[]{:S(2)}, u32[]{:S(2)}) async-start(bf16[4,256,1536]{2,1,0:T(8,128)(2,1)} %bitcast.226), calls=%async_computation.1 | async-start | bytes 6291456 | tf_op jit(solution)/shard_map/all_to_all | solution.py:812
  385.8 42.6 %collective-permute-start.46 = (bf16[3,2,96,1024]{3,2,1,0:T(8,128)(2,1)}, bf16[3,2,96,1024]{3,2,1,0:T(8,128)(2,1)}, u32[]{:S(2)}, u32[]{:S(2)}) collective-permute-start(bf16[3,2,96,1024]{3,2,1,0:T(8,128)(2,1)} %get-tuple-element.206), channel_id=1, source_target_pairs={{2,0},{6,2},{0,4},{4,6},{3,1},{7,3},{1,5},{5,7},{10,8},{14,10},{8,... | collective-permute-start | bytes 3538952 | tf_op jit(solution)/shard_map/ppermute | solution.py:809
  411.7 28.8 %collective-permute-start.48 = (bf16[2,2,4,48,768]{4,3,1,0,2:T(8,128)(2,1)}, bf16[2,2,4,48,768]{4,3,1,0,2:T(8,128)(2,1)}, u32[]{:S(2)}, u32[]{:S(2)}) collective-permute-start(bf16[2,2,4,48,768]{4,3,1,0,2:T(8,128)(2,1)} %copy_bitcast_fusion), channel_id=1, source_target_pairs={{0,1},{1,0},{2,3},{3,2},{4,5},{5,4},{6,7},{7,6},{8,9},{9,8},{10,11... | collective-permute-start | bytes 3538952 | tf_op jit(solution)/shard_map/ppermute | solution.py:797
  415.4 28.7 %collective-permute-start.53 = (bf16[1,2,96,1280]{3,2,1,0:T(8,128)(2,1)}, bf16[1,2,96,1280]{3,2,1,0:T(8,128)(2,1)}, u32[]{:S(2)}, u32[]{:S(2)}) collective-permute-start(bf16[1,2,96,1280]{3,2,1,0:T(8,128)(2,1)} %slice.124), channel_id=1, source_target_pairs={{2,0},{6,2},{0,4},{4,6},{3,1},{7,3},{1,5},{5,7},{10,8},{14,10},{8,... | collective-permute-start | bytes 1474568 | tf_op jit(solution)/shard_map/ppermute | solution.py:809
  416.2 69.4 %collective-permute-start.54 = (bf16[3,2,96,1024]{3,2,1,0:T(8,128)(2,1)}, bf16[3,2,96,1024]{3,2,1,0:T(8,128)(2,1)}, u32[]{:S(2)}, u32[]{:S(2)}) collective-permute-start(bf16[3,2,96,1024]{3,2,1,0:T(8,128)(2,1)} %get-tuple-element.205), channel_id=1, source_target_pairs={{0,2},{2,6},{4,0},{6,4},{1,3},{3,7},{5,1},{7,5},{8,10},{10,14},{12... | collective-permute-start | bytes 3538952 | tf_op jit(solution)/shard_map/ppermute | solution.py:806
  438.6 42.4 %collective-permute-start.56 = (bf16[3,2,96,1024]{3,2,1,0:T(8,128)(2,1)}, bf16[3,2,96,1024]{3,2,1,0:T(8,128)(2,1)}, u32[]{:S(2)}, u32[]{:S(2)}) collective-permute-start(bf16[3,2,96,1024]{3,2,1,0:T(8,128)(2,1)} %fusion.5), channel_id=1, source_target_pairs={{2,0},{6,2},{0,4},{4,6},{3,1},{7,3},{1,5},{5,7},{10,8},{14,10},{8,... | collective-permute-start | bytes 3538952 | tf_op jit(solution)/shard_map/ppermute | solution.py:809
  442.4 41.5 %collective-permute-start.50 = (bf16[256,1536]{1,0:T(8,128)(2,1)}, bf16[256,1536]{1,0:T(8,128)(2,1)}, u32[]{:S(2)}, u32[]{:S(2)}) collective-permute-start(bf16[256,1536]{1,0:T(8,128)(2,1)} %add_convert_fusion.3), channel_id=1, source_target_pairs={{0,16},{16,0},{1,17},{17,1},{2,18},{18,2},{3,19},{19,3},{4,20},{20... | collective-permute-start | bytes 2359304 | tf_op jit(solution)/shard_map/ppermute | solution.py:791
  448.8 43.3 %all-to-all-start.2 = ((bf16[4,3,48,1280]{3,2,1,0:T(8,128)(2,1)}), bf16[4,3,48,1280]{3,2,1,0:T(8,128)(2,1)}, u32[]{:S(2)}, u32[]{:S(2)}) async-start(bf16[4,3,48,1280]{3,2,1,0:T(8,128)(2,1)} %bitcast.216), calls=%async_computation.2 | async-start | bytes 2949120 | tf_op jit(solution)/shard_map/all_to_all | solution.py:812
  453.9 27.8 %collective-permute-start.57 = (bf16[2,2,4,48,256]{4,3,1,0,2:T(8,128)(2,1)}, bf16[2,2,4,48,256]{4,3,1,0,2:T(8,128)(2,1)S(1)}, u32[]{:S(2)}, u32[]{:S(2)}) collective-permute-start(bf16[2,2,4,48,256]{4,3,1,0,2:T(8,128)(2,1)} %copy_bitcast_fusion.1), channel_id=1, source_target_pairs={{0,1},{1,0},{2,3},{3,2},{4,5},{5,4},{6,7},{7,6},{8,9},{9,8},{10,11... | collective-permute-start | bytes 1179656 | tf_op jit(solution)/shard_map/ppermute | solution.py:797
  455.8 40.6 %collective-permute-start.49 = (bf16[256,1536]{1,0:T(8,128)(2,1)}, bf16[256,1536]{1,0:T(8,128)(2,1)}, u32[]{:S(2)}, u32[]{:S(2)}) collective-permute-start(bf16[256,1536]{1,0:T(8,128)(2,1)} %get-tuple-element.234), channel_id=1, source_target_pairs={{0,8},{8,0},{1,9},{9,1},{2,10},{10,2},{3,11},{11,3},{4,12},{12,4},... | collective-permute-start | bytes 2359304 | tf_op jit(solution)/shard_map/ppermute | solution.py:794
  481.0 20.8 %collective-permute-start.51 = (bf16[2,2,48,768]{3,2,1,0:T(8,128)(2,1)}, bf16[2,2,48,768]{3,2,1,0:T(8,128)(2,1)}, u32[]{:S(2)}, u32[]{:S(2)}) collective-permute-start(bf16[2,2,48,768]{3,2,1,0:T(8,128)(2,1)} %get-tuple-element.263), channel_id=1, source_target_pairs={{0,2},{2,6},{4,0},{6,4},{1,3},{3,7},{5,1},{7,5},{8,10},{10,14},{12... | collective-permute-start | bytes 884744 | tf_op jit(solution)/shard_map/ppermute | solution.py:806
  481.7 20.1 %collective-permute-start.52 = (bf16[2,2,48,768]{3,2,1,0:T(8,128)(2,1)}, bf16[2,2,48,768]{3,2,1,0:T(8,128)(2,1)}, u32[]{:S(2)}, u32[]{:S(2)}) collective-permute-start(bf16[2,2,48,768]{3,2,1,0:T(8,128)(2,1)} %get-tuple-element.262), channel_id=1, source_target_pairs={{2,0},{6,2},{0,4},{4,6},{3,1},{7,3},{1,5},{5,7},{10,8},{14,10},{8,... | collective-permute-start | bytes 884744 | tf_op jit(solution)/shard_map/ppermute | solution.py:809
  485.6 16.2 %collective-permute-start.58 = (bf16[2,2,48,256]{3,2,1,0:T(8,128)(2,1)}, bf16[2,2,48,256]{3,2,1,0:T(8,128)(2,1)}, u32[]{:S(2)}, u32[]{:S(2)}) collective-permute-start(bf16[2,2,48,256]{3,2,1,0:T(8,128)(2,1)} %get-tuple-element.273), channel_id=1, source_target_pairs={{0,2},{2,6},{4,0},{6,4},{1,3},{3,7},{5,1},{7,5},{8,10},{10,14},{12... | collective-permute-start | bytes 294920 | tf_op jit(solution)/shard_map/ppermute | solution.py:806
  485.6 16.2 %collective-permute-start.59 = (bf16[2,2,48,256]{3,2,1,0:T(8,128)(2,1)}, bf16[2,2,48,256]{3,2,1,0:T(8,128)(2,1)}, u32[]{:S(2)}, u32[]{:S(2)}) collective-permute-start(bf16[2,2,48,256]{3,2,1,0:T(8,128)(2,1)} %get-tuple-element.272), channel_id=1, source_target_pairs={{2,0},{6,2},{0,4},{4,6},{3,1},{7,3},{1,5},{5,7},{10,8},{14,10},{8,... | collective-permute-start | bytes 294920 | tf_op jit(solution)/shard_map/ppermute | solution.py:809
  492.2 20.3 %all-to-all-start.3 = ((bf16[4,3,48,1024]{3,2,1,0:T(8,128)(2,1)}), bf16[4,3,48,1024]{3,2,1,0:T(8,128)(2,1)}, u32[]{:S(2)}, u32[]{:S(2)}) async-start(bf16[4,3,48,1024]{3,2,1,0:T(8,128)(2,1)} %bitcast.221), calls=%async_computation.3 | async-start | bytes 2359296 | tf_op jit(solution)/shard_map/all_to_all | solution.py:812
  (60 other events, 817.5 us)
